TPU v7x, 32 devices: a whole 2x2x4 slice. The times are simulated.
32 devices in a mesh: seq: 8 (over z, y), mp: 4 (over x, core).
Axes of the slice: x: 2, y: 2, z: 4, core: 2. Of those that a mesh axis runs over, the one named last changes fastest.
Arguments:
- fresh_queries: bfloat16 [512, 2048], P('seq', 'mp'), may hold values from -120 to 120
- fresh_keys: bfloat16 [512, 1024], P('seq', 'mp'), may hold values from -6 to 6
- fresh_values: bfloat16 [512, 1024], P('seq', 'mp'), may hold values from -6 to 6
- cache: bfloat16 [2, 512, 1024], P(None, 'seq', 'mp'), may hold values from -6 to 6
- pool_root: int32 [8, 32], replicated, may hold values from 0 to 1
- branch_owner: int32 [8], replicated, may hold values from 0 to 7, each once
- branch_len: int32 [8], replicated, may hold values from 1 to 32, 128 in all
- branch_root: int32 [8], replicated, may hold values from 0 to 1
- request_branch: int32 [8, 4], P('seq'), may hold values from 0 to 7
- token_request: int32 [8, 64], P('seq'), may hold values from 0 to 3, never falling along the last dimension, each value on 1 to 32 neighbouring positions
- residual: bfloat16 [512, 2048], P('seq'), may hold values from -1.5 to 1.5
- wo_t: bfloat16 [2048, 2048], P('seq', 'mp'), may hold values from -0.125 to 0.125
- norm_gain: float32 [2048], replicated, may hold values from 0.1 to 1.9
- w_qkv: bfloat16 [2048, 4096], P('seq', 'mp'), may hold values from -0.125 to 0.125
Outputs:
- attn: bfloat16 [512, 2048], P('seq', 'mp')
- stream: bfloat16 [512, 2048], P('seq')
- qkv_next: bfloat16 [512, 4096], P('seq', 'mp')
Inputs may be any that keep to these rules, and one draw needn't show every extreme that they name: `token_request`: in each index's row the request number never falls, and each request has 1 to 32 tokens. `branch_owner`: each index of seq holds exactly one branch. `branch_len`: the longest branch has 32 rows.
All inputs are finite; a program needn't handle non-finite values.
Results may differ from a plain program's by a relative error of at most 0.018.
Values may be sent and summed in bfloat16 or wider, within the bound.
No kernel may reach another device: no remote copies, remote signals or barrier semaphores. Data moves between devices by JAX's collectives and lax.ppermute only.
A program may use at most 64 MiB of HBM per device.

v0:
```python
import jax
import jax.numpy as jnp
from jax import lax
from jax.sharding import PartitionSpec as P

QUERY_HEADS = 16
KEY_VALUE_HEADS = 8
HEAD_SIZE = 128


def cache_tags(pool_root, branch_owner, branch_len, root_count, slot_count):
    owner_count = pool_root.shape[0]
    branch_count = branch_owner.shape[0]
    branch_ids = jnp.arange(branch_count, dtype=jnp.int32)
    owner_ids = jnp.arange(owner_count, dtype=jnp.int32)
    owned = jnp.sum(
        jnp.where(branch_owner[None, :] == owner_ids[:, None], branch_ids[None, :], 0), axis=1
    )
    owned_length = jnp.sum(
        jnp.where(branch_ids[None, :] == owned[:, None], branch_len[None, :], 0), axis=1
    )
    slot_ids = jnp.arange(slot_count, dtype=jnp.int32)
    branch_tags = jnp.where(
        slot_ids[None, :] < owned_length[:, None], root_count + owned[:, None], -1
    )
    return jnp.concatenate([pool_root, branch_tags], axis=1).reshape(-1)


def absorb(running, query_rows, key_row_block, value_rows, visible, score_scale):
    peak_old, total, mixed = running
    scores = (
        jnp.einsum("tkgd,rkd->tkgr", query_rows, key_row_block, preferred_element_type=jnp.float32)
        * score_scale
    )
    seen = visible[:, None, None, :]
    peak_new = jnp.maximum(peak_old, jnp.max(jnp.where(seen, scores, -jnp.inf), axis=-1))
    factor = jnp.exp(peak_old - peak_new)
    weights_full = jnp.where(seen, jnp.exp(scores - peak_new[..., None]), 0.0)
    total = total * factor + jnp.sum(weights_full, axis=-1)
    mixed = mixed * factor[..., None] + jnp.einsum(
        "tkgr,rkd->tkgd",
        weights_full.astype(jnp.bfloat16),
        value_rows,
        preferred_element_type=jnp.float32,
    )
    return (peak_new, total, mixed)


def on_device(
    fresh_queries,
    fresh_keys,
    fresh_values,
    cache,
    pool_root,
    branch_owner,
    branch_len,
    branch_root,
    request_branch,
    token_request,
    residual,
    wo_t,
    norm_gain,
    w_qkv,
):
    seq_count = lax.axis_size("seq")
    root_count = seq_count // 4
    tok_rows = fresh_queries.shape[0]
    kv_local = fresh_keys.shape[1] // HEAD_SIZE
    query_groups = QUERY_HEADS // KEY_VALUE_HEADS
    score_scale = HEAD_SIZE ** (-0.5)
    slot_count = cache.shape[1] - pool_root.shape[1]
    tags = cache_tags(pool_root, branch_owner, branch_len, root_count, slot_count)
    requests = token_request[0]
    local_branches = request_branch[0]
    request_ids = jnp.arange(local_branches.shape[0], dtype=jnp.int32)
    token_branch = jnp.sum(
        jnp.where(requests[:, None] == request_ids[None, :], local_branches[None, :], 0), axis=1
    )
    branch_ids = jnp.arange(branch_root.shape[0], dtype=jnp.int32)
    token_root = jnp.sum(
        jnp.where(token_branch[:, None] == branch_ids[None, :], branch_root[None, :], 0), axis=1
    )
    query_rows = fresh_queries.reshape(tok_rows, kv_local, query_groups, HEAD_SIZE)
    incoming_keys = fresh_keys.reshape(tok_rows, kv_local, HEAD_SIZE)
    incoming_values = fresh_values.reshape(tok_rows, kv_local, HEAD_SIZE)
    positions = jnp.arange(tok_rows, dtype=jnp.int32)
    own_visible = (requests[None, :] == requests[:, None]) & (
        positions[None, :] <= positions[:, None]
    )
    start_state = (
        jnp.full((tok_rows, kv_local, query_groups), -jnp.inf, jnp.float32),
        jnp.zeros((tok_rows, kv_local, query_groups), jnp.float32),
        jnp.zeros((tok_rows, kv_local, query_groups, HEAD_SIZE), jnp.float32),
    )
    start_state = absorb(
        start_state, query_rows, incoming_keys, incoming_values, own_visible, score_scale
    )
    state = start_state
    piece = lax.all_gather(cache, "seq", axis=1, tiled=True)
    rows = piece.shape[1]
    block = 512 if rows > 512 and rows % 512 == 0 else rows
    key_blocks = piece[0].reshape(rows // block, block, kv_local, HEAD_SIZE)
    value_blocks = piece[1].reshape(rows // block, block, kv_local, HEAD_SIZE)
    tag_blocks = tags.reshape(rows // block, block)

    def one_block(running, parts):
        key_row_block, value_rows, tag_rows = parts
        visible = (tag_rows[None, :] == token_root[:, None]) | (
            tag_rows[None, :] == root_count + token_branch[:, None]
        )
        updated = absorb(running, query_rows, key_row_block, value_rows, visible, score_scale)
        return (updated, None)

    state, unused = lax.scan(one_block, state, (key_blocks, value_blocks, tag_blocks))
    peak_final, total_final, mixed_final = state
    attn = (
        (mixed_final / total_final[..., None])
        .reshape(tok_rows, kv_local * query_groups * HEAD_SIZE)
        .astype(jnp.bfloat16)
    )
    partial_value = lax.dot_general(
        attn,
        lax.all_gather(wo_t, "seq", axis=0, tiled=True),
        (((1,), (1,)), ((), ())),
        preferred_element_type=jnp.float32,
    )
    summed = lax.psum(partial_value.astype(jnp.bfloat16), "mp").astype(jnp.float32)
    stream = (residual.astype(jnp.float32) + summed).astype(jnp.bfloat16)
    widened = stream.astype(jnp.float32)
    mean_square = jnp.mean(widened * widened, axis=-1, keepdims=True)
    normed = (widened * lax.rsqrt(mean_square + 1e-06) * norm_gain[None, :]).astype(jnp.bfloat16)
    qkv_sum = jnp.dot(
        normed, lax.all_gather(w_qkv, "seq", axis=0, tiled=True), preferred_element_type=jnp.float32
    )
    return (attn, stream, qkv_sum.astype(jnp.bfloat16))


def solution(mesh):
    return jax.shard_map(
        on_device,
        mesh=mesh,
        in_specs=(
            P("seq", "mp"),
            P("seq", "mp"),
            P("seq", "mp"),
            P(None, "seq", "mp"),
            P(),
            P(),
            P(),
            P(),
            P("seq", None),
            P("seq", None),
            P("seq", None),
            P("seq", "mp"),
            P(),
            P("seq", "mp"),
        ),
        out_specs=(P("seq", "mp"), P("seq", None), P("seq", "mp")),
        check_vma=False,
    )
```

profile of v0, /device:TPU:0, one launch (start us, length us, event | category | flops | bytes accessed | tf_op | source)
XLA Modules:
  0.0 183.8 jit_solution(1950141210834433936)
XLA Ops:
  7.2 0.7 all-gather.3.cloned.1.call-update
  8.0 0.8 select_reduce_fusion.4
  8.8 0.8 select_reduce_fusion.3
  9.6 0.1 fusion.30
  9.7 0.8 pad_add_fusion
  10.4 0.1 eq.129
  10.5 0.9 copy.46
  11.4 33.8 %all_gather.9 = bf16[2,512,256]{2,0,1:T(2,128)(2,1)S(1)} all-gather(bf16[2,64,256]{2,0,1:T(2,128)(2,1)S(1)} %copy.46), channel_id=1, replica_groups=mesh['seq'=8,'mp'=4] {'seq'}, dimensions={1}, use_global_device_ids=true | all-gather | bytes 589824 | tf_op jit(solution)/shard_map/all_gather | solution.py:99
  45.2 0.7 fusion.33
  45.9 0.7 copy.66
  46.6 0.9 reshape.162
  47.5 0.8 reshape.161
  48.3 0.8 reshape.163
  49.1 0.7 copy.67
  49.8 0.1 select_reduce_fusion.5
  49.9 0.1 select_reduce_fusion.2
  50.0 0.1 fusion.29
  50.0 0.1 compare_or_fusion
  50.1 0.2 select_reduce_fusion.1
  50.3 0.3 select_reduce_fusion
  50.7 0.2 fusion.10
  51.0 0.2 fusion.4
  51.2 0.3 fusion.6
  51.5 0.1 copy.52
  51.6 11.9 %all-gather.3.cloned.1.call-done = bf16[2048,512]{1,0:T(8,128)(2,1)} async-done(((bf16[256,512]{1,0:T(8,128)(2,1)}), bf16[2048,512]{1,0:T(8,128)(2,1)}) %all-gather.3.cloned.1.call-update) | async-done | bytes 2097168 | tf_op jit(solution)/shard_map/all_gather | solution.py:123
  63.5 3.0 %convolution_convert_fusion = bf16[64,2048]{1,0:T(8,128)(2,1)} fusion(bf16[64,512]{1,0:T(8,128)(2,1)S(1)} %convert_element_type.37, bf16[2048,512]{1,0:T(8,128)(2,1)} %all-gather.3.cloned.1.call-done), kind=kOutput, calls=%fused_computation | convolution fusion | flops 134348800 | bytes 2424832 | tf_op jit(solution)/shard_map/dot_general | solution.py:121
  66.6 0.0 all-gather.5.cloned.1.call-start
  66.6 0.7 all-gather.5.cloned.1.call-update
  67.3 30.4 %all-reduce.2.cloned.1.call-done = bf16[64,2048]{1,0:T(8,128)(2,1)} async-done(((bf16[64,2048]{1,0:T(8,128)(2,1)}), bf16[64,2048]{1,0:T(8,128)(2,1)}) %all-reduce.2.cloned.1.call-update) | async-done | bytes 262160 | tf_op jit(solution)/shard_map/psum | solution.py:127
  97.7 1.1 fusion.7
  98.9 74.6 %all-gather.5.cloned.1.call-done = bf16[2048,1024]{1,0:T(8,128)(2,1)} async-done(((bf16[256,1024]{1,0:T(8,128)(2,1)}), bf16[2048,1024]{1,0:T(8,128)(2,1)}) %all-gather.5.cloned.1.call-update) | async-done | bytes 4194320 | tf_op jit(solution)/shard_map/all_gather | solution.py:133
  173.5 3.7 %convolution_convert_fusion.1 = bf16[64,1024]{1,0:T(8,128)(2,1)} fusion(bf16[2048,1024]{1,0:T(8,128)(2,1)} %all-gather.5.cloned.1.call-done, bf16[64,2048]{1,0:T(8,128)(2,1)S(1)} %get-tuple-element.24, f32[2048]{0:T(1024)S(1)} %copy-done.3, f32[64]{0:T(128)S(1)} %add_rsqrt_fusion), kind=kOutput, calls=%fused_computation.3 | convolution fusion | flops 269025280 | bytes 4595968 | tf_op jit(solution)/shard_map/dot_general | solution.py:132
  (24 shorter events, 0.2 us)
Async XLA Ops:
  7.2 42.6 %copy-start.4 = (s32[1,64]{1,0:T(1,128)S(1)}, s32[1,64]{1,0:T(1,128)}, u32[]{:S(2)}) copy-start(s32[1,64]{1,0:T(1,128)} %param.23) | copy-start | bytes 772
  7.2 42.6 %copy-start.5 = (s32[1,4]{1,0:T(1,128)S(1)}, s32[1,4]{1,0:T(1,128)}, u32[]{:S(2)}) copy-start(s32[1,4]{1,0:T(1,128)} %param.22) | copy-start | bytes 52
  7.2 42.7 %copy-start.6 = (s32[8]{0:T(128)S(1)}, s32[8]{0:T(128)}, u32[]{:S(2)}) copy-start(s32[8]{0:T(128)} %param.21) | copy-start | bytes 100
  7.2 56.3 %all-gather.3.cloned.1.call-start = ((), (), s32[]{:S(2)}) async-start(), calls=%async_computation | async-start | bytes 2359296 | tf_op jit(solution)/shard_map/all_gather | solution.py:123
  7.9 89.8 %all-reduce.2.cloned.1.call-start = ((), (), s32[]{:S(2)}) async-start(), calls=%async_computation.1 | async-start | bytes 524288 | tf_op jit(solution)/shard_map/psum | solution.py:127
  46.6 51.1 %copy-start.2 = (bf16[64,2048]{1,0:T(8,128)(2,1)S(1)}, bf16[64,2048]{1,0:T(8,128)(2,1)}, u32[]{:S(2)}) copy-start(bf16[64,2048]{1,0:T(8,128)(2,1)} %param.24) | copy-start | bytes 786436
  49.1 124.5 %copy-start.3 = (f32[2048]{0:T(1024)S(1)}, f32[2048]{0:T(1024)}, u32[]{:S(2)}) copy-start(f32[2048]{0:T(1024)} %param.26) | copy-start | bytes 24580
  51.6 125.7 %copy-start.1 = (bf16[64,512]{1,0:T(8,128)(2,1)}, bf16[64,512]{1,0:T(8,128)(2,1)S(1)}, u32[]{:S(2)}) copy-start(bf16[64,512]{1,0:T(8,128)(2,1)S(1)} %convert_element_type.37) | copy-start | bytes 196612
  66.6 107.0 %all-gather.5.cloned.1.call-start = ((), (), s32[]{:S(2)}) async-start(), calls=%async_computation.2 | async-start | bytes 4718592 | tf_op jit(solution)/shard_map/all_gather | solution.py:133
  98.9 78.4 %copy-start = (bf16[64,2048]{1,0:T(8,128)(2,1)}, bf16[64,2048]{1,0:T(8,128)(2,1)S(1)}, u32[]{:S(2)}) copy-start(bf16[64,2048]{1,0:T(8,128)(2,1)S(1)} %get-tuple-element.24) | copy-start | bytes 786436
Sparse Core Ops, SparseCore 0:
  10.2 53.2 all-gather.2
  66.7 30.9 all-reduce.1
  100.1 73.4 all-gather.4
where the time goes:
time: 184 us
  waiting for transfers between devices  118 us (64%)
  blocking collectives  33.8 us (18%)
  between operations  13.9 us (8%)
  matrix products  7.8 us (4%)
  local copies, waits for them, and re-layouts  5.66 us (3%)
  other arithmetic  4.24 us (2%)
    all_gather x1, waiting for transfers between devices, on_device(): lax.all_gather(w_qkv, 'seq', axis=0, tiled=True)  74.6 us
    all_gather x1, blocking collectives, on_device(): piece = lax.all_gather(cache, 'seq', axis=1, tiled=True)  33.8 us
    psum x1, waiting for transfers between devices, on_device(): lax.psum(partial_value.astype(jnp.bfloat16), 'mp').astype(jnp.float32)  30.4 us
    all_gather x1, waiting for transfers between devices, on_device(): lax.all_gather(wo_t, 'seq', axis=0, tiled=True)  11.9 us
    dot_general x1, matrix products, on_device(): jnp.dot(normed, lax.all_gather(w_qkv, 'seq', axis=0, tiled=True), preferr...  3.73 us
  transfers between devices with their start and end apart: 3, of which 3 were waited for; matrix products, arithmetic and copies ran while one was open for 6% of the time, Pallas kernels for 0%

commit v1 on v0

--- a/solution.py
+++ b/solution.py
@@ -1,18 +1,24 @@
+import functools
+
 import jax
 import jax.numpy as jnp
 from jax import lax
+from jax.experimental import pallas as pl
+from jax.experimental.pallas import tpu as pltpu
 from jax.sharding import PartitionSpec as P
 
 QUERY_HEADS = 16
 KEY_VALUE_HEADS = 8
 HEAD_SIZE = 128
-
-
-def cache_tags(pool_root, branch_owner, branch_len, root_count, slot_count):
-    owner_count = pool_root.shape[0]
+NT = (((1,), (1,)), ((), ()))
+TN = (((0,), (0,)), ((), ()))
+F32 = jnp.float32
+BF16 = jnp.bfloat16
+
+
+def cache_tags(pool_root, branch_owner, branch_len, root_count, slot_count, owner_ids):
     branch_count = branch_owner.shape[0]
     branch_ids = jnp.arange(branch_count, dtype=jnp.int32)
-    owner_ids = jnp.arange(owner_count, dtype=jnp.int32)
     owned = jnp.sum(
         jnp.where(branch_owner[None, :] == owner_ids[:, None], branch_ids[None, :], 0), axis=1
     )
@@ -24,6 +30,225 @@
         slot_ids[None, :] < owned_length[:, None], root_count + owned[:, None], -1
     )
     return jnp.concatenate([pool_root, branch_tags], axis=1).reshape(-1)
+
+
+def token_nodes(request_branch, token_request, branch_root):
+    requests = token_request[0]
+    local_branches = request_branch[0]
+    request_ids = jnp.arange(local_branches.shape[0], dtype=jnp.int32)
+    token_branch = jnp.sum(
+        jnp.where(requests[:, None] == request_ids[None, :], local_branches[None, :], 0), axis=1
+    )
+    branch_ids = jnp.arange(branch_root.shape[0], dtype=jnp.int32)
+    token_root = jnp.sum(
+        jnp.where(token_branch[:, None] == branch_ids[None, :], branch_root[None, :], 0), axis=1
+    )
+    return requests, token_branch, token_root
+
+
+def attend_kernel(*refs):
+    q_ref, kf_ref, vf_ref, bias_ref = refs[:4]
+    cache_refs, out_ref = refs[4:-1], refs[-1]
+    tok = q_ref.shape[0]
+    bias = bias_ref[...]
+    for k in range(kf_ref.shape[1] // HEAD_SIZE):
+        lanes = slice(k * HEAD_SIZE, (k + 1) * HEAD_SIZE)
+        first = slice(2 * k * HEAD_SIZE, (2 * k + 1) * HEAD_SIZE)
+        second = slice((2 * k + 1) * HEAD_SIZE, (2 * k + 2) * HEAD_SIZE)
+        keys = jnp.concatenate([kf_ref[:, lanes]] + [c[0, :, lanes] for c in cache_refs], axis=0)
+        values = jnp.concatenate([vf_ref[:, lanes]] + [c[1, :, lanes] for c in cache_refs], axis=0)
+        queries = jnp.concatenate([q_ref[:, first], q_ref[:, second]], axis=0)
+        scores = (
+            lax.dot_general(keys, queries, NT, preferred_element_type=F32) * HEAD_SIZE**-0.5 + bias
+        )
+        peak = jnp.max(scores, axis=0, keepdims=True)
+        prob = jnp.exp(scores - peak)
+        total = jnp.sum(prob, axis=0, keepdims=True)
+        mixed = lax.dot_general(values, prob.astype(BF16), TN, preferred_element_type=F32)
+        attn = (mixed / total).T.astype(BF16)
+        out_ref[:, first] = attn[:tok]
+        out_ref[:, second] = attn[tok:]
+
+
+def project_kernel(a0, a1, a2, a3, own_ref, par_ref, o0, o1, o2, o3, hold):
+    m = lax.axis_index("mp")
+    attn = jnp.concatenate([a0[...], a1[...], a2[...], a3[...]], axis=0)
+    half = own_ref.shape[0]
+    hold[:, :half] = lax.dot_general(attn, own_ref[...], NT, preferred_element_type=F32)
+    hold[:, half:] = lax.dot_general(attn, par_ref[...], NT, preferred_element_type=F32)
+    width = o0.shape[1]
+    for j, out in enumerate((o0, o1, o2, o3)):
+        at = pl.multiple_of((m ^ j) * width, width)
+        out[...] = hold[:, pl.ds(at, width)].astype(out.dtype)
+
+
+def residual_offset(e, k, half, width):
+    return pl.multiple_of((e ^ (k // 2)) * half + (k % 2) * width, width)
+
+
+def pick_kernel(res_ref, o1, o2, o3):
+    e, m = lax.axis_index("seq"), lax.axis_index("mp")
+    width = o1.shape[1]
+    for s, out in ((1, o1), (2, o2), (3, o3)):
+        at = residual_offset(e ^ (2 * s), m, 2 * width, width)
+        out[...] = res_ref[:, pl.ds(at, width)]
+
+
+def combine_kernel(r0, r1, r2, r3, res_ref, s1, s2, s3, out, t0, t1, t2, t3):
+    e, m = lax.axis_index("seq"), lax.axis_index("mp")
+    width = out.shape[1]
+    tok = res_ref.shape[0]
+    at = residual_offset(e, m, 2 * width, width)
+    rest = jnp.concatenate([res_ref[:, pl.ds(at, width)], s1[...], s2[...], s3[...]], axis=0)
+    total = r0[...] + r1[...].astype(F32) + r2[...].astype(F32) + r3[...].astype(F32)
+    stream = (rest.astype(F32) + total).astype(BF16)
+    out[...] = stream
+    for s, part in enumerate((t0, t1, t2, t3)):
+        part[...] = stream[s * tok : (s + 1) * tok]
+
+
+def qkv_kernel(
+    x0, x1, x2, x3, gain_ref, own_ref, par_ref, t0, t1, t2, t3, o0, o1, o2, o3, piece, hold
+):
+    e, m = lax.axis_index("seq"), lax.axis_index("mp")
+    width = x0.shape[1]
+    half = 2 * width
+    tok = o0.shape[0]
+    for j, part in enumerate((x0, x1, x2, x3)):
+        k = m ^ j
+        gain = gain_ref[:, pl.ds(residual_offset(e, k, half, width), width)]
+        hold[:, pl.ds(pl.multiple_of(k * width, width), width)] = (
+            part[...].astype(F32) * gain
+        ).astype(BF16)
+    for s, part in enumerate((t0, t1, t2, t3)):
+        piece[:, s * width : (s + 1) * width] = part[...]
+    for s, out in enumerate((o1, o2, o3, o0)):
+        rows = slice(((s + 1) % 4) * tok, ((s + 1) % 4 + 1) * tok)
+        out[...] = (
+            jnp.dot(hold[rows, :half], own_ref[...], preferred_element_type=F32)
+            + jnp.dot(hold[rows, half:], par_ref[...], preferred_element_type=F32)
+        ).astype(out.dtype)
+
+
+def finish_kernel(y0, y1, y2, y3, p0, p1, p2, p3, qkv_ref, stream_ref):
+    e, m = lax.axis_index("seq"), lax.axis_index("mp")
+    width = p0.shape[1] // 4
+    squares = jnp.zeros((p0.shape[0], width), F32)
+    for j, part in enumerate((p0, p1, p2, p3)):
+        for s in range(4):
+            block = part[:, s * width : (s + 1) * width]
+            wide = block.astype(F32)
+            squares = squares + wide * wide
+            at = residual_offset(e ^ (2 * s), m ^ j, 2 * width, width)
+            stream_ref[:, pl.ds(at, width)] = block
+    mean_square = jnp.sum(squares, axis=1, keepdims=True) / stream_ref.shape[1]
+    total = y0[...] + y1[...].astype(F32) + y2[...].astype(F32) + y3[...].astype(F32)
+    qkv_ref[...] = (total * lax.rsqrt(mean_square + 1e-06)).astype(BF16)
+
+
+def call(kernel, out_shape, args, scratch=(), flops=0, moved=1 << 20):
+    return pl.pallas_call(
+        kernel,
+        out_shape=out_shape,
+        in_specs=[pl.BlockSpec(memory_space=pltpu.VMEM)] * len(args),
+        out_specs=jax.tree.map(lambda _: pl.BlockSpec(memory_space=pltpu.VMEM), out_shape),
+        scratch_shapes=list(scratch),
+        compiler_params=pltpu.CompilerParams(vmem_limit_bytes=24 << 20),
+        cost_estimate=pl.CostEstimate(flops=flops, bytes_accessed=moved, transcendentals=0),
+    )(*args)
+
+
+def swap(value, axis, count, bits):
+    return lax.ppermute(value, axis, [(i, i ^ bits) for i in range(count)])
+
+
+def on_block(
+    fresh_queries,
+    fresh_keys,
+    fresh_values,
+    cache,
+    pool_root,
+    branch_owner,
+    branch_len,
+    branch_root,
+    request_branch,
+    token_request,
+    residual,
+    wo_t,
+    norm_gain,
+    w_qkv,
+):
+    seq_count = lax.axis_size("seq")
+    root_count = seq_count // 4
+    tok = fresh_queries.shape[0]
+    e = lax.axis_index("seq")
+
+    blocks = [cache] + [swap(cache, "seq", 8, s) for s in range(1, 8)]
+    wo_pair = swap(wo_t, "seq", 8, 1)
+    width = wo_t.shape[0] // 2
+    sds = jax.ShapeDtypeStruct
+    picked = call(pick_kernel, [sds((tok, width), BF16)] * 3, (residual,))
+    beside = [swap(picked[s - 1], "seq", 8, 2 * s) for s in range(1, 4)]
+    wq_pair = swap(w_qkv, "seq", 8, 1)
+
+    relative = e ^ jnp.arange(seq_count, dtype=jnp.int32)
+    rows = jnp.arange(seq_count, dtype=jnp.int32)
+    pool_relative = jnp.sum(
+        jnp.where(relative[:, None, None] == rows[None, :, None], pool_root[None], 0), axis=1
+    )
+    slot_count = cache.shape[1] - pool_root.shape[1]
+    tags = cache_tags(pool_relative, branch_owner, branch_len, root_count, slot_count, relative)
+    requests, token_branch, token_root = token_nodes(request_branch, token_request, branch_root)
+    positions = jnp.arange(tok, dtype=jnp.int32)
+    own_seen = (requests[None, :] == requests[:, None]) & (
+        positions[:, None] <= positions[None, :]
+    )
+    pool_seen = (tags[:, None] == token_root[None, :]) | (
+        tags[:, None] == root_count + token_branch[None, :]
+    )
+    seen = jnp.concatenate([own_seen, pool_seen], axis=0)
+    bias = jnp.where(jnp.concatenate([seen, seen], axis=1), 0.0, -1e30).astype(F32)
+
+    attn = call(
+        attend_kernel,
+        sds(fresh_queries.shape, BF16),
+        (fresh_queries, fresh_keys, fresh_values, bias, *blocks),
+        flops=1 << 26,
+    )
+    attns = [attn] + [swap(attn, "seq", 8, 2 * s) for s in range(1, 4)]
+    sums = call(
+        project_kernel,
+        [sds((4 * tok, width), F32)] + [sds((4 * tok, width), BF16)] * 3,
+        (*attns, wo_t, wo_pair),
+        scratch=[pltpu.VMEM((4 * tok, 4 * width), F32)],
+        flops=1 << 27,
+    )
+    sums = [sums[0]] + [swap(sums[j], "mp", 4, j) for j in range(1, 4)]
+    made = call(
+        combine_kernel,
+        [sds((4 * tok, width), BF16)] + [sds((tok, width), BF16)] * 4,
+        (*sums, residual, *beside),
+    )
+    stream_parts = [made[0]] + [swap(made[0], "mp", 4, j) for j in range(1, 4)]
+    home = [made[1]] + [swap(made[1 + s], "seq", 8, 2 * s) for s in range(1, 4)]
+    columns = w_qkv.shape[1]
+    partial = call(
+        qkv_kernel,
+        [sds((tok, columns), F32)]
+        + [sds((tok, columns), BF16)] * 3
+        + [sds((tok, 4 * width), BF16)],
+        (*stream_parts, norm_gain[None, :], w_qkv, wq_pair, *home),
+        scratch=[pltpu.VMEM((4 * tok, 4 * width), BF16)],
+        flops=1 << 28,
+    )
+    back = [partial[0]] + [swap(partial[s], "seq", 8, 2 * s) for s in range(1, 4)]
+    pieces = [partial[4]] + [swap(partial[4], "mp", 4, j) for j in range(1, 4)]
+    qkv_next, stream = call(
+        finish_kernel,
+        [sds((tok, columns), BF16), sds(residual.shape, BF16)],
+        (*back, *pieces),
+    )
+    return attn, stream, qkv_next
 
 
 def absorb(running, query_rows, key_row_block, value_rows, visible, score_scale):
@@ -69,17 +294,9 @@
     query_groups = QUERY_HEADS // KEY_VALUE_HEADS
     score_scale = HEAD_SIZE ** (-0.5)
     slot_count = cache.shape[1] - pool_root.shape[1]
-    tags = cache_tags(pool_root, branch_owner, branch_len, root_count, slot_count)
-    requests = token_request[0]
-    local_branches = request_branch[0]
-    request_ids = jnp.arange(local_branches.shape[0], dtype=jnp.int32)
-    token_branch = jnp.sum(
-        jnp.where(requests[:, None] == request_ids[None, :], local_branches[None, :], 0), axis=1
-    )
-    branch_ids = jnp.arange(branch_root.shape[0], dtype=jnp.int32)
-    token_root = jnp.sum(
-        jnp.where(token_branch[:, None] == branch_ids[None, :], branch_root[None, :], 0), axis=1
-    )
+    owner_ids = jnp.arange(seq_count, dtype=jnp.int32)
+    tags = cache_tags(pool_root, branch_owner, branch_len, root_count, slot_count, owner_ids)
+    requests, token_branch, token_root = token_nodes(request_branch, token_request, branch_root)
     query_rows = fresh_queries.reshape(tok_rows, kv_local, query_groups, HEAD_SIZE)
     incoming_keys = fresh_keys.reshape(tok_rows, kv_local, HEAD_SIZE)
     incoming_values = fresh_values.reshape(tok_rows, kv_local, HEAD_SIZE)
@@ -92,10 +309,9 @@
         jnp.zeros((tok_rows, kv_local, query_groups), jnp.float32),
         jnp.zeros((tok_rows, kv_local, query_groups, HEAD_SIZE), jnp.float32),
     )
-    start_state = absorb(
+    state = absorb(
         start_state, query_rows, incoming_keys, incoming_values, own_visible, score_scale
     )
-    state = start_state
     piece = lax.all_gather(cache, "seq", axis=1, tiled=True)
     rows = piece.shape[1]
     block = 512 if rows > 512 and rows % 512 == 0 else rows
@@ -136,8 +352,9 @@
 
 
 def solution(mesh):
+    small = mesh.shape["seq"] == 8 and mesh.shape["mp"] == 4
     return jax.shard_map(
-        on_device,
+        on_block if small else on_device,
         mesh=mesh,
         in_specs=(
             P("seq", "mp"),

time: 184 us -> 92 us (0.50)
  waiting for transfers between devices: 118 us -> 49.4 us
  starting transfers between devices: 0.12 us -> 34.5 us
  blocking collectives: 33.8 us -> 0 us
  between operations: 13.9 us -> 0.91 us
  matrix products: 7.8 us -> 0 us
  local copies, waits for them, and re-layouts: 5.66 us -> 1.5 us
  Pallas kernels: 0 us -> 3.58 us
  other arithmetic: 4.24 us -> 1.21 us
    all_gather x2 -> x0, waiting for transfers between devices: 86.5 us -> none  [the longest x1 74.6 us: on_device(): lax.all_gather(w_qkv, 'seq', axis=0, tiled=True)]
    ppermute x0 -> x30, waiting for transfers between devices: none -> 49.4 us  [swap(): return lax.ppermute(value, axis, [(i, i ^ bits) for i in range(count)])]
    ppermute x0 -> x30, starting transfers between devices: none -> 34.5 us  [swap(): return lax.ppermute(value, axis, [(i, i ^ bits) for i in range(count)])]
    all_gather x1 -> x0, blocking collectives: 33.8 us -> none  [on_device(): piece = lax.all_gather(cache, 'seq', axis=1, tiled=True)]
    psum x1 -> x0, waiting for transfers between devices: 30.4 us -> none  [on_device(): lax.psum(partial_value.astype(jnp.bfloat16), 'mp').astype(jnp.float32)]
    dot_general x6 -> x0, matrix products: 7.8 us -> none  [the longest x1 3.73 us: on_device(): jnp.dot(normed, lax.all_gather(w_qkv, 'seq', axis=0, tiled=True), preferr...]
    pallas_call x0 -> x6, Pallas kernels: none -> 3.58 us  [call(): pl.pallas_call(kernel, out_shape=out_shape, in_specs=[pl.BlockSpec(memory...]
    reshape x3 -> x0, local copies, waits for them, and re-layouts: 2.45 us -> none  [the longest x1 0.9 us: on_device(): fresh_queries.reshape(tok_rows, kv_local, query_groups, HEAD_SIZE)]
  transfers between devices with their start and end apart: 3 -> 30, of which waited for: 3 -> 12; matrix products, arithmetic and copies ran while one was open for 6% -> 1% of each run, Pallas kernels for 0% -> 2%
where the time goes in v1:
time: 92 us; the launch traced here: 91.1 us
  waiting for transfers between devices  49.4 us (54%)
  starting transfers between devices  34.5 us (38%)
  Pallas kernels  3.58 us (4%)
  local copies, waits for them, and re-layouts  1.5 us (2%)
  other arithmetic  1.21 us (1%)
    ppermute x30, waiting for transfers between devices, swap(): return lax.ppermute(value, axis, [(i, i ^ bits) for i in range(count)])  49.4 us
    ppermute x30, starting transfers between devices, swap(): return lax.ppermute(value, axis, [(i, i ^ bits) for i in range(count)])  34.5 us
    pallas_call x6, Pallas kernels, call(): pl.pallas_call(kernel, out_shape=out_shape, in_specs=[pl.BlockSpec(memory...  3.58 us
  transfers between devices with their start and end apart: 30, of which 12 were waited for; matrix products, arithmetic and copies ran while one was open for 1% of the time, Pallas kernels for 2%

profile of v1, /device:TPU:0, one launch (start us, length us, event | category | flops | bytes accessed | tf_op | source)
XLA Modules:
  0.0 91.1 jit_solution(17211231643812797995)
XLA Ops:
  0.6 5.1 %collective-permute-start.5 = (bf16[2,64,256]{2,1,0:T(8,128)(2,1)}, bf16[2,64,256]{2,1,0:T(8,128)(2,1)S(1)}, u32[]{:S(2)}, u32[]{:S(2)}) collective-permute-start(bf16[2,64,256]{2,1,0:T(8,128)(2,1)} %refs_4_.1), channel_id=1, source_target_pairs={{0,24},{4,28},{8,16},{12,20},{16,8},{20,12},{24,0},{28,4},{1,25},{... | collective-permute-start | bytes 196616 | tf_op jit(solution)/shard_map/ppermute | solution.py:162
  6.1 3.5 %collective-permute-start.3 = (bf16[2,64,256]{2,1,0:T(8,128)(2,1)}, bf16[2,64,256]{2,1,0:T(8,128)(2,1)S(1)}, u32[]{:S(2)}, u32[]{:S(2)}) collective-permute-start(bf16[2,64,256]{2,1,0:T(8,128)(2,1)} %refs_4_.1), channel_id=1, source_target_pairs={{0,16},{4,20},{8,24},{12,28},{16,0},{20,4},{24,8},{28,12},{1,17},{... | collective-permute-start | bytes 196616 | tf_op jit(solution)/shard_map/ppermute | solution.py:162
  9.6 1.0 %collective-permute-start.10 = (bf16[256,512]{1,0:T(8,128)(2,1)}, bf16[256,512]{1,0:T(8,128)(2,1)S(1)}, u32[]{:S(2)}, u32[]{:S(2)}) collective-permute-start(bf16[256,512]{1,0:T(8,128)(2,1)} %own_ref.2), channel_id=1, source_target_pairs={{0,4},{4,0},{8,12},{12,8},{16,20},{20,16},{24,28},{28,24},{1,5},{5... | collective-permute-start | bytes 786440 | tf_op jit(solution)/shard_map/ppermute | solution.py:162
  12.3 1.1 %collective-permute-start.20 = (bf16[256,1024]{1,0:T(8,128)(2,1)}, bf16[256,1024]{1,0:T(8,128)(2,1)S(1)}, u32[]{:S(2)}, u32[]{:S(2)}) collective-permute-start(bf16[256,1024]{1,0:T(8,128)(2,1)} %own_ref.3), channel_id=1, source_target_pairs={{0,4},{4,0},{8,12},{12,8},{16,20},{20,16},{24,28},{28,24},{1,5},{5... | collective-permute-start | bytes 1572872 | tf_op jit(solution)/shard_map/ppermute | solution.py:162
  14.3 1.3 %collective-permute-start.1 = (bf16[2,64,256]{2,1,0:T(8,128)(2,1)S(1)}, bf16[2,64,256]{2,1,0:T(8,128)(2,1)S(1)}, u32[]{:S(2)}, u32[]{:S(2)}) collective-permute-start(bf16[2,64,256]{2,1,0:T(8,128)(2,1)S(1)} %copy-done.5), channel_id=1, source_target_pairs={{0,8},{4,12},{8,0},{12,4},{16,24},{20,28},{24,16},{28,20},{1,9},{5... | collective-permute-start | bytes 196616 | tf_op jit(solution)/shard_map/ppermute | solution.py:162
  15.6 1.5 %collective-permute-start = (bf16[2,64,256]{2,1,0:T(8,128)(2,1)S(1)}, bf16[2,64,256]{2,1,0:T(8,128)(2,1)S(1)}, u32[]{:S(2)}, u32[]{:S(2)}) collective-permute-start(bf16[2,64,256]{2,1,0:T(8,128)(2,1)S(1)} %copy-done.5), channel_id=1, source_target_pairs={{0,4},{4,0},{8,12},{12,8},{16,20},{20,16},{24,28},{28,24},{1,5},{5... | collective-permute-start | bytes 196616 | tf_op jit(solution)/shard_map/ppermute | solution.py:162
  17.1 1.8 %collective-permute-start.6 = (bf16[2,64,256]{2,1,0:T(8,128)(2,1)S(1)}, bf16[2,64,256]{2,1,0:T(8,128)(2,1)S(1)}, u32[]{:S(2)}, u32[]{:S(2)}) collective-permute-start(bf16[2,64,256]{2,1,0:T(8,128)(2,1)S(1)} %copy-done.5), channel_id=1, source_target_pairs={{0,28},{4,24},{8,20},{12,16},{16,12},{20,8},{24,4},{28,0},{1,29},{... | collective-permute-start | bytes 196616 | tf_op jit(solution)/shard_map/ppermute | solution.py:162
  19.1 14.8 %collective-permute-done.refs_5_ = bf16[2,64,256]{2,1,0:T(8,128)(2,1)S(1)} collective-permute-done((bf16[2,64,256]{2,1,0:T(8,128)(2,1)S(1)}, bf16[2,64,256]{2,1,0:T(8,128)(2,1)S(1)}, u32[]{:S(2)}, u32[]{:S(2)}) %collective-permute-start) | collective-permute-done | bytes 65568 | tf_op jit(solution)/shard_map/ppermute | solution.py:162
  33.9 1.3 %shard_map.157.a0 = bf16[64,512]{1,0:T(8,128)(2,1)} custom-call(bf16[64,512]{1,0:T(8,128)(2,1)S(1)} %copy-done.4, bf16[64,256]{1,0:T(8,128)(2,1)S(1)} %copy-done.6, bf16[64,256]{1,0:T(8,128)(2,1)S(1)} %copy-done.7, f32[576,128]{1,0:T(8,128)S(1)} %add_select_fusion.refs_3_, bf16[2,64,256]{2,1,0:T(8,128)(2,1)S(1)} %copy-done.5, ...), custom_call_target="tpu_custom_call" | custom-call | flops 67108864 | bytes 1048576 | tf_op jit(solution)/shard_map/pallas_call | solution.py:150
  35.2 0.8 collective-permute-start.9
  36.8 2.9 %collective-permute-start.7 = (bf16[64,512]{1,0:T(8,128)(2,1)}, bf16[64,512]{1,0:T(8,128)(2,1)S(1)}, u32[]{:S(2)}, u32[]{:S(2)}) collective-permute-start(bf16[64,512]{1,0:T(8,128)(2,1)} %shard_map.157.a0), channel_id=1, source_target_pairs={{0,8},{4,12},{8,0},{12,4},{16,24},{20,28},{24,16},{28,20},{1,9},{5... | collective-permute-start | bytes 196616 | tf_op jit(solution)/shard_map/ppermute | solution.py:162
  39.6 2.3 %collective-permute-done.9.a3 = bf16[64,512]{1,0:T(8,128)(2,1)S(1)} collective-permute-done((bf16[64,512]{1,0:T(8,128)(2,1)}, bf16[64,512]{1,0:T(8,128)(2,1)S(1)}, u32[]{:S(2)}, u32[]{:S(2)}) %collective-permute-start.9) | collective-permute-done | bytes 65568 | tf_op jit(solution)/shard_map/ppermute | solution.py:162
  41.9 1.4 %collective-permute-done.8.a2 = bf16[64,512]{1,0:T(8,128)(2,1)S(1)} collective-permute-done((bf16[64,512]{1,0:T(8,128)(2,1)}, bf16[64,512]{1,0:T(8,128)(2,1)S(1)}, u32[]{:S(2)}, u32[]{:S(2)}) %collective-permute-start.8) | collective-permute-done | bytes 65568 | tf_op jit(solution)/shard_map/ppermute | solution.py:162
  43.3 0.8 copy-done.3
  44.7 1.6 %collective-permute-start.12 = (bf16[256,128]{1,0:T(8,128)(2,1)S(1)}, bf16[256,128]{1,0:T(8,128)(2,1)S(1)}, u32[]{:S(2)}, u32[]{:S(2)}) collective-permute-start(bf16[256,128]{1,0:T(8,128)(2,1)S(1)} %get-tuple-element.24), channel_id=1, source_target_pairs={{0,2},{1,3},{2,0},{3,1},{4,6},{5,7},{6,4},{7,5},{8,10},{9,11},{10,... | collective-permute-start | bytes 196616 | tf_op jit(solution)/shard_map/ppermute | solution.py:162
  46.6 0.9 collective-permute-start.14
  47.4 3.0 %collective-permute-done.14.s1 = bf16[64,128]{1,0:T(8,128)(2,1)S(1)} collective-permute-done((bf16[64,128]{1,0:T(8,128)(2,1)S(1)}, bf16[64,128]{1,0:T(8,128)(2,1)S(1)}, u32[]{:S(2)}, u32[]{:S(2)}) %collective-permute-start.14) | collective-permute-done | bytes 16416 | tf_op jit(solution)/shard_map/ppermute | solution.py:162
  50.8 4.2 %collective-permute-done.15.s2 = bf16[64,128]{1,0:T(8,128)(2,1)S(1)} collective-permute-done((bf16[64,128]{1,0:T(8,128)(2,1)S(1)}, bf16[64,128]{1,0:T(8,128)(2,1)S(1)}, u32[]{:S(2)}, u32[]{:S(2)}) %collective-permute-start.15) | collective-permute-done | bytes 16416 | tf_op jit(solution)/shard_map/ppermute | solution.py:162
  55.0 1.5 %collective-permute-start.16 = (bf16[64,128]{1,0:T(8,128)(2,1)S(1)}, bf16[64,128]{1,0:T(8,128)(2,1)S(1)}, u32[]{:S(2)}, u32[]{:S(2)}) collective-permute-start(bf16[64,128]{1,0:T(8,128)(2,1)S(1)} %get-tuple-element.28), channel_id=1, source_target_pairs={{0,24},{4,28},{8,16},{12,20},{16,8},{20,12},{24,0},{28,4},{1,25},{... | collective-permute-start | bytes 49160 | tf_op jit(solution)/shard_map/ppermute | solution.py:162
  56.5 4.0 %collective-permute-done.16.s3 = bf16[64,128]{1,0:T(8,128)(2,1)S(1)} collective-permute-done((bf16[64,128]{1,0:T(8,128)(2,1)S(1)}, bf16[64,128]{1,0:T(8,128)(2,1)S(1)}, u32[]{:S(2)}, u32[]{:S(2)}) %collective-permute-start.16) | collective-permute-done | bytes 16416 | tf_op jit(solution)/shard_map/ppermute | solution.py:162
  60.7 1.6 %collective-permute-start.18 = (bf16[256,128]{1,0:T(8,128)(2,1)S(1)}, bf16[256,128]{1,0:T(8,128)(2,1)S(1)}, u32[]{:S(2)}, u32[]{:S(2)}) collective-permute-start(bf16[256,128]{1,0:T(8,128)(2,1)S(1)} %get-tuple-element.29.x0), channel_id=1, source_target_pairs={{0,2},{1,3},{2,0},{3,1},{4,6},{5,7},{6,4},{7,5},{8,10},{9,11},{10,... | collective-permute-start | bytes 196616 | tf_op jit(solution)/shard_map/ppermute | solution.py:162
  62.5 3.7 %collective-permute-done.21.t1 = bf16[64,128]{1,0:T(8,128)(2,1)S(1)} collective-permute-done((bf16[64,128]{1,0:T(8,128)(2,1)S(1)}, bf16[64,128]{1,0:T(8,128)(2,1)S(1)}, u32[]{:S(2)}, u32[]{:S(2)}) %collective-permute-start.21) | collective-permute-done | bytes 16416 | tf_op jit(solution)/shard_map/ppermute | solution.py:162
  66.4 4.6 %collective-permute-done.22.t2 = bf16[64,128]{1,0:T(8,128)(2,1)S(1)} collective-permute-done((bf16[64,128]{1,0:T(8,128)(2,1)S(1)}, bf16[64,128]{1,0:T(8,128)(2,1)S(1)}, u32[]{:S(2)}, u32[]{:S(2)}) %collective-permute-start.22) | collective-permute-done | bytes 16416 | tf_op jit(solution)/shard_map/ppermute | solution.py:162
  70.9 1.5 %collective-permute-start.23 = (bf16[64,128]{1,0:T(8,128)(2,1)S(1)}, bf16[64,128]{1,0:T(8,128)(2,1)S(1)}, u32[]{:S(2)}, u32[]{:S(2)}) collective-permute-start(bf16[64,128]{1,0:T(8,128)(2,1)S(1)} %get-tuple-element.33), channel_id=1, source_target_pairs={{0,24},{4,28},{8,16},{12,20},{16,8},{20,12},{24,0},{28,4},{1,25},{... | collective-permute-start | bytes 49160 | tf_op jit(solution)/shard_map/ppermute | solution.py:162
  72.5 4.0 %collective-permute-done.23.t3 = bf16[64,128]{1,0:T(8,128)(2,1)S(1)} collective-permute-done((bf16[64,128]{1,0:T(8,128)(2,1)S(1)}, bf16[64,128]{1,0:T(8,128)(2,1)S(1)}, u32[]{:S(2)}, u32[]{:S(2)}) %collective-permute-start.23) | collective-permute-done | bytes 16416 | tf_op jit(solution)/shard_map/ppermute | solution.py:162
  76.5 0.9 shard_map.161
  77.6 2.1 %collective-permute-start.25 = (bf16[64,1024]{1,0:T(8,128)(2,1)S(1)}, bf16[64,1024]{1,0:T(8,128)(2,1)S(1)}, u32[]{:S(2)}, u32[]{:S(2)}) collective-permute-start(bf16[64,1024]{1,0:T(8,128)(2,1)S(1)} %get-tuple-element.36), channel_id=1, source_target_pairs={{0,16},{4,20},{8,24},{12,28},{16,0},{20,4},{24,8},{28,12},{1,17},{... | collective-permute-start | bytes 393224 | tf_op jit(solution)/shard_map/ppermute | solution.py:162
  79.7 2.3 %collective-permute-start.26 = (bf16[64,1024]{1,0:T(8,128)(2,1)S(1)}, bf16[64,1024]{1,0:T(8,128)(2,1)S(1)}, u32[]{:S(2)}, u32[]{:S(2)}) collective-permute-start(bf16[64,1024]{1,0:T(8,128)(2,1)S(1)} %get-tuple-element.37), channel_id=1, source_target_pairs={{0,24},{4,28},{8,16},{12,20},{16,8},{20,12},{24,0},{28,4},{1,25},{... | collective-permute-start | bytes 393224 | tf_op jit(solution)/shard_map/ppermute | solution.py:162
  82.0 1.5 %collective-permute-start.28 = (bf16[64,512]{1,0:T(8,128)(2,1)S(1)}, bf16[64,512]{1,0:T(8,128)(2,1)S(1)}, u32[]{:S(2)}, u32[]{:S(2)}) collective-permute-start(bf16[64,512]{1,0:T(8,128)(2,1)S(1)} %get-tuple-element.38.p0), channel_id=1, source_target_pairs={{0,2},{1,3},{2,0},{3,1},{4,6},{5,7},{6,4},{7,5},{8,10},{9,11},{10,... | collective-permute-start | bytes 196616 | tf_op jit(solution)/shard_map/ppermute | solution.py:162
  83.5 3.2 %collective-permute-done.28.p2 = bf16[64,512]{1,0:T(8,128)(2,1)S(1)} collective-permute-done((bf16[64,512]{1,0:T(8,128)(2,1)S(1)}, bf16[64,512]{1,0:T(8,128)(2,1)S(1)}, u32[]{:S(2)}, u32[]{:S(2)}) %collective-permute-start.28) | collective-permute-done | bytes 65568 | tf_op jit(solution)/shard_map/ppermute | solution.py:162
  86.6 3.5 %collective-permute-done.25.y2 = bf16[64,1024]{1,0:T(8,128)(2,1)S(1)} collective-permute-done((bf16[64,1024]{1,0:T(8,128)(2,1)S(1)}, bf16[64,1024]{1,0:T(8,128)(2,1)S(1)}, u32[]{:S(2)}, u32[]{:S(2)}) %collective-permute-start.25) | collective-permute-done | bytes 131104 | tf_op jit(solution)/shard_map/ppermute | solution.py:162
  90.2 0.9 shard_map.162
  (79 shorter events, 5.7 us)
Async XLA Ops:
  0.6 11.7 %collective-permute-start.5 = (bf16[2,64,256]{2,1,0:T(8,128)(2,1)}, bf16[2,64,256]{2,1,0:T(8,128)(2,1)S(1)}, u32[]{:S(2)}, u32[]{:S(2)}) collective-permute-start(bf16[2,64,256]{2,1,0:T(8,128)(2,1)} %refs_4_.1), channel_id=1, source_target_pairs={{0,24},{4,28},{8,16},{12,20},{16,8},{20,12},{24,0},{28,4},{1,25},{... | collective-permute-start | bytes 196616 | tf_op jit(solution)/shard_map/ppermute | solution.py:162
  5.7 8.5 %collective-permute-start.4 = (bf16[2,64,256]{2,1,0:T(8,128)(2,1)}, bf16[2,64,256]{2,1,0:T(8,128)(2,1)S(1)}, u32[]{:S(2)}, u32[]{:S(2)}) collective-permute-start(bf16[2,64,256]{2,1,0:T(8,128)(2,1)} %refs_4_.1), channel_id=1, source_target_pairs={{0,20},{4,16},{8,28},{12,24},{16,4},{20,0},{24,12},{28,8},{1,21},{... | collective-permute-start | bytes 196616 | tf_op jit(solution)/shard_map/ppermute | solution.py:162
  6.1 9.4 %collective-permute-start.3 = (bf16[2,64,256]{2,1,0:T(8,128)(2,1)}, bf16[2,64,256]{2,1,0:T(8,128)(2,1)S(1)}, u32[]{:S(2)}, u32[]{:S(2)}) collective-permute-start(bf16[2,64,256]{2,1,0:T(8,128)(2,1)} %refs_4_.1), channel_id=1, source_target_pairs={{0,16},{4,20},{8,24},{12,28},{16,0},{20,4},{24,8},{28,12},{1,17},{... | collective-permute-start | bytes 196616 | tf_op jit(solution)/shard_map/ppermute | solution.py:162
  9.6 7.5 %collective-permute-start.2 = (bf16[2,64,256]{2,1,0:T(8,128)(2,1)}, bf16[2,64,256]{2,1,0:T(8,128)(2,1)S(1)}, u32[]{:S(2)}, u32[]{:S(2)}) collective-permute-start(bf16[2,64,256]{2,1,0:T(8,128)(2,1)} %refs_4_.1), channel_id=1, source_target_pairs={{0,12},{4,8},{8,4},{12,0},{16,28},{20,24},{24,20},{28,16},{1,13},{... | collective-permute-start | bytes 196616 | tf_op jit(solution)/shard_map/ppermute | solution.py:162
  9.6 33.7 %collective-permute-start.10 = (bf16[256,512]{1,0:T(8,128)(2,1)}, bf16[256,512]{1,0:T(8,128)(2,1)S(1)}, u32[]{:S(2)}, u32[]{:S(2)}) collective-permute-start(bf16[256,512]{1,0:T(8,128)(2,1)} %own_ref.2), channel_id=1, source_target_pairs={{0,4},{4,0},{8,12},{12,8},{16,20},{20,16},{24,28},{28,24},{1,5},{5... | collective-permute-start | bytes 786440 | tf_op jit(solution)/shard_map/ppermute | solution.py:162
  12.3 64.1 %collective-permute-start.20 = (bf16[256,1024]{1,0:T(8,128)(2,1)}, bf16[256,1024]{1,0:T(8,128)(2,1)S(1)}, u32[]{:S(2)}, u32[]{:S(2)}) collective-permute-start(bf16[256,1024]{1,0:T(8,128)(2,1)} %own_ref.3), channel_id=1, source_target_pairs={{0,4},{4,0},{8,12},{12,8},{16,20},{20,16},{24,28},{28,24},{1,5},{5... | collective-permute-start | bytes 1572872 | tf_op jit(solution)/shard_map/ppermute | solution.py:162
  14.3 4.8 %collective-permute-start.1 = (bf16[2,64,256]{2,1,0:T(8,128)(2,1)S(1)}, bf16[2,64,256]{2,1,0:T(8,128)(2,1)S(1)}, u32[]{:S(2)}, u32[]{:S(2)}) collective-permute-start(bf16[2,64,256]{2,1,0:T(8,128)(2,1)S(1)} %copy-done.5), channel_id=1, source_target_pairs={{0,8},{4,12},{8,0},{12,4},{16,24},{20,28},{24,16},{28,20},{1,9},{5... | collective-permute-start | bytes 196616 | tf_op jit(solution)/shard_map/ppermute | solution.py:162
  15.6 18.3 %collective-permute-start = (bf16[2,64,256]{2,1,0:T(8,128)(2,1)S(1)}, bf16[2,64,256]{2,1,0:T(8,128)(2,1)S(1)}, u32[]{:S(2)}, u32[]{:S(2)}) collective-permute-start(bf16[2,64,256]{2,1,0:T(8,128)(2,1)S(1)} %copy-done.5), channel_id=1, source_target_pairs={{0,4},{4,0},{8,12},{12,8},{16,20},{20,16},{24,28},{28,24},{1,5},{5... | collective-permute-start | bytes 196616 | tf_op jit(solution)/shard_map/ppermute | solution.py:162
  17.1 16.8 %collective-permute-start.6 = (bf16[2,64,256]{2,1,0:T(8,128)(2,1)S(1)}, bf16[2,64,256]{2,1,0:T(8,128)(2,1)S(1)}, u32[]{:S(2)}, u32[]{:S(2)}) collective-permute-start(bf16[2,64,256]{2,1,0:T(8,128)(2,1)S(1)} %copy-done.5), channel_id=1, source_target_pairs={{0,28},{4,24},{8,20},{12,16},{16,12},{20,8},{24,4},{28,0},{1,29},{... | collective-permute-start | bytes 196616 | tf_op jit(solution)/shard_map/ppermute | solution.py:162
  19.1 24.2 %copy-start.2 = (bf16[256,512]{1,0:T(8,128)(2,1)S(1)}, bf16[256,512]{1,0:T(8,128)(2,1)}, u32[]{:S(2)}) copy-start(bf16[256,512]{1,0:T(8,128)(2,1)} %own_ref.2) | copy-start | bytes 786436
  35.2 6.7 %collective-permute-start.9 = (bf16[64,512]{1,0:T(8,128)(2,1)}, bf16[64,512]{1,0:T(8,128)(2,1)S(1)}, u32[]{:S(2)}, u32[]{:S(2)}) collective-permute-start(bf16[64,512]{1,0:T(8,128)(2,1)} %shard_map.157.a0), channel_id=1, source_target_pairs={{0,24},{4,28},{8,16},{12,20},{16,8},{20,12},{24,0},{28,4},{1,25},{... | collective-permute-start | bytes 196616 | tf_op jit(solution)/shard_map/ppermute | solution.py:162
  36.0 7.3 %collective-permute-start.8 = (bf16[64,512]{1,0:T(8,128)(2,1)}, bf16[64,512]{1,0:T(8,128)(2,1)S(1)}, u32[]{:S(2)}, u32[]{:S(2)}) collective-permute-start(bf16[64,512]{1,0:T(8,128)(2,1)} %shard_map.157.a0), channel_id=1, source_target_pairs={{0,16},{4,20},{8,24},{12,28},{16,0},{20,4},{24,8},{28,12},{1,17},{... | collective-permute-start | bytes 196616 | tf_op jit(solution)/shard_map/ppermute | solution.py:162
  36.8 6.6 %collective-permute-start.7 = (bf16[64,512]{1,0:T(8,128)(2,1)}, bf16[64,512]{1,0:T(8,128)(2,1)S(1)}, u32[]{:S(2)}, u32[]{:S(2)}) collective-permute-start(bf16[64,512]{1,0:T(8,128)(2,1)} %shard_map.157.a0), channel_id=1, source_target_pairs={{0,8},{4,12},{8,0},{12,4},{16,24},{20,28},{24,16},{28,20},{1,9},{5... | collective-permute-start | bytes 196616 | tf_op jit(solution)/shard_map/ppermute | solution.py:162
  44.6 31.9 %copy-start.1 = (bf16[256,1024]{1,0:T(8,128)(2,1)S(1)}, bf16[256,1024]{1,0:T(8,128)(2,1)}, u32[]{:S(2)}) copy-start(bf16[256,1024]{1,0:T(8,128)(2,1)} %own_ref.3) | copy-start | bytes 1572868
  44.6 15.9 %collective-permute-start.11 = (bf16[256,128]{1,0:T(8,128)(2,1)S(1)}, bf16[256,128]{1,0:T(8,128)(2,1)S(1)}, u32[]{:S(2)}, u32[]{:S(2)}) collective-permute-start(bf16[256,128]{1,0:T(8,128)(2,1)S(1)} %get-tuple-element.23), channel_id=1, source_target_pairs={{0,1},{1,0},{2,3},{3,2},{4,5},{5,4},{6,7},{7,6},{8,9},{9,8},{10,11... | collective-permute-start | bytes 196616 | tf_op jit(solution)/shard_map/ppermute | solution.py:162
  44.7 15.9 %collective-permute-start.12 = (bf16[256,128]{1,0:T(8,128)(2,1)S(1)}, bf16[256,128]{1,0:T(8,128)(2,1)S(1)}, u32[]{:S(2)}, u32[]{:S(2)}) collective-permute-start(bf16[256,128]{1,0:T(8,128)(2,1)S(1)} %get-tuple-element.24), channel_id=1, source_target_pairs={{0,2},{1,3},{2,0},{3,1},{4,6},{5,7},{6,4},{7,5},{8,10},{9,11},{10,... | collective-permute-start | bytes 196616 | tf_op jit(solution)/shard_map/ppermute | solution.py:162
  46.2 14.3 %collective-permute-start.13 = (bf16[256,128]{1,0:T(8,128)(2,1)S(1)}, bf16[256,128]{1,0:T(8,128)(2,1)S(1)}, u32[]{:S(2)}, u32[]{:S(2)}) collective-permute-start(bf16[256,128]{1,0:T(8,128)(2,1)S(1)} %get-tuple-element.25), channel_id=1, source_target_pairs={{0,3},{1,2},{2,1},{3,0},{4,7},{5,6},{6,5},{7,4},{8,11},{9,10},{10,... | collective-permute-start | bytes 196616 | tf_op jit(solution)/shard_map/ppermute | solution.py:162
  46.6 3.8 %collective-permute-start.14 = (bf16[64,128]{1,0:T(8,128)(2,1)S(1)}, bf16[64,128]{1,0:T(8,128)(2,1)S(1)}, u32[]{:S(2)}, u32[]{:S(2)}) collective-permute-start(bf16[64,128]{1,0:T(8,128)(2,1)S(1)} %get-tuple-element.26), channel_id=1, source_target_pairs={{0,8},{4,12},{8,0},{12,4},{16,24},{20,28},{24,16},{28,20},{1,9},{5... | collective-permute-start | bytes 49160 | tf_op jit(solution)/shard_map/ppermute | solution.py:162
  50.4 4.6 %collective-permute-start.15 = (bf16[64,128]{1,0:T(8,128)(2,1)S(1)}, bf16[64,128]{1,0:T(8,128)(2,1)S(1)}, u32[]{:S(2)}, u32[]{:S(2)}) collective-permute-start(bf16[64,128]{1,0:T(8,128)(2,1)S(1)} %get-tuple-element.27), channel_id=1, source_target_pairs={{0,16},{4,20},{8,24},{12,28},{16,0},{20,4},{24,8},{28,12},{1,17},{... | collective-permute-start | bytes 49160 | tf_op jit(solution)/shard_map/ppermute | solution.py:162
  55.0 5.5 %collective-permute-start.16 = (bf16[64,128]{1,0:T(8,128)(2,1)S(1)}, bf16[64,128]{1,0:T(8,128)(2,1)S(1)}, u32[]{:S(2)}, u32[]{:S(2)}) collective-permute-start(bf16[64,128]{1,0:T(8,128)(2,1)S(1)} %get-tuple-element.28), channel_id=1, source_target_pairs={{0,24},{4,28},{8,16},{12,20},{16,8},{20,12},{24,0},{28,4},{1,25},{... | collective-permute-start | bytes 49160 | tf_op jit(solution)/shard_map/ppermute | solution.py:162
  60.6 15.8 %collective-permute-start.19 = (bf16[256,128]{1,0:T(8,128)(2,1)S(1)}, bf16[256,128]{1,0:T(8,128)(2,1)S(1)}, u32[]{:S(2)}, u32[]{:S(2)}) collective-permute-start(bf16[256,128]{1,0:T(8,128)(2,1)S(1)} %get-tuple-element.29.x0), channel_id=1, source_target_pairs={{0,3},{1,2},{2,1},{3,0},{4,7},{5,6},{6,5},{7,4},{8,11},{9,10},{10,... | collective-permute-start | bytes 196616 | tf_op jit(solution)/shard_map/ppermute | solution.py:162
  60.7 15.8 %collective-permute-start.18 = (bf16[256,128]{1,0:T(8,128)(2,1)S(1)}, bf16[256,128]{1,0:T(8,128)(2,1)S(1)}, u32[]{:S(2)}, u32[]{:S(2)}) collective-permute-start(bf16[256,128]{1,0:T(8,128)(2,1)S(1)} %get-tuple-element.29.x0), channel_id=1, source_target_pairs={{0,2},{1,3},{2,0},{3,1},{4,6},{5,7},{6,4},{7,5},{8,10},{9,11},{10,... | collective-permute-start | bytes 196616 | tf_op jit(solution)/shard_map/ppermute | solution.py:162
  62.3 14.2 %collective-permute-start.17 = (bf16[256,128]{1,0:T(8,128)(2,1)S(1)}, bf16[256,128]{1,0:T(8,128)(2,1)S(1)}, u32[]{:S(2)}, u32[]{:S(2)}) collective-permute-start(bf16[256,128]{1,0:T(8,128)(2,1)S(1)} %get-tuple-element.29.x0), channel_id=1, source_target_pairs={{0,1},{1,0},{2,3},{3,2},{4,5},{5,4},{6,7},{7,6},{8,9},{9,8},{10,11... | collective-permute-start | bytes 196616 | tf_op jit(solution)/shard_map/ppermute | solution.py:162
  62.5 3.7 %collective-permute-start.21 = (bf16[64,128]{1,0:T(8,128)(2,1)S(1)}, bf16[64,128]{1,0:T(8,128)(2,1)S(1)}, u32[]{:S(2)}, u32[]{:S(2)}) collective-permute-start(bf16[64,128]{1,0:T(8,128)(2,1)S(1)} %get-tuple-element.31), channel_id=1, source_target_pairs={{0,8},{4,12},{8,0},{12,4},{16,24},{20,28},{24,16},{28,20},{1,9},{5... | collective-permute-start | bytes 49160 | tf_op jit(solution)/shard_map/ppermute | solution.py:162
  66.3 4.6 %collective-permute-start.22 = (bf16[64,128]{1,0:T(8,128)(2,1)S(1)}, bf16[64,128]{1,0:T(8,128)(2,1)S(1)}, u32[]{:S(2)}, u32[]{:S(2)}) collective-permute-start(bf16[64,128]{1,0:T(8,128)(2,1)S(1)} %get-tuple-element.32), channel_id=1, source_target_pairs={{0,16},{4,20},{8,24},{12,28},{16,0},{20,4},{24,8},{28,12},{1,17},{... | collective-permute-start | bytes 49160 | tf_op jit(solution)/shard_map/ppermute | solution.py:162
  70.9 5.5 %collective-permute-start.23 = (bf16[64,128]{1,0:T(8,128)(2,1)S(1)}, bf16[64,128]{1,0:T(8,128)(2,1)S(1)}, u32[]{:S(2)}, u32[]{:S(2)}) collective-permute-start(bf16[64,128]{1,0:T(8,128)(2,1)S(1)} %get-tuple-element.33), channel_id=1, source_target_pairs={{0,24},{4,28},{8,16},{12,20},{16,8},{20,12},{24,0},{28,4},{1,25},{... | collective-permute-start | bytes 49160 | tf_op jit(solution)/shard_map/ppermute | solution.py:162
  77.4 6.0 %collective-permute-start.29 = (bf16[64,512]{1,0:T(8,128)(2,1)S(1)}, bf16[64,512]{1,0:T(8,128)(2,1)S(1)}, u32[]{:S(2)}, u32[]{:S(2)}) collective-permute-start(bf16[64,512]{1,0:T(8,128)(2,1)S(1)} %get-tuple-element.38.p0), channel_id=1, source_target_pairs={{0,3},{1,2},{2,1},{3,0},{4,7},{5,6},{6,5},{7,4},{8,11},{9,10},{10,... | collective-permute-start | bytes 196616 | tf_op jit(solution)/shard_map/ppermute | solution.py:162
  77.5 9.1 %collective-permute-start.24 = (bf16[64,1024]{1,0:T(8,128)(2,1)S(1)}, bf16[64,1024]{1,0:T(8,128)(2,1)S(1)}, u32[]{:S(2)}, u32[]{:S(2)}) collective-permute-start(bf16[64,1024]{1,0:T(8,128)(2,1)S(1)} %get-tuple-element.35), channel_id=1, source_target_pairs={{0,8},{4,12},{8,0},{12,4},{16,24},{20,28},{24,16},{28,20},{1,9},{5... | collective-permute-start | bytes 393224 | tf_op jit(solution)/shard_map/ppermute | solution.py:162
  77.6 12.6 %collective-permute-start.25 = (bf16[64,1024]{1,0:T(8,128)(2,1)S(1)}, bf16[64,1024]{1,0:T(8,128)(2,1)S(1)}, u32[]{:S(2)}, u32[]{:S(2)}) collective-permute-start(bf16[64,1024]{1,0:T(8,128)(2,1)S(1)} %get-tuple-element.36), channel_id=1, source_target_pairs={{0,16},{4,20},{8,24},{12,28},{16,0},{20,4},{24,8},{28,12},{1,17},{... | collective-permute-start | bytes 393224 | tf_op jit(solution)/shard_map/ppermute | solution.py:162
  79.7 10.5 %collective-permute-start.26 = (bf16[64,1024]{1,0:T(8,128)(2,1)S(1)}, bf16[64,1024]{1,0:T(8,128)(2,1)S(1)}, u32[]{:S(2)}, u32[]{:S(2)}) collective-permute-start(bf16[64,1024]{1,0:T(8,128)(2,1)S(1)} %get-tuple-element.37), channel_id=1, source_target_pairs={{0,24},{4,28},{8,16},{12,20},{16,8},{20,12},{24,0},{28,4},{1,25},{... | collective-permute-start | bytes 393224 | tf_op jit(solution)/shard_map/ppermute | solution.py:162
  82.0 4.7 %collective-permute-start.28 = (bf16[64,512]{1,0:T(8,128)(2,1)S(1)}, bf16[64,512]{1,0:T(8,128)(2,1)S(1)}, u32[]{:S(2)}, u32[]{:S(2)}) collective-permute-start(bf16[64,512]{1,0:T(8,128)(2,1)S(1)} %get-tuple-element.38.p0), channel_id=1, source_target_pairs={{0,2},{1,3},{2,0},{3,1},{4,6},{5,7},{6,4},{7,5},{8,10},{9,11},{10,... | collective-permute-start | bytes 196616 | tf_op jit(solution)/shard_map/ppermute | solution.py:162
  83.4 3.2 %collective-permute-start.27 = (bf16[64,512]{1,0:T(8,128)(2,1)S(1)}, bf16[64,512]{1,0:T(8,128)(2,1)S(1)}, u32[]{:S(2)}, u32[]{:S(2)}) collective-permute-start(bf16[64,512]{1,0:T(8,128)(2,1)S(1)} %get-tuple-element.38.p0), channel_id=1, source_target_pairs={{0,1},{1,0},{2,3},{3,2},{4,5},{5,4},{6,7},{7,6},{8,9},{9,8},{10,11... | collective-permute-start | bytes 196616 | tf_op jit(solution)/shard_map/ppermute | solution.py:162
  (13 other events, 98.4 us)

commit v2 on v0

--- a/solution.py
+++ b/solution.py
@@ -1,18 +1,23 @@
 import jax
 import jax.numpy as jnp
 from jax import lax
+from jax.experimental import pallas as pl
+from jax.experimental.pallas import tpu as pltpu
 from jax.sharding import PartitionSpec as P
 
 QUERY_HEADS = 16
 KEY_VALUE_HEADS = 8
 HEAD_SIZE = 128
-
-
-def cache_tags(pool_root, branch_owner, branch_len, root_count, slot_count):
-    owner_count = pool_root.shape[0]
+NT = (((1,), (1,)), ((), ()))
+TN = (((0,), (0,)), ((), ()))
+F32 = jnp.float32
+HIDDEN = -1e30
+BF16 = jnp.bfloat16
+
+
+def cache_tags(pool_root, branch_owner, branch_len, root_count, slot_count, owner_ids):
     branch_count = branch_owner.shape[0]
     branch_ids = jnp.arange(branch_count, dtype=jnp.int32)
-    owner_ids = jnp.arange(owner_count, dtype=jnp.int32)
     owned = jnp.sum(
         jnp.where(branch_owner[None, :] == owner_ids[:, None], branch_ids[None, :], 0), axis=1
     )
@@ -24,6 +29,335 @@
         slot_ids[None, :] < owned_length[:, None], root_count + owned[:, None], -1
     )
     return jnp.concatenate([pool_root, branch_tags], axis=1).reshape(-1)
+
+
+def token_nodes(request_branch, token_request, branch_root):
+    requests = token_request[0]
+    local_branches = request_branch[0]
+    request_ids = jnp.arange(local_branches.shape[0], dtype=jnp.int32)
+    token_branch = jnp.sum(
+        jnp.where(requests[:, None] == request_ids[None, :], local_branches[None, :], 0), axis=1
+    )
+    branch_ids = jnp.arange(branch_root.shape[0], dtype=jnp.int32)
+    token_root = jnp.sum(
+        jnp.where(token_branch[:, None] == branch_ids[None, :], branch_root[None, :], 0), axis=1
+    )
+    return requests, token_branch, token_root
+
+
+def feature_offset(e, half):
+    return pl.multiple_of(e * half, half)
+
+
+def distances(c):
+    return (1 - c, c, 3 - c, 2 + c)
+
+
+def head_lanes(h):
+    return slice(h * HEAD_SIZE, (h + 1) * HEAD_SIZE)
+
+
+def softmax_part(q_ref, k, keys, values, bias):
+    queries = jnp.concatenate([q_ref[:, head_lanes(2 * k)], q_ref[:, head_lanes(2 * k + 1)]], axis=0)
+    scores = (
+        lax.dot_general(keys, queries, NT, preferred_element_type=F32) * HEAD_SIZE**-0.5 + bias
+    )
+    peak = jnp.max(scores, axis=0, keepdims=True)
+    prob = jnp.exp(scores - peak)
+    total = jnp.sum(prob, axis=0, keepdims=True)
+    mixed = lax.dot_general(values, prob.astype(BF16), TN, preferred_element_type=F32)
+    log_sum = jnp.broadcast_to(peak + jnp.log(total), mixed.shape)
+    return (mixed / total).T, log_sum.T
+
+
+def lend_kernel(ask_ref, tags_ref, roots_ref, c0, c1, c2, c3, out_ref):
+    tok = ask_ref.shape[0]
+    caches = (c0, c1, c2, c3)
+    heads = 2 * c0.shape[2] // HEAD_SIZE
+    wide = heads * HEAD_SIZE
+    lane = lax.broadcasted_iota(jnp.int32, (tok, HEAD_SIZE), 1)
+    facts = ask_ref[:, wide:].astype(F32)
+    request = facts[:, :1].astype(jnp.int32) + 1
+    branch = jnp.sum(jnp.where(lane == request, facts, 0.0), axis=1, keepdims=True)
+    branch = branch.astype(jnp.int32)
+    root_count = lax.axis_size("seq") // 4
+    ids = lax.broadcasted_iota(jnp.int32, (tok, roots_ref.shape[1]), 1)
+    root = jnp.sum(
+        jnp.where(ids == branch, roots_ref[...].astype(F32), 0.0), axis=1, keepdims=True
+    ).astype(jnp.int32)
+    seen = (tags_ref[...] == root) | (tags_ref[...] == root_count + branch)
+    bias = jnp.where(seen, 0.0, HIDDEN).astype(F32).T
+    bias = jnp.concatenate([bias, bias], axis=1)
+    stats = jnp.zeros((tok, HEAD_SIZE), F32)
+    for k in range(heads // 2):
+        keys = jnp.concatenate([c[0, :, head_lanes(k)] for c in caches], axis=0)
+        values = jnp.concatenate([c[1, :, head_lanes(k)] for c in caches], axis=0)
+        mixed, log_sum = softmax_part(ask_ref, k, keys, values, bias)
+        for g in range(2):
+            h, rows = 2 * k + g, slice(g * tok, (g + 1) * tok)
+            out_ref[:, head_lanes(h)] = mixed[rows].astype(BF16)
+            rest = log_sum[rows]
+            for i in range(3):
+                digit = rest.astype(BF16).astype(F32)
+                stats = jnp.where(lane == i * heads + h, digit, stats)
+                rest = rest - digit
+    out_ref[:, wide:] = stats.astype(BF16)
+
+
+def own_kernel(q_ref, kf_ref, vf_ref, bias_ref, c0, c1, c2, c3, out_ref, log_ref):
+    tok = q_ref.shape[0]
+    caches = (c0, c1, c2, c3)
+    bias = bias_ref[...]
+    lane = lax.broadcasted_iota(jnp.int32, (tok, HEAD_SIZE), 1)
+    logs = jnp.zeros((tok, HEAD_SIZE), F32)
+    for k in range(kf_ref.shape[1] // HEAD_SIZE):
+        lanes = head_lanes(k)
+        keys = jnp.concatenate([kf_ref[:, lanes]] + [c[0, :, lanes] for c in caches], axis=0)
+        values = jnp.concatenate([vf_ref[:, lanes]] + [c[1, :, lanes] for c in caches], axis=0)
+        mixed, log_sum = softmax_part(q_ref, k, keys, values, bias)
+        for g in range(2):
+            h, rows = 2 * k + g, slice(g * tok, (g + 1) * tok)
+            out_ref[:, head_lanes(h)] = mixed[rows]
+            logs = jnp.where(lane == h, log_sum[rows], logs)
+    log_ref[...] = logs
+
+
+def merge_kernel(mine_ref, log_ref, lent_ref, res_ref, out_ref, s1, s2, s3, s4):
+    e, m = lax.axis_index("seq"), lax.axis_index("mp")
+    wide = mine_ref.shape[1]
+    heads = wide // HEAD_SIZE
+    sends = (s1, s2, s3, s4)
+    digits = lent_ref[:, wide:].astype(F32)
+    for h in range(heads):
+        mine = log_ref[:, h : h + 1]
+        lent = (digits[:, h : h + 1] + digits[:, heads + h : heads + h + 1]) + digits[
+            :, 2 * heads + h : 2 * heads + h + 1
+        ]
+        top = jnp.maximum(mine, lent)
+        mine, lent = jnp.exp(mine - top), jnp.exp(lent - top)
+        both = mine * mine_ref[:, head_lanes(h)] + lent * lent_ref[:, head_lanes(h)].astype(F32)
+        attn = (both / (mine + lent)).astype(BF16)
+        for ref in (out_ref, *sends):
+            ref[:, head_lanes(h)] = attn
+    quarter = s1.shape[1] - wide
+    for s, ref in zip(distances(m % 2), sends):
+        at = feature_offset(e ^ (2 * s) ^ (m // 2), 2 * quarter) + (m % 2) * quarter
+        ref[:, wide:] = res_ref[:, pl.ds(pl.multiple_of(at, quarter), quarter)]
+
+
+def project_kernel(g1, g2, g3, g4, own_ref, y_ref, core_ref, both_ref, out_ref, hold):
+    m = lax.axis_index("mp")
+    half, wide = own_ref.shape
+    tok = g1.shape[0]
+    quarter = half // 2
+    mine = jnp.concatenate([g2[:, :wide], g4[:, :wide]], axis=0)
+    other = jnp.concatenate([g1[:, :wide], g3[:, :wide]], axis=0)
+    for h, (w_mine, w_other) in enumerate(((own_ref, core_ref), (y_ref, both_ref))):
+        hold[:, h * half : (h + 1) * half] = lax.dot_general(
+            mine, w_mine[...], NT, preferred_element_type=F32
+        ) + lax.dot_general(other, w_other[...], NT, preferred_element_type=F32)
+    for k, (first, second) in ((m, (g2, g4)), (m ^ 1, (g1, g3))):
+        at = pl.ds(pl.multiple_of(k * quarter, quarter), quarter)
+        hold[:tok, at] += first[:, wide:].astype(F32)
+        hold[tok:, at] += second[:, wide:].astype(F32)
+    out_ref[...] = hold[...].astype(BF16)
+
+
+def qkv_kernel(stream_ref, gain_ref, own_ref, y_ref, core_ref, both_ref, o1, o2, o3, o4):
+    e = lax.axis_index("seq")
+    half = own_ref.shape[0]
+    tok = o1.shape[0]
+    stream = stream_ref[...].astype(F32)
+    near = gain_ref[:, pl.ds(feature_offset(e, half), half)]
+    far = gain_ref[:, pl.ds(feature_offset(e ^ 1, half), half)]
+    left = (stream[:, :half] * near).astype(BF16)
+    right = (stream[:, half:] * far).astype(BF16)
+    for first, second, w_left, w_right in ((o1, o3, core_ref, both_ref), (o2, o4, own_ref, y_ref)):
+        product = jnp.dot(left, w_left[...], preferred_element_type=F32) + jnp.dot(
+            right, w_right[...], preferred_element_type=F32
+        )
+        first[...] = product[:tok].astype(BF16)
+        second[...] = product[tok:].astype(BF16)
+
+
+def pack_kernel(h1, h2, out_ref):
+    width = h1.shape[1]
+    out_ref[:, :width] = h1[...]
+    out_ref[:, width:] = h2[...]
+
+
+def add_kernel(a_ref, b_ref, out_ref, first_ref, second_ref):
+    tok = first_ref.shape[0]
+    stream = (a_ref[...].astype(F32) + b_ref[...].astype(F32)).astype(BF16)
+    out_ref[...] = stream
+    first_ref[...] = stream[:tok]
+    second_ref[...] = stream[tok:]
+
+
+def finish_kernel(y1, y2, y3, y4, near_ref, far_ref, qkv_ref, stream_ref):
+    e, m = lax.axis_index("seq"), lax.axis_index("mp")
+    half = near_ref.shape[1] // 4
+    tok, width = stream_ref.shape
+    squares = jnp.zeros((tok, half), F32)
+    for ref, c in ((near_ref, m % 2), (far_ref, 1 - m % 2)):
+        for i, s in enumerate((c, 2 + c)):
+            for y in range(2):
+                block = ref[:, (2 * i + y) * half : (2 * i + y + 1) * half]
+                stream_ref[:, pl.ds(feature_offset(e ^ (2 * s) ^ y, half), half)] = block
+                wide = block.astype(F32)
+                squares = squares + wide * wide
+    mean_square = jnp.sum(squares, axis=1, keepdims=True) / width
+    total = (y1[...].astype(F32) + y2[...].astype(F32)) + (
+        y3[...].astype(F32) + y4[...].astype(F32)
+    )
+    qkv_ref[...] = (total * lax.rsqrt(mean_square + 1e-06)).astype(BF16)
+
+
+def call(kernel, out_shape, args, scratch=(), flops=0, moved=1 << 20):
+    return pl.pallas_call(
+        kernel,
+        out_shape=out_shape,
+        in_specs=[pl.BlockSpec(memory_space=pltpu.VMEM)] * len(args),
+        out_specs=jax.tree.map(lambda _: pl.BlockSpec(memory_space=pltpu.VMEM), out_shape),
+        scratch_shapes=list(scratch),
+        compiler_params=pltpu.CompilerParams(vmem_limit_bytes=24 << 20),
+        cost_estimate=pl.CostEstimate(flops=flops, bytes_accessed=moved, transcendentals=0),
+    )(*args)
+
+
+def swap(value, axis, count, bits):
+    return lax.ppermute(value, axis, [(i, i ^ bits) for i in range(count)])
+
+
+def routes():
+    made = []
+    for order in range(4):
+        pairs = []
+        for e in range(8):
+            for m in range(4):
+                s = distances(m % 2)[order]
+                target = (e ^ (2 * s)) * 4 + (m & 2) + s % 2
+                pairs.append((e * 4 + m, target))
+        made.append(pairs)
+    return made
+
+
+def on_block(
+    fresh_queries,
+    fresh_keys,
+    fresh_values,
+    cache,
+    pool_root,
+    branch_owner,
+    branch_len,
+    branch_root,
+    request_branch,
+    token_request,
+    residual,
+    wo_t,
+    norm_gain,
+    w_qkv,
+):
+    seq_count = lax.axis_size("seq")
+    root_count = seq_count // 4
+    tok, wide = fresh_queries.shape
+    half = wo_t.shape[0]
+    columns = w_qkv.shape[1]
+    e = lax.axis_index("seq")
+    sds = jax.ShapeDtypeStruct
+    out_routes = routes()
+    home_routes = [[(b, a) for a, b in pairs] for pairs in out_routes]
+
+    z2, z3, z1 = (swap(cache, "seq", 8, 2 * s) for s in (2, 3, 1))
+    facts = jnp.concatenate(
+        [token_request.reshape(tok, 1), jnp.broadcast_to(request_branch, (tok, request_branch.shape[1]))],
+        axis=1,
+    ).astype(BF16)
+    facts = jnp.pad(facts, ((0, 0), (0, HEAD_SIZE - facts.shape[1])))
+    ask = swap(jnp.concatenate([fresh_queries, facts], axis=1), "seq", 8, 1)
+
+    near_ids = e ^ (2 * jnp.arange(seq_count // 2, dtype=jnp.int32))
+    rows = jnp.arange(seq_count, dtype=jnp.int32)
+    near_pool = jnp.sum(
+        jnp.where(near_ids[:, None, None] == rows[None, :, None], pool_root[None], 0), axis=1
+    )
+    slot_count = cache.shape[1] - pool_root.shape[1]
+    tags = cache_tags(near_pool, branch_owner, branch_len, root_count, slot_count, near_ids)
+    requests, token_branch, token_root = token_nodes(request_branch, token_request, branch_root)
+    positions = jnp.arange(tok, dtype=jnp.int32)
+    own_seen = (requests[None, :] == requests[:, None]) & (
+        positions[:, None] <= positions[None, :]
+    )
+    near_seen = (tags[:, None] == token_root[None, :]) | (
+        tags[:, None] == root_count + token_branch[None, :]
+    )
+    seen = jnp.concatenate([own_seen, near_seen], axis=0)
+    bias = jnp.where(jnp.concatenate([seen, seen], axis=1), 0.0, HIDDEN).astype(F32)
+
+    wo_y = swap(wo_t, "seq", 8, 1)
+    near_cache = [cache, z1, z2, z3]
+    lend = call(
+        lend_kernel,
+        sds((tok, wide + HEAD_SIZE), BF16),
+        (ask, tags[None, :], branch_root[None, :], *near_cache),
+        flops=1 << 25,
+    )
+    lend, bias = lax.optimization_barrier((lend, bias))
+    lent = swap(lend, "seq", 8, 1)
+    mine, mine_log = call(
+        own_kernel,
+        [sds((tok, wide), F32), sds((tok, HEAD_SIZE), F32)],
+        (fresh_queries, fresh_keys, fresh_values, bias, *near_cache),
+        flops=1 << 25,
+    )
+    mine, wo_y, wo_later, wq_later = lax.optimization_barrier((mine, wo_y, wo_t, w_qkv))
+    wo_core = swap(wo_later, "mp", 4, 1)
+    wo_both = swap(wo_y, "mp", 4, 1)
+    wq_core = swap(wq_later, "mp", 4, 1)
+    wq_y = swap(wq_later, "seq", 8, 1)
+    lent, wo_core, wo_both, wq_core = lax.optimization_barrier((lent, wo_core, wo_both, wq_core))
+    attn, *sends = call(
+        merge_kernel,
+        [sds((tok, wide), BF16)] + [sds((tok, wide + half // 2), BF16)] * 4,
+        (mine, mine_log, lent, residual),
+    )
+    g3, g4, g1, g2 = (
+        lax.ppermute(sends[i], ("seq", "mp"), out_routes[i]) for i in (2, 3, 0, 1)
+    )
+    wq_y, g1, g2, g3, g4 = lax.optimization_barrier((wq_y, g1, g2, g3, g4))
+    wq_both = swap(wq_y, "mp", 4, 1)
+    part = call(
+        project_kernel,
+        sds((2 * tok, 2 * half), BF16),
+        (g1, g2, g3, g4, wo_t, wo_y, wo_core, wo_both),
+        scratch=[pltpu.VMEM((2 * tok, 2 * half), F32)],
+        flops=1 << 27,
+    )
+    part_x = swap(part, "mp", 4, 2)
+    stream_part, first, second = call(
+        add_kernel,
+        [sds((2 * tok, 2 * half), BF16)] + [sds((tok, 2 * half), BF16)] * 2,
+        (part, part_x),
+    )
+    home = [
+        lax.ppermute(v, ("seq", "mp"), r) for v, r in zip((first, second), home_routes[1::2])
+    ]
+    made = call(
+        qkv_kernel,
+        [sds((tok, columns), BF16)] * 4,
+        (stream_part, norm_gain[None, :], w_qkv, wq_y, wq_core, wq_both),
+        flops=1 << 28,
+    )
+    back = [lax.ppermute(made[i], ("seq", "mp"), home_routes[i]) for i in (2, 3, 0, 1)]
+    home, made = lax.optimization_barrier((home, made))
+    near = call(pack_kernel, sds((tok, 4 * half), BF16), tuple(home))
+    far = swap(near, "mp", 4, 1)
+    qkv_next, stream = call(
+        finish_kernel,
+        [sds((tok, columns), BF16), sds(residual.shape, BF16)],
+        (*back, near, far),
+    )
+    return attn, stream, qkv_next
 
 
 def absorb(running, query_rows, key_row_block, value_rows, visible, score_scale):
@@ -69,17 +403,9 @@
     query_groups = QUERY_HEADS // KEY_VALUE_HEADS
     score_scale = HEAD_SIZE ** (-0.5)
     slot_count = cache.shape[1] - pool_root.shape[1]
-    tags = cache_tags(pool_root, branch_owner, branch_len, root_count, slot_count)
-    requests = token_request[0]
-    local_branches = request_branch[0]
-    request_ids = jnp.arange(local_branches.shape[0], dtype=jnp.int32)
-    token_branch = jnp.sum(
-        jnp.where(requests[:, None] == request_ids[None, :], local_branches[None, :], 0), axis=1
-    )
-    branch_ids = jnp.arange(branch_root.shape[0], dtype=jnp.int32)
-    token_root = jnp.sum(
-        jnp.where(token_branch[:, None] == branch_ids[None, :], branch_root[None, :], 0), axis=1
-    )
+    owner_ids = jnp.arange(seq_count, dtype=jnp.int32)
+    tags = cache_tags(pool_root, branch_owner, branch_len, root_count, slot_count, owner_ids)
+    requests, token_branch, token_root = token_nodes(request_branch, token_request, branch_root)
     query_rows = fresh_queries.reshape(tok_rows, kv_local, query_groups, HEAD_SIZE)
     incoming_keys = fresh_keys.reshape(tok_rows, kv_local, HEAD_SIZE)
     incoming_values = fresh_values.reshape(tok_rows, kv_local, HEAD_SIZE)
@@ -92,10 +418,9 @@
         jnp.zeros((tok_rows, kv_local, query_groups), jnp.float32),
         jnp.zeros((tok_rows, kv_local, query_groups, HEAD_SIZE), jnp.float32),
     )
-    start_state = absorb(
+    state = absorb(
         start_state, query_rows, incoming_keys, incoming_values, own_visible, score_scale
     )
-    state = start_state
     piece = lax.all_gather(cache, "seq", axis=1, tiled=True)
     rows = piece.shape[1]
     block = 512 if rows > 512 and rows % 512 == 0 else rows
@@ -136,8 +461,9 @@
 
 
 def solution(mesh):
+    small = mesh.shape["seq"] == 8 and mesh.shape["mp"] == 4
     return jax.shard_map(
-        on_device,
+        on_block if small else on_device,
         mesh=mesh,
         in_specs=(
             P("seq", "mp"),

time: 184 us -> 75 us (0.41)
  waiting for transfers between devices: 118 us -> 41.1 us
  blocking collectives: 33.8 us -> 0 us
  starting transfers between devices: 0.12 us -> 23.8 us
  between operations: 13.9 us -> 0.9 us
  matrix products: 7.8 us -> 0 us
  Pallas kernels: 0 us -> 4.19 us
  local copies, waits for them, and re-layouts: 5.66 us -> 1.97 us
    all_gather x2 -> x0, waiting for transfers between devices: 86.5 us -> none  [the longest x1 74.6 us: on_device(): lax.all_gather(w_qkv, 'seq', axis=0, tiled=True)]
    ppermute x0 -> x23, waiting for transfers between devices: none -> 41.1 us  [the longest x13 21.2 us: swap(): return lax.ppermute(value, axis, [(i, i ^ bits) for i in range(count)])]
    all_gather x1 -> x0, blocking collectives: 33.8 us -> none  [on_device(): piece = lax.all_gather(cache, 'seq', axis=1, tiled=True)]
    psum x1 -> x0, waiting for transfers between devices: 30.4 us -> none  [on_device(): lax.psum(partial_value.astype(jnp.bfloat16), 'mp').astype(jnp.float32)]
    ppermute x0 -> x23, starting transfers between devices: none -> 23.8 us  [the longest x13 11.9 us: swap(): return lax.ppermute(value, axis, [(i, i ^ bits) for i in range(count)])]
    dot_general x6 -> x0, matrix products: 7.8 us -> none  [the longest x1 3.73 us: on_device(): jnp.dot(normed, lax.all_gather(w_qkv, 'seq', axis=0, tiled=True), preferr...]
    pallas_call x0 -> x8, Pallas kernels: none -> 4.19 us  [call(): pl.pallas_call(kernel, out_shape=out_shape, in_specs=[pl.BlockSpec(memory...]
    reshape x3 -> x0, local copies, waits for them, and re-layouts: 2.45 us -> none  [the longest x1 0.9 us: on_device(): fresh_queries.reshape(tok_rows, kv_local, query_groups, HEAD_SIZE)]
  transfers between devices with their start and end apart: 3 -> 23, of which waited for: 3 -> 8; matrix products, arithmetic and copies ran while one was open for 6% -> 4% of each run, Pallas kernels for 0% -> 5%
where the time goes in v2:
time: 75 us; the launch traced here: 74.7 us
  waiting for transfers between devices  41.1 us (55%)
  starting transfers between devices  23.8 us (32%)
  Pallas kernels  4.19 us (6%)
  other arithmetic  2.74 us (4%)
  local copies, waits for them, and re-layouts  1.97 us (3%)
  between operations  0.9 us (1%)
    ppermute x13, waiting for transfers between devices, swap(): return lax.ppermute(value, axis, [(i, i ^ bits) for i in range(count)])  21.2 us
    ppermute x13, starting transfers between devices, swap(): return lax.ppermute(value, axis, [(i, i ^ bits) for i in range(count)])  11.9 us
    ppermute x4, waiting for transfers between devices, on_block(): lax.ppermute(sends[i], ('seq', 'mp'), out_routes[i])  7.87 us
    ppermute x2, waiting for transfers between devices, on_block(): lax.ppermute(v, ('seq', 'mp'), r)  6.04 us
    ppermute x4, waiting for transfers between devices, on_block(): lax.ppermute(made[i], ('seq', 'mp'), home_routes[i])  5.92 us
    ppermute x4, starting transfers between devices, on_block(): lax.ppermute(sends[i], ('seq', 'mp'), out_routes[i])  5.62 us
    ppermute x4, starting transfers between devices, on_block(): lax.ppermute(made[i], ('seq', 'mp'), home_routes[i])  5.58 us
    pallas_call x8, Pallas kernels, call(): pl.pallas_call(kernel, out_shape=out_shape, in_specs=[pl.BlockSpec(memory...  4.19 us
  transfers between devices with their start and end apart: 23, of which 8 were waited for; matrix products, arithmetic and copies ran while one was open for 4% of the time, Pallas kernels for 5%

profile of v2, /device:TPU:0, one launch (start us, length us, event | category | flops | bytes accessed | tf_op | source)
XLA Modules:
  0.0 74.7 jit_solution(3799044560395069354)
XLA Ops:
  0.6 3.1 %collective-permute-start.1 = (bf16[2,64,256]{2,1,0:T(8,128)(2,1)}, bf16[2,64,256]{2,1,0:T(8,128)(2,1)S(1)}, u32[]{:S(2)}, u32[]{:S(2)}) collective-permute-start(bf16[2,64,256]{2,1,0:T(8,128)(2,1)} %c0.3), channel_id=1, source_target_pairs={{0,8},{4,12},{8,0},{12,4},{16,24},{20,28},{24,16},{28,20},{1,9},{5... | collective-permute-start | bytes 196616 | tf_op jit(solution)/shard_map/ppermute | solution.py:229
  3.7 2.6 %collective-permute-start.2 = (bf16[2,64,256]{2,1,0:T(8,128)(2,1)}, bf16[2,64,256]{2,1,0:T(8,128)(2,1)S(1)}, u32[]{:S(2)}, u32[]{:S(2)}) collective-permute-start(bf16[2,64,256]{2,1,0:T(8,128)(2,1)} %c0.3), channel_id=1, source_target_pairs={{0,16},{4,20},{8,24},{12,28},{16,0},{20,4},{24,8},{28,12},{1,17},{... | collective-permute-start | bytes 196616 | tf_op jit(solution)/shard_map/ppermute | solution.py:229
  6.3 0.7 convert_bitcast_fusion
  7.3 0.8 %fusion.1 = bf16[64,640]{1,0:T(8,128)(2,1)S(1)} fusion(bf16[64,5]{1,0:T(8,128)(2,1)S(1)} %copy.19, bf16[64,512]{1,0:T(8,128)(2,1)} %q_ref.1), kind=kLoop, calls=%fused_computation.4 | loop fusion | flops 245760 | bytes 148096 | tf_op jit(solution)/shard_map/concatenate | solution.py:277
  8.1 1.7 %collective-permute-start = (bf16[64,640]{1,0:T(8,128)(2,1)S(1)}, bf16[64,640]{1,0:T(8,128)(2,1)S(1)}, u32[]{:S(2)}, u32[]{:S(2)}) collective-permute-start(bf16[64,640]{1,0:T(8,128)(2,1)S(1)} %fusion.1), channel_id=1, source_target_pairs={{0,4},{4,0},{8,12},{12,8},{16,20},{20,16},{24,28},{28,24},{1,5},{5... | collective-permute-start | bytes 245768 | tf_op jit(solution)/shard_map/ppermute | solution.py:229
  9.8 0.3 collective-permute-start.4
  10.2 0.6 copy-done.11
  11.8 0.6 copy-done.10
  13.0 0.5 collective-permute-done.ask_ref
  13.6 0.9 %shard_map.157 = bf16[64,640]{1,0:T(8,128)(2,1)S(1)} custom-call(bf16[64,640]{1,0:T(8,128)(2,1)S(1)} %collective-permute-done.ask_ref, s32[1,256]{1,0:T(1,128)S(1)} %broadcast_in_dim_reshape.2.tags_ref, s32[1,8]{1,0:T(1,128)S(1)} %bitcast.8, bf16[2,64,256]{2,1,0:T(8,128)(2,1)S(1)} %copy-done.3, bf16[2,64,256]{2,1,0:T(8,128)(2,1)S(1)} %collective-permute-done.1.c1, ...), custom_call_target="tpu_custom_call" | custom-call | flops 33554432 | bytes 1048576 | tf_op jit(solution)/shard_map/pallas_call | solution.py:217
  14.6 0.5 shard_map.158
  15.1 2.8 %collective-permute-done.4.y_ref = bf16[256,512]{1,0:T(8,128)(2,1)S(1)} collective-permute-done((bf16[256,512]{1,0:T(8,128)(2,1)}, bf16[256,512]{1,0:T(8,128)(2,1)S(1)}, u32[]{:S(2)}, u32[]{:S(2)}) %collective-permute-start.4) | collective-permute-done | bytes 262176 | tf_op jit(solution)/shard_map/ppermute | solution.py:229
  17.9 0.9 %collective-permute-start.9 = (bf16[256,1024]{1,0:T(8,128)(2,1)S(1)}, bf16[256,1024]{1,0:T(8,128)(2,1)S(1)}, u32[]{:S(2)}, u32[]{:S(2)}) collective-permute-start(bf16[256,1024]{1,0:T(8,128)(2,1)S(1)} %copy-done), channel_id=1, source_target_pairs={{0,4},{4,0},{8,12},{12,8},{16,20},{20,16},{24,28},{28,24},{1,5},{5... | collective-permute-start | bytes 1572872 | tf_op jit(solution)/shard_map/ppermute | solution.py:229
  19.1 0.3 collective-permute-start.7
  19.4 1.1 %collective-permute-start.5 = (bf16[64,640]{1,0:T(8,128)(2,1)S(1)}, bf16[64,640]{1,0:T(8,128)(2,1)S(1)}, u32[]{:S(2)}, u32[]{:S(2)}) collective-permute-start(bf16[64,640]{1,0:T(8,128)(2,1)S(1)} %shard_map.157), channel_id=1, source_target_pairs={{0,4},{4,0},{8,12},{12,8},{16,20},{20,16},{24,28},{28,24},{1,5},{5... | collective-permute-start | bytes 245768 | tf_op jit(solution)/shard_map/ppermute | solution.py:229
  20.5 13.6 %collective-permute-done.5.lent_ref = bf16[64,640]{1,0:T(8,128)(2,1)S(1)} collective-permute-done((bf16[64,640]{1,0:T(8,128)(2,1)S(1)}, bf16[64,640]{1,0:T(8,128)(2,1)S(1)}, u32[]{:S(2)}, u32[]{:S(2)}) %collective-permute-start.5) | collective-permute-done | bytes 81952 | tf_op jit(solution)/shard_map/ppermute | solution.py:229
  34.0 0.9 %shard_map.159 = (bf16[64,512]{1,0:T(8,128)(2,1)}, bf16[64,640]{1,0:T(8,128)(2,1)S(1)}, bf16[64,640]{1,0:T(8,128)(2,1)S(1)}, bf16[64,640]{1,0:T(8,128)(2,1)S(1)}, bf16[64,640]{1,0:T(8,128)(2,1)S(1)}) custom-call(f32[64,512]{1,0:T(8,128)S(1)} %get-tuple-element.38.mine_ref, f32[64,128]{1,0:T(8,128)S(1)} %get-tuple-element.39.log_ref, ...), custom_call_target="tpu_custom_call" | custom-call | bytes 1048576 | tf_op jit(solution)/shard_map/pallas_call | solution.py:217
  34.9 0.7 collective-permute-start.11
  35.6 5.0 %collective-permute-start.12 = (bf16[64,640]{1,0:T(8,128)(2,1)S(1)}, bf16[64,640]{1,0:T(8,128)(2,1)S(1)}, u32[]{:S(2)}, u32[]{:S(2)}) collective-permute-start(bf16[64,640]{1,0:T(8,128)(2,1)S(1)} %get-tuple-element.48), channel_id=1, source_target_pairs={{0,25},{1,16},{2,27},{3,18},{4,29},{5,20},{6,31},{7,22},{8,17},{9,... | collective-permute-start | bytes 245768 | tf_op jit(solution)/shard_map/ppermute | solution.py:325
  40.6 6.8 %collective-permute-done.12.g3 = bf16[64,640]{1,0:T(8,128)(2,1)S(1)} collective-permute-done((bf16[64,640]{1,0:T(8,128)(2,1)S(1)}, bf16[64,640]{1,0:T(8,128)(2,1)S(1)}, u32[]{:S(2)}, u32[]{:S(2)}) %collective-permute-start.12) | collective-permute-done | bytes 81952 | tf_op jit(solution)/shard_map/ppermute | solution.py:325
  47.4 1.1 %collective-permute-done.13.g4 = bf16[64,640]{1,0:T(8,128)(2,1)S(1)} collective-permute-done((bf16[64,640]{1,0:T(8,128)(2,1)S(1)}, bf16[64,640]{1,0:T(8,128)(2,1)S(1)}, u32[]{:S(2)}, u32[]{:S(2)}) %collective-permute-start.13) | collective-permute-done | bytes 81952 | tf_op jit(solution)/shard_map/ppermute | solution.py:325
  48.5 0.5 shard_map.160.a_ref
  49.0 1.6 %collective-permute-start.14 = (bf16[128,512]{1,0:T(8,128)(2,1)S(1)}, bf16[128,512]{1,0:T(8,128)(2,1)S(1)}, u32[]{:S(2)}, u32[]{:S(2)}) collective-permute-start(bf16[128,512]{1,0:T(8,128)(2,1)S(1)} %shard_map.160.a_ref), channel_id=1, source_target_pairs={{0,2},{1,3},{2,0},{3,1},{4,6},{5,7},{6,4},{7,5},{8,10},{9,11},{10,... | collective-permute-start | bytes 393224 | tf_op jit(solution)/shard_map/ppermute | solution.py:229
  50.5 4.4 %collective-permute-done.14.b_ref = bf16[128,512]{1,0:T(8,128)(2,1)S(1)} collective-permute-done((bf16[128,512]{1,0:T(8,128)(2,1)S(1)}, bf16[128,512]{1,0:T(8,128)(2,1)S(1)}, u32[]{:S(2)}, u32[]{:S(2)}) %collective-permute-start.14) | collective-permute-done | bytes 131104 | tf_op jit(solution)/shard_map/ppermute | solution.py:229
  55.0 0.7 collective-permute-start.20
  55.8 0.4 shard_map.162
  56.2 3.5 %collective-permute-start.16 = (bf16[64,1024]{1,0:T(8,128)(2,1)S(1)}, bf16[64,1024]{1,0:T(8,128)(2,1)S(1)}, u32[]{:S(2)}, u32[]{:S(2)}) collective-permute-start(bf16[64,1024]{1,0:T(8,128)(2,1)S(1)} %get-tuple-element.59), channel_id=1, source_target_pairs={{25,0},{16,1},{27,2},{18,3},{29,4},{20,5},{31,6},{22,7},{17,8},{24... | collective-permute-start | bytes 393224 | tf_op jit(solution)/shard_map/ppermute | solution.py:351
  59.8 1.4 %collective-permute-start.17 = (bf16[64,1024]{1,0:T(8,128)(2,1)S(1)}, bf16[64,1024]{1,0:T(8,128)(2,1)S(1)}, u32[]{:S(2)}, u32[]{:S(2)}) collective-permute-start(bf16[64,1024]{1,0:T(8,128)(2,1)S(1)} %get-tuple-element.60), channel_id=1, source_target_pairs={{16,0},{25,1},{18,2},{27,3},{20,4},{29,5},{22,6},{31,7},{24,8},{17... | collective-permute-start | bytes 393224 | tf_op jit(solution)/shard_map/ppermute | solution.py:351
  61.2 0.7 collective-permute-start.19
  61.8 6.0 %collective-permute-done.21.h2 = bf16[64,512]{1,0:T(8,128)(2,1)S(1)} collective-permute-done((bf16[64,512]{1,0:T(8,128)(2,1)S(1)}, bf16[64,512]{1,0:T(8,128)(2,1)S(1)}, u32[]{:S(2)}, u32[]{:S(2)}) %collective-permute-start.21) | collective-permute-done | bytes 65568 | tf_op jit(solution)/shard_map/ppermute | solution.py:343
  68.0 5.9 %collective-permute-done.17.y2 = bf16[64,1024]{1,0:T(8,128)(2,1)S(1)} collective-permute-done((bf16[64,1024]{1,0:T(8,128)(2,1)S(1)}, bf16[64,1024]{1,0:T(8,128)(2,1)S(1)}, u32[]{:S(2)}, u32[]{:S(2)}) %collective-permute-start.17) | collective-permute-done | bytes 131104 | tf_op jit(solution)/shard_map/ppermute | solution.py:351
  73.9 0.8 %shard_map.164 = (bf16[64,1024]{1,0:T(8,128)(2,1)}, bf16[64,2048]{1,0:T(8,128)(2,1)}) custom-call(bf16[64,1024]{1,0:T(8,128)(2,1)S(1)} %collective-permute-done.16.y1, bf16[64,1024]{1,0:T(8,128)(2,1)S(1)} %collective-permute-done.17.y2, bf16[64,1024]{1,0:T(8,128)(2,1)S(1)} %collective-permute-done.18.y3, bf16[64,1024]{1,0:T(8,128)(2,1)S(1)} %collective-permute-done.19.y4, ...), custom_call_target="tpu_custom_call" | custom-call | bytes 1048576 | tf_op jit(solution)/shard_map/pallas_call | solution.py:217
  (72 shorter events, 2.5 us)
Async XLA Ops:
  0.6 6.4 %copy-start.13 = (s32[1,4]{1,0:T(1,128)S(1)}, s32[1,4]{1,0:T(1,128)}, u32[]{:S(2)}) copy-start(s32[1,4]{1,0:T(1,128)} %param.22) | copy-start | bytes 52
  0.6 12.3 %collective-permute-start.1 = (bf16[2,64,256]{2,1,0:T(8,128)(2,1)}, bf16[2,64,256]{2,1,0:T(8,128)(2,1)S(1)}, u32[]{:S(2)}, u32[]{:S(2)}) collective-permute-start(bf16[2,64,256]{2,1,0:T(8,128)(2,1)} %c0.3), channel_id=1, source_target_pairs={{0,8},{4,12},{8,0},{12,4},{16,24},{20,28},{24,16},{28,20},{1,9},{5... | collective-permute-start | bytes 196616 | tf_op jit(solution)/shard_map/ppermute | solution.py:229
  3.7 9.2 %collective-permute-start.2 = (bf16[2,64,256]{2,1,0:T(8,128)(2,1)}, bf16[2,64,256]{2,1,0:T(8,128)(2,1)S(1)}, u32[]{:S(2)}, u32[]{:S(2)}) collective-permute-start(bf16[2,64,256]{2,1,0:T(8,128)(2,1)} %c0.3), channel_id=1, source_target_pairs={{0,16},{4,20},{8,24},{12,28},{16,0},{20,4},{24,8},{28,12},{1,17},{... | collective-permute-start | bytes 196616 | tf_op jit(solution)/shard_map/ppermute | solution.py:229
  6.3 6.6 %collective-permute-start.3 = (bf16[2,64,256]{2,1,0:T(8,128)(2,1)}, bf16[2,64,256]{2,1,0:T(8,128)(2,1)S(1)}, u32[]{:S(2)}, u32[]{:S(2)}) collective-permute-start(bf16[2,64,256]{2,1,0:T(8,128)(2,1)} %c0.3), channel_id=1, source_target_pairs={{0,24},{4,28},{8,16},{12,20},{16,8},{20,12},{24,0},{28,4},{1,25},{... | collective-permute-start | bytes 196616 | tf_op jit(solution)/shard_map/ppermute | solution.py:229
  8.1 5.3 %collective-permute-start = (bf16[64,640]{1,0:T(8,128)(2,1)S(1)}, bf16[64,640]{1,0:T(8,128)(2,1)S(1)}, u32[]{:S(2)}, u32[]{:S(2)}) collective-permute-start(bf16[64,640]{1,0:T(8,128)(2,1)S(1)} %fusion.1), channel_id=1, source_target_pairs={{0,4},{4,0},{8,12},{12,8},{16,20},{20,16},{24,28},{28,24},{1,5},{5... | collective-permute-start | bytes 245768 | tf_op jit(solution)/shard_map/ppermute | solution.py:229
  9.8 8.1 %collective-permute-start.4 = (bf16[256,512]{1,0:T(8,128)(2,1)}, bf16[256,512]{1,0:T(8,128)(2,1)S(1)}, u32[]{:S(2)}, u32[]{:S(2)}) collective-permute-start(bf16[256,512]{1,0:T(8,128)(2,1)} %own_ref.2), channel_id=1, source_target_pairs={{0,4},{4,0},{8,12},{12,8},{16,20},{20,16},{24,28},{28,24},{1,5},{5... | collective-permute-start | bytes 786440 | tf_op jit(solution)/shard_map/ppermute | solution.py:229
  10.1 0.8 %copy-start.12 = (s32[8]{0:T(128)S(1)}, s32[8]{0:T(128)}, u32[]{:S(2)}) copy-start(s32[8]{0:T(128)} %param.20) | copy-start | bytes 100
  11.8 2.7 %copy-start.6 = (bf16[64,256]{1,0:T(8,128)(2,1)S(1)}, bf16[64,256]{1,0:T(8,128)(2,1)}, u32[]{:S(2)}) copy-start(bf16[64,256]{1,0:T(8,128)(2,1)} %vf_ref.1) | copy-start | bytes 98308
  12.6 2.0 %copy-start.5 = (bf16[64,256]{1,0:T(8,128)(2,1)S(1)}, bf16[64,256]{1,0:T(8,128)(2,1)}, u32[]{:S(2)}) copy-start(bf16[64,256]{1,0:T(8,128)(2,1)} %kf_ref.1) | copy-start | bytes 98308
  12.8 0.8 %copy-start.3 = (bf16[2,64,256]{2,1,0:T(8,128)(2,1)S(1)}, bf16[2,64,256]{2,1,0:T(8,128)(2,1)}, u32[]{:S(2)}) copy-start(bf16[2,64,256]{2,1,0:T(8,128)(2,1)} %c0.3) | copy-start | bytes 196612
  12.8 1.8 %copy-start.1 = (bf16[64,512]{1,0:T(8,128)(2,1)S(1)}, bf16[64,512]{1,0:T(8,128)(2,1)}, u32[]{:S(2)}) copy-start(bf16[64,512]{1,0:T(8,128)(2,1)} %q_ref.1) | copy-start | bytes 196612
  12.8 6.1 %copy-start.4 = (bf16[256,512]{1,0:T(8,128)(2,1)S(1)}, bf16[256,512]{1,0:T(8,128)(2,1)}, u32[]{:S(2)}) copy-start(bf16[256,512]{1,0:T(8,128)(2,1)} %own_ref.2) | copy-start | bytes 786436
  12.9 5.0 %copy-start = (bf16[256,1024]{1,0:T(8,128)(2,1)S(1)}, bf16[256,1024]{1,0:T(8,128)(2,1)}, u32[]{:S(2)}) copy-start(bf16[256,1024]{1,0:T(8,128)(2,1)} %own_ref.3) | copy-start | bytes 1572868
  14.6 19.4 %copy-start.2 = (bf16[64,2048]{1,0:T(8,128)(2,1)S(1)}, bf16[64,2048]{1,0:T(8,128)(2,1)}, u32[]{:S(2)}) copy-start(bf16[64,2048]{1,0:T(8,128)(2,1)} %res_ref.1) | copy-start | bytes 786436
  17.9 16.1 %collective-permute-start.8 = (bf16[256,1024]{1,0:T(8,128)(2,1)S(1)}, bf16[256,1024]{1,0:T(8,128)(2,1)S(1)}, u32[]{:S(2)}, u32[]{:S(2)}) collective-permute-start(bf16[256,1024]{1,0:T(8,128)(2,1)S(1)} %copy-done), channel_id=1, source_target_pairs={{0,1},{1,0},{2,3},{3,2},{4,5},{5,4},{6,7},{7,6},{8,9},{9,8},{10,11... | collective-permute-start | bytes 1572872 | tf_op jit(solution)/shard_map/ppermute | solution.py:229
  17.9 22.6 %collective-permute-start.9 = (bf16[256,1024]{1,0:T(8,128)(2,1)S(1)}, bf16[256,1024]{1,0:T(8,128)(2,1)S(1)}, u32[]{:S(2)}, u32[]{:S(2)}) collective-permute-start(bf16[256,1024]{1,0:T(8,128)(2,1)S(1)} %copy-done), channel_id=1, source_target_pairs={{0,4},{4,0},{8,12},{12,8},{16,20},{20,16},{24,28},{28,24},{1,5},{5... | collective-permute-start | bytes 1572872 | tf_op jit(solution)/shard_map/ppermute | solution.py:229
  18.9 15.1 %collective-permute-start.6 = (bf16[256,512]{1,0:T(8,128)(2,1)S(1)}, bf16[256,512]{1,0:T(8,128)(2,1)S(1)}, u32[]{:S(2)}, u32[]{:S(2)}) collective-permute-start(bf16[256,512]{1,0:T(8,128)(2,1)S(1)} %copy-done.4), channel_id=1, source_target_pairs={{0,1},{1,0},{2,3},{3,2},{4,5},{5,4},{6,7},{7,6},{8,9},{9,8},{10,11... | collective-permute-start | bytes 786440 | tf_op jit(solution)/shard_map/ppermute | solution.py:229
  19.1 14.9 %collective-permute-start.7 = (bf16[256,512]{1,0:T(8,128)(2,1)S(1)}, bf16[256,512]{1,0:T(8,128)(2,1)S(1)}, u32[]{:S(2)}, u32[]{:S(2)}) collective-permute-start(bf16[256,512]{1,0:T(8,128)(2,1)S(1)} %collective-permute-done.4.y_ref), channel_id=1, source_target_pairs={{0,1},{1,0},{2,3},{3,2},{4,5},{5,4},{6,7},{7,6},{8,9},{9,8},{10,11... | collective-permute-start | bytes 786440 | tf_op jit(solution)/shard_map/ppermute | solution.py:229
  19.4 14.6 %collective-permute-start.5 = (bf16[64,640]{1,0:T(8,128)(2,1)S(1)}, bf16[64,640]{1,0:T(8,128)(2,1)S(1)}, u32[]{:S(2)}, u32[]{:S(2)}) collective-permute-start(bf16[64,640]{1,0:T(8,128)(2,1)S(1)} %shard_map.157), channel_id=1, source_target_pairs={{0,4},{4,0},{8,12},{12,8},{16,20},{20,16},{24,28},{28,24},{1,5},{5... | collective-permute-start | bytes 245768 | tf_op jit(solution)/shard_map/ppermute | solution.py:229
  34.9 5.6 %collective-permute-start.10 = (bf16[64,640]{1,0:T(8,128)(2,1)S(1)}, bf16[64,640]{1,0:T(8,128)(2,1)S(1)}, u32[]{:S(2)}, u32[]{:S(2)}) collective-permute-start(bf16[64,640]{1,0:T(8,128)(2,1)S(1)} %get-tuple-element.46), channel_id=1, source_target_pairs={{0,9},{1,0},{2,11},{3,2},{4,13},{5,4},{6,15},{7,6},{8,1},{9,8},{10... | collective-permute-start | bytes 245768 | tf_op jit(solution)/shard_map/ppermute | solution.py:325
  34.9 5.6 %collective-permute-start.11 = (bf16[64,640]{1,0:T(8,128)(2,1)S(1)}, bf16[64,640]{1,0:T(8,128)(2,1)S(1)}, u32[]{:S(2)}, u32[]{:S(2)}) collective-permute-start(bf16[64,640]{1,0:T(8,128)(2,1)S(1)} %get-tuple-element.47), channel_id=1, source_target_pairs={{0,0},{1,9},{2,2},{3,11},{4,4},{5,13},{6,6},{7,15},{8,8},{9,1},{10... | collective-permute-start | bytes 245768 | tf_op jit(solution)/shard_map/ppermute | solution.py:325
  35.6 11.7 %collective-permute-start.12 = (bf16[64,640]{1,0:T(8,128)(2,1)S(1)}, bf16[64,640]{1,0:T(8,128)(2,1)S(1)}, u32[]{:S(2)}, u32[]{:S(2)}) collective-permute-start(bf16[64,640]{1,0:T(8,128)(2,1)S(1)} %get-tuple-element.48), channel_id=1, source_target_pairs={{0,25},{1,16},{2,27},{3,18},{4,29},{5,20},{6,31},{7,22},{8,17},{9,... | collective-permute-start | bytes 245768 | tf_op jit(solution)/shard_map/ppermute | solution.py:325
  40.6 7.9 %collective-permute-start.13 = (bf16[64,640]{1,0:T(8,128)(2,1)S(1)}, bf16[64,640]{1,0:T(8,128)(2,1)S(1)}, u32[]{:S(2)}, u32[]{:S(2)}) collective-permute-start(bf16[64,640]{1,0:T(8,128)(2,1)S(1)} %get-tuple-element.49), channel_id=1, source_target_pairs={{0,16},{1,25},{2,18},{3,27},{4,20},{5,29},{6,22},{7,31},{8,24},{9,... | collective-permute-start | bytes 245768 | tf_op jit(solution)/shard_map/ppermute | solution.py:325
  48.5 7.3 %collective-permute-start.15 = (bf16[256,1024]{1,0:T(8,128)(2,1)S(1)}, bf16[256,1024]{1,0:T(8,128)(2,1)S(1)}, u32[]{:S(2)}, u32[]{:S(2)}) collective-permute-start(bf16[256,1024]{1,0:T(8,128)(2,1)S(1)} %collective-permute-done.9.y_ref), channel_id=1, source_target_pairs={{0,1},{1,0},{2,3},{3,2},{4,5},{5,4},{6,7},{7,6},{8,9},{9,8},{10,11... | collective-permute-start | bytes 1572872 | tf_op jit(solution)/shard_map/ppermute | solution.py:229
  49.0 6.0 %collective-permute-start.14 = (bf16[128,512]{1,0:T(8,128)(2,1)S(1)}, bf16[128,512]{1,0:T(8,128)(2,1)S(1)}, u32[]{:S(2)}, u32[]{:S(2)}) collective-permute-start(bf16[128,512]{1,0:T(8,128)(2,1)S(1)} %shard_map.160.a_ref), channel_id=1, source_target_pairs={{0,2},{1,3},{2,0},{3,1},{4,6},{5,7},{6,4},{7,5},{8,10},{9,11},{10,... | collective-permute-start | bytes 393224 | tf_op jit(solution)/shard_map/ppermute | solution.py:229
  55.0 6.1 %collective-permute-start.20 = (bf16[64,512]{1,0:T(8,128)(2,1)S(1)}, bf16[64,512]{1,0:T(8,128)(2,1)S(1)}, u32[]{:S(2)}, u32[]{:S(2)}) collective-permute-start(bf16[64,512]{1,0:T(8,128)(2,1)S(1)} %get-tuple-element.63), channel_id=1, source_target_pairs={{0,0},{9,1},{2,2},{11,3},{4,4},{13,5},{6,6},{15,7},{8,8},{1,9},{10... | collective-permute-start | bytes 196616 | tf_op jit(solution)/shard_map/ppermute | solution.py:343
  55.7 12.2 %collective-permute-start.21 = (bf16[64,512]{1,0:T(8,128)(2,1)S(1)}, bf16[64,512]{1,0:T(8,128)(2,1)S(1)}, u32[]{:S(2)}, u32[]{:S(2)}) collective-permute-start(bf16[64,512]{1,0:T(8,128)(2,1)S(1)} %get-tuple-element.64), channel_id=1, source_target_pairs={{16,0},{25,1},{18,2},{27,3},{20,4},{29,5},{22,6},{31,7},{24,8},{17... | collective-permute-start | bytes 196616 | tf_op jit(solution)/shard_map/ppermute | solution.py:343
  56.2 11.7 %collective-permute-start.16 = (bf16[64,1024]{1,0:T(8,128)(2,1)S(1)}, bf16[64,1024]{1,0:T(8,128)(2,1)S(1)}, u32[]{:S(2)}, u32[]{:S(2)}) collective-permute-start(bf16[64,1024]{1,0:T(8,128)(2,1)S(1)} %get-tuple-element.59), channel_id=1, source_target_pairs={{25,0},{16,1},{27,2},{18,3},{29,4},{20,5},{31,6},{22,7},{17,8},{24... | collective-permute-start | bytes 393224 | tf_op jit(solution)/shard_map/ppermute | solution.py:351
  59.8 14.1 %collective-permute-start.17 = (bf16[64,1024]{1,0:T(8,128)(2,1)S(1)}, bf16[64,1024]{1,0:T(8,128)(2,1)S(1)}, u32[]{:S(2)}, u32[]{:S(2)}) collective-permute-start(bf16[64,1024]{1,0:T(8,128)(2,1)S(1)} %get-tuple-element.60), channel_id=1, source_target_pairs={{16,0},{25,1},{18,2},{27,3},{20,4},{29,5},{22,6},{31,7},{24,8},{17... | collective-permute-start | bytes 393224 | tf_op jit(solution)/shard_map/ppermute | solution.py:351
  61.1 12.7 %collective-permute-start.18 = (bf16[64,1024]{1,0:T(8,128)(2,1)S(1)}, bf16[64,1024]{1,0:T(8,128)(2,1)S(1)}, u32[]{:S(2)}, u32[]{:S(2)}) collective-permute-start(bf16[64,1024]{1,0:T(8,128)(2,1)S(1)} %get-tuple-element.61), channel_id=1, source_target_pairs={{9,0},{0,1},{11,2},{2,3},{13,4},{4,5},{15,6},{6,7},{1,8},{8,9},{3,... | collective-permute-start | bytes 393224 | tf_op jit(solution)/shard_map/ppermute | solution.py:351
  61.2 12.7 %collective-permute-start.19 = (bf16[64,1024]{1,0:T(8,128)(2,1)S(1)}, bf16[64,1024]{1,0:T(8,128)(2,1)S(1)}, u32[]{:S(2)}, u32[]{:S(2)}) collective-permute-start(bf16[64,1024]{1,0:T(8,128)(2,1)S(1)} %get-tuple-element.62), channel_id=1, source_target_pairs={{0,0},{9,1},{2,2},{11,3},{4,4},{13,5},{6,6},{15,7},{8,8},{1,9},{10... | collective-permute-start | bytes 393224 | tf_op jit(solution)/shard_map/ppermute | solution.py:351
  67.9 6.0 %collective-permute-start.22 = (bf16[64,1024]{1,0:T(8,128)(2,1)S(1)}, bf16[64,1024]{1,0:T(8,128)(2,1)S(1)}, u32[]{:S(2)}, u32[]{:S(2)}) collective-permute-start(bf16[64,1024]{1,0:T(8,128)(2,1)S(1)} %shard_map.163.near_ref), channel_id=1, source_target_pairs={{0,1},{1,0},{2,3},{3,2},{4,5},{5,4},{6,7},{7,6},{8,9},{9,8},{10,11... | collective-permute-start | bytes 393224 | tf_op jit(solution)/shard_map/ppermute | solution.py:229
  (5 other events, 3.5 us)

commit v3 on v2

v3 whole, which is shorter than its diff:
```python
import jax
import jax.numpy as jnp
from jax import lax
from jax.experimental import pallas as pl
from jax.experimental.pallas import tpu as pltpu
from jax.sharding import Mesh
from jax.sharding import PartitionSpec as P

QUERY_HEADS = 16
KEY_VALUE_HEADS = 8
HEAD_SIZE = 128
NT = (((1,), (1,)), ((), ()))
TN = (((0,), (0,)), ((), ()))
F32 = jnp.float32
HIDDEN = -1e30
BF16 = jnp.bfloat16


def cache_tags(pool_root, branch_owner, branch_len, root_count, slot_count, owner_ids):
    branch_count = branch_owner.shape[0]
    branch_ids = jnp.arange(branch_count, dtype=jnp.int32)
    owned = jnp.sum(
        jnp.where(branch_owner[None, :] == owner_ids[:, None], branch_ids[None, :], 0), axis=1
    )
    owned_length = jnp.sum(
        jnp.where(branch_ids[None, :] == owned[:, None], branch_len[None, :], 0), axis=1
    )
    slot_ids = jnp.arange(slot_count, dtype=jnp.int32)
    branch_tags = jnp.where(
        slot_ids[None, :] < owned_length[:, None], root_count + owned[:, None], -1
    )
    return jnp.concatenate([pool_root, branch_tags], axis=1).reshape(-1)


def token_nodes(request_branch, token_request, branch_root):
    requests = token_request[0]
    local_branches = request_branch[0]
    request_ids = jnp.arange(local_branches.shape[0], dtype=jnp.int32)
    token_branch = jnp.sum(
        jnp.where(requests[:, None] == request_ids[None, :], local_branches[None, :], 0), axis=1
    )
    branch_ids = jnp.arange(branch_root.shape[0], dtype=jnp.int32)
    token_root = jnp.sum(
        jnp.where(token_branch[:, None] == branch_ids[None, :], branch_root[None, :], 0), axis=1
    )
    return requests, token_branch, token_root


def feature_offset(e, half):
    return pl.multiple_of(e * half, half)


def head_lanes(h):
    return slice(h * HEAD_SIZE, (h + 1) * HEAD_SIZE)


def seq_index():
    return 2 * lax.axis_index("z") + lax.axis_index("y")


def own_nodes(request, branches_ref, roots_ref):
    branch, root = jnp.zeros_like(request), jnp.zeros_like(request)
    for r in range(branches_ref.shape[1]):
        b = branches_ref[0, r]
        branch = jnp.where(request == r, b, branch)
        root = jnp.where(request == r, roots_ref[b], root)
    return branch, root


def cache_bias(branch, root, pool_ref, owner_ref, length_ref, root_count):
    e = seq_index()
    owners, slots = pool_ref.shape
    by_row = pool_ref[...].astype(F32).T
    lane = lax.broadcasted_iota(jnp.int32, by_row.shape, 1)
    slot = lax.broadcasted_iota(jnp.int32, (slots, branch.shape[1]), 0)
    pieces = []
    for s in range(owners // 2):
        holder = e ^ (2 * s)
        held = jnp.sum(jnp.where(lane == holder, by_row, 0.0), axis=1, keepdims=True)
        owned, length = 0, 0
        for b in range(owners):
            here = owner_ref[b] == holder
            owned = jnp.where(here, b, owned)
            length = jnp.where(here, length_ref[b], length)
        pieces.append(held.astype(jnp.int32) == root)
        pieces.append((slot < length) & (branch == owned))
    return jnp.concatenate([jnp.where(seen, 0.0, HIDDEN) for seen in pieces], axis=0)


def softmax_part(q_ref, k, keys, values, bias):
    tok = bias.shape[1] // 2
    queries = jnp.concatenate(
        [q_ref[:tok, head_lanes(2 * k)], q_ref[:tok, head_lanes(2 * k + 1)]], axis=0
    )
    scores = (
        lax.dot_general(keys, queries, NT, preferred_element_type=F32) * HEAD_SIZE**-0.5 + bias
    )
    peak = jnp.max(scores, axis=0, keepdims=True)
    prob = jnp.exp(scores - peak)
    total = jnp.sum(prob, axis=0, keepdims=True)
    mixed = lax.dot_general(values, prob.astype(BF16), TN, preferred_element_type=F32)
    log_sum = jnp.broadcast_to(peak + jnp.log(total), mixed.shape)
    return (mixed / total).T, log_sum.T


def ask_kernel(q_ref, request_ref, branches_ref, roots_ref, out_ref):
    tok = q_ref.shape[0]
    branch, root = own_nodes(request_ref[...], branches_ref, roots_ref)
    rows = out_ref.shape[0] - tok
    which = lax.broadcasted_iota(jnp.int32, (rows, tok), 0)
    out_ref[:tok, :] = q_ref[...]
    out_ref[tok:, :tok] = jnp.where(which == 0, branch, root).astype(F32).astype(BF16)


def lend_kernel(ask_ref, pool_ref, owner_ref, length_ref, c0, c1, c2, c3, out_ref):
    tok = out_ref.shape[0]
    caches = (c0, c1, c2, c3)
    heads = 2 * c0.shape[2] // HEAD_SIZE
    wide = heads * HEAD_SIZE
    nodes = ask_ref[tok:, :tok].astype(F32).astype(jnp.int32)
    root_count = lax.axis_size("z") * lax.axis_size("y") // 4
    bias = cache_bias(nodes[:1], nodes[1:2], pool_ref, owner_ref, length_ref, root_count)
    bias = jnp.concatenate([bias, bias], axis=1)
    lane = lax.broadcasted_iota(jnp.int32, (tok, HEAD_SIZE), 1)
    stats = jnp.zeros((tok, HEAD_SIZE), F32)
    for k in range(heads // 2):
        keys = jnp.concatenate([c[0, :, head_lanes(k)] for c in caches], axis=0)
        values = jnp.concatenate([c[1, :, head_lanes(k)] for c in caches], axis=0)
        mixed, log_sum = softmax_part(ask_ref, k, keys, values, bias)
        for g in range(2):
            h, rows = 2 * k + g, slice(g * tok, (g + 1) * tok)
            out_ref[:, head_lanes(h)] = mixed[rows].astype(BF16)
            rest = log_sum[rows]
            for i in range(3):
                digit = rest.astype(BF16).astype(F32)
                stats = jnp.where(lane == i * heads + h, digit, stats)
                rest = rest - digit
    out_ref[:, wide:] = stats.astype(BF16)


def own_kernel(
    q_ref, kf_ref, vf_ref, request_ref, branches_ref, roots_ref, pool_ref, owner_ref, length_ref,
    c0, c1, c2, c3, lend_ref, out_ref, log_ref,
):
    tok = q_ref.shape[0]
    caches = (c0, c1, c2, c3)
    request = request_ref[...]
    branch, root = own_nodes(request, branches_ref, roots_ref)
    root_count = lax.axis_size("z") * lax.axis_size("y") // 4
    down = jnp.broadcast_to(request.astype(F32), (8, tok)).T[:, :1].astype(jnp.int32)
    key_at = lax.broadcasted_iota(jnp.int32, (tok, tok), 0)
    token_at = lax.broadcasted_iota(jnp.int32, (tok, tok), 1)
    fresh = jnp.where((down == request) & (key_at <= token_at), 0.0, HIDDEN)
    bias = jnp.concatenate(
        [fresh, cache_bias(branch, root, pool_ref, owner_ref, length_ref, root_count)], axis=0
    )
    bias = jnp.concatenate([bias, bias], axis=1)
    lane = lax.broadcasted_iota(jnp.int32, (tok, HEAD_SIZE), 1)
    logs = jnp.zeros((tok, HEAD_SIZE), F32)
    for k in range(kf_ref.shape[1] // HEAD_SIZE):
        lanes = head_lanes(k)
        keys = jnp.concatenate([kf_ref[:, lanes]] + [c[0, :, lanes] for c in caches], axis=0)
        values = jnp.concatenate([vf_ref[:, lanes]] + [c[1, :, lanes] for c in caches], axis=0)
        mixed, log_sum = softmax_part(q_ref, k, keys, values, bias)
        for g in range(2):
            h, rows = 2 * k + g, slice(g * tok, (g + 1) * tok)
            out_ref[:, head_lanes(h)] = mixed[rows]
            logs = jnp.where(lane == h, log_sum[rows], logs)
    log_ref[...] = logs


def merge_kernel(mine_ref, log_ref, lent_ref, res_ref, out_ref, send_ref):
    y, m = lax.axis_index("y"), 2 * lax.axis_index("x") + lax.axis_index("c")
    tok, wide = mine_ref.shape
    heads = wide // HEAD_SIZE
    part = tok // 2
    digits = lent_ref[:, wide:].astype(F32)
    for h in range(heads):
        mine = log_ref[:, h : h + 1]
        lent = (digits[:, h : h + 1] + digits[:, heads + h : heads + h + 1]) + digits[
            :, 2 * heads + h : 2 * heads + h + 1
        ]
        top = jnp.maximum(mine, lent)
        mine, lent = jnp.exp(mine - top), jnp.exp(lent - top)
        both = mine * mine_ref[:, head_lanes(h)] + lent * lent_ref[:, head_lanes(h)].astype(F32)
        attn = (both / (mine + lent)).astype(BF16)
        out_ref[:, head_lanes(h)] = attn
        for to in range(send_ref.shape[0]):
            c = to % 2
            send_ref[to, :, head_lanes(h)] = attn[c * part : (c + 1) * part]
    quarter = send_ref.shape[2] - wide
    for z in range(send_ref.shape[0] // 2):
        at = feature_offset((2 * z + y) ^ (m // 2), 2 * quarter) + (m % 2) * quarter
        block = res_ref[:, pl.ds(pl.multiple_of(at, quarter), quarter)]
        for c in range(2):
            send_ref[2 * z + c, :, wide:] = block[c * part : (c + 1) * part]


def project_kernel(g_ref, own_ref, y_ref, core_ref, both_ref, out_ref, hold):
    x, c = lax.axis_index("x"), lax.axis_index("c")
    half, wide = own_ref.shape
    part = g_ref.shape[1]
    quarter = half // 2
    chips = g_ref.shape[0] // 2
    mine = jnp.concatenate([g_ref[2 * z + c, :, :wide] for z in range(chips)], axis=0)
    other = jnp.concatenate([g_ref[2 * z + 1 - c, :, :wide] for z in range(chips)], axis=0)
    for h, (w_mine, w_other) in enumerate(((own_ref, core_ref), (y_ref, both_ref))):
        hold[:, h * half : (h + 1) * half] = lax.dot_general(
            mine, w_mine[...], NT, preferred_element_type=F32
        ) + lax.dot_general(other, w_other[...], NT, preferred_element_type=F32)
    for core in range(2):
        at = pl.ds(pl.multiple_of((2 * x + core) * quarter, quarter), quarter)
        for z in range(chips):
            hold[z * part : (z + 1) * part, at] += g_ref[2 * z + core, :, wide:].astype(F32)
    out_ref[...] = hold[...].astype(BF16)


def qkv_kernel(a_ref, b_ref, gain_ref, own_ref, y_ref, core_ref, both_ref, out_ref):
    e, c = seq_index(), lax.axis_index("c")
    half, columns = own_ref.shape
    part = out_ref.shape[1]
    whole = (a_ref[...].astype(F32) + b_ref[...].astype(F32)).astype(BF16)
    stream = whole.astype(F32)
    near = gain_ref[:, pl.ds(feature_offset(e, half), half)]
    far = gain_ref[:, pl.ds(feature_offset(e ^ 1, half), half)]
    left = (stream[:, :half] * near).astype(BF16)
    right = (stream[:, half:] * far).astype(BF16)
    for core, w_left, w_right in ((c, own_ref, y_ref), (1 - c, core_ref, both_ref)):
        product = jnp.dot(left, w_left[...], preferred_element_type=F32) + jnp.dot(
            right, w_right[...], preferred_element_type=F32
        )
        for z in range(out_ref.shape[0] // 2):
            rows = slice(z * part, (z + 1) * part)
            out_ref[2 * z + core, :, :columns] = product[rows].astype(BF16)
            out_ref[2 * z + core, :, columns:] = whole[rows]


def finish_kernel(got_ref, qkv_ref, stream_ref):
    y = lax.axis_index("y")
    columns = qkv_ref.shape[1]
    part = got_ref.shape[1]
    half = (got_ref.shape[2] - columns) // 2
    for c in range(2):
        rows = slice(c * part, (c + 1) * part)
        squares = jnp.zeros((part, half), F32)
        total = jnp.zeros((part, columns), F32)
        for z in range(got_ref.shape[0] // 2):
            total = total + got_ref[2 * z + c, :, :columns].astype(F32)
            for side in range(2):
                at = columns + side * half
                block = got_ref[2 * z + c, :, at : at + half]
                stream_ref[rows, pl.ds(feature_offset(2 * z + (y ^ side), half), half)] = block
                wide = block.astype(F32)
                squares = squares + wide * wide
        mean_square = jnp.sum(squares, axis=1, keepdims=True) / stream_ref.shape[1]
        qkv_ref[rows, :] = (total * lax.rsqrt(mean_square + 1e-06)).astype(BF16)


def call(kernel, out_shape, args, scratch=(), scalars=(), flops=0, moved=1 << 20):
    vmem, smem = pl.BlockSpec(memory_space=pltpu.VMEM), pl.BlockSpec(memory_space=pltpu.SMEM)
    return pl.pallas_call(
        kernel,
        out_shape=out_shape,
        in_specs=[smem if i in scalars else vmem for i in range(len(args))],
        out_specs=jax.tree.map(lambda _: vmem, out_shape),
        scratch_shapes=list(scratch),
        compiler_params=pltpu.CompilerParams(vmem_limit_bytes=24 << 20),
        cost_estimate=pl.CostEstimate(flops=flops, bytes_accessed=moved, transcendentals=0),
    )(*args)


def swap(value, axis, bits=1):
    return lax.ppermute(value, axis, [(i, i ^ bits) for i in range(lax.axis_size(axis))])


def on_block(
    fresh_queries,
    fresh_keys,
    fresh_values,
    cache,
    pool_root,
    branch_owner,
    branch_len,
    branch_root,
    request_branch,
    token_request,
    residual,
    wo_t,
    norm_gain,
    w_qkv,
):
    tok, wide = fresh_queries.shape
    half = wo_t.shape[0]
    columns = w_qkv.shape[1]
    chips = lax.axis_size("z")
    sds = jax.ShapeDtypeStruct

    z1, z2, z3 = (swap(cache, "z", s) for s in (1, 2, 3))
    caches = (cache, z1, z2, z3)
    ask = swap(
        call(
            ask_kernel,
            sds((tok + 16, wide), BF16),
            (fresh_queries, token_request, request_branch, branch_root),
            scalars=(2, 3),
        ),
        "y",
    )
    wo_y = swap(wo_t, "y")
    lend = call(
        lend_kernel,
        sds((tok, wide + HEAD_SIZE), BF16),
        (ask, pool_root, branch_owner, branch_len, *caches),
        scalars=(2, 3),
        flops=1 << 25,
    )
    lent = swap(lend, "y")
    mine, mine_log = call(
        own_kernel,
        [sds((tok, wide), F32), sds((tok, HEAD_SIZE), F32)],
        (
            fresh_queries, fresh_keys, fresh_values, token_request, request_branch, branch_root,
            pool_root, branch_owner, branch_len, *caches, lend,
        ),
        scalars=(4, 5, 7, 8),
        flops=1 << 25,
    )
    mine, wo_y, wo_later, wq_later = lax.optimization_barrier((mine, wo_y, wo_t, w_qkv))
    wo_core = swap(wo_later, "c")
    wo_both = swap(wo_y, "c")
    wq_core = swap(wq_later, "c")
    wq_y = swap(wq_later, "y")
    attn, send = call(
        merge_kernel,
        [sds((tok, wide), BF16), sds((2 * chips, tok // 2, wide + half // 2), BF16)],
        (mine, mine_log, lent, residual),
    )
    got = lax.all_to_all(send, ("z", "c"), 0, 0, tiled=True)
    part = call(
        project_kernel,
        sds((chips * tok // 2, 2 * half), BF16),
        (got, wo_t, wo_y, wo_core, wo_both),
        scratch=[pltpu.VMEM((chips * tok // 2, 2 * half), F32)],
        flops=1 << 27,
    )
    part_x = swap(part, "x")
    wq_y, part = lax.optimization_barrier((wq_y, part))
    wq_both = swap(wq_y, "c")
    made = call(
        qkv_kernel,
        sds((2 * chips, tok // 2, columns + 2 * half), BF16),
        (part, part_x, norm_gain[None, :], w_qkv, wq_y, wq_core, wq_both),
        flops=1 << 28,
    )
    back = lax.all_to_all(made, ("z", "c"), 0, 0, tiled=True)
    qkv_next, stream = call(
        finish_kernel,
        [sds((tok, columns), BF16), sds(residual.shape, BF16)],
        (back,),
    )
    return attn, stream, qkv_next


def absorb(running, query_rows, key_row_block, value_rows, visible, score_scale):
    peak_old, total, mixed = running
    scores = (
        jnp.einsum("tkgd,rkd->tkgr", query_rows, key_row_block, preferred_element_type=jnp.float32)
        * score_scale
    )
    seen = visible[:, None, None, :]
    peak_new = jnp.maximum(peak_old, jnp.max(jnp.where(seen, scores, -jnp.inf), axis=-1))
    factor = jnp.exp(peak_old - peak_new)
    weights_full = jnp.where(seen, jnp.exp(scores - peak_new[..., None]), 0.0)
    total = total * factor + jnp.sum(weights_full, axis=-1)
    mixed = mixed * factor[..., None] + jnp.einsum(
        "tkgr,rkd->tkgd",
        weights_full.astype(jnp.bfloat16),
        value_rows,
        preferred_element_type=jnp.float32,
    )
    return (peak_new, total, mixed)


def on_device(
    fresh_queries,
    fresh_keys,
    fresh_values,
    cache,
    pool_root,
    branch_owner,
    branch_len,
    branch_root,
    request_branch,
    token_request,
    residual,
    wo_t,
    norm_gain,
    w_qkv,
):
    seq_count = lax.axis_size("seq")
    root_count = seq_count // 4
    tok_rows = fresh_queries.shape[0]
    kv_local = fresh_keys.shape[1] // HEAD_SIZE
    query_groups = QUERY_HEADS // KEY_VALUE_HEADS
    score_scale = HEAD_SIZE ** (-0.5)
    slot_count = cache.shape[1] - pool_root.shape[1]
    owner_ids = jnp.arange(seq_count, dtype=jnp.int32)
    tags = cache_tags(pool_root, branch_owner, branch_len, root_count, slot_count, owner_ids)
    requests, token_branch, token_root = token_nodes(request_branch, token_request, branch_root)
    query_rows = fresh_queries.reshape(tok_rows, kv_local, query_groups, HEAD_SIZE)
    incoming_keys = fresh_keys.reshape(tok_rows, kv_local, HEAD_SIZE)
    incoming_values = fresh_values.reshape(tok_rows, kv_local, HEAD_SIZE)
    positions = jnp.arange(tok_rows, dtype=jnp.int32)
    own_visible = (requests[None, :] == requests[:, None]) & (
        positions[None, :] <= positions[:, None]
    )
    start_state = (
        jnp.full((tok_rows, kv_local, query_groups), -jnp.inf, jnp.float32),
        jnp.zeros((tok_rows, kv_local, query_groups), jnp.float32),
        jnp.zeros((tok_rows, kv_local, query_groups, HEAD_SIZE), jnp.float32),
    )
    state = absorb(
        start_state, query_rows, incoming_keys, incoming_values, own_visible, score_scale
    )
    piece = lax.all_gather(cache, "seq", axis=1, tiled=True)
    rows = piece.shape[1]
    block = 512 if rows > 512 and rows % 512 == 0 else rows
    key_blocks = piece[0].reshape(rows // block, block, kv_local, HEAD_SIZE)
    value_blocks = piece[1].reshape(rows // block, block, kv_local, HEAD_SIZE)
    tag_blocks = tags.reshape(rows // block, block)

    def one_block(running, parts):
        key_row_block, value_rows, tag_rows = parts
        visible = (tag_rows[None, :] == token_root[:, None]) | (
            tag_rows[None, :] == root_count + token_branch[:, None]
        )
        updated = absorb(running, query_rows, key_row_block, value_rows, visible, score_scale)
        return (updated, None)

    state, unused = lax.scan(one_block, state, (key_blocks, value_blocks, tag_blocks))
    peak_final, total_final, mixed_final = state
    attn = (
        (mixed_final / total_final[..., None])
        .reshape(tok_rows, kv_local * query_groups * HEAD_SIZE)
        .astype(jnp.bfloat16)
    )
    partial_value = lax.dot_general(
        attn,
        lax.all_gather(wo_t, "seq", axis=0, tiled=True),
        (((1,), (1,)), ((), ())),
        preferred_element_type=jnp.float32,
    )
    summed = lax.psum(partial_value.astype(jnp.bfloat16), "mp").astype(jnp.float32)
    stream = (residual.astype(jnp.float32) + summed).astype(jnp.bfloat16)
    widened = stream.astype(jnp.float32)
    mean_square = jnp.mean(widened * widened, axis=-1, keepdims=True)
    normed = (widened * lax.rsqrt(mean_square + 1e-06) * norm_gain[None, :]).astype(jnp.bfloat16)
    qkv_sum = jnp.dot(
        normed, lax.all_gather(w_qkv, "seq", axis=0, tiled=True), preferred_element_type=jnp.float32
    )
    return (attn, stream, qkv_sum.astype(jnp.bfloat16))


def solution(mesh):
    small = mesh.shape["seq"] == 8 and mesh.shape["mp"] == 4
    seq, mp = "seq", "mp"
    if small:
        mesh = Mesh(mesh.devices.reshape(4, 2, 2, 2), ("z", "y", "x", "c"))
        seq, mp = ("z", "y"), ("x", "c")
    return jax.shard_map(
        on_block if small else on_device,
        mesh=mesh,
        in_specs=(
            P(seq, mp),
            P(seq, mp),
            P(seq, mp),
            P(None, seq, mp),
            P(),
            P(),
            P(),
            P(),
            P(seq, None),
            P(seq, None),
            P(seq, None),
            P(seq, mp),
            P(),
            P(seq, mp),
        ),
        out_specs=(P(seq, mp), P(seq, None), P(seq, mp)),
        check_vma=False,
    )
```

time: 75 us -> 74.7 us (level)
  blocking collectives: 0 us -> 25.5 us
  waiting for transfers between devices: 41.1 us -> 22.3 us
  starting transfers between devices: 23.8 us -> 16.9 us
  other arithmetic: 2.74 us -> 0 us
  Pallas kernels: 4.19 us -> 5.93 us
  local copies, waits for them, and re-layouts: 1.97 us -> 3 us
    ppermute x23 -> x12, waiting for transfers between devices: 41.1 us -> 14.6 us  [swap(): lax.ppermute(value, axis, [(i, i ^ bits) for i in range(lax.axis_size(axi...]
    all_to_all x0 -> x1, blocking collectives: none -> 25.5 us  [on_block(): back = lax.all_to_all(made, ('z', 'c'), 0, 0, tiled=True)]
    ppermute x23 -> x12, starting transfers between devices: 23.8 us -> 13 us  [swap(): lax.ppermute(value, axis, [(i, i ^ bits) for i in range(lax.axis_size(axi...]
    all_to_all x0 -> x1, waiting for transfers between devices: none -> 7.63 us  [on_block(): got = lax.all_to_all(send, ('z', 'c'), 0, 0, tiled=True)]
    all_to_all x0 -> x1, starting transfers between devices: none -> 3.85 us  [on_block(): got = lax.all_to_all(send, ('z', 'c'), 0, 0, tiled=True)]
    pallas_call x8 -> x7, Pallas kernels: 4.19 us -> 5.93 us  [call(): pl.pallas_call(kernel, out_shape=out_shape, in_specs=[smem if i in scalar...]
    unnamed x28 -> x30, local copies, waits for them, and re-layouts: 1.61 us -> 3 us
    concatenate x3 -> x0, other arithmetic: 1 us -> none  [the longest x1 0.85 us: on_block(): ask = swap(jnp.concatenate([fresh_queries, facts], axis=1), 'seq', 8, 1)]
  transfers between devices with their start and end apart: 23 -> 13, of which waited for: 8 -> 8; matrix products, arithmetic and copies ran while one was open for 4% -> 0% of each run, Pallas kernels for 5% -> 5%
where the time goes in v3:
time: 74.7 us; the launch traced here: 74.3 us
  blocking collectives  25.5 us (34%)
  waiting for transfers between devices  22.3 us (30%)
  starting transfers between devices  16.9 us (23%)
  Pallas kernels  5.93 us (8%)
  local copies, waits for them, and re-layouts  3 us (4%)
  between operations  0.76 us (1%)
    all_to_all x1, blocking collectives, on_block(): back = lax.all_to_all(made, ('z', 'c'), 0, 0, tiled=True)  25.5 us
    ppermute x12, waiting for transfers between devices, swap(): lax.ppermute(value, axis, [(i, i ^ bits) for i in range(lax.axis_size(axi...  14.6 us
    ppermute x12, starting transfers between devices, swap(): lax.ppermute(value, axis, [(i, i ^ bits) for i in range(lax.axis_size(axi...  13 us
    all_to_all x1, waiting for transfers between devices, on_block(): got = lax.all_to_all(send, ('z', 'c'), 0, 0, tiled=True)  7.63 us
    pallas_call x7, Pallas kernels, call(): pl.pallas_call(kernel, out_shape=out_shape, in_specs=[smem if i in scalar...  5.93 us
    all_to_all x1, starting transfers between devices, on_block(): got = lax.all_to_all(send, ('z', 'c'), 0, 0, tiled=True)  3.85 us
    unnamed x30, local copies, waits for them, and re-layouts  3 us
  transfers between devices with their start and end apart: 13, of which 8 were waited for; matrix products, arithmetic and copies ran while one was open for 0% of the time, Pallas kernels for 5%

profile of v3, /device:TPU:0, one launch (start us, length us, event | category | flops | bytes accessed | tf_op | source)
XLA Modules:
  0.0 74.3 jit_solution(7822991397466861738)
XLA Ops:
  0.6 3.0 %collective-permute-start.4 = (bf16[256,512]{1,0:T(8,128)(2,1)}, bf16[256,512]{1,0:T(8,128)(2,1)S(1)}, u32[]{:S(2)}, u32[]{:S(2)}) collective-permute-start(bf16[256,512]{1,0:T(8,128)(2,1)} %own_ref.2), channel_id=1, source_target_pairs={{0,4},{4,0},{1,5},{5,1},{2,6},{6,2},{3,7},{7,3},{8,12},{12,8},{9,1... | collective-permute-start | bytes 786440 | tf_op jit(solution)/shard_map/ppermute | solution.py:273
  3.7 0.8 %copy-done.2 = bf16[64,512]{1,0:T(8,128)(2,1)S(1)} copy-done((bf16[64,512]{1,0:T(8,128)(2,1)S(1)}, bf16[64,512]{1,0:T(8,128)(2,1)}, u32[]{:S(2)}) %copy-start.2) | copy-done | bytes 65560
  4.5 0.7 copy-done.10
  5.2 0.7 copy-done.11
  5.8 0.7 copy-done.12
  6.5 0.6 shard_map.157
  7.1 0.1 collective-permute-start.3
  7.2 0.1 copy-done.5
  7.3 3.9 %collective-permute-start.2 = (bf16[2,64,256]{2,1,0:T(8,128)(2,1)S(1)}, bf16[2,64,256]{2,1,0:T(8,128)(2,1)S(1)}, u32[]{:S(2)}, u32[]{:S(2)}) collective-permute-start(bf16[2,64,256]{2,1,0:T(8,128)(2,1)S(1)} %copy-done.5), channel_id=1, source_target_pairs={{0,24},{8,16},{16,8},{24,0},{1,25},{9,17},{17,9},{25,1},{2,26},{10... | collective-permute-start | bytes 196616 | tf_op jit(solution)/shard_map/ppermute | solution.py:273
  11.3 0.6 collective-permute-start
  11.8 2.4 %collective-permute-done.2.c3 = bf16[2,64,256]{2,1,0:T(8,128)(2,1)S(1)} collective-permute-done((bf16[2,64,256]{2,1,0:T(8,128)(2,1)S(1)}, bf16[2,64,256]{2,1,0:T(8,128)(2,1)S(1)}, u32[]{:S(2)}, u32[]{:S(2)}) %collective-permute-start.2) | collective-permute-done | bytes 65568 | tf_op jit(solution)/shard_map/ppermute | solution.py:273
  14.3 2.3 %collective-permute-done.1.c2 = bf16[2,64,256]{2,1,0:T(8,128)(2,1)S(1)} collective-permute-done((bf16[2,64,256]{2,1,0:T(8,128)(2,1)S(1)}, bf16[2,64,256]{2,1,0:T(8,128)(2,1)S(1)}, u32[]{:S(2)}, u32[]{:S(2)}) %collective-permute-start.1) | collective-permute-done | bytes 65568 | tf_op jit(solution)/shard_map/ppermute | solution.py:273
  16.5 1.3 %shard_map.158.lend_ref = bf16[64,640]{1,0:T(8,128)(2,1)S(1)} custom-call(bf16[80,512]{1,0:T(8,128)(2,1)S(1)} %collective-permute-done.3.ask_ref, s32[8,32]{1,0:T(8,128)S(1)} %copy-done.8, s32[8]{0:T(128)S(1)} %copy-done.13, s32[8]{0:T(128)S(1)} %copy-done.14, bf16[2,64,256]{2,1,0:T(8,128)(2,1)S(1)} %copy-done.5, ...), custom_call_target="tpu_custom_call" | custom-call | flops 33554432 | bytes 1048576 | tf_op jit(solution)/shard_map/pallas_call | solution.py:261
  17.9 1.6 %collective-permute-start.5 = (bf16[64,640]{1,0:T(8,128)(2,1)S(1)}, bf16[64,640]{1,0:T(8,128)(2,1)S(1)}, u32[]{:S(2)}, u32[]{:S(2)}) collective-permute-start(bf16[64,640]{1,0:T(8,128)(2,1)S(1)} %shard_map.158.lend_ref), channel_id=1, source_target_pairs={{0,4},{4,0},{1,5},{5,1},{2,6},{6,2},{3,7},{7,3},{8,12},{12,8},{9,1... | collective-permute-start | bytes 245768 | tf_op jit(solution)/shard_map/ppermute | solution.py:273
  19.5 1.3 %shard_map.159 = (f32[64,512]{1,0:T(8,128)S(1)}, f32[64,128]{1,0:T(8,128)S(1)}) custom-call(bf16[64,512]{1,0:T(8,128)(2,1)S(1)} %copy-done.3, bf16[64,256]{1,0:T(8,128)(2,1)S(1)} %copy-done.6, bf16[64,256]{1,0:T(8,128)(2,1)S(1)} %copy-done.7, s32[1,64]{1,0:T(1,128)S(1)} %copy-done.10, s32[1,4]{1,0:T(1,128)S(1)} %copy-done.11, s32[8]{0:T(128)S(1)} %copy-done.12, ...), custom_call_target="tpu_custom_call" | custom-call | flops 33554432 | bytes 1048576 | tf_op jit(solution)/shard_map/pallas_call | solution.py:261
  20.8 1.6 %collective-permute-done.5.lent_ref = bf16[64,640]{1,0:T(8,128)(2,1)S(1)} collective-permute-done((bf16[64,640]{1,0:T(8,128)(2,1)S(1)}, bf16[64,640]{1,0:T(8,128)(2,1)S(1)}, u32[]{:S(2)}, u32[]{:S(2)}) %collective-permute-start.5) | collective-permute-done | bytes 81952 | tf_op jit(solution)/shard_map/ppermute | solution.py:273
  22.4 1.0 %shard_map.160 = (bf16[64,512]{1,0:T(8,128)(2,1)}, bf16[8,32,640]{2,1,0:T(8,128)(2,1)}) custom-call(f32[64,512]{1,0:T(8,128)S(1)} %get-tuple-element.16.mine_ref, f32[64,128]{1,0:T(8,128)S(1)} %get-tuple-element.17.log_ref, bf16[64,640]{1,0:T(8,128)(2,1)S(1)} %collective-permute-done.5.lent_ref, bf16[64,2048]{1,0:T(8,128)(2,1)S(1)} %copy-done.1), custom_call_target="tpu_custom_call" | custom-call | bytes 1048576 | tf_op jit(solution)/shard_map/pallas_call | solution.py:261
  23.4 3.8 %all-to-all-start = ((bf16[8,32,640]{2,1,0:T(8,128)(2,1)}), bf16[8,32,640]{2,1,0:T(8,128)(2,1)S(1)}, u32[]{:S(2)}, u32[]{:S(2)}) async-start(bf16[8,32,640]{2,1,0:T(8,128)(2,1)} %get-tuple-element.20), calls=%async_computation | async-start | bytes 655360 | tf_op jit(solution)/shard_map/all_to_all | solution.py:338
  27.3 1.6 %collective-permute-start.6 = (bf16[256,1024]{1,0:T(8,128)(2,1)S(1)}, bf16[256,1024]{1,0:T(8,128)(2,1)S(1)}, u32[]{:S(2)}, u32[]{:S(2)}) collective-permute-start(bf16[256,1024]{1,0:T(8,128)(2,1)S(1)} %copy-done), channel_id=1, source_target_pairs={{0,4},{4,0},{1,5},{5,1},{2,6},{6,2},{3,7},{7,3},{8,12},{12,8},{9,1... | collective-permute-start | bytes 1572872 | tf_op jit(solution)/shard_map/ppermute | solution.py:273
  28.9 0.2 collective-permute-start.7
  29.1 0.3 collective-permute-start.8
  29.4 0.2 collective-permute-start.10
  29.6 0.8 %collective-permute-done.7.core_ref = bf16[256,512]{1,0:T(8,128)(2,1)S(1)} collective-permute-done((bf16[256,512]{1,0:T(8,128)(2,1)S(1)}, bf16[256,512]{1,0:T(8,128)(2,1)S(1)}, u32[]{:S(2)}, u32[]{:S(2)}) %collective-permute-start.7) | collective-permute-done | bytes 262176 | tf_op jit(solution)/shard_map/ppermute | solution.py:273
  30.4 0.4 collective-permute-done.8.both_ref
  30.8 7.6 %all-to-all-done.g_ref = bf16[8,32,640]{2,1,0:T(8,128)(2,1)S(1)} async-done(((bf16[8,32,640]{2,1,0:T(8,128)(2,1)}), bf16[8,32,640]{2,1,0:T(8,128)(2,1)S(1)}, u32[]{:S(2)}, u32[]{:S(2)}) %all-to-all-start) | async-done | bytes 327712 | tf_op jit(solution)/shard_map/all_to_all | solution.py:338
  38.4 0.5 shard_map.161.a_ref
  39.0 2.7 %collective-permute-done.6.y_ref = bf16[256,1024]{1,0:T(8,128)(2,1)S(1)} collective-permute-done((bf16[256,1024]{1,0:T(8,128)(2,1)S(1)}, bf16[256,1024]{1,0:T(8,128)(2,1)S(1)}, u32[]{:S(2)}, u32[]{:S(2)}) %collective-permute-start.6) | collective-permute-done | bytes 524320 | tf_op jit(solution)/shard_map/ppermute | solution.py:273
  41.7 1.5 %collective-permute-start.9 = (bf16[128,512]{1,0:T(8,128)(2,1)S(1)}, bf16[128,512]{1,0:T(8,128)(2,1)S(1)}, u32[]{:S(2)}, u32[]{:S(2)}) collective-permute-start(bf16[128,512]{1,0:T(8,128)(2,1)S(1)} %shard_map.161.a_ref), channel_id=1, source_target_pairs={{0,2},{2,0},{1,3},{3,1},{4,6},{6,4},{5,7},{7,5},{8,10},{10,8},{9,1... | collective-permute-start | bytes 393224 | tf_op jit(solution)/shard_map/ppermute | solution.py:273
  43.2 4.4 %collective-permute-done.9.b_ref = bf16[128,512]{1,0:T(8,128)(2,1)S(1)} collective-permute-done((bf16[128,512]{1,0:T(8,128)(2,1)S(1)}, bf16[128,512]{1,0:T(8,128)(2,1)S(1)}, u32[]{:S(2)}, u32[]{:S(2)}) %collective-permute-start.9) | collective-permute-done | bytes 131104 | tf_op jit(solution)/shard_map/ppermute | solution.py:273
  47.6 0.5 shard_map.162
  48.0 25.5 %all_to_all.10.got_ref = bf16[8,32,1536]{2,1,0:T(8,128)(2,1)S(1)} all-to-all(bf16[8,32,1536]{2,1,0:T(8,128)(2,1)S(1)} %shard_map.162), channel_id=1, replica_groups=mesh['z'=4,'y'=2,'x'=2,'c'=2] {'z','c'}, dimensions={0} | all-to-all | bytes 1572864 | tf_op jit(solution)/shard_map/all_to_all | solution.py:355
  73.6 0.8 %shard_map.163 = (bf16[64,1024]{1,0:T(8,128)(2,1)}, bf16[64,2048]{1,0:T(8,128)(2,1)}) custom-call(bf16[8,32,1536]{2,1,0:T(8,128)(2,1)S(1)} %all_to_all.10.got_ref), custom_call_target="tpu_custom_call" | custom-call | bytes 1048576 | tf_op jit(solution)/shard_map/pallas_call | solution.py:261
  (32 shorter events, 0.1 us)
Async XLA Ops:
  0.6 20.1 %collective-permute-start.4 = (bf16[256,512]{1,0:T(8,128)(2,1)}, bf16[256,512]{1,0:T(8,128)(2,1)S(1)}, u32[]{:S(2)}, u32[]{:S(2)}) collective-permute-start(bf16[256,512]{1,0:T(8,128)(2,1)} %own_ref.2), channel_id=1, source_target_pairs={{0,4},{4,0},{1,5},{5,1},{2,6},{6,2},{3,7},{7,3},{8,12},{12,8},{9,1... | collective-permute-start | bytes 786440 | tf_op jit(solution)/shard_map/ppermute | solution.py:273
  3.7 0.8 %copy-start.2 = (bf16[64,512]{1,0:T(8,128)(2,1)S(1)}, bf16[64,512]{1,0:T(8,128)(2,1)}, u32[]{:S(2)}) copy-start(bf16[64,512]{1,0:T(8,128)(2,1)} %q_ref.3) | copy-start | bytes 196612
  4.5 0.7 copy-start.10
  5.2 0.7 copy-start.11
  5.8 0.7 copy-start.12
  6.5 0.8 %copy-start.5 = (bf16[2,64,256]{2,1,0:T(8,128)(2,1)S(1)}, bf16[2,64,256]{2,1,0:T(8,128)(2,1)}, u32[]{:S(2)}) copy-start(bf16[2,64,256]{2,1,0:T(8,128)(2,1)} %c0.3) | copy-start | bytes 196612
  6.5 10.0 %copy-start.8 = (s32[8,32]{1,0:T(8,128)S(1)}, s32[8,32]{1,0:T(8,128)}, u32[]{:S(2)}) copy-start(s32[8,32]{1,0:T(8,128)} %pool_ref.3) | copy-start | bytes 3076
  6.5 10.0 %copy-start.13 = (s32[8]{0:T(128)S(1)}, s32[8]{0:T(128)}, u32[]{:S(2)}) copy-start(s32[8]{0:T(128)} %owner_ref.3) | copy-start | bytes 100
  6.5 10.1 %copy-start.14 = (s32[8]{0:T(128)S(1)}, s32[8]{0:T(128)}, u32[]{:S(2)}) copy-start(s32[8]{0:T(128)} %length_ref.3) | copy-start | bytes 100
  7.0 12.4 %copy-start.3 = (bf16[64,512]{1,0:T(8,128)(2,1)S(1)}, bf16[64,512]{1,0:T(8,128)(2,1)}, u32[]{:S(2)}) copy-start(bf16[64,512]{1,0:T(8,128)(2,1)} %q_ref.3) | copy-start | bytes 196612
  7.1 12.4 %copy-start.6 = (bf16[64,256]{1,0:T(8,128)(2,1)S(1)}, bf16[64,256]{1,0:T(8,128)(2,1)}, u32[]{:S(2)}) copy-start(bf16[64,256]{1,0:T(8,128)(2,1)} %kf_ref.1) | copy-start | bytes 98308
  7.1 12.4 %copy-start.7 = (bf16[64,256]{1,0:T(8,128)(2,1)S(1)}, bf16[64,256]{1,0:T(8,128)(2,1)}, u32[]{:S(2)}) copy-start(bf16[64,256]{1,0:T(8,128)(2,1)} %vf_ref.1) | copy-start | bytes 98308
  7.1 9.4 %collective-permute-start.3 = (bf16[80,512]{1,0:T(8,128)(2,1)S(1)}, bf16[80,512]{1,0:T(8,128)(2,1)S(1)}, u32[]{:S(2)}, u32[]{:S(2)}) collective-permute-start(bf16[80,512]{1,0:T(8,128)(2,1)S(1)} %shard_map.157), channel_id=1, source_target_pairs={{0,4},{4,0},{1,5},{5,1},{2,6},{6,2},{3,7},{7,3},{8,12},{12,8},{9,1... | collective-permute-start | bytes 245768 | tf_op jit(solution)/shard_map/ppermute | solution.py:273
  7.3 6.9 %collective-permute-start.2 = (bf16[2,64,256]{2,1,0:T(8,128)(2,1)S(1)}, bf16[2,64,256]{2,1,0:T(8,128)(2,1)S(1)}, u32[]{:S(2)}, u32[]{:S(2)}) collective-permute-start(bf16[2,64,256]{2,1,0:T(8,128)(2,1)S(1)} %copy-done.5), channel_id=1, source_target_pairs={{0,24},{8,16},{16,8},{24,0},{1,25},{9,17},{17,9},{25,1},{2,26},{10... | collective-permute-start | bytes 196616 | tf_op jit(solution)/shard_map/ppermute | solution.py:273
  11.3 5.2 %collective-permute-start.1 = (bf16[2,64,256]{2,1,0:T(8,128)(2,1)S(1)}, bf16[2,64,256]{2,1,0:T(8,128)(2,1)S(1)}, u32[]{:S(2)}, u32[]{:S(2)}) collective-permute-start(bf16[2,64,256]{2,1,0:T(8,128)(2,1)S(1)} %copy-done.5), channel_id=1, source_target_pairs={{0,16},{8,24},{16,0},{24,8},{1,17},{9,25},{17,1},{25,9},{2,18},{10... | collective-permute-start | bytes 196616 | tf_op jit(solution)/shard_map/ppermute | solution.py:273
  11.3 5.2 %collective-permute-start = (bf16[2,64,256]{2,1,0:T(8,128)(2,1)S(1)}, bf16[2,64,256]{2,1,0:T(8,128)(2,1)S(1)}, u32[]{:S(2)}, u32[]{:S(2)}) collective-permute-start(bf16[2,64,256]{2,1,0:T(8,128)(2,1)S(1)} %copy-done.5), channel_id=1, source_target_pairs={{0,8},{8,0},{16,24},{24,16},{1,9},{9,1},{17,25},{25,17},{2,10},{10... | collective-permute-start | bytes 196616 | tf_op jit(solution)/shard_map/ppermute | solution.py:273
  17.9 4.5 %copy-start.1 = (bf16[64,2048]{1,0:T(8,128)(2,1)S(1)}, bf16[64,2048]{1,0:T(8,128)(2,1)}, u32[]{:S(2)}) copy-start(bf16[64,2048]{1,0:T(8,128)(2,1)} %res_ref.1) | copy-start | bytes 786436
  17.9 4.5 %collective-permute-start.5 = (bf16[64,640]{1,0:T(8,128)(2,1)S(1)}, bf16[64,640]{1,0:T(8,128)(2,1)S(1)}, u32[]{:S(2)}, u32[]{:S(2)}) collective-permute-start(bf16[64,640]{1,0:T(8,128)(2,1)S(1)} %shard_map.158.lend_ref), channel_id=1, source_target_pairs={{0,4},{4,0},{1,5},{5,1},{2,6},{6,2},{3,7},{7,3},{8,12},{12,8},{9,1... | collective-permute-start | bytes 245768 | tf_op jit(solution)/shard_map/ppermute | solution.py:273
  22.4 4.9 %copy-start = (bf16[256,1024]{1,0:T(8,128)(2,1)S(1)}, bf16[256,1024]{1,0:T(8,128)(2,1)}, u32[]{:S(2)}) copy-start(bf16[256,1024]{1,0:T(8,128)(2,1)} %own_ref.3) | copy-start | bytes 1572868
  23.4 5.5 %copy-start.4 = (bf16[256,512]{1,0:T(8,128)(2,1)S(1)}, bf16[256,512]{1,0:T(8,128)(2,1)}, u32[]{:S(2)}) copy-start(bf16[256,512]{1,0:T(8,128)(2,1)} %own_ref.2) | copy-start | bytes 786436
  23.4 15.0 %all-to-all-start = ((bf16[8,32,640]{2,1,0:T(8,128)(2,1)}), bf16[8,32,640]{2,1,0:T(8,128)(2,1)S(1)}, u32[]{:S(2)}, u32[]{:S(2)}) async-start(bf16[8,32,640]{2,1,0:T(8,128)(2,1)} %get-tuple-element.20), calls=%async_computation | async-start | bytes 655360 | tf_op jit(solution)/shard_map/all_to_all | solution.py:338
  27.3 20.3 %copy-start.9 = (f32[2048]{0:T(1024)S(1)}, f32[2048]{0:T(1024)}, u32[]{:S(2)}) copy-start(f32[2048]{0:T(1024)} %param.26) | copy-start | bytes 24580
  27.3 14.4 %collective-permute-start.6 = (bf16[256,1024]{1,0:T(8,128)(2,1)S(1)}, bf16[256,1024]{1,0:T(8,128)(2,1)S(1)}, u32[]{:S(2)}, u32[]{:S(2)}) collective-permute-start(bf16[256,1024]{1,0:T(8,128)(2,1)S(1)} %copy-done), channel_id=1, source_target_pairs={{0,4},{4,0},{1,5},{5,1},{2,6},{6,2},{3,7},{7,3},{8,12},{12,8},{9,1... | collective-permute-start | bytes 1572872 | tf_op jit(solution)/shard_map/ppermute | solution.py:273
  28.9 1.5 %collective-permute-start.7 = (bf16[256,512]{1,0:T(8,128)(2,1)S(1)}, bf16[256,512]{1,0:T(8,128)(2,1)S(1)}, u32[]{:S(2)}, u32[]{:S(2)}) collective-permute-start(bf16[256,512]{1,0:T(8,128)(2,1)S(1)} %copy-done.4), channel_id=1, source_target_pairs={{0,1},{1,0},{2,3},{3,2},{4,5},{5,4},{6,7},{7,6},{8,9},{9,8},{10,11... | collective-permute-start | bytes 786440 | tf_op jit(solution)/shard_map/ppermute | solution.py:273
  29.1 1.7 %collective-permute-start.8 = (bf16[256,512]{1,0:T(8,128)(2,1)S(1)}, bf16[256,512]{1,0:T(8,128)(2,1)S(1)}, u32[]{:S(2)}, u32[]{:S(2)}) collective-permute-start(bf16[256,512]{1,0:T(8,128)(2,1)S(1)} %collective-permute-done.4.y_ref), channel_id=1, source_target_pairs={{0,1},{1,0},{2,3},{3,2},{4,5},{5,4},{6,7},{7,6},{8,9},{9,8},{10,11... | collective-permute-start | bytes 786440 | tf_op jit(solution)/shard_map/ppermute | solution.py:273
  29.4 13.8 %collective-permute-start.10 = (bf16[256,1024]{1,0:T(8,128)(2,1)S(1)}, bf16[256,1024]{1,0:T(8,128)(2,1)S(1)}, u32[]{:S(2)}, u32[]{:S(2)}) collective-permute-start(bf16[256,1024]{1,0:T(8,128)(2,1)S(1)} %copy-done), channel_id=1, source_target_pairs={{0,1},{1,0},{2,3},{3,2},{4,5},{5,4},{6,7},{7,6},{8,9},{9,8},{10,11... | collective-permute-start | bytes 1572872 | tf_op jit(solution)/shard_map/ppermute | solution.py:273
  41.7 5.9 %collective-permute-start.11 = (bf16[256,1024]{1,0:T(8,128)(2,1)S(1)}, bf16[256,1024]{1,0:T(8,128)(2,1)S(1)}, u32[]{:S(2)}, u32[]{:S(2)}) collective-permute-start(bf16[256,1024]{1,0:T(8,128)(2,1)S(1)} %collective-permute-done.6.y_ref), channel_id=1, source_target_pairs={{0,1},{1,0},{2,3},{3,2},{4,5},{5,4},{6,7},{7,6},{8,9},{9,8},{10,11... | collective-permute-start | bytes 1572872 | tf_op jit(solution)/shard_map/ppermute | solution.py:273
  41.7 5.9 %collective-permute-start.9 = (bf16[128,512]{1,0:T(8,128)(2,1)S(1)}, bf16[128,512]{1,0:T(8,128)(2,1)S(1)}, u32[]{:S(2)}, u32[]{:S(2)}) collective-permute-start(bf16[128,512]{1,0:T(8,128)(2,1)S(1)} %shard_map.161.a_ref), channel_id=1, source_target_pairs={{0,2},{2,0},{1,3},{3,1},{4,6},{6,4},{5,7},{7,5},{8,10},{10,8},{9,1... | collective-permute-start | bytes 393224 | tf_op jit(solution)/shard_map/ppermute | solution.py:273

commit v4 on v1

v4 whole, which is shorter than its diff:
```python
import jax
import jax.numpy as jnp
from jax import lax
from jax.experimental import pallas as pl
from jax.experimental.pallas import tpu as pltpu
from jax.sharding import Mesh
from jax.sharding import PartitionSpec as P

QUERY_HEADS = 16
KEY_VALUE_HEADS = 8
HEAD_SIZE = 128
NT = (((1,), (1,)), ((), ()))
TN = (((0,), (0,)), ((), ()))
F32 = jnp.float32
HIDDEN = -1e30
BF16 = jnp.bfloat16


def cache_tags(pool_root, branch_owner, branch_len, root_count, slot_count, owner_ids):
    branch_count = branch_owner.shape[0]
    branch_ids = jnp.arange(branch_count, dtype=jnp.int32)
    owned = jnp.sum(
        jnp.where(branch_owner[None, :] == owner_ids[:, None], branch_ids[None, :], 0), axis=1
    )
    owned_length = jnp.sum(
        jnp.where(branch_ids[None, :] == owned[:, None], branch_len[None, :], 0), axis=1
    )
    slot_ids = jnp.arange(slot_count, dtype=jnp.int32)
    branch_tags = jnp.where(
        slot_ids[None, :] < owned_length[:, None], root_count + owned[:, None], -1
    )
    return jnp.concatenate([pool_root, branch_tags], axis=1).reshape(-1)


def token_nodes(request_branch, token_request, branch_root):
    requests = token_request[0]
    local_branches = request_branch[0]
    request_ids = jnp.arange(local_branches.shape[0], dtype=jnp.int32)
    token_branch = jnp.sum(
        jnp.where(requests[:, None] == request_ids[None, :], local_branches[None, :], 0), axis=1
    )
    branch_ids = jnp.arange(branch_root.shape[0], dtype=jnp.int32)
    token_root = jnp.sum(
        jnp.where(token_branch[:, None] == branch_ids[None, :], branch_root[None, :], 0), axis=1
    )
    return requests, token_branch, token_root


def head_lanes(h):
    return slice(h * HEAD_SIZE, (h + 1) * HEAD_SIZE)


def seq_index():
    return 2 * lax.axis_index("z") + lax.axis_index("y")


def own_nodes(request, branches_ref, roots_ref):
    branch, root = jnp.zeros_like(request), jnp.zeros_like(request)
    for r in range(branches_ref.shape[1]):
        b = branches_ref[0, r]
        branch = jnp.where(request == r, b, branch)
        root = jnp.where(request == r, roots_ref[b], root)
    return branch, root


def cache_bias(branch, root, pool_ref, owner_ref, length_ref, root_count):
    e = seq_index()
    owners, slots = pool_ref.shape
    by_row = pool_ref[...].astype(F32).T
    lane = lax.broadcasted_iota(jnp.int32, by_row.shape, 1)
    slot = lax.broadcasted_iota(jnp.int32, (slots, branch.shape[1]), 0)
    pieces = []
    for s in range(owners):
        holder = e ^ s
        held = jnp.sum(jnp.where(lane == holder, by_row, 0.0), axis=1, keepdims=True)
        owned, length = 0, 0
        for b in range(owners):
            here = owner_ref[b] == holder
            owned = jnp.where(here, b, owned)
            length = jnp.where(here, length_ref[b], length)
        pieces.append(held.astype(jnp.int32) == root)
        pieces.append((slot < length) & (branch == owned))
    return jnp.concatenate([jnp.where(seen, 0.0, HIDDEN) for seen in pieces], axis=0)


def chunk_offset(e, k, width):
    return pl.multiple_of((e ^ (k // 2)) * (2 * width) + (k % 2) * width, width)


def mp_index():
    return 2 * lax.axis_index("x") + lax.axis_index("c")


def attend_kernel(
    q_ref, kf_ref, vf_ref, request_ref, branches_ref, roots_ref, pool_ref, owner_ref, length_ref,
    res_ref, *refs,
):
    caches, out_ref, sends = refs[:-5], refs[-5], refs[-4:]
    e, m = seq_index(), mp_index()
    tok, wide = q_ref.shape
    request = request_ref[...]
    branch, root = own_nodes(request, branches_ref, roots_ref)
    root_count = lax.axis_size("z") * lax.axis_size("y") // 4
    down = jnp.broadcast_to(request.astype(F32), (8, tok)).T[:, :1].astype(jnp.int32)
    key_at = lax.broadcasted_iota(jnp.int32, (tok, tok), 0)
    token_at = lax.broadcasted_iota(jnp.int32, (tok, tok), 1)
    fresh = jnp.where((down == request) & (key_at <= token_at), 0.0, HIDDEN)
    bias = jnp.concatenate(
        [fresh, cache_bias(branch, root, pool_ref, owner_ref, length_ref, root_count)], axis=0
    )
    bias = jnp.concatenate([bias, bias], axis=1)
    for k in range(kf_ref.shape[1] // HEAD_SIZE):
        lanes, first, second = head_lanes(k), head_lanes(2 * k), head_lanes(2 * k + 1)
        keys = jnp.concatenate([kf_ref[:, lanes]] + [c[0, :, lanes] for c in caches], axis=0)
        values = jnp.concatenate([vf_ref[:, lanes]] + [c[1, :, lanes] for c in caches], axis=0)
        queries = jnp.concatenate([q_ref[:, first], q_ref[:, second]], axis=0)
        scores = (
            lax.dot_general(keys, queries, NT, preferred_element_type=F32) * HEAD_SIZE**-0.5 + bias
        )
        peak = jnp.max(scores, axis=0, keepdims=True)
        prob = jnp.exp(scores - peak)
        total = jnp.sum(prob, axis=0, keepdims=True)
        mixed = lax.dot_general(values, prob.astype(BF16), TN, preferred_element_type=F32)
        attn = (mixed / total).T.astype(BF16)
        for ref in (out_ref, *sends):
            ref[:, first] = attn[:tok]
            ref[:, second] = attn[tok:]
    width = sends[0].shape[1] - wide
    for s, ref in enumerate(sends):
        ref[:, wide:] = res_ref[:, pl.ds(chunk_offset(e ^ (2 * s), m, width), width)]


def project_kernel(a0, a1, a2, a3, own_ref, par_ref, o0, o1, o2, o3, hold):
    m = mp_index()
    half, wide = own_ref.shape
    blocks = (a0, a1, a2, a3)
    attn = jnp.concatenate([a[:, :wide] for a in blocks], axis=0)
    rest = jnp.concatenate([a[:, wide:] for a in blocks], axis=0)
    hold[:, :half] = lax.dot_general(attn, own_ref[...], NT, preferred_element_type=F32)
    hold[:, half:] = lax.dot_general(attn, par_ref[...], NT, preferred_element_type=F32)
    width = o0.shape[1]
    for j, out in enumerate((o0, o1, o2, o3)):
        chunk = hold[:, pl.ds(pl.multiple_of((m ^ j) * width, width), width)]
        out[...] = chunk + rest.astype(F32) if j == 0 else chunk.astype(BF16)


def combine_kernel(r0, r1, r2, r3, out, t0, t1, t2, t3):
    tok = t0.shape[0]
    stream = (
        r0[...] + r1[...].astype(F32) + r2[...].astype(F32) + r3[...].astype(F32)
    ).astype(BF16)
    out[...] = stream
    for s, part in enumerate((t0, t1, t2, t3)):
        part[...] = stream[s * tok : (s + 1) * tok]


def qkv_kernel(x0, x1, x2, x3, gain_ref, own_ref, par_ref, o0, o1, o2, o3, hold):
    e, m = seq_index(), mp_index()
    width = x0.shape[1]
    half = 2 * width
    tok = o0.shape[0]
    for j, part in enumerate((x0, x1, x2, x3)):
        k = m ^ j
        gain = gain_ref[:, pl.ds(chunk_offset(e, k, width), width)]
        hold[:, pl.ds(pl.multiple_of(k * width, width), width)] = (
            part[...].astype(F32) * gain
        ).astype(BF16)
    product = jnp.dot(hold[:, :half], own_ref[...], preferred_element_type=F32) + jnp.dot(
        hold[:, half:], par_ref[...], preferred_element_type=F32
    )
    for s, out in enumerate((o0, o1, o2, o3)):
        out[...] = product[s * tok : (s + 1) * tok].astype(out.dtype)


def pack_kernel(t0, t1, t2, t3, out_ref):
    width = t0.shape[1]
    for s, part in enumerate((t0, t1, t2, t3)):
        out_ref[:, s * width : (s + 1) * width] = part[...]


def finish_kernel(y0, y1, y2, y3, p0, p1, p2, p3, qkv_ref, stream_ref):
    e, m = seq_index(), mp_index()
    width = p0.shape[1] // 4
    squares = jnp.zeros((p0.shape[0], width), F32)
    for j, part in enumerate((p0, p1, p2, p3)):
        for s in range(4):
            block = part[:, s * width : (s + 1) * width]
            wide = block.astype(F32)
            squares = squares + wide * wide
            stream_ref[:, pl.ds(chunk_offset(e ^ (2 * s), m ^ j, width), width)] = block
    mean_square = jnp.sum(squares, axis=1, keepdims=True) / stream_ref.shape[1]
    total = y0[...] + y1[...].astype(F32) + y2[...].astype(F32) + y3[...].astype(F32)
    qkv_ref[...] = (total * lax.rsqrt(mean_square + 1e-06)).astype(BF16)


def call(kernel, out_shape, args, scratch=(), scalars=(), flops=0, moved=1 << 20):
    vmem, smem = pl.BlockSpec(memory_space=pltpu.VMEM), pl.BlockSpec(memory_space=pltpu.SMEM)
    return pl.pallas_call(
        kernel,
        out_shape=out_shape,
        in_specs=[smem if i in scalars else vmem for i in range(len(args))],
        out_specs=jax.tree.map(lambda _: vmem, out_shape),
        scratch_shapes=list(scratch),
        compiler_params=pltpu.CompilerParams(vmem_limit_bytes=24 << 20),
        cost_estimate=pl.CostEstimate(flops=flops, bytes_accessed=moved, transcendentals=0),
    )(*args)


def swap(value, axes, bits):
    count = lax.axis_size(axes)
    return lax.ppermute(value, axes, [(i, i ^ bits) for i in range(count)])


def on_block(
    fresh_queries,
    fresh_keys,
    fresh_values,
    cache,
    pool_root,
    branch_owner,
    branch_len,
    branch_root,
    request_branch,
    token_request,
    residual,
    wo_t,
    norm_gain,
    w_qkv,
):
    tok, wide = fresh_queries.shape
    width = wo_t.shape[0] // 2
    columns = w_qkv.shape[1]
    sds = jax.ShapeDtypeStruct
    seq, mp = ("z", "y"), ("x", "c")

    far = {s: swap(cache, seq, s) for s in (4, 6, 5, 7, 2, 3, 1)}
    blocks = [cache] + [far[s] for s in range(1, 8)]
    blocks, wo_later = lax.optimization_barrier((blocks, wo_t))
    wo_pair = swap(wo_later, "y", 1)
    attn, *sends = call(
        attend_kernel,
        [sds((tok, wide), BF16)] + [sds((tok, wide + width), BF16)] * 4,
        (
            fresh_queries, fresh_keys, fresh_values, token_request, request_branch, branch_root,
            pool_root, branch_owner, branch_len, residual, *blocks,
        ),
        scalars=(4, 5, 7, 8),
        flops=1 << 26,
    )
    own_send, wq_later = lax.optimization_barrier((sends[0], w_qkv))
    wq_pair = swap(wq_later, "y", 1)
    a2, a3, a1 = (swap(sends[s], "z", s) for s in (2, 3, 1))
    sums = call(
        project_kernel,
        [sds((4 * tok, width), F32)] + [sds((4 * tok, width), BF16)] * 3,
        (own_send, a1, a2, a3, wo_t, wo_pair),
        scratch=[pltpu.VMEM((4 * tok, 4 * width), F32)],
        flops=1 << 27,
    )
    sums = [sums[0]] + [swap(sums[j], mp, j) for j in range(1, 4)]
    made = call(
        combine_kernel,
        [sds((4 * tok, width), BF16)] + [sds((tok, width), BF16)] * 4,
        tuple(sums),
    )
    slices = [made[0]] + [swap(made[0], mp, j) for j in range(1, 4)]
    home = [made[1]] + [swap(made[1 + s], "z", s) for s in range(1, 4)]
    partial = call(
        qkv_kernel,
        [sds((tok, columns), F32)] + [sds((tok, columns), BF16)] * 3,
        (*slices, norm_gain[None, :], w_qkv, wq_pair),
        scratch=[pltpu.VMEM((4 * tok, 4 * width), BF16)],
        flops=1 << 28,
    )
    y1, y2, y3 = (swap(partial[s], "z", s) for s in (1, 2, 3))
    home, y1 = lax.optimization_barrier((home, y1))
    packed = call(pack_kernel, sds((tok, 4 * width), BF16), tuple(home))
    pieces = [packed] + [swap(packed, mp, j) for j in range(1, 4)]
    qkv_next, stream = call(
        finish_kernel,
        [sds((tok, columns), BF16), sds(residual.shape, BF16)],
        (partial[0], y1, y2, y3, *pieces),
    )
    return attn, stream, qkv_next


def absorb(running, query_rows, key_row_block, value_rows, visible, score_scale):
    peak_old, total, mixed = running
    scores = (
        jnp.einsum("tkgd,rkd->tkgr", query_rows, key_row_block, preferred_element_type=jnp.float32)
        * score_scale
    )
    seen = visible[:, None, None, :]
    peak_new = jnp.maximum(peak_old, jnp.max(jnp.where(seen, scores, -jnp.inf), axis=-1))
    factor = jnp.exp(peak_old - peak_new)
    weights_full = jnp.where(seen, jnp.exp(scores - peak_new[..., None]), 0.0)
    total = total * factor + jnp.sum(weights_full, axis=-1)
    mixed = mixed * factor[..., None] + jnp.einsum(
        "tkgr,rkd->tkgd",
        weights_full.astype(jnp.bfloat16),
        value_rows,
        preferred_element_type=jnp.float32,
    )
    return (peak_new, total, mixed)


def on_device(
    fresh_queries,
    fresh_keys,
    fresh_values,
    cache,
    pool_root,
    branch_owner,
    branch_len,
    branch_root,
    request_branch,
    token_request,
    residual,
    wo_t,
    norm_gain,
    w_qkv,
):
    seq_count = lax.axis_size("seq")
    root_count = seq_count // 4
    tok_rows = fresh_queries.shape[0]
    kv_local = fresh_keys.shape[1] // HEAD_SIZE
    query_groups = QUERY_HEADS // KEY_VALUE_HEADS
    score_scale = HEAD_SIZE ** (-0.5)
    slot_count = cache.shape[1] - pool_root.shape[1]
    owner_ids = jnp.arange(seq_count, dtype=jnp.int32)
    tags = cache_tags(pool_root, branch_owner, branch_len, root_count, slot_count, owner_ids)
    requests, token_branch, token_root = token_nodes(request_branch, token_request, branch_root)
    query_rows = fresh_queries.reshape(tok_rows, kv_local, query_groups, HEAD_SIZE)
    incoming_keys = fresh_keys.reshape(tok_rows, kv_local, HEAD_SIZE)
    incoming_values = fresh_values.reshape(tok_rows, kv_local, HEAD_SIZE)
    positions = jnp.arange(tok_rows, dtype=jnp.int32)
    own_visible = (requests[None, :] == requests[:, None]) & (
        positions[None, :] <= positions[:, None]
    )
    start_state = (
        jnp.full((tok_rows, kv_local, query_groups), -jnp.inf, jnp.float32),
        jnp.zeros((tok_rows, kv_local, query_groups), jnp.float32),
        jnp.zeros((tok_rows, kv_local, query_groups, HEAD_SIZE), jnp.float32),
    )
    state = absorb(
        start_state, query_rows, incoming_keys, incoming_values, own_visible, score_scale
    )
    piece = lax.all_gather(cache, "seq", axis=1, tiled=True)
    rows = piece.shape[1]
    block = 512 if rows > 512 and rows % 512 == 0 else rows
    key_blocks = piece[0].reshape(rows // block, block, kv_local, HEAD_SIZE)
    value_blocks = piece[1].reshape(rows // block, block, kv_local, HEAD_SIZE)
    tag_blocks = tags.reshape(rows // block, block)

    def one_block(running, parts):
        key_row_block, value_rows, tag_rows = parts
        visible = (tag_rows[None, :] == token_root[:, None]) | (
            tag_rows[None, :] == root_count + token_branch[:, None]
        )
        updated = absorb(running, query_rows, key_row_block, value_rows, visible, score_scale)
        return (updated, None)

    state, unused = lax.scan(one_block, state, (key_blocks, value_blocks, tag_blocks))
    peak_final, total_final, mixed_final = state
    attn = (
        (mixed_final / total_final[..., None])
        .reshape(tok_rows, kv_local * query_groups * HEAD_SIZE)
        .astype(jnp.bfloat16)
    )
    partial_value = lax.dot_general(
        attn,
        lax.all_gather(wo_t, "seq", axis=0, tiled=True),
        (((1,), (1,)), ((), ())),
        preferred_element_type=jnp.float32,
    )
    summed = lax.psum(partial_value.astype(jnp.bfloat16), "mp").astype(jnp.float32)
    stream = (residual.astype(jnp.float32) + summed).astype(jnp.bfloat16)
    widened = stream.astype(jnp.float32)
    mean_square = jnp.mean(widened * widened, axis=-1, keepdims=True)
    normed = (widened * lax.rsqrt(mean_square + 1e-06) * norm_gain[None, :]).astype(jnp.bfloat16)
    qkv_sum = jnp.dot(
        normed, lax.all_gather(w_qkv, "seq", axis=0, tiled=True), preferred_element_type=jnp.float32
    )
    return (attn, stream, qkv_sum.astype(jnp.bfloat16))


def solution(mesh):
    small = mesh.shape["seq"] == 8 and mesh.shape["mp"] == 4
    seq, mp = "seq", "mp"
    if small:
        mesh = Mesh(mesh.devices.reshape(4, 2, 2, 2), ("z", "y", "x", "c"))
        seq, mp = ("z", "y"), ("x", "c")
    return jax.shard_map(
        on_block if small else on_device,
        mesh=mesh,
        in_specs=(
            P(seq, mp),
            P(seq, mp),
            P(seq, mp),
            P(None, seq, mp),
            P(),
            P(),
            P(),
            P(),
            P(seq, None),
            P(seq, None),
            P(seq, None),
            P(seq, mp),
            P(),
            P(seq, mp),
        ),
        out_specs=(P(seq, mp), P(seq, None), P(seq, mp)),
        check_vma=False,
    )
```

time: 92 us -> 85.1 us (0.925)
  waiting for transfers between devices: 49.4 us -> 38.2 us
  local copies, waits for them, and re-layouts: 1.5 us -> 8.11 us
  other arithmetic: 1.21 us -> 0 us
    ppermute x30 -> x27, waiting for transfers between devices: 49.4 us -> 38.2 us  [swap(): return lax.ppermute(value, axes, [(i, i ^ bits) for i in range(count)])]
    unnamed x30 -> x28, local copies, waits for them, and re-layouts: 1.43 us -> 8.11 us
    ppermute x30 -> x27, starting transfers between devices: 34.5 us -> 33.6 us  [swap(): return lax.ppermute(value, axes, [(i, i ^ bits) for i in range(count)])]
  transfers between devices with their start and end apart: 30 -> 27, of which waited for: 12 -> 16; matrix products, arithmetic and copies ran while one was open for 1% -> 0% of each run, Pallas kernels for 2% -> 1%
where the time goes in v4:
time: 85.1 us; the launch traced here: 84.6 us
  waiting for transfers between devices  38.2 us (45%)
  starting transfers between devices  33.6 us (39%)
  local copies, waits for them, and re-layouts  8.11 us (10%)
  Pallas kernels  3.91 us (5%)
    ppermute x27, waiting for transfers between devices, swap(): return lax.ppermute(value, axes, [(i, i ^ bits) for i in range(count)])  38.2 us
    ppermute x27, starting transfers between devices, swap(): return lax.ppermute(value, axes, [(i, i ^ bits) for i in range(count)])  33.6 us
    unnamed x28, local copies, waits for them, and re-layouts  8.11 us
    pallas_call x6, Pallas kernels, call(): pl.pallas_call(kernel, out_shape=out_shape, in_specs=[smem if i in scalar...  3.91 us
  transfers between devices with their start and end apart: 27, of which 16 were waited for; matrix products, arithmetic and copies ran while one was open for 0% of the time, Pallas kernels for 1%

profile of v4, /device:TPU:0, one launch (start us, length us, event | category | flops | bytes accessed | tf_op | source)
XLA Modules:
  0.0 84.6 jit_solution(12703716236219756906)
XLA Ops:
  0.6 5.1 %collective-permute-start.5 = (bf16[2,64,256]{2,1,0:T(8,128)(2,1)}, bf16[2,64,256]{2,1,0:T(8,128)(2,1)S(1)}, u32[]{:S(2)}, u32[]{:S(2)}) collective-permute-start(bf16[2,64,256]{2,1,0:T(8,128)(2,1)} %refs_0_), channel_id=1, source_target_pairs={{0,24},{4,28},{8,16},{12,20},{16,8},{20,12},{24,0},{28,4},{1,25},{... | collective-permute-start | bytes 196616 | tf_op jit(solution)/shard_map/ppermute | solution.py:211
  6.2 3.5 %collective-permute-start.3 = (bf16[2,64,256]{2,1,0:T(8,128)(2,1)}, bf16[2,64,256]{2,1,0:T(8,128)(2,1)S(1)}, u32[]{:S(2)}, u32[]{:S(2)}) collective-permute-start(bf16[2,64,256]{2,1,0:T(8,128)(2,1)} %refs_0_), channel_id=1, source_target_pairs={{0,16},{4,20},{8,24},{12,28},{16,0},{20,4},{24,8},{28,12},{1,17},{... | collective-permute-start | bytes 196616 | tf_op jit(solution)/shard_map/ppermute | solution.py:211
  9.6 2.0 %collective-permute-start.1 = (bf16[2,64,256]{2,1,0:T(8,128)(2,1)}, bf16[2,64,256]{2,1,0:T(8,128)(2,1)S(1)}, u32[]{:S(2)}, u32[]{:S(2)}) collective-permute-start(bf16[2,64,256]{2,1,0:T(8,128)(2,1)} %refs_0_), channel_id=1, source_target_pairs={{0,8},{4,12},{8,0},{12,4},{16,24},{20,28},{24,16},{28,20},{1,9},{5... | collective-permute-start | bytes 196616 | tf_op jit(solution)/shard_map/ppermute | solution.py:211
  11.6 1.5 %collective-permute-start = (bf16[2,64,256]{2,1,0:T(8,128)(2,1)}, bf16[2,64,256]{2,1,0:T(8,128)(2,1)S(1)}, u32[]{:S(2)}, u32[]{:S(2)}) collective-permute-start(bf16[2,64,256]{2,1,0:T(8,128)(2,1)} %refs_0_), channel_id=1, source_target_pairs={{0,4},{4,0},{8,12},{12,8},{16,20},{20,16},{24,28},{28,24},{1,5},{5... | collective-permute-start | bytes 196616 | tf_op jit(solution)/shard_map/ppermute | solution.py:211
  13.1 1.1 %collective-permute-done.4.refs_5_ = bf16[2,64,256]{2,1,0:T(8,128)(2,1)S(1)} collective-permute-done((bf16[2,64,256]{2,1,0:T(8,128)(2,1)}, bf16[2,64,256]{2,1,0:T(8,128)(2,1)S(1)}, u32[]{:S(2)}, u32[]{:S(2)}) %collective-permute-start.4) | collective-permute-done | bytes 65568 | tf_op jit(solution)/shard_map/ppermute | solution.py:211
  14.2 2.0 %collective-permute-start.6 = (bf16[2,64,256]{2,1,0:T(8,128)(2,1)}, bf16[2,64,256]{2,1,0:T(8,128)(2,1)S(1)}, u32[]{:S(2)}, u32[]{:S(2)}) collective-permute-start(bf16[2,64,256]{2,1,0:T(8,128)(2,1)} %refs_0_), channel_id=1, source_target_pairs={{0,28},{4,24},{8,20},{12,16},{16,12},{20,8},{24,4},{28,0},{1,29},{... | collective-permute-start | bytes 196616 | tf_op jit(solution)/shard_map/ppermute | solution.py:211
  17.2 4.2 %collective-permute-done.6.refs_7_ = bf16[2,64,256]{2,1,0:T(8,128)(2,1)S(1)} collective-permute-done((bf16[2,64,256]{2,1,0:T(8,128)(2,1)}, bf16[2,64,256]{2,1,0:T(8,128)(2,1)S(1)}, u32[]{:S(2)}, u32[]{:S(2)}) %collective-permute-start.6) | collective-permute-done | bytes 65568 | tf_op jit(solution)/shard_map/ppermute | solution.py:211
  21.4 0.9 %copy-done.1 = bf16[64,2048]{1,0:T(8,128)(2,1)S(1)} copy-done((bf16[64,2048]{1,0:T(8,128)(2,1)S(1)}, bf16[64,2048]{1,0:T(8,128)(2,1)}, u32[]{:S(2)}) %copy-start.1) | copy-done | bytes 262168
  29.5 2.1 %shard_map.157 = (bf16[64,512]{1,0:T(8,128)(2,1)}, bf16[64,640]{1,0:T(8,128)(2,1)S(1)}, bf16[64,640]{1,0:T(8,128)(2,1)S(1)}, bf16[64,640]{1,0:T(8,128)(2,1)S(1)}, bf16[64,640]{1,0:T(8,128)(2,1)S(1)}) custom-call(bf16[64,512]{1,0:T(8,128)(2,1)S(1)} %copy-done.3, bf16[64,256]{1,0:T(8,128)(2,1)S(1)} %copy-done.5, bf16[64,256]{1,0:T(8,128)(2,1)S(1)} %copy-done.6, ...), custom_call_target="tpu_custom_call" | custom-call | flops 67108864 | bytes 1048576 | tf_op jit(solution)/shard_map/pallas_call | solution.py:198
  31.6 1.0 %collective-permute-start.17 = (bf16[256,1024]{1,0:T(8,128)(2,1)S(1)}, bf16[256,1024]{1,0:T(8,128)(2,1)S(1)}, u32[]{:S(2)}, u32[]{:S(2)}) collective-permute-start(bf16[256,1024]{1,0:T(8,128)(2,1)S(1)} %copy-done), channel_id=1, source_target_pairs={{0,4},{4,0},{1,5},{5,1},{2,6},{6,2},{3,7},{7,3},{8,12},{12,8},{9,1... | collective-permute-start | bytes 1572872 | tf_op jit(solution)/shard_map/ppermute | solution.py:211
  32.6 1.0 %collective-permute-start.10 = (bf16[256,512]{1,0:T(8,128)(2,1)S(1)}, bf16[256,512]{1,0:T(8,128)(2,1)S(1)}, u32[]{:S(2)}, u32[]{:S(2)}) collective-permute-start(bf16[256,512]{1,0:T(8,128)(2,1)S(1)} %copy-done.2), channel_id=1, source_target_pairs={{0,4},{4,0},{1,5},{5,1},{2,6},{6,2},{3,7},{7,3},{8,12},{12,8},{9,1... | collective-permute-start | bytes 786440 | tf_op jit(solution)/shard_map/ppermute | solution.py:211
  33.6 3.8 %collective-permute-start.8 = (bf16[64,640]{1,0:T(8,128)(2,1)S(1)}, bf16[64,640]{1,0:T(8,128)(2,1)S(1)}, u32[]{:S(2)}, u32[]{:S(2)}) collective-permute-start(bf16[64,640]{1,0:T(8,128)(2,1)S(1)} %get-tuple-element.51), channel_id=1, source_target_pairs={{0,16},{8,24},{16,0},{24,8},{1,17},{9,25},{17,1},{25,9},{2,18},{10... | collective-permute-start | bytes 245768 | tf_op jit(solution)/shard_map/ppermute | solution.py:211
  38.0 0.9 %collective-permute-done.7.a1 = bf16[64,640]{1,0:T(8,128)(2,1)S(1)} collective-permute-done((bf16[64,640]{1,0:T(8,128)(2,1)S(1)}, bf16[64,640]{1,0:T(8,128)(2,1)S(1)}, u32[]{:S(2)}, u32[]{:S(2)}) %collective-permute-start.7) | collective-permute-done | bytes 81952 | tf_op jit(solution)/shard_map/ppermute | solution.py:211
  38.9 1.8 %collective-permute-done.8.a2 = bf16[64,640]{1,0:T(8,128)(2,1)S(1)} collective-permute-done((bf16[64,640]{1,0:T(8,128)(2,1)S(1)}, bf16[64,640]{1,0:T(8,128)(2,1)S(1)}, u32[]{:S(2)}, u32[]{:S(2)}) %collective-permute-start.8) | collective-permute-done | bytes 81952 | tf_op jit(solution)/shard_map/ppermute | solution.py:211
  40.7 2.9 %collective-permute-done.9.a3 = bf16[64,640]{1,0:T(8,128)(2,1)S(1)} collective-permute-done((bf16[64,640]{1,0:T(8,128)(2,1)S(1)}, bf16[64,640]{1,0:T(8,128)(2,1)S(1)}, u32[]{:S(2)}, u32[]{:S(2)}) %collective-permute-start.9) | collective-permute-done | bytes 81952 | tf_op jit(solution)/shard_map/ppermute | solution.py:211
  43.6 5.9 %collective-permute-done.10.par_ref = bf16[256,512]{1,0:T(8,128)(2,1)S(1)} collective-permute-done((bf16[256,512]{1,0:T(8,128)(2,1)S(1)}, bf16[256,512]{1,0:T(8,128)(2,1)S(1)}, u32[]{:S(2)}, u32[]{:S(2)}) %collective-permute-start.10) | collective-permute-done | bytes 262176 | tf_op jit(solution)/shard_map/ppermute | solution.py:211
  50.0 1.6 %collective-permute-start.12 = (bf16[256,128]{1,0:T(8,128)(2,1)S(1)}, bf16[256,128]{1,0:T(8,128)(2,1)S(1)}, u32[]{:S(2)}, u32[]{:S(2)}) collective-permute-start(bf16[256,128]{1,0:T(8,128)(2,1)S(1)} %get-tuple-element.56), channel_id=1, source_target_pairs={{0,2},{1,3},{2,0},{3,1},{4,6},{5,7},{6,4},{7,5},{8,10},{9,11},{10,... | collective-permute-start | bytes 196616 | tf_op jit(solution)/shard_map/ppermute | solution.py:211
  51.9 2.6 %collective-permute-done.12.r2 = bf16[256,128]{1,0:T(8,128)(2,1)S(1)} collective-permute-done((bf16[256,128]{1,0:T(8,128)(2,1)S(1)}, bf16[256,128]{1,0:T(8,128)(2,1)S(1)}, u32[]{:S(2)}, u32[]{:S(2)}) %collective-permute-start.12) | collective-permute-done | bytes 65568 | tf_op jit(solution)/shard_map/ppermute | solution.py:211
  54.5 1.1 %collective-permute-done.13.r3 = bf16[256,128]{1,0:T(8,128)(2,1)S(1)} collective-permute-done((bf16[256,128]{1,0:T(8,128)(2,1)S(1)}, bf16[256,128]{1,0:T(8,128)(2,1)S(1)}, u32[]{:S(2)}, u32[]{:S(2)}) %collective-permute-start.13) | collective-permute-done | bytes 65568 | tf_op jit(solution)/shard_map/ppermute | solution.py:211
  55.7 1.3 %collective-permute-start.16 = (bf16[256,128]{1,0:T(8,128)(2,1)S(1)}, bf16[256,128]{1,0:T(8,128)(2,1)S(1)}, u32[]{:S(2)}, u32[]{:S(2)}) collective-permute-start(bf16[256,128]{1,0:T(8,128)(2,1)S(1)} %get-tuple-element.58.x0), channel_id=1, source_target_pairs={{0,3},{1,2},{2,1},{3,0},{4,7},{5,6},{6,5},{7,4},{8,11},{9,10},{10,... | collective-permute-start | bytes 196616 | tf_op jit(solution)/shard_map/ppermute | solution.py:211
  57.6 2.3 %collective-permute-done.16.x3 = bf16[256,128]{1,0:T(8,128)(2,1)S(1)} collective-permute-done((bf16[256,128]{1,0:T(8,128)(2,1)S(1)}, bf16[256,128]{1,0:T(8,128)(2,1)S(1)}, u32[]{:S(2)}, u32[]{:S(2)}) %collective-permute-start.16) | collective-permute-done | bytes 65568 | tf_op jit(solution)/shard_map/ppermute | solution.py:211
  59.9 1.7 %collective-permute-done.15.x2 = bf16[256,128]{1,0:T(8,128)(2,1)S(1)} collective-permute-done((bf16[256,128]{1,0:T(8,128)(2,1)S(1)}, bf16[256,128]{1,0:T(8,128)(2,1)S(1)}, u32[]{:S(2)}, u32[]{:S(2)}) %collective-permute-start.15) | collective-permute-done | bytes 65568 | tf_op jit(solution)/shard_map/ppermute | solution.py:211
  62.1 1.6 %collective-permute-start.22 = (bf16[64,1024]{1,0:T(8,128)(2,1)S(1)}, bf16[64,1024]{1,0:T(8,128)(2,1)S(1)}, u32[]{:S(2)}, u32[]{:S(2)}) collective-permute-start(bf16[64,1024]{1,0:T(8,128)(2,1)S(1)} %get-tuple-element.67), channel_id=1, source_target_pairs={{0,16},{8,24},{16,0},{24,8},{1,17},{9,25},{17,1},{25,9},{2,18},{10... | collective-permute-start | bytes 393224 | tf_op jit(solution)/shard_map/ppermute | solution.py:211
  63.8 2.7 %collective-permute-start.23 = (bf16[64,1024]{1,0:T(8,128)(2,1)S(1)}, bf16[64,1024]{1,0:T(8,128)(2,1)S(1)}, u32[]{:S(2)}, u32[]{:S(2)}) collective-permute-start(bf16[64,1024]{1,0:T(8,128)(2,1)S(1)} %get-tuple-element.68), channel_id=1, source_target_pairs={{0,24},{8,16},{16,8},{24,0},{1,25},{9,17},{17,9},{25,1},{2,26},{10... | collective-permute-start | bytes 393224 | tf_op jit(solution)/shard_map/ppermute | solution.py:211
  66.5 1.6 %collective-permute-start.19 = (bf16[64,128]{1,0:T(8,128)(2,1)S(1)}, bf16[64,128]{1,0:T(8,128)(2,1)S(1)}, u32[]{:S(2)}, u32[]{:S(2)}) collective-permute-start(bf16[64,128]{1,0:T(8,128)(2,1)S(1)} %get-tuple-element.63), channel_id=1, source_target_pairs={{0,16},{8,24},{16,0},{24,8},{1,17},{9,25},{17,1},{25,9},{2,18},{10... | collective-permute-start | bytes 49160 | tf_op jit(solution)/shard_map/ppermute | solution.py:211
  68.2 3.2 %collective-permute-done.18.t1 = bf16[64,128]{1,0:T(8,128)(2,1)S(1)} collective-permute-done((bf16[64,128]{1,0:T(8,128)(2,1)S(1)}, bf16[64,128]{1,0:T(8,128)(2,1)S(1)}, u32[]{:S(2)}, u32[]{:S(2)}) %collective-permute-start.18) | collective-permute-done | bytes 16416 | tf_op jit(solution)/shard_map/ppermute | solution.py:211
  71.3 0.9 %collective-permute-start.20 = (bf16[64,128]{1,0:T(8,128)(2,1)S(1)}, bf16[64,128]{1,0:T(8,128)(2,1)S(1)}, u32[]{:S(2)}, u32[]{:S(2)}) collective-permute-start(bf16[64,128]{1,0:T(8,128)(2,1)S(1)} %get-tuple-element.64), channel_id=1, source_target_pairs={{0,24},{8,16},{16,8},{24,0},{1,25},{9,17},{17,9},{25,1},{2,26},{10... | collective-permute-start | bytes 49160 | tf_op jit(solution)/shard_map/ppermute | solution.py:211
  72.3 5.6 %collective-permute-done.19.t2 = bf16[64,128]{1,0:T(8,128)(2,1)S(1)} collective-permute-done((bf16[64,128]{1,0:T(8,128)(2,1)S(1)}, bf16[64,128]{1,0:T(8,128)(2,1)S(1)}, u32[]{:S(2)}, u32[]{:S(2)}) %collective-permute-start.19) | collective-permute-done | bytes 16416 | tf_op jit(solution)/shard_map/ppermute | solution.py:211
  78.0 1.5 %collective-permute-start.25 = (bf16[64,512]{1,0:T(8,128)(2,1)S(1)}, bf16[64,512]{1,0:T(8,128)(2,1)S(1)}, u32[]{:S(2)}, u32[]{:S(2)}) collective-permute-start(bf16[64,512]{1,0:T(8,128)(2,1)S(1)} %shard_map.161.p0), channel_id=1, source_target_pairs={{0,2},{1,3},{2,0},{3,1},{4,6},{5,7},{6,4},{7,5},{8,10},{9,11},{10,... | collective-permute-start | bytes 196616 | tf_op jit(solution)/shard_map/ppermute | solution.py:211
  79.8 2.5 %collective-permute-done.26.p3 = bf16[64,512]{1,0:T(8,128)(2,1)S(1)} collective-permute-done((bf16[64,512]{1,0:T(8,128)(2,1)S(1)}, bf16[64,512]{1,0:T(8,128)(2,1)S(1)}, u32[]{:S(2)}, u32[]{:S(2)}) %collective-permute-start.26) | collective-permute-done | bytes 65568 | tf_op jit(solution)/shard_map/ppermute | solution.py:211
  82.3 1.4 %collective-permute-done.25.p2 = bf16[64,512]{1,0:T(8,128)(2,1)S(1)} collective-permute-done((bf16[64,512]{1,0:T(8,128)(2,1)S(1)}, bf16[64,512]{1,0:T(8,128)(2,1)S(1)}, u32[]{:S(2)}, u32[]{:S(2)}) %collective-permute-start.25) | collective-permute-done | bytes 65568 | tf_op jit(solution)/shard_map/ppermute | solution.py:211
  83.7 0.9 %shard_map.162 = (bf16[64,1024]{1,0:T(8,128)(2,1)}, bf16[64,2048]{1,0:T(8,128)(2,1)}) custom-call(f32[64,1024]{1,0:T(8,128)S(1)} %get-tuple-element.60.y0, bf16[64,1024]{1,0:T(8,128)(2,1)S(1)} %collective-permute-done.21.y1, bf16[64,1024]{1,0:T(8,128)(2,1)S(1)} %collective-permute-done.22.y2, bf16[64,1024]{1,0:T(8,128)(2,1)S(1)} %collective-permute-done.23.y3, ...), custom_call_target="tpu_custom_call" | custom-call | bytes 1048576 | tf_op jit(solution)/shard_map/pallas_call | solution.py:198
  (56 shorter events, 11.7 us)
Async XLA Ops:
  0.6 31.0 %copy-start = (bf16[256,1024]{1,0:T(8,128)(2,1)S(1)}, bf16[256,1024]{1,0:T(8,128)(2,1)}, u32[]{:S(2)}) copy-start(bf16[256,1024]{1,0:T(8,128)(2,1)} %own_ref.3) | copy-start | bytes 1572868
  0.6 11.0 %collective-permute-start.5 = (bf16[2,64,256]{2,1,0:T(8,128)(2,1)}, bf16[2,64,256]{2,1,0:T(8,128)(2,1)S(1)}, u32[]{:S(2)}, u32[]{:S(2)}) collective-permute-start(bf16[2,64,256]{2,1,0:T(8,128)(2,1)} %refs_0_), channel_id=1, source_target_pairs={{0,24},{4,28},{8,16},{12,20},{16,8},{20,12},{24,0},{28,4},{1,25},{... | collective-permute-start | bytes 196616 | tf_op jit(solution)/shard_map/ppermute | solution.py:211
  5.8 8.5 %collective-permute-start.4 = (bf16[2,64,256]{2,1,0:T(8,128)(2,1)}, bf16[2,64,256]{2,1,0:T(8,128)(2,1)S(1)}, u32[]{:S(2)}, u32[]{:S(2)}) collective-permute-start(bf16[2,64,256]{2,1,0:T(8,128)(2,1)} %refs_0_), channel_id=1, source_target_pairs={{0,20},{4,16},{8,28},{12,24},{16,4},{20,0},{24,12},{28,8},{1,21},{... | collective-permute-start | bytes 196616 | tf_op jit(solution)/shard_map/ppermute | solution.py:211
  6.2 10.1 %collective-permute-start.3 = (bf16[2,64,256]{2,1,0:T(8,128)(2,1)}, bf16[2,64,256]{2,1,0:T(8,128)(2,1)S(1)}, u32[]{:S(2)}, u32[]{:S(2)}) collective-permute-start(bf16[2,64,256]{2,1,0:T(8,128)(2,1)} %refs_0_), channel_id=1, source_target_pairs={{0,16},{4,20},{8,24},{12,28},{16,0},{20,4},{24,8},{28,12},{1,17},{... | collective-permute-start | bytes 196616 | tf_op jit(solution)/shard_map/ppermute | solution.py:211
  9.6 7.2 %collective-permute-start.2 = (bf16[2,64,256]{2,1,0:T(8,128)(2,1)}, bf16[2,64,256]{2,1,0:T(8,128)(2,1)S(1)}, u32[]{:S(2)}, u32[]{:S(2)}) collective-permute-start(bf16[2,64,256]{2,1,0:T(8,128)(2,1)} %refs_0_), channel_id=1, source_target_pairs={{0,12},{4,8},{8,4},{12,0},{16,28},{20,24},{24,20},{28,16},{1,13},{... | collective-permute-start | bytes 196616 | tf_op jit(solution)/shard_map/ppermute | solution.py:211
  9.6 7.2 %collective-permute-start.1 = (bf16[2,64,256]{2,1,0:T(8,128)(2,1)}, bf16[2,64,256]{2,1,0:T(8,128)(2,1)S(1)}, u32[]{:S(2)}, u32[]{:S(2)}) collective-permute-start(bf16[2,64,256]{2,1,0:T(8,128)(2,1)} %refs_0_), channel_id=1, source_target_pairs={{0,8},{4,12},{8,0},{12,4},{16,24},{20,28},{24,16},{28,20},{1,9},{5... | collective-permute-start | bytes 196616 | tf_op jit(solution)/shard_map/ppermute | solution.py:211
  11.6 5.6 %collective-permute-start = (bf16[2,64,256]{2,1,0:T(8,128)(2,1)}, bf16[2,64,256]{2,1,0:T(8,128)(2,1)S(1)}, u32[]{:S(2)}, u32[]{:S(2)}) collective-permute-start(bf16[2,64,256]{2,1,0:T(8,128)(2,1)} %refs_0_), channel_id=1, source_target_pairs={{0,4},{4,0},{8,12},{12,8},{16,20},{20,16},{24,28},{28,24},{1,5},{5... | collective-permute-start | bytes 196616 | tf_op jit(solution)/shard_map/ppermute | solution.py:211
  14.2 7.2 %collective-permute-start.6 = (bf16[2,64,256]{2,1,0:T(8,128)(2,1)}, bf16[2,64,256]{2,1,0:T(8,128)(2,1)S(1)}, u32[]{:S(2)}, u32[]{:S(2)}) collective-permute-start(bf16[2,64,256]{2,1,0:T(8,128)(2,1)} %refs_0_), channel_id=1, source_target_pairs={{0,28},{4,24},{8,20},{12,16},{16,12},{20,8},{24,4},{28,0},{1,29},{... | collective-permute-start | bytes 196616 | tf_op jit(solution)/shard_map/ppermute | solution.py:211
  21.4 1.0 %copy-start.1 = (bf16[64,2048]{1,0:T(8,128)(2,1)S(1)}, bf16[64,2048]{1,0:T(8,128)(2,1)}, u32[]{:S(2)}) copy-start(bf16[64,2048]{1,0:T(8,128)(2,1)} %res_ref.1) | copy-start | bytes 786436
  22.4 0.8 copy-start.3
  29.5 3.1 %copy-start.2 = (bf16[256,512]{1,0:T(8,128)(2,1)S(1)}, bf16[256,512]{1,0:T(8,128)(2,1)}, u32[]{:S(2)}) copy-start(bf16[256,512]{1,0:T(8,128)(2,1)} %own_ref.2) | copy-start | bytes 786436
  31.6 29.9 %collective-permute-start.17 = (bf16[256,1024]{1,0:T(8,128)(2,1)S(1)}, bf16[256,1024]{1,0:T(8,128)(2,1)S(1)}, u32[]{:S(2)}, u32[]{:S(2)}) collective-permute-start(bf16[256,1024]{1,0:T(8,128)(2,1)S(1)} %copy-done), channel_id=1, source_target_pairs={{0,4},{4,0},{1,5},{5,1},{2,6},{6,2},{3,7},{7,3},{8,12},{12,8},{9,1... | collective-permute-start | bytes 1572872 | tf_op jit(solution)/shard_map/ppermute | solution.py:211
  32.6 16.9 %collective-permute-start.10 = (bf16[256,512]{1,0:T(8,128)(2,1)S(1)}, bf16[256,512]{1,0:T(8,128)(2,1)S(1)}, u32[]{:S(2)}, u32[]{:S(2)}) collective-permute-start(bf16[256,512]{1,0:T(8,128)(2,1)S(1)} %copy-done.2), channel_id=1, source_target_pairs={{0,4},{4,0},{1,5},{5,1},{2,6},{6,2},{3,7},{7,3},{8,12},{12,8},{9,1... | collective-permute-start | bytes 786440 | tf_op jit(solution)/shard_map/ppermute | solution.py:211
  33.6 5.3 %collective-permute-start.7 = (bf16[64,640]{1,0:T(8,128)(2,1)S(1)}, bf16[64,640]{1,0:T(8,128)(2,1)S(1)}, u32[]{:S(2)}, u32[]{:S(2)}) collective-permute-start(bf16[64,640]{1,0:T(8,128)(2,1)S(1)} %get-tuple-element.50), channel_id=1, source_target_pairs={{0,8},{8,0},{16,24},{24,16},{1,9},{9,1},{17,25},{25,17},{2,10},{10... | collective-permute-start | bytes 245768 | tf_op jit(solution)/shard_map/ppermute | solution.py:211
  33.6 7.1 %collective-permute-start.8 = (bf16[64,640]{1,0:T(8,128)(2,1)S(1)}, bf16[64,640]{1,0:T(8,128)(2,1)S(1)}, u32[]{:S(2)}, u32[]{:S(2)}) collective-permute-start(bf16[64,640]{1,0:T(8,128)(2,1)S(1)} %get-tuple-element.51), channel_id=1, source_target_pairs={{0,16},{8,24},{16,0},{24,8},{1,17},{9,25},{17,1},{25,9},{2,18},{10... | collective-permute-start | bytes 245768 | tf_op jit(solution)/shard_map/ppermute | solution.py:211
  37.4 6.2 %collective-permute-start.9 = (bf16[64,640]{1,0:T(8,128)(2,1)S(1)}, bf16[64,640]{1,0:T(8,128)(2,1)S(1)}, u32[]{:S(2)}, u32[]{:S(2)}) collective-permute-start(bf16[64,640]{1,0:T(8,128)(2,1)S(1)} %get-tuple-element.52), channel_id=1, source_target_pairs={{0,24},{8,16},{16,8},{24,0},{1,25},{9,17},{17,9},{25,1},{2,26},{10... | collective-permute-start | bytes 245768 | tf_op jit(solution)/shard_map/ppermute | solution.py:211
  49.9 1.9 %collective-permute-start.11 = (bf16[256,128]{1,0:T(8,128)(2,1)S(1)}, bf16[256,128]{1,0:T(8,128)(2,1)S(1)}, u32[]{:S(2)}, u32[]{:S(2)}) collective-permute-start(bf16[256,128]{1,0:T(8,128)(2,1)S(1)} %get-tuple-element.55), channel_id=1, source_target_pairs={{0,1},{1,0},{2,3},{3,2},{4,5},{5,4},{6,7},{7,6},{8,9},{9,8},{10,11... | collective-permute-start | bytes 196616 | tf_op jit(solution)/shard_map/ppermute | solution.py:211
  50.0 4.5 %collective-permute-start.12 = (bf16[256,128]{1,0:T(8,128)(2,1)S(1)}, bf16[256,128]{1,0:T(8,128)(2,1)S(1)}, u32[]{:S(2)}, u32[]{:S(2)}) collective-permute-start(bf16[256,128]{1,0:T(8,128)(2,1)S(1)} %get-tuple-element.56), channel_id=1, source_target_pairs={{0,2},{1,3},{2,0},{3,1},{4,6},{5,7},{6,4},{7,5},{8,10},{9,11},{10,... | collective-permute-start | bytes 196616 | tf_op jit(solution)/shard_map/ppermute | solution.py:211
  51.6 4.0 %collective-permute-start.13 = (bf16[256,128]{1,0:T(8,128)(2,1)S(1)}, bf16[256,128]{1,0:T(8,128)(2,1)S(1)}, u32[]{:S(2)}, u32[]{:S(2)}) collective-permute-start(bf16[256,128]{1,0:T(8,128)(2,1)S(1)} %get-tuple-element.57), channel_id=1, source_target_pairs={{0,3},{1,2},{2,1},{3,0},{4,7},{5,6},{6,5},{7,4},{8,11},{9,10},{10,... | collective-permute-start | bytes 196616 | tf_op jit(solution)/shard_map/ppermute | solution.py:211
  55.6 5.9 %copy-start.7 = (f32[2048]{0:T(1024)S(1)}, f32[2048]{0:T(1024)}, u32[]{:S(2)}) copy-start(f32[2048]{0:T(1024)} %param.26) | copy-start | bytes 24580
  55.7 4.2 %collective-permute-start.16 = (bf16[256,128]{1,0:T(8,128)(2,1)S(1)}, bf16[256,128]{1,0:T(8,128)(2,1)S(1)}, u32[]{:S(2)}, u32[]{:S(2)}) collective-permute-start(bf16[256,128]{1,0:T(8,128)(2,1)S(1)} %get-tuple-element.58.x0), channel_id=1, source_target_pairs={{0,3},{1,2},{2,1},{3,0},{4,7},{5,6},{6,5},{7,4},{8,11},{9,10},{10,... | collective-permute-start | bytes 196616 | tf_op jit(solution)/shard_map/ppermute | solution.py:211
  57.0 4.6 %collective-permute-start.15 = (bf16[256,128]{1,0:T(8,128)(2,1)S(1)}, bf16[256,128]{1,0:T(8,128)(2,1)S(1)}, u32[]{:S(2)}, u32[]{:S(2)}) collective-permute-start(bf16[256,128]{1,0:T(8,128)(2,1)S(1)} %get-tuple-element.58.x0), channel_id=1, source_target_pairs={{0,2},{1,3},{2,0},{3,1},{4,6},{5,7},{6,4},{7,5},{8,10},{9,11},{10,... | collective-permute-start | bytes 196616 | tf_op jit(solution)/shard_map/ppermute | solution.py:211
  57.5 4.0 %collective-permute-start.14 = (bf16[256,128]{1,0:T(8,128)(2,1)S(1)}, bf16[256,128]{1,0:T(8,128)(2,1)S(1)}, u32[]{:S(2)}, u32[]{:S(2)}) collective-permute-start(bf16[256,128]{1,0:T(8,128)(2,1)S(1)} %get-tuple-element.58.x0), channel_id=1, source_target_pairs={{0,1},{1,0},{2,3},{3,2},{4,5},{5,4},{6,7},{7,6},{8,9},{9,8},{10,11... | collective-permute-start | bytes 196616 | tf_op jit(solution)/shard_map/ppermute | solution.py:211
  62.1 15.8 %collective-permute-start.21 = (bf16[64,1024]{1,0:T(8,128)(2,1)S(1)}, bf16[64,1024]{1,0:T(8,128)(2,1)S(1)}, u32[]{:S(2)}, u32[]{:S(2)}) collective-permute-start(bf16[64,1024]{1,0:T(8,128)(2,1)S(1)} %get-tuple-element.65), channel_id=1, source_target_pairs={{0,8},{8,0},{16,24},{24,16},{1,9},{9,1},{17,25},{25,17},{2,10},{10... | collective-permute-start | bytes 393224 | tf_op jit(solution)/shard_map/ppermute | solution.py:211
  62.1 17.7 %collective-permute-start.22 = (bf16[64,1024]{1,0:T(8,128)(2,1)S(1)}, bf16[64,1024]{1,0:T(8,128)(2,1)S(1)}, u32[]{:S(2)}, u32[]{:S(2)}) collective-permute-start(bf16[64,1024]{1,0:T(8,128)(2,1)S(1)} %get-tuple-element.67), channel_id=1, source_target_pairs={{0,16},{8,24},{16,0},{24,8},{1,17},{9,25},{17,1},{25,9},{2,18},{10... | collective-permute-start | bytes 393224 | tf_op jit(solution)/shard_map/ppermute | solution.py:211
  63.8 16.0 %collective-permute-start.23 = (bf16[64,1024]{1,0:T(8,128)(2,1)S(1)}, bf16[64,1024]{1,0:T(8,128)(2,1)S(1)}, u32[]{:S(2)}, u32[]{:S(2)}) collective-permute-start(bf16[64,1024]{1,0:T(8,128)(2,1)S(1)} %get-tuple-element.68), channel_id=1, source_target_pairs={{0,24},{8,16},{16,8},{24,0},{1,25},{9,17},{17,9},{25,1},{2,26},{10... | collective-permute-start | bytes 393224 | tf_op jit(solution)/shard_map/ppermute | solution.py:211
  66.5 4.8 %collective-permute-start.18 = (bf16[64,128]{1,0:T(8,128)(2,1)S(1)}, bf16[64,128]{1,0:T(8,128)(2,1)S(1)}, u32[]{:S(2)}, u32[]{:S(2)}) collective-permute-start(bf16[64,128]{1,0:T(8,128)(2,1)S(1)} %get-tuple-element.62), channel_id=1, source_target_pairs={{0,8},{8,0},{16,24},{24,16},{1,9},{9,1},{17,25},{25,17},{2,10},{10... | collective-permute-start | bytes 49160 | tf_op jit(solution)/shard_map/ppermute | solution.py:211
  66.5 11.3 %collective-permute-start.19 = (bf16[64,128]{1,0:T(8,128)(2,1)S(1)}, bf16[64,128]{1,0:T(8,128)(2,1)S(1)}, u32[]{:S(2)}, u32[]{:S(2)}) collective-permute-start(bf16[64,128]{1,0:T(8,128)(2,1)S(1)} %get-tuple-element.63), channel_id=1, source_target_pairs={{0,16},{8,24},{16,0},{24,8},{1,17},{9,25},{17,1},{25,9},{2,18},{10... | collective-permute-start | bytes 49160 | tf_op jit(solution)/shard_map/ppermute | solution.py:211
  71.3 6.5 %collective-permute-start.20 = (bf16[64,128]{1,0:T(8,128)(2,1)S(1)}, bf16[64,128]{1,0:T(8,128)(2,1)S(1)}, u32[]{:S(2)}, u32[]{:S(2)}) collective-permute-start(bf16[64,128]{1,0:T(8,128)(2,1)S(1)} %get-tuple-element.64), channel_id=1, source_target_pairs={{0,24},{8,16},{16,8},{24,0},{1,25},{9,17},{17,9},{25,1},{2,26},{10... | collective-permute-start | bytes 49160 | tf_op jit(solution)/shard_map/ppermute | solution.py:211
  77.9 4.5 %collective-permute-start.26 = (bf16[64,512]{1,0:T(8,128)(2,1)S(1)}, bf16[64,512]{1,0:T(8,128)(2,1)S(1)}, u32[]{:S(2)}, u32[]{:S(2)}) collective-permute-start(bf16[64,512]{1,0:T(8,128)(2,1)S(1)} %shard_map.161.p0), channel_id=1, source_target_pairs={{0,3},{1,2},{2,1},{3,0},{4,7},{5,6},{6,5},{7,4},{8,11},{9,10},{10,... | collective-permute-start | bytes 196616 | tf_op jit(solution)/shard_map/ppermute | solution.py:211
  78.0 5.8 %collective-permute-start.25 = (bf16[64,512]{1,0:T(8,128)(2,1)S(1)}, bf16[64,512]{1,0:T(8,128)(2,1)S(1)}, u32[]{:S(2)}, u32[]{:S(2)}) collective-permute-start(bf16[64,512]{1,0:T(8,128)(2,1)S(1)} %shard_map.161.p0), channel_id=1, source_target_pairs={{0,2},{1,3},{2,0},{3,1},{4,6},{5,7},{6,4},{7,5},{8,10},{9,11},{10,... | collective-permute-start | bytes 196616 | tf_op jit(solution)/shard_map/ppermute | solution.py:211
  79.5 4.3 %collective-permute-start.24 = (bf16[64,512]{1,0:T(8,128)(2,1)S(1)}, bf16[64,512]{1,0:T(8,128)(2,1)S(1)}, u32[]{:S(2)}, u32[]{:S(2)}) collective-permute-start(bf16[64,512]{1,0:T(8,128)(2,1)S(1)} %shard_map.161.p0), channel_id=1, source_target_pairs={{0,1},{1,0},{2,3},{3,2},{4,5},{5,4},{6,7},{7,6},{8,9},{9,8},{10,11... | collective-permute-start | bytes 196616 | tf_op jit(solution)/shard_map/ppermute | solution.py:211
  (9 other events, 6.3 us)

commit v5 on v4

--- a/solution.py
+++ b/solution.py
@@ -54,35 +54,6 @@
     return 2 * lax.axis_index("z") + lax.axis_index("y")
 
 
-def own_nodes(request, branches_ref, roots_ref):
-    branch, root = jnp.zeros_like(request), jnp.zeros_like(request)
-    for r in range(branches_ref.shape[1]):
-        b = branches_ref[0, r]
-        branch = jnp.where(request == r, b, branch)
-        root = jnp.where(request == r, roots_ref[b], root)
-    return branch, root
-
-
-def cache_bias(branch, root, pool_ref, owner_ref, length_ref, root_count):
-    e = seq_index()
-    owners, slots = pool_ref.shape
-    by_row = pool_ref[...].astype(F32).T
-    lane = lax.broadcasted_iota(jnp.int32, by_row.shape, 1)
-    slot = lax.broadcasted_iota(jnp.int32, (slots, branch.shape[1]), 0)
-    pieces = []
-    for s in range(owners):
-        holder = e ^ s
-        held = jnp.sum(jnp.where(lane == holder, by_row, 0.0), axis=1, keepdims=True)
-        owned, length = 0, 0
-        for b in range(owners):
-            here = owner_ref[b] == holder
-            owned = jnp.where(here, b, owned)
-            length = jnp.where(here, length_ref[b], length)
-        pieces.append(held.astype(jnp.int32) == root)
-        pieces.append((slot < length) & (branch == owned))
-    return jnp.concatenate([jnp.where(seen, 0.0, HIDDEN) for seen in pieces], axis=0)
-
-
 def chunk_offset(e, k, width):
     return pl.multiple_of((e ^ (k // 2)) * (2 * width) + (k % 2) * width, width)
 
@@ -91,24 +62,11 @@
     return 2 * lax.axis_index("x") + lax.axis_index("c")
 
 
-def attend_kernel(
-    q_ref, kf_ref, vf_ref, request_ref, branches_ref, roots_ref, pool_ref, owner_ref, length_ref,
-    res_ref, *refs,
-):
+def attend_kernel(q_ref, kf_ref, vf_ref, res_ref, bias_ref, *refs):
     caches, out_ref, sends = refs[:-5], refs[-5], refs[-4:]
     e, m = seq_index(), mp_index()
     tok, wide = q_ref.shape
-    request = request_ref[...]
-    branch, root = own_nodes(request, branches_ref, roots_ref)
-    root_count = lax.axis_size("z") * lax.axis_size("y") // 4
-    down = jnp.broadcast_to(request.astype(F32), (8, tok)).T[:, :1].astype(jnp.int32)
-    key_at = lax.broadcasted_iota(jnp.int32, (tok, tok), 0)
-    token_at = lax.broadcasted_iota(jnp.int32, (tok, tok), 1)
-    fresh = jnp.where((down == request) & (key_at <= token_at), 0.0, HIDDEN)
-    bias = jnp.concatenate(
-        [fresh, cache_bias(branch, root, pool_ref, owner_ref, length_ref, root_count)], axis=0
-    )
-    bias = jnp.concatenate([bias, bias], axis=1)
+    bias = bias_ref[...]
     for k in range(kf_ref.shape[1] // HEAD_SIZE):
         lanes, first, second = head_lanes(k), head_lanes(2 * k), head_lanes(2 * k + 1)
         keys = jnp.concatenate([kf_ref[:, lanes]] + [c[0, :, lanes] for c in caches], axis=0)
@@ -154,7 +112,7 @@
         part[...] = stream[s * tok : (s + 1) * tok]
 
 
-def qkv_kernel(x0, x1, x2, x3, gain_ref, own_ref, par_ref, o0, o1, o2, o3, hold):
+def qkv_kernel(x0, x1, x2, x3, gain_ref, own_ref, par_ref, t0, t1, t2, t3, o0, o1, o2, o3, packed_ref, hold):
     e, m = seq_index(), mp_index()
     width = x0.shape[1]
     half = 2 * width
@@ -168,14 +126,10 @@
     product = jnp.dot(hold[:, :half], own_ref[...], preferred_element_type=F32) + jnp.dot(
         hold[:, half:], par_ref[...], preferred_element_type=F32
     )
+    for s, part in enumerate((t0, t1, t2, t3)):
+        packed_ref[:, s * width : (s + 1) * width] = part[...]
     for s, out in enumerate((o0, o1, o2, o3)):
         out[...] = product[s * tok : (s + 1) * tok].astype(out.dtype)
-
-
-def pack_kernel(t0, t1, t2, t3, out_ref):
-    width = t0.shape[1]
-    for s, part in enumerate((t0, t1, t2, t3)):
-        out_ref[:, s * width : (s + 1) * width] = part[...]
 
 
 def finish_kernel(y0, y1, y2, y3, p0, p1, p2, p3, qkv_ref, stream_ref):
@@ -193,12 +147,12 @@
     qkv_ref[...] = (total * lax.rsqrt(mean_square + 1e-06)).astype(BF16)
 
 
-def call(kernel, out_shape, args, scratch=(), scalars=(), flops=0, moved=1 << 20):
-    vmem, smem = pl.BlockSpec(memory_space=pltpu.VMEM), pl.BlockSpec(memory_space=pltpu.SMEM)
+def call(kernel, out_shape, args, scratch=(), flops=0, moved=1 << 20):
+    vmem = pl.BlockSpec(memory_space=pltpu.VMEM)
     return pl.pallas_call(
         kernel,
         out_shape=out_shape,
-        in_specs=[smem if i in scalars else vmem for i in range(len(args))],
+        in_specs=[vmem] * len(args),
         out_specs=jax.tree.map(lambda _: vmem, out_shape),
         scratch_shapes=list(scratch),
         compiler_params=pltpu.CompilerParams(vmem_limit_bytes=24 << 20),
@@ -235,16 +189,33 @@
 
     far = {s: swap(cache, seq, s) for s in (4, 6, 5, 7, 2, 3, 1)}
     blocks = [cache] + [far[s] for s in range(1, 8)]
-    blocks, wo_later = lax.optimization_barrier((blocks, wo_t))
-    wo_pair = swap(wo_later, "y", 1)
+    wo_pair = swap(wo_t, "y", 1)
+
+    holders = pool_root.shape[0]
+    root_count = holders // 4
+    rows = jnp.arange(holders, dtype=jnp.int32)
+    relative = seq_index() ^ rows
+    pool_relative = jnp.sum(
+        jnp.where(relative[:, None, None] == rows[None, :, None], pool_root[None], 0), axis=1
+    )
+    slot_count = cache.shape[1] - pool_root.shape[1]
+    tags = cache_tags(pool_relative, branch_owner, branch_len, root_count, slot_count, relative)
+    requests, token_branch, token_root = token_nodes(request_branch, token_request, branch_root)
+    positions = jnp.arange(tok, dtype=jnp.int32)
+    own_seen = (requests[None, :] == requests[:, None]) & (
+        positions[:, None] <= positions[None, :]
+    )
+    pool_seen = (tags[:, None] == token_root[None, :]) | (
+        tags[:, None] == root_count + token_branch[None, :]
+    )
+    seen = jnp.concatenate([own_seen, pool_seen], axis=0)
+    bias = jnp.where(jnp.concatenate([seen, seen], axis=1), 0.0, HIDDEN).astype(F32)
+
+    blocks, wo_pair = lax.optimization_barrier((blocks, wo_pair))
     attn, *sends = call(
         attend_kernel,
         [sds((tok, wide), BF16)] + [sds((tok, wide + width), BF16)] * 4,
-        (
-            fresh_queries, fresh_keys, fresh_values, token_request, request_branch, branch_root,
-            pool_root, branch_owner, branch_len, residual, *blocks,
-        ),
-        scalars=(4, 5, 7, 8),
+        (fresh_queries, fresh_keys, fresh_values, residual, bias, *blocks),
         flops=1 << 26,
     )
     own_send, wq_later = lax.optimization_barrier((sends[0], w_qkv))
@@ -263,18 +234,20 @@
         [sds((4 * tok, width), BF16)] + [sds((tok, width), BF16)] * 4,
         tuple(sums),
     )
+    made, wq_pair = lax.optimization_barrier((made, wq_pair))
     slices = [made[0]] + [swap(made[0], mp, j) for j in range(1, 4)]
     home = [made[1]] + [swap(made[1 + s], "z", s) for s in range(1, 4)]
-    partial = call(
+    *partial, packed = call(
         qkv_kernel,
-        [sds((tok, columns), F32)] + [sds((tok, columns), BF16)] * 3,
-        (*slices, norm_gain[None, :], w_qkv, wq_pair),
+        [sds((tok, columns), F32)]
+        + [sds((tok, columns), BF16)] * 3
+        + [sds((tok, 4 * width), BF16)],
+        (*slices, norm_gain[None, :], w_qkv, wq_pair, *home),
         scratch=[pltpu.VMEM((4 * tok, 4 * width), BF16)],
         flops=1 << 28,
     )
     y1, y2, y3 = (swap(partial[s], "z", s) for s in (1, 2, 3))
-    home, y1 = lax.optimization_barrier((home, y1))
-    packed = call(pack_kernel, sds((tok, 4 * width), BF16), tuple(home))
+    packed, y1 = lax.optimization_barrier((packed, y1))
     pieces = [packed] + [swap(packed, mp, j) for j in range(1, 4)]
     qkv_next, stream = call(
         finish_kernel,

time: 85.1 us -> 68.2 us (0.80)
  waiting for transfers between devices: 38.2 us -> 22 us
  local copies, waits for them, and re-layouts: 8.11 us -> 0.13 us
  other arithmetic: 0 us -> 5.27 us
  starting transfers between devices: 33.6 us -> 36.5 us
    ppermute x27, waiting for transfers between devices: 38.2 us -> 22 us  [swap(): return lax.ppermute(value, axes, [(i, i ^ bits) for i in range(count)])]
    unnamed x28 -> x16, local copies, waits for them, and re-layouts: 8.11 us -> 0.05 us
    reduce_sum x0 -> x5, other arithmetic: none -> 3.94 us  [the longest x1 0.84 us: cache_tags(): jnp.sum(jnp.where(branch_ids[None, :] == owned[:, None], branch_len[None,...]
    ppermute x27, starting transfers between devices: 33.6 us -> 36.5 us  [swap(): return lax.ppermute(value, axes, [(i, i ^ bits) for i in range(count)])]
    pallas_call x6 -> x5, Pallas kernels: 3.91 us -> 3.16 us  [call(): pl.pallas_call(kernel, out_shape=out_shape, in_specs=[vmem] * len(args),...]
  transfers between devices with their start and end apart: 27 -> 27, of which waited for: 16 -> 11; matrix products, arithmetic and copies ran while one was open for 0% -> 8% of each run, Pallas kernels for 1% -> 1%
where the time goes in v5:
time: 68.2 us; the launch traced here: 68 us
  starting transfers between devices  36.5 us (54%)
  waiting for transfers between devices  22 us (32%)
  other arithmetic  5.27 us (8%)
  Pallas kernels  3.16 us (5%)
  between operations  0.85 us (1%)
    ppermute x27, starting transfers between devices, swap(): return lax.ppermute(value, axes, [(i, i ^ bits) for i in range(count)])  36.5 us
    ppermute x27, waiting for transfers between devices, swap(): return lax.ppermute(value, axes, [(i, i ^ bits) for i in range(count)])  22 us
    pallas_call x5, Pallas kernels, call(): pl.pallas_call(kernel, out_shape=out_shape, in_specs=[vmem] * len(args),...  3.16 us
  transfers between devices with their start and end apart: 27, of which 11 were waited for; matrix products, arithmetic and copies ran while one was open for 8% of the time, Pallas kernels for 1%

profile of v5, /device:TPU:0, one launch (start us, length us, event | category | flops | bytes accessed | tf_op | source)
XLA Modules:
  0.0 68.0 jit_solution(17413410496412686205)
XLA Ops:
  0.6 5.1 %collective-permute-start.5 = (bf16[2,64,256]{2,1,0:T(8,128)(2,1)}, bf16[2,64,256]{2,1,0:T(8,128)(2,1)S(1)}, u32[]{:S(2)}, u32[]{:S(2)}) collective-permute-start(bf16[2,64,256]{2,1,0:T(8,128)(2,1)} %refs_0_), channel_id=1, source_target_pairs={{0,24},{4,28},{8,16},{12,20},{16,8},{20,12},{24,0},{28,4},{1,25},{... | collective-permute-start | bytes 196616 | tf_op jit(solution)/shard_map/ppermute | solution.py:165
  6.1 3.5 %collective-permute-start.3 = (bf16[2,64,256]{2,1,0:T(8,128)(2,1)}, bf16[2,64,256]{2,1,0:T(8,128)(2,1)S(1)}, u32[]{:S(2)}, u32[]{:S(2)}) collective-permute-start(bf16[2,64,256]{2,1,0:T(8,128)(2,1)} %refs_0_), channel_id=1, source_target_pairs={{0,16},{4,20},{8,24},{12,28},{16,0},{20,4},{24,8},{28,12},{1,17},{... | collective-permute-start | bytes 196616 | tf_op jit(solution)/shard_map/ppermute | solution.py:165
  9.6 1.0 %collective-permute-start.7 = (bf16[256,512]{1,0:T(8,128)(2,1)}, bf16[256,512]{1,0:T(8,128)(2,1)S(1)}, u32[]{:S(2)}, u32[]{:S(2)}) collective-permute-start(bf16[256,512]{1,0:T(8,128)(2,1)} %own_ref.2), channel_id=1, source_target_pairs={{0,4},{4,0},{1,5},{5,1},{2,6},{6,2},{3,7},{7,3},{8,12},{12,8},{9,1... | collective-permute-start | bytes 786440 | tf_op jit(solution)/shard_map/ppermute | solution.py:165
  10.7 0.8 %select_reduce_fusion.3 = s32[8]{0:T(128)S(1)} fusion(s32[8]{0:T(128)} %param.19, s32[8]{0:T(128)S(1)} %iota_xor_fusion), kind=kLoop, calls=%fused_computation.9 | loop fusion | flops 184 | bytes 96 | tf_op jit(solution)/shard_map/reduce_sum | solution.py:22
  11.6 0.8 %select_reduce_fusion.4 = s32[64]{0:T(128)S(1)} fusion(s32[4]{0:T(128)} %bitcast.6, s32[64]{0:T(128)} %bitcast.4), kind=kLoop, calls=%fused_computation.14 | loop fusion | flops 704 | bytes 528 | tf_op jit(solution)/shard_map/reduce_sum | solution.py:39
  13.1 0.8 %select_reduce_fusion.2 = s32[8]{0:T(128)S(1)} fusion(s32[8]{0:T(128)} %param.20, s32[8]{0:T(128)S(1)} %select_reduce_fusion.3), kind=kLoop, calls=%fused_computation.8 | loop fusion | flops 184 | bytes 96 | tf_op jit(solution)/shard_map/reduce_sum | solution.py:25
  14.0 0.8 %select_reduce_fusion = s32[8,32]{1,0:T(8,128)S(1)} fusion(s32[8,32]{1,0:T(8,128)} %param.18, pred[8,8]{1,0:T(8,128)(4,1)S(1)} %iota_compare_fusion.4), kind=kLoop, calls=%fused_computation.2 | loop fusion | flops 3840 | bytes 2112 | tf_op jit(solution)/shard_map/reduce_sum | solution.py:198
  15.1 0.8 %fusion = pred[64,64]{1,0:T(8,128)(4,1)S(1)} fusion(s32[64]{0:T(128)} %bitcast.5), kind=kLoop, calls=%fused_computation.4 | loop fusion | flops 12288 | bytes 4352 | tf_op jit(solution)/shard_map/and | solution.py:205
  15.9 2.5 %collective-permute-start.1 = (bf16[2,64,256]{2,1,0:T(8,128)(2,1)}, bf16[2,64,256]{2,1,0:T(8,128)(2,1)S(1)}, u32[]{:S(2)}, u32[]{:S(2)}) collective-permute-start(bf16[2,64,256]{2,1,0:T(8,128)(2,1)} %refs_0_), channel_id=1, source_target_pairs={{0,8},{4,12},{8,0},{12,4},{16,24},{20,28},{24,16},{28,20},{1,9},{5... | collective-permute-start | bytes 196616 | tf_op jit(solution)/shard_map/ppermute | solution.py:165
  19.0 1.2 %collective-permute-start.6 = (bf16[2,64,256]{2,1,0:T(8,128)(2,1)}, bf16[2,64,256]{2,1,0:T(8,128)(2,1)S(1)}, u32[]{:S(2)}, u32[]{:S(2)}) collective-permute-start(bf16[2,64,256]{2,1,0:T(8,128)(2,1)} %refs_0_), channel_id=1, source_target_pairs={{0,28},{4,24},{8,20},{12,16},{16,12},{20,8},{24,4},{28,0},{1,29},{... | collective-permute-start | bytes 196616 | tf_op jit(solution)/shard_map/ppermute | solution.py:165
  20.9 2.7 %collective-permute-done.refs_1_ = bf16[2,64,256]{2,1,0:T(8,128)(2,1)S(1)} collective-permute-done((bf16[2,64,256]{2,1,0:T(8,128)(2,1)}, bf16[2,64,256]{2,1,0:T(8,128)(2,1)S(1)}, u32[]{:S(2)}, u32[]{:S(2)}) %collective-permute-start) | collective-permute-done | bytes 65568 | tf_op jit(solution)/shard_map/ppermute | solution.py:165
  23.7 2.5 %collective-permute-done.6.refs_7_ = bf16[2,64,256]{2,1,0:T(8,128)(2,1)S(1)} collective-permute-done((bf16[2,64,256]{2,1,0:T(8,128)(2,1)}, bf16[2,64,256]{2,1,0:T(8,128)(2,1)S(1)}, u32[]{:S(2)}, u32[]{:S(2)}) %collective-permute-start.6) | collective-permute-done | bytes 65568 | tf_op jit(solution)/shard_map/ppermute | solution.py:165
  26.2 1.3 %shard_map.157 = (bf16[64,512]{1,0:T(8,128)(2,1)}, bf16[64,640]{1,0:T(8,128)(2,1)S(1)}, bf16[64,640]{1,0:T(8,128)(2,1)S(1)}, bf16[64,640]{1,0:T(8,128)(2,1)S(1)}, bf16[64,640]{1,0:T(8,128)(2,1)S(1)}) custom-call(bf16[64,512]{1,0:T(8,128)(2,1)S(1)} %copy-done.3, bf16[64,256]{1,0:T(8,128)(2,1)S(1)} %copy-done.5, bf16[64,256]{1,0:T(8,128)(2,1)S(1)} %copy-done.6, ...), custom_call_target="tpu_custom_call" | custom-call | flops 67108864 | bytes 1048576 | tf_op jit(solution)/shard_map/pallas_call | solution.py:152
  27.5 1.5 %collective-permute-start.14 = (bf16[256,1024]{1,0:T(8,128)(2,1)S(1)}, bf16[256,1024]{1,0:T(8,128)(2,1)S(1)}, u32[]{:S(2)}, u32[]{:S(2)}) collective-permute-start(bf16[256,1024]{1,0:T(8,128)(2,1)S(1)} %copy-done), channel_id=1, source_target_pairs={{0,4},{4,0},{1,5},{5,1},{2,6},{6,2},{3,7},{7,3},{8,12},{12,8},{9,1... | collective-permute-start | bytes 1572872 | tf_op jit(solution)/shard_map/ppermute | solution.py:165
  29.0 0.8 %collective-permute-start.9 = (bf16[64,640]{1,0:T(8,128)(2,1)S(1)}, bf16[64,640]{1,0:T(8,128)(2,1)S(1)}, u32[]{:S(2)}, u32[]{:S(2)}) collective-permute-start(bf16[64,640]{1,0:T(8,128)(2,1)S(1)} %get-tuple-element.55), channel_id=1, source_target_pairs={{0,16},{8,24},{16,0},{24,8},{1,17},{9,25},{17,1},{25,9},{2,18},{10... | collective-permute-start | bytes 245768 | tf_op jit(solution)/shard_map/ppermute | solution.py:165
  29.8 3.6 %collective-permute-start.10 = (bf16[64,640]{1,0:T(8,128)(2,1)S(1)}, bf16[64,640]{1,0:T(8,128)(2,1)S(1)}, u32[]{:S(2)}, u32[]{:S(2)}) collective-permute-start(bf16[64,640]{1,0:T(8,128)(2,1)S(1)} %get-tuple-element.56), channel_id=1, source_target_pairs={{0,24},{8,16},{16,8},{24,0},{1,25},{9,17},{17,9},{25,1},{2,26},{10... | collective-permute-start | bytes 245768 | tf_op jit(solution)/shard_map/ppermute | solution.py:165
  33.4 1.1 %collective-permute-done.8.a1 = bf16[64,640]{1,0:T(8,128)(2,1)S(1)} collective-permute-done((bf16[64,640]{1,0:T(8,128)(2,1)S(1)}, bf16[64,640]{1,0:T(8,128)(2,1)S(1)}, u32[]{:S(2)}, u32[]{:S(2)}) %collective-permute-start.8) | collective-permute-done | bytes 81952 | tf_op jit(solution)/shard_map/ppermute | solution.py:165
  34.6 2.3 %collective-permute-done.10.a3 = bf16[64,640]{1,0:T(8,128)(2,1)S(1)} collective-permute-done((bf16[64,640]{1,0:T(8,128)(2,1)S(1)}, bf16[64,640]{1,0:T(8,128)(2,1)S(1)}, u32[]{:S(2)}, u32[]{:S(2)}) %collective-permute-start.10) | collective-permute-done | bytes 81952 | tf_op jit(solution)/shard_map/ppermute | solution.py:165
  37.3 1.6 %collective-permute-start.12 = (bf16[256,128]{1,0:T(8,128)(2,1)S(1)}, bf16[256,128]{1,0:T(8,128)(2,1)S(1)}, u32[]{:S(2)}, u32[]{:S(2)}) collective-permute-start(bf16[256,128]{1,0:T(8,128)(2,1)S(1)} %get-tuple-element.60), channel_id=1, source_target_pairs={{0,2},{1,3},{2,0},{3,1},{4,6},{5,7},{6,4},{7,5},{8,10},{9,11},{10,... | collective-permute-start | bytes 196616 | tf_op jit(solution)/shard_map/ppermute | solution.py:165
  39.2 2.6 %collective-permute-done.12.r2 = bf16[256,128]{1,0:T(8,128)(2,1)S(1)} collective-permute-done((bf16[256,128]{1,0:T(8,128)(2,1)S(1)}, bf16[256,128]{1,0:T(8,128)(2,1)S(1)}, u32[]{:S(2)}, u32[]{:S(2)}) %collective-permute-start.12) | collective-permute-done | bytes 65568 | tf_op jit(solution)/shard_map/ppermute | solution.py:165
  41.9 1.1 %collective-permute-done.13.r3 = bf16[256,128]{1,0:T(8,128)(2,1)S(1)} collective-permute-done((bf16[256,128]{1,0:T(8,128)(2,1)S(1)}, bf16[256,128]{1,0:T(8,128)(2,1)S(1)}, u32[]{:S(2)}, u32[]{:S(2)}) %collective-permute-start.13) | collective-permute-done | bytes 65568 | tf_op jit(solution)/shard_map/ppermute | solution.py:165
  43.0 1.3 %collective-permute-start.17 = (bf16[256,128]{1,0:T(8,128)(2,1)S(1)}, bf16[256,128]{1,0:T(8,128)(2,1)S(1)}, u32[]{:S(2)}, u32[]{:S(2)}) collective-permute-start(bf16[256,128]{1,0:T(8,128)(2,1)S(1)} %get-tuple-element.68.x0), channel_id=1, source_target_pairs={{0,3},{1,2},{2,1},{3,0},{4,7},{5,6},{6,5},{7,4},{8,11},{9,10},{10,... | collective-permute-start | bytes 196616 | tf_op jit(solution)/shard_map/ppermute | solution.py:165
  44.9 0.7 %collective-permute-start.18 = (bf16[64,128]{1,0:T(8,128)(2,1)S(1)}, bf16[64,128]{1,0:T(8,128)(2,1)S(1)}, u32[]{:S(2)}, u32[]{:S(2)}) collective-permute-start(bf16[64,128]{1,0:T(8,128)(2,1)S(1)} %get-tuple-element.71), channel_id=1, source_target_pairs={{0,8},{8,0},{16,24},{24,16},{1,9},{9,1},{17,25},{25,17},{2,10},{10... | collective-permute-start | bytes 49160 | tf_op jit(solution)/shard_map/ppermute | solution.py:165
  45.7 2.6 %collective-permute-start.19 = (bf16[64,128]{1,0:T(8,128)(2,1)S(1)}, bf16[64,128]{1,0:T(8,128)(2,1)S(1)}, u32[]{:S(2)}, u32[]{:S(2)}) collective-permute-start(bf16[64,128]{1,0:T(8,128)(2,1)S(1)} %get-tuple-element.72), channel_id=1, source_target_pairs={{0,16},{8,24},{16,0},{24,8},{1,17},{9,25},{17,1},{25,9},{2,18},{10... | collective-permute-start | bytes 49160 | tf_op jit(solution)/shard_map/ppermute | solution.py:165
  48.7 2.8 %collective-permute-start.20 = (bf16[64,128]{1,0:T(8,128)(2,1)S(1)}, bf16[64,128]{1,0:T(8,128)(2,1)S(1)}, u32[]{:S(2)}, u32[]{:S(2)}) collective-permute-start(bf16[64,128]{1,0:T(8,128)(2,1)S(1)} %get-tuple-element.73), channel_id=1, source_target_pairs={{0,24},{8,16},{16,8},{24,0},{1,25},{9,17},{17,9},{25,1},{2,26},{10... | collective-permute-start | bytes 49160 | tf_op jit(solution)/shard_map/ppermute | solution.py:165
  51.5 2.7 %collective-permute-done.20.t3 = bf16[64,128]{1,0:T(8,128)(2,1)S(1)} collective-permute-done((bf16[64,128]{1,0:T(8,128)(2,1)S(1)}, bf16[64,128]{1,0:T(8,128)(2,1)S(1)}, u32[]{:S(2)}, u32[]{:S(2)}) %collective-permute-start.20) | collective-permute-done | bytes 16416 | tf_op jit(solution)/shard_map/ppermute | solution.py:165
  54.8 3.4 %collective-permute-start.22 = (bf16[64,1024]{1,0:T(8,128)(2,1)S(1)}, bf16[64,1024]{1,0:T(8,128)(2,1)S(1)}, u32[]{:S(2)}, u32[]{:S(2)}) collective-permute-start(bf16[64,1024]{1,0:T(8,128)(2,1)S(1)} %get-tuple-element.78), channel_id=1, source_target_pairs={{0,16},{8,24},{16,0},{24,8},{1,17},{9,25},{17,1},{25,9},{2,18},{10... | collective-permute-start | bytes 393224 | tf_op jit(solution)/shard_map/ppermute | solution.py:165
  58.2 1.0 %collective-permute-start.23 = (bf16[64,1024]{1,0:T(8,128)(2,1)S(1)}, bf16[64,1024]{1,0:T(8,128)(2,1)S(1)}, u32[]{:S(2)}, u32[]{:S(2)}) collective-permute-start(bf16[64,1024]{1,0:T(8,128)(2,1)S(1)} %get-tuple-element.79), channel_id=1, source_target_pairs={{0,24},{8,16},{16,8},{24,0},{1,25},{9,17},{17,9},{25,1},{2,26},{10... | collective-permute-start | bytes 393224 | tf_op jit(solution)/shard_map/ppermute | solution.py:165
  59.2 0.9 %collective-permute-done.21.y1 = bf16[64,1024]{1,0:T(8,128)(2,1)S(1)} collective-permute-done((bf16[64,1024]{1,0:T(8,128)(2,1)S(1)}, bf16[64,1024]{1,0:T(8,128)(2,1)S(1)}, u32[]{:S(2)}, u32[]{:S(2)}) %collective-permute-start.21) | collective-permute-done | bytes 131104 | tf_op jit(solution)/shard_map/ppermute | solution.py:165
  60.1 1.5 %collective-permute-start.25 = (bf16[64,512]{1,0:T(8,128)(2,1)S(1)}, bf16[64,512]{1,0:T(8,128)(2,1)S(1)}, u32[]{:S(2)}, u32[]{:S(2)}) collective-permute-start(bf16[64,512]{1,0:T(8,128)(2,1)S(1)} %get-tuple-element.80.p0), channel_id=1, source_target_pairs={{0,2},{1,3},{2,0},{3,1},{4,6},{5,7},{6,4},{7,5},{8,10},{9,11},{10,... | collective-permute-start | bytes 196616 | tf_op jit(solution)/shard_map/ppermute | solution.py:165
  62.0 5.1 %collective-permute-done.22.y2 = bf16[64,1024]{1,0:T(8,128)(2,1)S(1)} collective-permute-done((bf16[64,1024]{1,0:T(8,128)(2,1)S(1)}, bf16[64,1024]{1,0:T(8,128)(2,1)S(1)}, u32[]{:S(2)}, u32[]{:S(2)}) %collective-permute-start.22) | collective-permute-done | bytes 131104 | tf_op jit(solution)/shard_map/ppermute | solution.py:165
  67.1 0.9 %shard_map.161 = (bf16[64,1024]{1,0:T(8,128)(2,1)}, bf16[64,2048]{1,0:T(8,128)(2,1)}) custom-call(f32[64,1024]{1,0:T(8,128)S(1)} %get-tuple-element.74.y0, bf16[64,1024]{1,0:T(8,128)(2,1)S(1)} %collective-permute-done.21.y1, bf16[64,1024]{1,0:T(8,128)(2,1)S(1)} %collective-permute-done.22.y2, bf16[64,1024]{1,0:T(8,128)(2,1)S(1)} %collective-permute-done.23.y3, ...), custom_call_target="tpu_custom_call" | custom-call | bytes 1048576 | tf_op jit(solution)/shard_map/pallas_call | solution.py:152
  (58 shorter events, 5.6 us)
Async XLA Ops:
  0.6 25.5 %copy-start.1 = (bf16[64,2048]{1,0:T(8,128)(2,1)S(1)}, bf16[64,2048]{1,0:T(8,128)(2,1)}, u32[]{:S(2)}) copy-start(bf16[64,2048]{1,0:T(8,128)(2,1)} %res_ref.1) | copy-start | bytes 786436
  0.6 15.3 %collective-permute-start.5 = (bf16[2,64,256]{2,1,0:T(8,128)(2,1)}, bf16[2,64,256]{2,1,0:T(8,128)(2,1)S(1)}, u32[]{:S(2)}, u32[]{:S(2)}) collective-permute-start(bf16[2,64,256]{2,1,0:T(8,128)(2,1)} %refs_0_), channel_id=1, source_target_pairs={{0,24},{4,28},{8,16},{12,20},{16,8},{20,12},{24,0},{28,4},{1,25},{... | collective-permute-start | bytes 196616 | tf_op jit(solution)/shard_map/ppermute | solution.py:165
  5.8 12.7 %collective-permute-start.4 = (bf16[2,64,256]{2,1,0:T(8,128)(2,1)}, bf16[2,64,256]{2,1,0:T(8,128)(2,1)S(1)}, u32[]{:S(2)}, u32[]{:S(2)}) collective-permute-start(bf16[2,64,256]{2,1,0:T(8,128)(2,1)} %refs_0_), channel_id=1, source_target_pairs={{0,20},{4,16},{8,28},{12,24},{16,4},{20,0},{24,12},{28,8},{1,21},{... | collective-permute-start | bytes 196616 | tf_op jit(solution)/shard_map/ppermute | solution.py:165
  6.1 12.8 %collective-permute-start.3 = (bf16[2,64,256]{2,1,0:T(8,128)(2,1)}, bf16[2,64,256]{2,1,0:T(8,128)(2,1)S(1)}, u32[]{:S(2)}, u32[]{:S(2)}) collective-permute-start(bf16[2,64,256]{2,1,0:T(8,128)(2,1)} %refs_0_), channel_id=1, source_target_pairs={{0,16},{4,20},{8,24},{12,28},{16,0},{20,4},{24,8},{28,12},{1,17},{... | collective-permute-start | bytes 196616 | tf_op jit(solution)/shard_map/ppermute | solution.py:165
  9.6 10.7 %collective-permute-start.2 = (bf16[2,64,256]{2,1,0:T(8,128)(2,1)}, bf16[2,64,256]{2,1,0:T(8,128)(2,1)S(1)}, u32[]{:S(2)}, u32[]{:S(2)}) collective-permute-start(bf16[2,64,256]{2,1,0:T(8,128)(2,1)} %refs_0_), channel_id=1, source_target_pairs={{0,12},{4,8},{8,4},{12,0},{16,28},{20,24},{24,20},{28,16},{1,13},{... | collective-permute-start | bytes 196616 | tf_op jit(solution)/shard_map/ppermute | solution.py:165
  9.6 16.5 %collective-permute-start.7 = (bf16[256,512]{1,0:T(8,128)(2,1)}, bf16[256,512]{1,0:T(8,128)(2,1)S(1)}, u32[]{:S(2)}, u32[]{:S(2)}) collective-permute-start(bf16[256,512]{1,0:T(8,128)(2,1)} %own_ref.2), channel_id=1, source_target_pairs={{0,4},{4,0},{1,5},{5,1},{2,6},{6,2},{3,7},{7,3},{8,12},{12,8},{9,1... | collective-permute-start | bytes 786440 | tf_op jit(solution)/shard_map/ppermute | solution.py:165
  15.9 10.3 %copy-start.3 = (bf16[64,512]{1,0:T(8,128)(2,1)S(1)}, bf16[64,512]{1,0:T(8,128)(2,1)}, u32[]{:S(2)}) copy-start(bf16[64,512]{1,0:T(8,128)(2,1)} %q_ref.1) | copy-start | bytes 196612
  15.9 10.3 %copy-start.4 = (bf16[2,64,256]{2,1,0:T(8,128)(2,1)S(1)}, bf16[2,64,256]{2,1,0:T(8,128)(2,1)}, u32[]{:S(2)}) copy-start(bf16[2,64,256]{2,1,0:T(8,128)(2,1)} %refs_0_) | copy-start | bytes 196612
  15.9 5.0 %collective-permute-start.1 = (bf16[2,64,256]{2,1,0:T(8,128)(2,1)}, bf16[2,64,256]{2,1,0:T(8,128)(2,1)S(1)}, u32[]{:S(2)}, u32[]{:S(2)}) collective-permute-start(bf16[2,64,256]{2,1,0:T(8,128)(2,1)} %refs_0_), channel_id=1, source_target_pairs={{0,8},{4,12},{8,0},{12,4},{16,24},{20,28},{24,16},{28,20},{1,9},{5... | collective-permute-start | bytes 196616 | tf_op jit(solution)/shard_map/ppermute | solution.py:165
  18.5 5.2 %collective-permute-start = (bf16[2,64,256]{2,1,0:T(8,128)(2,1)}, bf16[2,64,256]{2,1,0:T(8,128)(2,1)S(1)}, u32[]{:S(2)}, u32[]{:S(2)}) collective-permute-start(bf16[2,64,256]{2,1,0:T(8,128)(2,1)} %refs_0_), channel_id=1, source_target_pairs={{0,4},{4,0},{8,12},{12,8},{16,20},{20,16},{24,28},{28,24},{1,5},{5... | collective-permute-start | bytes 196616 | tf_op jit(solution)/shard_map/ppermute | solution.py:165
  19.0 7.2 %collective-permute-start.6 = (bf16[2,64,256]{2,1,0:T(8,128)(2,1)}, bf16[2,64,256]{2,1,0:T(8,128)(2,1)S(1)}, u32[]{:S(2)}, u32[]{:S(2)}) collective-permute-start(bf16[2,64,256]{2,1,0:T(8,128)(2,1)} %refs_0_), channel_id=1, source_target_pairs={{0,28},{4,24},{8,20},{12,16},{16,12},{20,8},{24,4},{28,0},{1,29},{... | collective-permute-start | bytes 196616 | tf_op jit(solution)/shard_map/ppermute | solution.py:165
  20.3 16.5 %copy-start.2 = (bf16[256,512]{1,0:T(8,128)(2,1)S(1)}, bf16[256,512]{1,0:T(8,128)(2,1)}, u32[]{:S(2)}) copy-start(bf16[256,512]{1,0:T(8,128)(2,1)} %own_ref.2) | copy-start | bytes 786436
  27.5 15.5 %collective-permute-start.14 = (bf16[256,1024]{1,0:T(8,128)(2,1)S(1)}, bf16[256,1024]{1,0:T(8,128)(2,1)S(1)}, u32[]{:S(2)}, u32[]{:S(2)}) collective-permute-start(bf16[256,1024]{1,0:T(8,128)(2,1)S(1)} %copy-done), channel_id=1, source_target_pairs={{0,4},{4,0},{1,5},{5,1},{2,6},{6,2},{3,7},{7,3},{8,12},{12,8},{9,1... | collective-permute-start | bytes 1572872 | tf_op jit(solution)/shard_map/ppermute | solution.py:165
  29.0 5.5 %collective-permute-start.8 = (bf16[64,640]{1,0:T(8,128)(2,1)S(1)}, bf16[64,640]{1,0:T(8,128)(2,1)S(1)}, u32[]{:S(2)}, u32[]{:S(2)}) collective-permute-start(bf16[64,640]{1,0:T(8,128)(2,1)S(1)} %get-tuple-element.54), channel_id=1, source_target_pairs={{0,8},{8,0},{16,24},{24,16},{1,9},{9,1},{17,25},{25,17},{2,10},{10... | collective-permute-start | bytes 245768 | tf_op jit(solution)/shard_map/ppermute | solution.py:165
  29.0 5.5 %collective-permute-start.9 = (bf16[64,640]{1,0:T(8,128)(2,1)S(1)}, bf16[64,640]{1,0:T(8,128)(2,1)S(1)}, u32[]{:S(2)}, u32[]{:S(2)}) collective-permute-start(bf16[64,640]{1,0:T(8,128)(2,1)S(1)} %get-tuple-element.55), channel_id=1, source_target_pairs={{0,16},{8,24},{16,0},{24,8},{1,17},{9,25},{17,1},{25,9},{2,18},{10... | collective-permute-start | bytes 245768 | tf_op jit(solution)/shard_map/ppermute | solution.py:165
  29.8 7.0 %collective-permute-start.10 = (bf16[64,640]{1,0:T(8,128)(2,1)S(1)}, bf16[64,640]{1,0:T(8,128)(2,1)S(1)}, u32[]{:S(2)}, u32[]{:S(2)}) collective-permute-start(bf16[64,640]{1,0:T(8,128)(2,1)S(1)} %get-tuple-element.56), channel_id=1, source_target_pairs={{0,24},{8,16},{16,8},{24,0},{1,25},{9,17},{17,9},{25,1},{2,26},{10... | collective-permute-start | bytes 245768 | tf_op jit(solution)/shard_map/ppermute | solution.py:165
  37.3 1.9 %collective-permute-start.11 = (bf16[256,128]{1,0:T(8,128)(2,1)S(1)}, bf16[256,128]{1,0:T(8,128)(2,1)S(1)}, u32[]{:S(2)}, u32[]{:S(2)}) collective-permute-start(bf16[256,128]{1,0:T(8,128)(2,1)S(1)} %get-tuple-element.59), channel_id=1, source_target_pairs={{0,1},{1,0},{2,3},{3,2},{4,5},{5,4},{6,7},{7,6},{8,9},{9,8},{10,11... | collective-permute-start | bytes 196616 | tf_op jit(solution)/shard_map/ppermute | solution.py:165
  37.3 4.5 %collective-permute-start.12 = (bf16[256,128]{1,0:T(8,128)(2,1)S(1)}, bf16[256,128]{1,0:T(8,128)(2,1)S(1)}, u32[]{:S(2)}, u32[]{:S(2)}) collective-permute-start(bf16[256,128]{1,0:T(8,128)(2,1)S(1)} %get-tuple-element.60), channel_id=1, source_target_pairs={{0,2},{1,3},{2,0},{3,1},{4,6},{5,7},{6,4},{7,5},{8,10},{9,11},{10,... | collective-permute-start | bytes 196616 | tf_op jit(solution)/shard_map/ppermute | solution.py:165
  38.9 4.0 %collective-permute-start.13 = (bf16[256,128]{1,0:T(8,128)(2,1)S(1)}, bf16[256,128]{1,0:T(8,128)(2,1)S(1)}, u32[]{:S(2)}, u32[]{:S(2)}) collective-permute-start(bf16[256,128]{1,0:T(8,128)(2,1)S(1)} %get-tuple-element.61), channel_id=1, source_target_pairs={{0,3},{1,2},{2,1},{3,0},{4,7},{5,6},{6,5},{7,4},{8,11},{9,10},{10,... | collective-permute-start | bytes 196616 | tf_op jit(solution)/shard_map/ppermute | solution.py:165
  43.0 11.2 %copy-start.7 = (f32[2048]{0:T(1024)S(1)}, f32[2048]{0:T(1024)}, u32[]{:S(2)}) copy-start(f32[2048]{0:T(1024)} %param.26) | copy-start | bytes 24580
  43.0 11.2 %collective-permute-start.17 = (bf16[256,128]{1,0:T(8,128)(2,1)S(1)}, bf16[256,128]{1,0:T(8,128)(2,1)S(1)}, u32[]{:S(2)}, u32[]{:S(2)}) collective-permute-start(bf16[256,128]{1,0:T(8,128)(2,1)S(1)} %get-tuple-element.68.x0), channel_id=1, source_target_pairs={{0,3},{1,2},{2,1},{3,0},{4,7},{5,6},{6,5},{7,4},{8,11},{9,10},{10,... | collective-permute-start | bytes 196616 | tf_op jit(solution)/shard_map/ppermute | solution.py:165
  44.3 9.9 %collective-permute-start.16 = (bf16[256,128]{1,0:T(8,128)(2,1)S(1)}, bf16[256,128]{1,0:T(8,128)(2,1)S(1)}, u32[]{:S(2)}, u32[]{:S(2)}) collective-permute-start(bf16[256,128]{1,0:T(8,128)(2,1)S(1)} %get-tuple-element.68.x0), channel_id=1, source_target_pairs={{0,2},{1,3},{2,0},{3,1},{4,6},{5,7},{6,4},{7,5},{8,10},{9,11},{10,... | collective-permute-start | bytes 196616 | tf_op jit(solution)/shard_map/ppermute | solution.py:165
  44.9 9.4 %collective-permute-start.15 = (bf16[256,128]{1,0:T(8,128)(2,1)S(1)}, bf16[256,128]{1,0:T(8,128)(2,1)S(1)}, u32[]{:S(2)}, u32[]{:S(2)}) collective-permute-start(bf16[256,128]{1,0:T(8,128)(2,1)S(1)} %get-tuple-element.68.x0), channel_id=1, source_target_pairs={{0,1},{1,0},{2,3},{3,2},{4,5},{5,4},{6,7},{7,6},{8,9},{9,8},{10,11... | collective-permute-start | bytes 196616 | tf_op jit(solution)/shard_map/ppermute | solution.py:165
  44.9 3.7 %collective-permute-start.18 = (bf16[64,128]{1,0:T(8,128)(2,1)S(1)}, bf16[64,128]{1,0:T(8,128)(2,1)S(1)}, u32[]{:S(2)}, u32[]{:S(2)}) collective-permute-start(bf16[64,128]{1,0:T(8,128)(2,1)S(1)} %get-tuple-element.71), channel_id=1, source_target_pairs={{0,8},{8,0},{16,24},{24,16},{1,9},{9,1},{17,25},{25,17},{2,10},{10... | collective-permute-start | bytes 49160 | tf_op jit(solution)/shard_map/ppermute | solution.py:165
  45.7 5.8 %collective-permute-start.19 = (bf16[64,128]{1,0:T(8,128)(2,1)S(1)}, bf16[64,128]{1,0:T(8,128)(2,1)S(1)}, u32[]{:S(2)}, u32[]{:S(2)}) collective-permute-start(bf16[64,128]{1,0:T(8,128)(2,1)S(1)} %get-tuple-element.72), channel_id=1, source_target_pairs={{0,16},{8,24},{16,0},{24,8},{1,17},{9,25},{17,1},{25,9},{2,18},{10... | collective-permute-start | bytes 49160 | tf_op jit(solution)/shard_map/ppermute | solution.py:165
  48.7 5.5 %collective-permute-start.20 = (bf16[64,128]{1,0:T(8,128)(2,1)S(1)}, bf16[64,128]{1,0:T(8,128)(2,1)S(1)}, u32[]{:S(2)}, u32[]{:S(2)}) collective-permute-start(bf16[64,128]{1,0:T(8,128)(2,1)S(1)} %get-tuple-element.73), channel_id=1, source_target_pairs={{0,24},{8,16},{16,8},{24,0},{1,25},{9,17},{17,9},{25,1},{2,26},{10... | collective-permute-start | bytes 49160 | tf_op jit(solution)/shard_map/ppermute | solution.py:165
  54.7 5.4 %collective-permute-start.21 = (bf16[64,1024]{1,0:T(8,128)(2,1)S(1)}, bf16[64,1024]{1,0:T(8,128)(2,1)S(1)}, u32[]{:S(2)}, u32[]{:S(2)}) collective-permute-start(bf16[64,1024]{1,0:T(8,128)(2,1)S(1)} %get-tuple-element.76), channel_id=1, source_target_pairs={{0,8},{8,0},{16,24},{24,16},{1,9},{9,1},{17,25},{25,17},{2,10},{10... | collective-permute-start | bytes 393224 | tf_op jit(solution)/shard_map/ppermute | solution.py:165
  54.8 12.2 %collective-permute-start.22 = (bf16[64,1024]{1,0:T(8,128)(2,1)S(1)}, bf16[64,1024]{1,0:T(8,128)(2,1)S(1)}, u32[]{:S(2)}, u32[]{:S(2)}) collective-permute-start(bf16[64,1024]{1,0:T(8,128)(2,1)S(1)} %get-tuple-element.78), channel_id=1, source_target_pairs={{0,16},{8,24},{16,0},{24,8},{1,17},{9,25},{17,1},{25,9},{2,18},{10... | collective-permute-start | bytes 393224 | tf_op jit(solution)/shard_map/ppermute | solution.py:165
  58.2 8.8 %collective-permute-start.23 = (bf16[64,1024]{1,0:T(8,128)(2,1)S(1)}, bf16[64,1024]{1,0:T(8,128)(2,1)S(1)}, u32[]{:S(2)}, u32[]{:S(2)}) collective-permute-start(bf16[64,1024]{1,0:T(8,128)(2,1)S(1)} %get-tuple-element.79), channel_id=1, source_target_pairs={{0,24},{8,16},{16,8},{24,0},{1,25},{9,17},{17,9},{25,1},{2,26},{10... | collective-permute-start | bytes 393224 | tf_op jit(solution)/shard_map/ppermute | solution.py:165
  60.1 6.9 %collective-permute-start.26 = (bf16[64,512]{1,0:T(8,128)(2,1)S(1)}, bf16[64,512]{1,0:T(8,128)(2,1)S(1)}, u32[]{:S(2)}, u32[]{:S(2)}) collective-permute-start(bf16[64,512]{1,0:T(8,128)(2,1)S(1)} %get-tuple-element.80.p0), channel_id=1, source_target_pairs={{0,3},{1,2},{2,1},{3,0},{4,7},{5,6},{6,5},{7,4},{8,11},{9,10},{10,... | collective-permute-start | bytes 196616 | tf_op jit(solution)/shard_map/ppermute | solution.py:165
  60.1 6.9 %collective-permute-start.25 = (bf16[64,512]{1,0:T(8,128)(2,1)S(1)}, bf16[64,512]{1,0:T(8,128)(2,1)S(1)}, u32[]{:S(2)}, u32[]{:S(2)}) collective-permute-start(bf16[64,512]{1,0:T(8,128)(2,1)S(1)} %get-tuple-element.80.p0), channel_id=1, source_target_pairs={{0,2},{1,3},{2,0},{3,1},{4,6},{5,7},{6,4},{7,5},{8,10},{9,11},{10,... | collective-permute-start | bytes 196616 | tf_op jit(solution)/shard_map/ppermute | solution.py:165
  61.6 5.4 %collective-permute-start.24 = (bf16[64,512]{1,0:T(8,128)(2,1)S(1)}, bf16[64,512]{1,0:T(8,128)(2,1)S(1)}, u32[]{:S(2)}, u32[]{:S(2)}) collective-permute-start(bf16[64,512]{1,0:T(8,128)(2,1)S(1)} %get-tuple-element.80.p0), channel_id=1, source_target_pairs={{0,1},{1,0},{2,3},{3,2},{4,5},{5,4},{6,7},{7,6},{8,9},{9,8},{10,11... | collective-permute-start | bytes 196616 | tf_op jit(solution)/shard_map/ppermute | solution.py:165
  (3 other events, 27.8 us)

commit v6 on v5

--- a/solution.py
+++ b/solution.py
@@ -32,18 +32,14 @@
     return jnp.concatenate([pool_root, branch_tags], axis=1).reshape(-1)
 
 
-def token_nodes(request_branch, token_request, branch_root):
+def token_branches(request_branch, token_request):
     requests = token_request[0]
     local_branches = request_branch[0]
     request_ids = jnp.arange(local_branches.shape[0], dtype=jnp.int32)
     token_branch = jnp.sum(
         jnp.where(requests[:, None] == request_ids[None, :], local_branches[None, :], 0), axis=1
     )
-    branch_ids = jnp.arange(branch_root.shape[0], dtype=jnp.int32)
-    token_root = jnp.sum(
-        jnp.where(token_branch[:, None] == branch_ids[None, :], branch_root[None, :], 0), axis=1
-    )
-    return requests, token_branch, token_root
+    return requests, token_branch
 
 
 def head_lanes(h):
@@ -62,11 +58,25 @@
     return 2 * lax.axis_index("x") + lax.axis_index("c")
 
 
-def attend_kernel(q_ref, kf_ref, vf_ref, res_ref, bias_ref, *refs):
+def attend_kernel(local_ref, res_ref, bias_ref, *refs):
     caches, out_ref, sends = refs[:-5], refs[-5], refs[-4:]
     e, m = seq_index(), mp_index()
-    tok, wide = q_ref.shape
-    bias = bias_ref[...]
+    tok, wide = out_ref.shape
+    kv = caches[0].shape[2]
+    q_ref, kf_ref, vf_ref = (
+        local_ref.at[:, :wide],
+        local_ref.at[:, wide : wide + kv],
+        local_ref.at[:, wide + kv :],
+    )
+    rows = caches[0].shape[1]
+    bias = jnp.concatenate(
+        [bias_ref[:tok]]
+        + [
+            bias_ref[pl.ds(pl.multiple_of(tok + (e ^ s) * rows, rows), rows), :]
+            for s in range(len(caches))
+        ],
+        axis=0,
+    )
     for k in range(kf_ref.shape[1] // HEAD_SIZE):
         lanes, first, second = head_lanes(k), head_lanes(2 * k), head_lanes(2 * k + 1)
         keys = jnp.concatenate([kf_ref[:, lanes]] + [c[0, :, lanes] for c in caches], axis=0)
@@ -112,7 +122,7 @@
         part[...] = stream[s * tok : (s + 1) * tok]
 
 
-def qkv_kernel(x0, x1, x2, x3, gain_ref, own_ref, par_ref, t0, t1, t2, t3, o0, o1, o2, o3, packed_ref, hold):
+def qkv_kernel(x0, x1, x2, x3, gain_ref, own_ref, par_ref, o0, o1, o2, o3, hold):
     e, m = seq_index(), mp_index()
     width = x0.shape[1]
     half = 2 * width
@@ -126,10 +136,14 @@
     product = jnp.dot(hold[:, :half], own_ref[...], preferred_element_type=F32) + jnp.dot(
         hold[:, half:], par_ref[...], preferred_element_type=F32
     )
-    for s, part in enumerate((t0, t1, t2, t3)):
-        packed_ref[:, s * width : (s + 1) * width] = part[...]
     for s, out in enumerate((o0, o1, o2, o3)):
         out[...] = product[s * tok : (s + 1) * tok].astype(out.dtype)
+
+
+def pack_kernel(t0, t1, t2, t3, out_ref):
+    width = t0.shape[1]
+    for s, part in enumerate((t0, t1, t2, t3)):
+        out_ref[:, s * width : (s + 1) * width] = part[...]
 
 
 def finish_kernel(y0, y1, y2, y3, p0, p1, p2, p3, qkv_ref, stream_ref):
@@ -185,74 +199,79 @@
     width = wo_t.shape[0] // 2
     columns = w_qkv.shape[1]
     sds = jax.ShapeDtypeStruct
-    seq, mp = ("z", "y"), ("x", "c")
-
-    far = {s: swap(cache, seq, s) for s in (4, 6, 5, 7, 2, 3, 1)}
-    blocks = [cache] + [far[s] for s in range(1, 8)]
-    wo_pair = swap(wo_t, "y", 1)
+    mp = ("x", "c")
+
+    along = [cache] + [swap(cache, "z", s) for s in range(1, 4)]
+    beside = swap(cache, "y", 1)
 
     holders = pool_root.shape[0]
-    root_count = holders // 4
-    rows = jnp.arange(holders, dtype=jnp.int32)
-    relative = seq_index() ^ rows
-    pool_relative = jnp.sum(
-        jnp.where(relative[:, None, None] == rows[None, :, None], pool_root[None], 0), axis=1
-    )
-    slot_count = cache.shape[1] - pool_root.shape[1]
-    tags = cache_tags(pool_relative, branch_owner, branch_len, root_count, slot_count, relative)
-    requests, token_branch, token_root = token_nodes(request_branch, token_request, branch_root)
+    requests, token_branch = token_branches(request_branch, token_request)
+    branch_ids = jnp.arange(branch_root.shape[0], dtype=jnp.int32)
+    chosen = token_branch[:, None] == branch_ids[None, :]
+    token_root, token_owner, token_length = (
+        jnp.sum(jnp.where(chosen, per_branch[None, :], 0), axis=1)
+        for per_branch in (branch_root, branch_owner, branch_len)
+    )
     positions = jnp.arange(tok, dtype=jnp.int32)
     own_seen = (requests[None, :] == requests[:, None]) & (
         positions[:, None] <= positions[None, :]
     )
-    pool_seen = (tags[:, None] == token_root[None, :]) | (
-        tags[:, None] == root_count + token_branch[None, :]
-    )
+    slot_count = cache.shape[1] - pool_root.shape[1]
+    slots = jnp.arange(slot_count, dtype=jnp.int32)
+    at = jnp.arange(holders, dtype=jnp.int32)
+    root_seen = pool_root[:, :, None] == token_root[None, None, :]
+    branch_seen = (token_owner[None, None, :] == at[:, None, None]) & (
+        slots[None, :, None] < token_length[None, None, :]
+    )
+    pool_seen = jnp.concatenate([root_seen, branch_seen], axis=1).reshape(-1, tok)
     seen = jnp.concatenate([own_seen, pool_seen], axis=0)
     bias = jnp.where(jnp.concatenate([seen, seen], axis=1), 0.0, HIDDEN).astype(F32)
 
-    blocks, wo_pair = lax.optimization_barrier((blocks, wo_pair))
+    local = jnp.concatenate([fresh_queries, fresh_keys, fresh_values], axis=1)
+    along[1:], bias, local = lax.optimization_barrier((along[1:], bias, local))
+    across = [beside] + [swap(mine, "y", 1) for mine in along[1:]]
+    blocks = [block for pair in zip(along, across) for block in pair]
+    blocks, wo_later = lax.optimization_barrier((blocks, wo_t))
+    wo_pair = swap(wo_later, "y", 1)
     attn, *sends = call(
         attend_kernel,
         [sds((tok, wide), BF16)] + [sds((tok, wide + width), BF16)] * 4,
-        (fresh_queries, fresh_keys, fresh_values, residual, bias, *blocks),
+        (local, residual, bias, *blocks),
         flops=1 << 26,
     )
-    own_send, wq_later = lax.optimization_barrier((sends[0], w_qkv))
-    wq_pair = swap(wq_later, "y", 1)
     a2, a3, a1 = (swap(sends[s], "z", s) for s in (2, 3, 1))
     sums = call(
         project_kernel,
         [sds((4 * tok, width), F32)] + [sds((4 * tok, width), BF16)] * 3,
-        (own_send, a1, a2, a3, wo_t, wo_pair),
+        (sends[0], a1, a2, a3, wo_t, wo_pair),
         scratch=[pltpu.VMEM((4 * tok, 4 * width), F32)],
         flops=1 << 27,
     )
-    sums = [sums[0]] + [swap(sums[j], mp, j) for j in range(1, 4)]
+    own_sum, wq_later = lax.optimization_barrier((sums[0], w_qkv))
+    wq_pair = swap(wq_later, "y", 1)
+    sums = [own_sum] + [swap(sums[j], mp, j) for j in range(1, 4)]
     made = call(
         combine_kernel,
         [sds((4 * tok, width), BF16)] + [sds((tok, width), BF16)] * 4,
         tuple(sums),
     )
-    made, wq_pair = lax.optimization_barrier((made, wq_pair))
     slices = [made[0]] + [swap(made[0], mp, j) for j in range(1, 4)]
     home = [made[1]] + [swap(made[1 + s], "z", s) for s in range(1, 4)]
-    *partial, packed = call(
+    partial = call(
         qkv_kernel,
-        [sds((tok, columns), F32)]
-        + [sds((tok, columns), BF16)] * 3
-        + [sds((tok, 4 * width), BF16)],
-        (*slices, norm_gain[None, :], w_qkv, wq_pair, *home),
+        [sds((tok, columns), F32)] + [sds((tok, columns), BF16)] * 3,
+        (*slices, norm_gain[None, :], w_qkv, wq_pair),
         scratch=[pltpu.VMEM((4 * tok, 4 * width), BF16)],
         flops=1 << 28,
     )
     y1, y2, y3 = (swap(partial[s], "z", s) for s in (1, 2, 3))
-    packed, y1 = lax.optimization_barrier((packed, y1))
+    home, own_partial = lax.optimization_barrier((home, partial[0]))
+    packed = call(pack_kernel, sds((tok, 4 * width), BF16), tuple(home))
     pieces = [packed] + [swap(packed, mp, j) for j in range(1, 4)]
     qkv_next, stream = call(
         finish_kernel,
         [sds((tok, columns), BF16), sds(residual.shape, BF16)],
-        (partial[0], y1, y2, y3, *pieces),
+        (own_partial, y1, y2, y3, *pieces),
     )
     return attn, stream, qkv_next
 
@@ -302,7 +321,11 @@
     slot_count = cache.shape[1] - pool_root.shape[1]
     owner_ids = jnp.arange(seq_count, dtype=jnp.int32)
     tags = cache_tags(pool_root, branch_owner, branch_len, root_count, slot_count, owner_ids)
-    requests, token_branch, token_root = token_nodes(request_branch, token_request, branch_root)
+    requests, token_branch = token_branches(request_branch, token_request)
+    branch_ids = jnp.arange(branch_root.shape[0], dtype=jnp.int32)
+    token_root = jnp.sum(
+        jnp.where(token_branch[:, None] == branch_ids[None, :], branch_root[None, :], 0), axis=1
+    )
     query_rows = fresh_queries.reshape(tok_rows, kv_local, query_groups, HEAD_SIZE)
     incoming_keys = fresh_keys.reshape(tok_rows, kv_local, HEAD_SIZE)
     incoming_values = fresh_values.reshape(tok_rows, kv_local, HEAD_SIZE)

time: 68.2 us -> 63.9 us (0.937)
  starting transfers between devices: 36.5 us -> 29.6 us
  other arithmetic: 5.27 us -> 0.56 us
  waiting for transfers between devices: 22 us -> 26.5 us
  local copies, waits for them, and re-layouts: 0.13 us -> 2.55 us
    ppermute x27, starting transfers between devices: 36.5 us -> 29.6 us  [swap(): return lax.ppermute(value, axes, [(i, i ^ bits) for i in range(count)])]
    ppermute x27, waiting for transfers between devices: 22 us -> 26.5 us  [swap(): return lax.ppermute(value, axes, [(i, i ^ bits) for i in range(count)])]
    reduce_sum x5 -> x2, other arithmetic: 3.94 us -> 0.17 us  [the longest x1 0.09 us: on_block(): jnp.sum(jnp.where(chosen, per_branch[None, :], 0), axis=1)]
    unnamed x16 -> x28, local copies, waits for them, and re-layouts: 0.05 us -> 2.55 us
    and x1, other arithmetic: 0.81 us -> 0.08 us  [on_block(): (requests[None, :] == requests[:, None]) & (positions[:, None] <= positio...]
    pallas_call x5 -> x6, Pallas kernels: 3.16 us -> 3.16 us  [call(): pl.pallas_call(kernel, out_shape=out_shape, in_specs=[vmem] * len(args),...]
  transfers between devices with their start and end apart: 27 -> 27, of which waited for: 11 -> 15; matrix products, arithmetic and copies ran while one was open for 8% -> 1% of each run, Pallas kernels for 1% -> 3%
where the time goes in v6:
time: 63.9 us; the launch traced here: 63.1 us
  starting transfers between devices  29.6 us (46%)
  waiting for transfers between devices  26.5 us (41%)
  Pallas kernels  3.16 us (5%)
  local copies, waits for them, and re-layouts  2.55 us (4%)
  between operations  0.84 us (1%)
    ppermute x27, starting transfers between devices, swap(): return lax.ppermute(value, axes, [(i, i ^ bits) for i in range(count)])  29.6 us
    ppermute x27, waiting for transfers between devices, swap(): return lax.ppermute(value, axes, [(i, i ^ bits) for i in range(count)])  26.5 us
    pallas_call x6, Pallas kernels, call(): pl.pallas_call(kernel, out_shape=out_shape, in_specs=[vmem] * len(args),...  3.16 us
    unnamed x28, local copies, waits for them, and re-layouts  2.55 us
  transfers between devices with their start and end apart: 27, of which 15 were waited for; matrix products, arithmetic and copies ran while one was open for 1% of the time, Pallas kernels for 3%

profile of v6, /device:TPU:0, one launch (start us, length us, event | category | flops | bytes accessed | tf_op | source)
XLA Modules:
  0.0 63.1 jit_solution(16511530158409397399)
XLA Ops:
  0.6 5.1 %collective-permute-start.2 = (bf16[2,64,256]{2,1,0:T(8,128)(2,1)}, bf16[2,64,256]{2,1,0:T(8,128)(2,1)S(1)}, u32[]{:S(2)}, u32[]{:S(2)}) collective-permute-start(bf16[2,64,256]{2,1,0:T(8,128)(2,1)} %refs_0_), channel_id=1, source_target_pairs={{0,24},{8,16},{16,8},{24,0},{1,25},{9,17},{17,9},{25,1},{2,26},{10... | collective-permute-start | bytes 196616 | tf_op jit(solution)/shard_map/ppermute | solution.py:179
  6.4 1.7 %collective-permute-start.3 = (bf16[2,64,256]{2,1,0:T(8,128)(2,1)}, bf16[2,64,256]{2,1,0:T(8,128)(2,1)S(1)}, u32[]{:S(2)}, u32[]{:S(2)}) collective-permute-start(bf16[2,64,256]{2,1,0:T(8,128)(2,1)} %refs_0_), channel_id=1, source_target_pairs={{0,4},{4,0},{1,5},{5,1},{2,6},{6,2},{3,7},{7,3},{8,12},{12,8},{9,1... | collective-permute-start | bytes 196616 | tf_op jit(solution)/shard_map/ppermute | solution.py:179
  9.6 0.7 %copy-done.8 = s32[8,32]{1,0:T(8,128)S(1)} copy-done((s32[8,32]{1,0:T(8,128)S(1)}, s32[8,32]{1,0:T(8,128)}, u32[]{:S(2)}) %copy-start.8) | copy-done | bytes 1048
  11.6 1.5 %collective-permute-start.4 = (bf16[2,64,256]{2,1,0:T(8,128)(2,1)S(1)}, bf16[2,64,256]{2,1,0:T(8,128)(2,1)S(1)}, u32[]{:S(2)}, u32[]{:S(2)}) collective-permute-start(bf16[2,64,256]{2,1,0:T(8,128)(2,1)S(1)} %collective-permute-done.refs_2_), channel_id=1, source_target_pairs={{0,4},{4,0},{1,5},{5,1},{2,6},{6,2},{3,7},{7,3},{8,12},{12,8},{9,1... | collective-permute-start | bytes 196616 | tf_op jit(solution)/shard_map/ppermute | solution.py:179
  13.6 1.5 %collective-permute-start.6 = (bf16[2,64,256]{2,1,0:T(8,128)(2,1)S(1)}, bf16[2,64,256]{2,1,0:T(8,128)(2,1)S(1)}, u32[]{:S(2)}, u32[]{:S(2)}) collective-permute-start(bf16[2,64,256]{2,1,0:T(8,128)(2,1)S(1)} %collective-permute-done.2.refs_6_), channel_id=1, source_target_pairs={{0,4},{4,0},{1,5},{5,1},{2,6},{6,2},{3,7},{7,3},{8,12},{12,8},{9,1... | collective-permute-start | bytes 196616 | tf_op jit(solution)/shard_map/ppermute | solution.py:179
  15.1 1.3 %collective-permute-done.4.refs_3_ = bf16[2,64,256]{2,1,0:T(8,128)(2,1)S(1)} collective-permute-done((bf16[2,64,256]{2,1,0:T(8,128)(2,1)S(1)}, bf16[2,64,256]{2,1,0:T(8,128)(2,1)S(1)}, u32[]{:S(2)}, u32[]{:S(2)}) %collective-permute-start.4) | collective-permute-done | bytes 65568 | tf_op jit(solution)/shard_map/ppermute | solution.py:179
  16.4 1.5 %collective-permute-done.5.refs_5_ = bf16[2,64,256]{2,1,0:T(8,128)(2,1)S(1)} collective-permute-done((bf16[2,64,256]{2,1,0:T(8,128)(2,1)S(1)}, bf16[2,64,256]{2,1,0:T(8,128)(2,1)S(1)}, u32[]{:S(2)}, u32[]{:S(2)}) %collective-permute-start.5) | collective-permute-done | bytes 65568 | tf_op jit(solution)/shard_map/ppermute | solution.py:179
  17.9 0.7 %collective-permute-done.6.refs_7_ = bf16[2,64,256]{2,1,0:T(8,128)(2,1)S(1)} collective-permute-done((bf16[2,64,256]{2,1,0:T(8,128)(2,1)S(1)}, bf16[2,64,256]{2,1,0:T(8,128)(2,1)S(1)}, u32[]{:S(2)}, u32[]{:S(2)}) %collective-permute-start.6) | collective-permute-done | bytes 65568 | tf_op jit(solution)/shard_map/ppermute | solution.py:179
  18.7 1.1 %collective-permute-start.10 = (bf16[256,512]{1,0:T(8,128)(2,1)S(1)}, bf16[256,512]{1,0:T(8,128)(2,1)S(1)}, u32[]{:S(2)}, u32[]{:S(2)}) collective-permute-start(bf16[256,512]{1,0:T(8,128)(2,1)S(1)} %copy-done.2), channel_id=1, source_target_pairs={{0,4},{4,0},{1,5},{5,1},{2,6},{6,2},{3,7},{7,3},{8,12},{12,8},{9,1... | collective-permute-start | bytes 786440 | tf_op jit(solution)/shard_map/ppermute | solution.py:179
  19.8 1.3 %shard_map.157 = (bf16[64,512]{1,0:T(8,128)(2,1)}, bf16[64,640]{1,0:T(8,128)(2,1)S(1)}, bf16[64,640]{1,0:T(8,128)(2,1)S(1)}, bf16[64,640]{1,0:T(8,128)(2,1)S(1)}, bf16[64,640]{1,0:T(8,128)(2,1)S(1)}) custom-call(bf16[64,1024]{1,0:T(8,128)(2,1)S(1)} %pad_maximum_fusion.local_ref, bf16[64,2048]{1,0:T(8,128)(2,1)S(1)} %copy-done.1, ...), custom_call_target="tpu_custom_call" | custom-call | flops 67108864 | bytes 1048576 | tf_op jit(solution)/shard_map/pallas_call | solution.py:166
  21.1 1.1 %collective-permute-start.7 = (bf16[64,640]{1,0:T(8,128)(2,1)S(1)}, bf16[64,640]{1,0:T(8,128)(2,1)S(1)}, u32[]{:S(2)}, u32[]{:S(2)}) collective-permute-start(bf16[64,640]{1,0:T(8,128)(2,1)S(1)} %get-tuple-element.59), channel_id=1, source_target_pairs={{0,8},{8,0},{16,24},{24,16},{1,9},{9,1},{17,25},{25,17},{2,10},{10... | collective-permute-start | bytes 245768 | tf_op jit(solution)/shard_map/ppermute | solution.py:179
  22.2 2.2 %collective-permute-start.8 = (bf16[64,640]{1,0:T(8,128)(2,1)S(1)}, bf16[64,640]{1,0:T(8,128)(2,1)S(1)}, u32[]{:S(2)}, u32[]{:S(2)}) collective-permute-start(bf16[64,640]{1,0:T(8,128)(2,1)S(1)} %get-tuple-element.60), channel_id=1, source_target_pairs={{0,16},{8,24},{16,0},{24,8},{1,17},{9,25},{17,1},{25,9},{2,18},{10... | collective-permute-start | bytes 245768 | tf_op jit(solution)/shard_map/ppermute | solution.py:179
  24.4 1.1 %collective-permute-start.9 = (bf16[64,640]{1,0:T(8,128)(2,1)S(1)}, bf16[64,640]{1,0:T(8,128)(2,1)S(1)}, u32[]{:S(2)}, u32[]{:S(2)}) collective-permute-start(bf16[64,640]{1,0:T(8,128)(2,1)S(1)} %get-tuple-element.61), channel_id=1, source_target_pairs={{0,24},{8,16},{16,8},{24,0},{1,25},{9,17},{17,9},{25,1},{2,26},{10... | collective-permute-start | bytes 245768 | tf_op jit(solution)/shard_map/ppermute | solution.py:179
  25.5 3.0 %collective-permute-done.8.a2 = bf16[64,640]{1,0:T(8,128)(2,1)S(1)} collective-permute-done((bf16[64,640]{1,0:T(8,128)(2,1)S(1)}, bf16[64,640]{1,0:T(8,128)(2,1)S(1)}, u32[]{:S(2)}, u32[]{:S(2)}) %collective-permute-start.8) | collective-permute-done | bytes 81952 | tf_op jit(solution)/shard_map/ppermute | solution.py:179
  28.5 2.1 %collective-permute-done.9.a3 = bf16[64,640]{1,0:T(8,128)(2,1)S(1)} collective-permute-done((bf16[64,640]{1,0:T(8,128)(2,1)S(1)}, bf16[64,640]{1,0:T(8,128)(2,1)S(1)}, u32[]{:S(2)}, u32[]{:S(2)}) %collective-permute-start.9) | collective-permute-done | bytes 81952 | tf_op jit(solution)/shard_map/ppermute | solution.py:179
  31.0 1.3 %collective-permute-start.20 = (bf16[256,1024]{1,0:T(8,128)(2,1)S(1)}, bf16[256,1024]{1,0:T(8,128)(2,1)S(1)}, u32[]{:S(2)}, u32[]{:S(2)}) collective-permute-start(bf16[256,1024]{1,0:T(8,128)(2,1)S(1)} %copy-done), channel_id=1, source_target_pairs={{0,4},{4,0},{1,5},{5,1},{2,6},{6,2},{3,7},{7,3},{8,12},{12,8},{9,1... | collective-permute-start | bytes 1572872 | tf_op jit(solution)/shard_map/ppermute | solution.py:179
  32.3 1.5 %collective-permute-start.12 = (bf16[256,128]{1,0:T(8,128)(2,1)S(1)}, bf16[256,128]{1,0:T(8,128)(2,1)S(1)}, u32[]{:S(2)}, u32[]{:S(2)}) collective-permute-start(bf16[256,128]{1,0:T(8,128)(2,1)S(1)} %get-tuple-element.66), channel_id=1, source_target_pairs={{0,2},{1,3},{2,0},{3,1},{4,6},{5,7},{6,4},{7,5},{8,10},{9,11},{10,... | collective-permute-start | bytes 196616 | tf_op jit(solution)/shard_map/ppermute | solution.py:179
  34.2 2.7 %collective-permute-done.12.r2 = bf16[256,128]{1,0:T(8,128)(2,1)S(1)} collective-permute-done((bf16[256,128]{1,0:T(8,128)(2,1)S(1)}, bf16[256,128]{1,0:T(8,128)(2,1)S(1)}, u32[]{:S(2)}, u32[]{:S(2)}) %collective-permute-start.12) | collective-permute-done | bytes 65568 | tf_op jit(solution)/shard_map/ppermute | solution.py:179
  36.8 1.1 %collective-permute-done.13.r3 = bf16[256,128]{1,0:T(8,128)(2,1)S(1)} collective-permute-done((bf16[256,128]{1,0:T(8,128)(2,1)S(1)}, bf16[256,128]{1,0:T(8,128)(2,1)S(1)}, u32[]{:S(2)}, u32[]{:S(2)}) %collective-permute-start.13) | collective-permute-done | bytes 65568 | tf_op jit(solution)/shard_map/ppermute | solution.py:179
  38.0 1.6 %collective-permute-start.19 = (bf16[256,128]{1,0:T(8,128)(2,1)S(1)}, bf16[256,128]{1,0:T(8,128)(2,1)S(1)}, u32[]{:S(2)}, u32[]{:S(2)}) collective-permute-start(bf16[256,128]{1,0:T(8,128)(2,1)S(1)} %get-tuple-element.72.x0), channel_id=1, source_target_pairs={{0,3},{1,2},{2,1},{3,0},{4,7},{5,6},{6,5},{7,4},{8,11},{9,10},{10,... | collective-permute-start | bytes 196616 | tf_op jit(solution)/shard_map/ppermute | solution.py:179
  40.1 1.9 %collective-permute-done.19.x3 = bf16[256,128]{1,0:T(8,128)(2,1)S(1)} collective-permute-done((bf16[256,128]{1,0:T(8,128)(2,1)S(1)}, bf16[256,128]{1,0:T(8,128)(2,1)S(1)}, u32[]{:S(2)}, u32[]{:S(2)}) %collective-permute-start.19) | collective-permute-done | bytes 65568 | tf_op jit(solution)/shard_map/ppermute | solution.py:179
  42.0 0.9 %collective-permute-start.15 = (bf16[64,128]{1,0:T(8,128)(2,1)S(1)}, bf16[64,128]{1,0:T(8,128)(2,1)S(1)}, u32[]{:S(2)}, u32[]{:S(2)}) collective-permute-start(bf16[64,128]{1,0:T(8,128)(2,1)S(1)} %get-tuple-element.70), channel_id=1, source_target_pairs={{0,16},{8,24},{16,0},{24,8},{1,17},{9,25},{17,1},{25,9},{2,18},{10... | collective-permute-start | bytes 49160 | tf_op jit(solution)/shard_map/ppermute | solution.py:179
  42.9 0.9 %collective-permute-done.18.x2 = bf16[256,128]{1,0:T(8,128)(2,1)S(1)} collective-permute-done((bf16[256,128]{1,0:T(8,128)(2,1)S(1)}, bf16[256,128]{1,0:T(8,128)(2,1)S(1)}, u32[]{:S(2)}, u32[]{:S(2)}) %collective-permute-start.18) | collective-permute-done | bytes 65568 | tf_op jit(solution)/shard_map/ppermute | solution.py:179
  43.8 1.0 %collective-permute-start.16 = (bf16[64,128]{1,0:T(8,128)(2,1)S(1)}, bf16[64,128]{1,0:T(8,128)(2,1)S(1)}, u32[]{:S(2)}, u32[]{:S(2)}) collective-permute-start(bf16[64,128]{1,0:T(8,128)(2,1)S(1)} %get-tuple-element.71), channel_id=1, source_target_pairs={{0,24},{8,16},{16,8},{24,0},{1,25},{9,17},{17,9},{25,1},{2,26},{10... | collective-permute-start | bytes 49160 | tf_op jit(solution)/shard_map/ppermute | solution.py:179
  45.3 1.4 %collective-permute-done.15.t2 = bf16[64,128]{1,0:T(8,128)(2,1)S(1)} collective-permute-done((bf16[64,128]{1,0:T(8,128)(2,1)S(1)}, bf16[64,128]{1,0:T(8,128)(2,1)S(1)}, u32[]{:S(2)}, u32[]{:S(2)}) %collective-permute-start.15) | collective-permute-done | bytes 16416 | tf_op jit(solution)/shard_map/ppermute | solution.py:179
  46.7 2.6 %collective-permute-done.16.t3 = bf16[64,128]{1,0:T(8,128)(2,1)S(1)} collective-permute-done((bf16[64,128]{1,0:T(8,128)(2,1)S(1)}, bf16[64,128]{1,0:T(8,128)(2,1)S(1)}, u32[]{:S(2)}, u32[]{:S(2)}) %collective-permute-start.16) | collective-permute-done | bytes 16416 | tf_op jit(solution)/shard_map/ppermute | solution.py:179
  49.5 1.5 %collective-permute-start.22 = (bf16[64,1024]{1,0:T(8,128)(2,1)S(1)}, bf16[64,1024]{1,0:T(8,128)(2,1)S(1)}, u32[]{:S(2)}, u32[]{:S(2)}) collective-permute-start(bf16[64,1024]{1,0:T(8,128)(2,1)S(1)} %get-tuple-element.77), channel_id=1, source_target_pairs={{0,16},{8,24},{16,0},{24,8},{1,17},{9,25},{17,1},{25,9},{2,18},{10... | collective-permute-start | bytes 393224 | tf_op jit(solution)/shard_map/ppermute | solution.py:179
  51.1 2.8 %collective-permute-start.23 = (bf16[64,1024]{1,0:T(8,128)(2,1)S(1)}, bf16[64,1024]{1,0:T(8,128)(2,1)S(1)}, u32[]{:S(2)}, u32[]{:S(2)}) collective-permute-start(bf16[64,1024]{1,0:T(8,128)(2,1)S(1)} %get-tuple-element.78), channel_id=1, source_target_pairs={{0,24},{8,16},{16,8},{24,0},{1,25},{9,17},{17,9},{25,1},{2,26},{10... | collective-permute-start | bytes 393224 | tf_op jit(solution)/shard_map/ppermute | solution.py:179
  53.9 1.4 %collective-permute-start.25 = (bf16[64,512]{1,0:T(8,128)(2,1)S(1)}, bf16[64,512]{1,0:T(8,128)(2,1)S(1)}, u32[]{:S(2)}, u32[]{:S(2)}) collective-permute-start(bf16[64,512]{1,0:T(8,128)(2,1)S(1)} %shard_map.161.p0), channel_id=1, source_target_pairs={{0,2},{1,3},{2,0},{3,1},{4,6},{5,7},{6,4},{7,5},{8,10},{9,11},{10,... | collective-permute-start | bytes 196616 | tf_op jit(solution)/shard_map/ppermute | solution.py:179
  55.3 3.2 %collective-permute-done.25.p2 = bf16[64,512]{1,0:T(8,128)(2,1)S(1)} collective-permute-done((bf16[64,512]{1,0:T(8,128)(2,1)S(1)}, bf16[64,512]{1,0:T(8,128)(2,1)S(1)}, u32[]{:S(2)}, u32[]{:S(2)}) %collective-permute-start.25) | collective-permute-done | bytes 65568 | tf_op jit(solution)/shard_map/ppermute | solution.py:179
  58.5 3.7 %collective-permute-done.22.y2 = bf16[64,1024]{1,0:T(8,128)(2,1)S(1)} collective-permute-done((bf16[64,1024]{1,0:T(8,128)(2,1)S(1)}, bf16[64,1024]{1,0:T(8,128)(2,1)S(1)}, u32[]{:S(2)}, u32[]{:S(2)}) %collective-permute-start.22) | collective-permute-done | bytes 131104 | tf_op jit(solution)/shard_map/ppermute | solution.py:179
  62.2 0.9 %shard_map.162 = (bf16[64,1024]{1,0:T(8,128)(2,1)}, bf16[64,2048]{1,0:T(8,128)(2,1)}) custom-call(f32[64,1024]{1,0:T(8,128)S(1)} %get-tuple-element.75.y0, bf16[64,1024]{1,0:T(8,128)(2,1)S(1)} %collective-permute-done.21.y1, bf16[64,1024]{1,0:T(8,128)(2,1)S(1)} %collective-permute-done.22.y2, bf16[64,1024]{1,0:T(8,128)(2,1)S(1)} %collective-permute-done.23.y3, ...), custom_call_target="tpu_custom_call" | custom-call | bytes 1048576 | tf_op jit(solution)/shard_map/pallas_call | solution.py:166
  (65 shorter events, 6.0 us)
Async XLA Ops:
  0.6 7.4 %copy-start.9 = (s32[1,64]{1,0:T(1,128)S(1)}, s32[1,64]{1,0:T(1,128)}, u32[]{:S(2)}) copy-start(s32[1,64]{1,0:T(1,128)} %param.23) | copy-start | bytes 772
  0.6 10.6 %collective-permute-start.2 = (bf16[2,64,256]{2,1,0:T(8,128)(2,1)}, bf16[2,64,256]{2,1,0:T(8,128)(2,1)S(1)}, u32[]{:S(2)}, u32[]{:S(2)}) collective-permute-start(bf16[2,64,256]{2,1,0:T(8,128)(2,1)} %refs_0_), channel_id=1, source_target_pairs={{0,24},{8,16},{16,8},{24,0},{1,25},{9,17},{17,9},{25,1},{2,26},{10... | collective-permute-start | bytes 196616 | tf_op jit(solution)/shard_map/ppermute | solution.py:179
  5.8 5.8 %collective-permute-start.1 = (bf16[2,64,256]{2,1,0:T(8,128)(2,1)}, bf16[2,64,256]{2,1,0:T(8,128)(2,1)S(1)}, u32[]{:S(2)}, u32[]{:S(2)}) collective-permute-start(bf16[2,64,256]{2,1,0:T(8,128)(2,1)} %refs_0_), channel_id=1, source_target_pairs={{0,16},{8,24},{16,0},{24,8},{1,17},{9,25},{17,1},{25,9},{2,18},{10... | collective-permute-start | bytes 196616 | tf_op jit(solution)/shard_map/ppermute | solution.py:179
  5.8 5.8 %collective-permute-start = (bf16[2,64,256]{2,1,0:T(8,128)(2,1)}, bf16[2,64,256]{2,1,0:T(8,128)(2,1)S(1)}, u32[]{:S(2)}, u32[]{:S(2)}) collective-permute-start(bf16[2,64,256]{2,1,0:T(8,128)(2,1)} %refs_0_), channel_id=1, source_target_pairs={{0,8},{8,0},{16,24},{24,16},{1,9},{9,1},{17,25},{25,17},{2,10},{10... | collective-permute-start | bytes 196616 | tf_op jit(solution)/shard_map/ppermute | solution.py:179
  6.4 8.7 %collective-permute-start.3 = (bf16[2,64,256]{2,1,0:T(8,128)(2,1)}, bf16[2,64,256]{2,1,0:T(8,128)(2,1)S(1)}, u32[]{:S(2)}, u32[]{:S(2)}) collective-permute-start(bf16[2,64,256]{2,1,0:T(8,128)(2,1)} %refs_0_), channel_id=1, source_target_pairs={{0,4},{4,0},{1,5},{5,1},{2,6},{6,2},{3,7},{7,3},{8,12},{12,8},{9,1... | collective-permute-start | bytes 196616 | tf_op jit(solution)/shard_map/ppermute | solution.py:179
  10.5 8.2 %copy-start.2 = (bf16[256,512]{1,0:T(8,128)(2,1)S(1)}, bf16[256,512]{1,0:T(8,128)(2,1)}, u32[]{:S(2)}) copy-start(bf16[256,512]{1,0:T(8,128)(2,1)} %own_ref.2) | copy-start | bytes 786436
  10.5 9.3 %copy-start.1 = (bf16[64,2048]{1,0:T(8,128)(2,1)S(1)}, bf16[64,2048]{1,0:T(8,128)(2,1)}, u32[]{:S(2)}) copy-start(bf16[64,2048]{1,0:T(8,128)(2,1)} %res_ref.1) | copy-start | bytes 786436
  11.2 8.5 %copy-start.3 = (bf16[2,64,256]{2,1,0:T(8,128)(2,1)S(1)}, bf16[2,64,256]{2,1,0:T(8,128)(2,1)}, u32[]{:S(2)}) copy-start(bf16[2,64,256]{2,1,0:T(8,128)(2,1)} %refs_0_) | copy-start | bytes 196612
  11.6 4.8 %collective-permute-start.4 = (bf16[2,64,256]{2,1,0:T(8,128)(2,1)S(1)}, bf16[2,64,256]{2,1,0:T(8,128)(2,1)S(1)}, u32[]{:S(2)}, u32[]{:S(2)}) collective-permute-start(bf16[2,64,256]{2,1,0:T(8,128)(2,1)S(1)} %collective-permute-done.refs_2_), channel_id=1, source_target_pairs={{0,4},{4,0},{1,5},{5,1},{2,6},{6,2},{3,7},{7,3},{8,12},{12,8},{9,1... | collective-permute-start | bytes 196616 | tf_op jit(solution)/shard_map/ppermute | solution.py:179
  13.1 4.9 %collective-permute-start.5 = (bf16[2,64,256]{2,1,0:T(8,128)(2,1)S(1)}, bf16[2,64,256]{2,1,0:T(8,128)(2,1)S(1)}, u32[]{:S(2)}, u32[]{:S(2)}) collective-permute-start(bf16[2,64,256]{2,1,0:T(8,128)(2,1)S(1)} %collective-permute-done.1.refs_4_), channel_id=1, source_target_pairs={{0,4},{4,0},{1,5},{5,1},{2,6},{6,2},{3,7},{7,3},{8,12},{12,8},{9,1... | collective-permute-start | bytes 196616 | tf_op jit(solution)/shard_map/ppermute | solution.py:179
  13.6 5.0 %collective-permute-start.6 = (bf16[2,64,256]{2,1,0:T(8,128)(2,1)S(1)}, bf16[2,64,256]{2,1,0:T(8,128)(2,1)S(1)}, u32[]{:S(2)}, u32[]{:S(2)}) collective-permute-start(bf16[2,64,256]{2,1,0:T(8,128)(2,1)S(1)} %collective-permute-done.2.refs_6_), channel_id=1, source_target_pairs={{0,4},{4,0},{1,5},{5,1},{2,6},{6,2},{3,7},{7,3},{8,12},{12,8},{9,1... | collective-permute-start | bytes 196616 | tf_op jit(solution)/shard_map/ppermute | solution.py:179
  18.7 11.9 %collective-permute-start.10 = (bf16[256,512]{1,0:T(8,128)(2,1)S(1)}, bf16[256,512]{1,0:T(8,128)(2,1)S(1)}, u32[]{:S(2)}, u32[]{:S(2)}) collective-permute-start(bf16[256,512]{1,0:T(8,128)(2,1)S(1)} %copy-done.2), channel_id=1, source_target_pairs={{0,4},{4,0},{1,5},{5,1},{2,6},{6,2},{3,7},{7,3},{8,12},{12,8},{9,1... | collective-permute-start | bytes 786440 | tf_op jit(solution)/shard_map/ppermute | solution.py:179
  21.1 10.0 %copy-start = (bf16[256,1024]{1,0:T(8,128)(2,1)S(1)}, bf16[256,1024]{1,0:T(8,128)(2,1)}, u32[]{:S(2)}) copy-start(bf16[256,1024]{1,0:T(8,128)(2,1)} %own_ref.3) | copy-start | bytes 1572868
  21.1 4.5 %collective-permute-start.7 = (bf16[64,640]{1,0:T(8,128)(2,1)S(1)}, bf16[64,640]{1,0:T(8,128)(2,1)S(1)}, u32[]{:S(2)}, u32[]{:S(2)}) collective-permute-start(bf16[64,640]{1,0:T(8,128)(2,1)S(1)} %get-tuple-element.59), channel_id=1, source_target_pairs={{0,8},{8,0},{16,24},{24,16},{1,9},{9,1},{17,25},{25,17},{2,10},{10... | collective-permute-start | bytes 245768 | tf_op jit(solution)/shard_map/ppermute | solution.py:179
  22.2 6.4 %collective-permute-start.8 = (bf16[64,640]{1,0:T(8,128)(2,1)S(1)}, bf16[64,640]{1,0:T(8,128)(2,1)S(1)}, u32[]{:S(2)}, u32[]{:S(2)}) collective-permute-start(bf16[64,640]{1,0:T(8,128)(2,1)S(1)} %get-tuple-element.60), channel_id=1, source_target_pairs={{0,16},{8,24},{16,0},{24,8},{1,17},{9,25},{17,1},{25,9},{2,18},{10... | collective-permute-start | bytes 245768 | tf_op jit(solution)/shard_map/ppermute | solution.py:179
  24.4 6.2 %collective-permute-start.9 = (bf16[64,640]{1,0:T(8,128)(2,1)S(1)}, bf16[64,640]{1,0:T(8,128)(2,1)S(1)}, u32[]{:S(2)}, u32[]{:S(2)}) collective-permute-start(bf16[64,640]{1,0:T(8,128)(2,1)S(1)} %get-tuple-element.61), channel_id=1, source_target_pairs={{0,24},{8,16},{16,8},{24,0},{1,25},{9,17},{17,9},{25,1},{2,26},{10... | collective-permute-start | bytes 245768 | tf_op jit(solution)/shard_map/ppermute | solution.py:179
  31.0 13.8 %collective-permute-start.20 = (bf16[256,1024]{1,0:T(8,128)(2,1)S(1)}, bf16[256,1024]{1,0:T(8,128)(2,1)S(1)}, u32[]{:S(2)}, u32[]{:S(2)}) collective-permute-start(bf16[256,1024]{1,0:T(8,128)(2,1)S(1)} %copy-done), channel_id=1, source_target_pairs={{0,4},{4,0},{1,5},{5,1},{2,6},{6,2},{3,7},{7,3},{8,12},{12,8},{9,1... | collective-permute-start | bytes 1572872 | tf_op jit(solution)/shard_map/ppermute | solution.py:179
  32.3 1.9 %collective-permute-start.11 = (bf16[256,128]{1,0:T(8,128)(2,1)S(1)}, bf16[256,128]{1,0:T(8,128)(2,1)S(1)}, u32[]{:S(2)}, u32[]{:S(2)}) collective-permute-start(bf16[256,128]{1,0:T(8,128)(2,1)S(1)} %get-tuple-element.65), channel_id=1, source_target_pairs={{0,1},{1,0},{2,3},{3,2},{4,5},{5,4},{6,7},{7,6},{8,9},{9,8},{10,11... | collective-permute-start | bytes 196616 | tf_op jit(solution)/shard_map/ppermute | solution.py:179
  32.3 4.5 %collective-permute-start.12 = (bf16[256,128]{1,0:T(8,128)(2,1)S(1)}, bf16[256,128]{1,0:T(8,128)(2,1)S(1)}, u32[]{:S(2)}, u32[]{:S(2)}) collective-permute-start(bf16[256,128]{1,0:T(8,128)(2,1)S(1)} %get-tuple-element.66), channel_id=1, source_target_pairs={{0,2},{1,3},{2,0},{3,1},{4,6},{5,7},{6,4},{7,5},{8,10},{9,11},{10,... | collective-permute-start | bytes 196616 | tf_op jit(solution)/shard_map/ppermute | solution.py:179
  33.8 4.1 %collective-permute-start.13 = (bf16[256,128]{1,0:T(8,128)(2,1)S(1)}, bf16[256,128]{1,0:T(8,128)(2,1)S(1)}, u32[]{:S(2)}, u32[]{:S(2)}) collective-permute-start(bf16[256,128]{1,0:T(8,128)(2,1)S(1)} %get-tuple-element.67), channel_id=1, source_target_pairs={{0,3},{1,2},{2,1},{3,0},{4,7},{5,6},{6,5},{7,4},{8,11},{9,10},{10,... | collective-permute-start | bytes 196616 | tf_op jit(solution)/shard_map/ppermute | solution.py:179
  38.0 4.0 %collective-permute-start.19 = (bf16[256,128]{1,0:T(8,128)(2,1)S(1)}, bf16[256,128]{1,0:T(8,128)(2,1)S(1)}, u32[]{:S(2)}, u32[]{:S(2)}) collective-permute-start(bf16[256,128]{1,0:T(8,128)(2,1)S(1)} %get-tuple-element.72.x0), channel_id=1, source_target_pairs={{0,3},{1,2},{2,1},{3,0},{4,7},{5,6},{6,5},{7,4},{8,11},{9,10},{10,... | collective-permute-start | bytes 196616 | tf_op jit(solution)/shard_map/ppermute | solution.py:179
  39.5 4.3 %collective-permute-start.18 = (bf16[256,128]{1,0:T(8,128)(2,1)S(1)}, bf16[256,128]{1,0:T(8,128)(2,1)S(1)}, u32[]{:S(2)}, u32[]{:S(2)}) collective-permute-start(bf16[256,128]{1,0:T(8,128)(2,1)S(1)} %get-tuple-element.72.x0), channel_id=1, source_target_pairs={{0,2},{1,3},{2,0},{3,1},{4,6},{5,7},{6,4},{7,5},{8,10},{9,11},{10,... | collective-permute-start | bytes 196616 | tf_op jit(solution)/shard_map/ppermute | solution.py:179
  40.1 4.7 %collective-permute-start.17 = (bf16[256,128]{1,0:T(8,128)(2,1)S(1)}, bf16[256,128]{1,0:T(8,128)(2,1)S(1)}, u32[]{:S(2)}, u32[]{:S(2)}) collective-permute-start(bf16[256,128]{1,0:T(8,128)(2,1)S(1)} %get-tuple-element.72.x0), channel_id=1, source_target_pairs={{0,1},{1,0},{2,3},{3,2},{4,5},{5,4},{6,7},{7,6},{8,9},{9,8},{10,11... | collective-permute-start | bytes 196616 | tf_op jit(solution)/shard_map/ppermute | solution.py:179
  40.1 5.2 %collective-permute-start.14 = (bf16[64,128]{1,0:T(8,128)(2,1)S(1)}, bf16[64,128]{1,0:T(8,128)(2,1)S(1)}, u32[]{:S(2)}, u32[]{:S(2)}) collective-permute-start(bf16[64,128]{1,0:T(8,128)(2,1)S(1)} %get-tuple-element.69), channel_id=1, source_target_pairs={{0,8},{8,0},{16,24},{24,16},{1,9},{9,1},{17,25},{25,17},{2,10},{10... | collective-permute-start | bytes 49160 | tf_op jit(solution)/shard_map/ppermute | solution.py:179
  42.0 4.7 %collective-permute-start.15 = (bf16[64,128]{1,0:T(8,128)(2,1)S(1)}, bf16[64,128]{1,0:T(8,128)(2,1)S(1)}, u32[]{:S(2)}, u32[]{:S(2)}) collective-permute-start(bf16[64,128]{1,0:T(8,128)(2,1)S(1)} %get-tuple-element.70), channel_id=1, source_target_pairs={{0,16},{8,24},{16,0},{24,8},{1,17},{9,25},{17,1},{25,9},{2,18},{10... | collective-permute-start | bytes 49160 | tf_op jit(solution)/shard_map/ppermute | solution.py:179
  43.8 5.5 %collective-permute-start.16 = (bf16[64,128]{1,0:T(8,128)(2,1)S(1)}, bf16[64,128]{1,0:T(8,128)(2,1)S(1)}, u32[]{:S(2)}, u32[]{:S(2)}) collective-permute-start(bf16[64,128]{1,0:T(8,128)(2,1)S(1)} %get-tuple-element.71), channel_id=1, source_target_pairs={{0,24},{8,16},{16,8},{24,0},{1,25},{9,17},{17,9},{25,1},{2,26},{10... | collective-permute-start | bytes 49160 | tf_op jit(solution)/shard_map/ppermute | solution.py:179
  49.4 6.0 %collective-permute-start.26 = (bf16[64,512]{1,0:T(8,128)(2,1)S(1)}, bf16[64,512]{1,0:T(8,128)(2,1)S(1)}, u32[]{:S(2)}, u32[]{:S(2)}) collective-permute-start(bf16[64,512]{1,0:T(8,128)(2,1)S(1)} %shard_map.161.p0), channel_id=1, source_target_pairs={{0,3},{1,2},{2,1},{3,0},{4,7},{5,6},{6,5},{7,4},{8,11},{9,10},{10,... | collective-permute-start | bytes 196616 | tf_op jit(solution)/shard_map/ppermute | solution.py:179
  49.5 9.1 %collective-permute-start.21 = (bf16[64,1024]{1,0:T(8,128)(2,1)S(1)}, bf16[64,1024]{1,0:T(8,128)(2,1)S(1)}, u32[]{:S(2)}, u32[]{:S(2)}) collective-permute-start(bf16[64,1024]{1,0:T(8,128)(2,1)S(1)} %get-tuple-element.76), channel_id=1, source_target_pairs={{0,8},{8,0},{16,24},{24,16},{1,9},{9,1},{17,25},{25,17},{2,10},{10... | collective-permute-start | bytes 393224 | tf_op jit(solution)/shard_map/ppermute | solution.py:179
  49.5 12.7 %collective-permute-start.22 = (bf16[64,1024]{1,0:T(8,128)(2,1)S(1)}, bf16[64,1024]{1,0:T(8,128)(2,1)S(1)}, u32[]{:S(2)}, u32[]{:S(2)}) collective-permute-start(bf16[64,1024]{1,0:T(8,128)(2,1)S(1)} %get-tuple-element.77), channel_id=1, source_target_pairs={{0,16},{8,24},{16,0},{24,8},{1,17},{9,25},{17,1},{25,9},{2,18},{10... | collective-permute-start | bytes 393224 | tf_op jit(solution)/shard_map/ppermute | solution.py:179
  51.1 11.2 %collective-permute-start.23 = (bf16[64,1024]{1,0:T(8,128)(2,1)S(1)}, bf16[64,1024]{1,0:T(8,128)(2,1)S(1)}, u32[]{:S(2)}, u32[]{:S(2)}) collective-permute-start(bf16[64,1024]{1,0:T(8,128)(2,1)S(1)} %get-tuple-element.78), channel_id=1, source_target_pairs={{0,24},{8,16},{16,8},{24,0},{1,25},{9,17},{17,9},{25,1},{2,26},{10... | collective-permute-start | bytes 393224 | tf_op jit(solution)/shard_map/ppermute | solution.py:179
  53.9 4.6 %collective-permute-start.25 = (bf16[64,512]{1,0:T(8,128)(2,1)S(1)}, bf16[64,512]{1,0:T(8,128)(2,1)S(1)}, u32[]{:S(2)}, u32[]{:S(2)}) collective-permute-start(bf16[64,512]{1,0:T(8,128)(2,1)S(1)} %shard_map.161.p0), channel_id=1, source_target_pairs={{0,2},{1,3},{2,0},{3,1},{4,6},{5,7},{6,4},{7,5},{8,10},{9,11},{10,... | collective-permute-start | bytes 196616 | tf_op jit(solution)/shard_map/ppermute | solution.py:179
  55.3 3.2 %collective-permute-start.24 = (bf16[64,512]{1,0:T(8,128)(2,1)S(1)}, bf16[64,512]{1,0:T(8,128)(2,1)S(1)}, u32[]{:S(2)}, u32[]{:S(2)}) collective-permute-start(bf16[64,512]{1,0:T(8,128)(2,1)S(1)} %shard_map.161.p0), channel_id=1, source_target_pairs={{0,1},{1,0},{2,3},{3,2},{4,5},{5,4},{6,7},{7,6},{8,9},{9,8},{10,11... | collective-permute-start | bytes 196616 | tf_op jit(solution)/shard_map/ppermute | solution.py:179
  (9 other events, 12.7 us)

commit v7 on v6

--- a/solution.py
+++ b/solution.py
@@ -231,8 +231,9 @@
     along[1:], bias, local = lax.optimization_barrier((along[1:], bias, local))
     across = [beside] + [swap(mine, "y", 1) for mine in along[1:]]
     blocks = [block for pair in zip(along, across) for block in pair]
-    blocks, wo_later = lax.optimization_barrier((blocks, wo_t))
-    wo_pair = swap(wo_later, "y", 1)
+    wo_pair = swap(wo_t, "y", 1)
+    blocks, wo_pair, wq_later = lax.optimization_barrier((blocks, wo_pair, w_qkv))
+    wq_pair = swap(wq_later, "y", 1)
     attn, *sends = call(
         attend_kernel,
         [sds((tok, wide), BF16)] + [sds((tok, wide + width), BF16)] * 4,
@@ -247,14 +248,13 @@
         scratch=[pltpu.VMEM((4 * tok, 4 * width), F32)],
         flops=1 << 27,
     )
-    own_sum, wq_later = lax.optimization_barrier((sums[0], w_qkv))
-    wq_pair = swap(wq_later, "y", 1)
-    sums = [own_sum] + [swap(sums[j], mp, j) for j in range(1, 4)]
+    sums = [sums[0]] + [swap(sums[j], mp, j) for j in range(1, 4)]
     made = call(
         combine_kernel,
         [sds((4 * tok, width), BF16)] + [sds((tok, width), BF16)] * 4,
         tuple(sums),
     )
+    made, wq_pair = lax.optimization_barrier((made, wq_pair))
     slices = [made[0]] + [swap(made[0], mp, j) for j in range(1, 4)]
     home = [made[1]] + [swap(made[1 + s], "z", s) for s in range(1, 4)]
     partial = call(

time: 63.9 us -> 63.6 us (level)
  other arithmetic: 0.56 us -> 3.5 us
  local copies, waits for them, and re-layouts: 2.55 us -> 0.03 us
  waiting for transfers between devices: 26.5 us -> 25.1 us
    unnamed x28 -> x12, local copies, waits for them, and re-layouts: 2.55 us -> 0.03 us
    ppermute x27, waiting for transfers between devices: 26.5 us -> 25.1 us  [swap(): return lax.ppermute(value, axes, [(i, i ^ bits) for i in range(count)])]
    concatenate x1, other arithmetic: 0.01 us -> 0.92 us  [on_block(): local = jnp.concatenate([fresh_queries, fresh_keys, fresh_values], axis=1)]
    eq x1, other arithmetic: 0.1 us -> 0.79 us  [on_block(): root_seen = pool_root[:, :, None] == token_root[None, None, :]]
    reduce_sum x1, other arithmetic: 0.09 us -> 0.77 us  [on_block(): jnp.sum(jnp.where(chosen, per_branch[None, :], 0), axis=1)]
    reduce_sum x1, other arithmetic: 0.08 us -> 0.74 us  [token_branches(): jnp.sum(jnp.where(requests[:, None] == request_ids[None, :], local_branch...]
  transfers between devices with their start and end apart: 27 -> 27, of which waited for: 15 -> 12; matrix products, arithmetic and copies ran while one was open for 1% -> 6% of each run, Pallas kernels for 3% -> 4%
where the time goes in v7:
time: 63.6 us; the launch traced here: 62.8 us
  starting transfers between devices  30.2 us (47%)
  waiting for transfers between devices  25.1 us (39%)
  other arithmetic  3.5 us (6%)
  Pallas kernels  3.16 us (5%)
  between operations  0.82 us (1%)
    ppermute x27, starting transfers between devices, swap(): return lax.ppermute(value, axes, [(i, i ^ bits) for i in range(count)])  30.2 us
    ppermute x27, waiting for transfers between devices, swap(): return lax.ppermute(value, axes, [(i, i ^ bits) for i in range(count)])  25.1 us
    pallas_call x6, Pallas kernels, call(): pl.pallas_call(kernel, out_shape=out_shape, in_specs=[vmem] * len(args),...  3.16 us
  transfers between devices with their start and end apart: 27, of which 12 were waited for; matrix products, arithmetic and copies ran while one was open for 6% of the time, Pallas kernels for 4%

profile of v7, /device:TPU:0, one launch (start us, length us, event | category | flops | bytes accessed | tf_op | source)
XLA Modules:
  0.0 62.8 jit_solution(12473874202762914021)
XLA Ops:
  0.7 5.1 %collective-permute-start.2 = (bf16[2,64,256]{2,1,0:T(8,128)(2,1)}, bf16[2,64,256]{2,1,0:T(8,128)(2,1)S(1)}, u32[]{:S(2)}, u32[]{:S(2)}) collective-permute-start(bf16[2,64,256]{2,1,0:T(8,128)(2,1)} %refs_0_), channel_id=1, source_target_pairs={{0,24},{8,16},{16,8},{24,0},{1,25},{9,17},{17,9},{25,1},{2,26},{10... | collective-permute-start | bytes 196616 | tf_op jit(solution)/shard_map/ppermute | solution.py:179
  5.8 0.6 %collective-permute-start = (bf16[2,64,256]{2,1,0:T(8,128)(2,1)}, bf16[2,64,256]{2,1,0:T(8,128)(2,1)S(1)}, u32[]{:S(2)}, u32[]{:S(2)}) collective-permute-start(bf16[2,64,256]{2,1,0:T(8,128)(2,1)} %refs_0_), channel_id=1, source_target_pairs={{0,8},{8,0},{16,24},{24,16},{1,9},{9,1},{17,25},{25,17},{2,10},{10... | collective-permute-start | bytes 196616 | tf_op jit(solution)/shard_map/ppermute | solution.py:179
  6.4 1.7 %collective-permute-start.3 = (bf16[2,64,256]{2,1,0:T(8,128)(2,1)}, bf16[2,64,256]{2,1,0:T(8,128)(2,1)S(1)}, u32[]{:S(2)}, u32[]{:S(2)}) collective-permute-start(bf16[2,64,256]{2,1,0:T(8,128)(2,1)} %refs_0_), channel_id=1, source_target_pairs={{0,4},{4,0},{1,5},{5,1},{2,6},{6,2},{3,7},{7,3},{8,12},{12,8},{9,1... | collective-permute-start | bytes 196616 | tf_op jit(solution)/shard_map/ppermute | solution.py:179
  8.5 0.7 %select_reduce_fusion.3 = s32[64]{0:T(128)S(1)} fusion(s32[4]{0:T(128)} %bitcast.8, s32[64]{0:T(128)S(1)} %bitcast.7), kind=kLoop, calls=%fused_computation.13 | loop fusion | flops 704 | bytes 528 | tf_op jit(solution)/shard_map/reduce_sum | solution.py:39
  9.3 0.8 %select_reduce_fusion.2 = (s32[64]{0:T(128)S(1)}, s32[64]{0:T(128)S(1)}, s32[64]{0:T(128)S(1)}) fusion(s32[8]{0:T(128)} %param.21, s32[64]{0:T(128)S(1)} %select_reduce_fusion.3, s32[8]{0:T(128)} %param.20, s32[8]{0:T(128)} %param.19), kind=kLoop, calls=%fused_computation.11 | loop fusion | flops 3392 | bytes 1120 | tf_op jit(solution)/shard_map/reduce_sum | solution.py:212
  10.1 0.8 %broadcast_compare_fusion = (pred[8,32,64]{2,1,0:T(8,128)(4,1)S(1)}, pred[8,32,64]{2,1,0:T(8,128)(4,1)S(1)}) fusion(s32[64]{0:T(128)S(1)} %get-tuple-element.95, s32[8,32]{1,0:T(8,128)} %param.18, pred[32,64]{1,0:T(8,128)(4,1)S(1)} %iota_compare_fusion.1, pred[8,64]{1,0:T(8,128)(4,1)S(1)} %iota_compare_fusion.2), kind=kLoop, calls=%fused_computation.3 | loop fusion | flops 32768 | bytes 36608 | tf_op jit(solution)/shard_map/eq | solution.py:222
  11.1 0.9 %pad_maximum_fusion.local_ref = bf16[64,1024]{1,0:T(8,128)(2,1)S(1)} fusion(bf16[64,256]{1,0:T(8,128)(2,1)} %param.16, bf16[64,256]{1,0:T(8,128)(2,1)} %param.15, bf16[64,512]{1,0:T(8,128)(2,1)} %param.14), kind=kLoop, calls=%fused_computation.2 | loop fusion | flops 393216 | bytes 262144 | tf_op jit(solution)/shard_map/concatenate | solution.py:230
  12.0 1.7 %collective-permute-start.4 = (bf16[2,64,256]{2,1,0:T(8,128)(2,1)S(1)}, bf16[2,64,256]{2,1,0:T(8,128)(2,1)S(1)}, u32[]{:S(2)}, u32[]{:S(2)}) collective-permute-start(bf16[2,64,256]{2,1,0:T(8,128)(2,1)S(1)} %collective-permute-done.refs_2_), channel_id=1, source_target_pairs={{0,4},{4,0},{1,5},{5,1},{2,6},{6,2},{3,7},{7,3},{8,12},{12,8},{9,1... | collective-permute-start | bytes 196616 | tf_op jit(solution)/shard_map/ppermute | solution.py:179
  14.1 1.7 %collective-permute-start.6 = (bf16[2,64,256]{2,1,0:T(8,128)(2,1)S(1)}, bf16[2,64,256]{2,1,0:T(8,128)(2,1)S(1)}, u32[]{:S(2)}, u32[]{:S(2)}) collective-permute-start(bf16[2,64,256]{2,1,0:T(8,128)(2,1)S(1)} %collective-permute-done.2.refs_6_), channel_id=1, source_target_pairs={{0,4},{4,0},{1,5},{5,1},{2,6},{6,2},{3,7},{7,3},{8,12},{12,8},{9,1... | collective-permute-start | bytes 196616 | tf_op jit(solution)/shard_map/ppermute | solution.py:179
  15.8 3.1 %collective-permute-done.4.refs_3_ = bf16[2,64,256]{2,1,0:T(8,128)(2,1)S(1)} collective-permute-done((bf16[2,64,256]{2,1,0:T(8,128)(2,1)S(1)}, bf16[2,64,256]{2,1,0:T(8,128)(2,1)S(1)}, u32[]{:S(2)}, u32[]{:S(2)}) %collective-permute-start.4) | collective-permute-done | bytes 65568 | tf_op jit(solution)/shard_map/ppermute | solution.py:179
  18.9 0.7 %collective-permute-done.5.refs_5_ = bf16[2,64,256]{2,1,0:T(8,128)(2,1)S(1)} collective-permute-done((bf16[2,64,256]{2,1,0:T(8,128)(2,1)S(1)}, bf16[2,64,256]{2,1,0:T(8,128)(2,1)S(1)}, u32[]{:S(2)}, u32[]{:S(2)}) %collective-permute-start.5) | collective-permute-done | bytes 65568 | tf_op jit(solution)/shard_map/ppermute | solution.py:179
  19.6 0.7 %collective-permute-done.6.refs_7_ = bf16[2,64,256]{2,1,0:T(8,128)(2,1)S(1)} collective-permute-done((bf16[2,64,256]{2,1,0:T(8,128)(2,1)S(1)}, bf16[2,64,256]{2,1,0:T(8,128)(2,1)S(1)}, u32[]{:S(2)}, u32[]{:S(2)}) %collective-permute-start.6) | collective-permute-done | bytes 65568 | tf_op jit(solution)/shard_map/ppermute | solution.py:179
  20.3 1.0 %collective-permute-start.14 = (bf16[256,1024]{1,0:T(8,128)(2,1)S(1)}, bf16[256,1024]{1,0:T(8,128)(2,1)S(1)}, u32[]{:S(2)}, u32[]{:S(2)}) collective-permute-start(bf16[256,1024]{1,0:T(8,128)(2,1)S(1)} %copy-done), channel_id=1, source_target_pairs={{0,4},{4,0},{1,5},{5,1},{2,6},{6,2},{3,7},{7,3},{8,12},{12,8},{9,1... | collective-permute-start | bytes 1572872 | tf_op jit(solution)/shard_map/ppermute | solution.py:179
  21.3 1.3 %shard_map.157 = (bf16[64,512]{1,0:T(8,128)(2,1)}, bf16[64,640]{1,0:T(8,128)(2,1)S(1)}, bf16[64,640]{1,0:T(8,128)(2,1)S(1)}, bf16[64,640]{1,0:T(8,128)(2,1)S(1)}, bf16[64,640]{1,0:T(8,128)(2,1)S(1)}) custom-call(bf16[64,1024]{1,0:T(8,128)(2,1)S(1)} %pad_maximum_fusion.local_ref, bf16[64,2048]{1,0:T(8,128)(2,1)S(1)} %copy-done.1, ...), custom_call_target="tpu_custom_call" | custom-call | flops 67108864 | bytes 1048576 | tf_op jit(solution)/shard_map/pallas_call | solution.py:166
  22.6 1.4 %collective-permute-start.8 = (bf16[64,640]{1,0:T(8,128)(2,1)S(1)}, bf16[64,640]{1,0:T(8,128)(2,1)S(1)}, u32[]{:S(2)}, u32[]{:S(2)}) collective-permute-start(bf16[64,640]{1,0:T(8,128)(2,1)S(1)} %get-tuple-element.64), channel_id=1, source_target_pairs={{0,8},{8,0},{16,24},{24,16},{1,9},{9,1},{17,25},{25,17},{2,10},{10... | collective-permute-start | bytes 245768 | tf_op jit(solution)/shard_map/ppermute | solution.py:179
  23.9 2.6 %collective-permute-start.9 = (bf16[64,640]{1,0:T(8,128)(2,1)S(1)}, bf16[64,640]{1,0:T(8,128)(2,1)S(1)}, u32[]{:S(2)}, u32[]{:S(2)}) collective-permute-start(bf16[64,640]{1,0:T(8,128)(2,1)S(1)} %get-tuple-element.65), channel_id=1, source_target_pairs={{0,16},{8,24},{16,0},{24,8},{1,17},{9,25},{17,1},{25,9},{2,18},{10... | collective-permute-start | bytes 245768 | tf_op jit(solution)/shard_map/ppermute | solution.py:179
  27.2 3.7 %collective-permute-done.9.a2 = bf16[64,640]{1,0:T(8,128)(2,1)S(1)} collective-permute-done((bf16[64,640]{1,0:T(8,128)(2,1)S(1)}, bf16[64,640]{1,0:T(8,128)(2,1)S(1)}, u32[]{:S(2)}, u32[]{:S(2)}) %collective-permute-start.9) | collective-permute-done | bytes 81952 | tf_op jit(solution)/shard_map/ppermute | solution.py:179
  30.9 1.9 %collective-permute-done.10.a3 = bf16[64,640]{1,0:T(8,128)(2,1)S(1)} collective-permute-done((bf16[64,640]{1,0:T(8,128)(2,1)S(1)}, bf16[64,640]{1,0:T(8,128)(2,1)S(1)}, u32[]{:S(2)}, u32[]{:S(2)}) %collective-permute-start.10) | collective-permute-done | bytes 81952 | tf_op jit(solution)/shard_map/ppermute | solution.py:179
  33.3 1.6 %collective-permute-start.12 = (bf16[256,128]{1,0:T(8,128)(2,1)S(1)}, bf16[256,128]{1,0:T(8,128)(2,1)S(1)}, u32[]{:S(2)}, u32[]{:S(2)}) collective-permute-start(bf16[256,128]{1,0:T(8,128)(2,1)S(1)} %get-tuple-element.70), channel_id=1, source_target_pairs={{0,2},{1,3},{2,0},{3,1},{4,6},{5,7},{6,4},{7,5},{8,10},{9,11},{10,... | collective-permute-start | bytes 196616 | tf_op jit(solution)/shard_map/ppermute | solution.py:179
  35.2 2.6 %collective-permute-done.12.r2 = bf16[256,128]{1,0:T(8,128)(2,1)S(1)} collective-permute-done((bf16[256,128]{1,0:T(8,128)(2,1)S(1)}, bf16[256,128]{1,0:T(8,128)(2,1)S(1)}, u32[]{:S(2)}, u32[]{:S(2)}) %collective-permute-start.12) | collective-permute-done | bytes 65568 | tf_op jit(solution)/shard_map/ppermute | solution.py:179
  37.9 1.1 %collective-permute-done.13.r3 = bf16[256,128]{1,0:T(8,128)(2,1)S(1)} collective-permute-done((bf16[256,128]{1,0:T(8,128)(2,1)S(1)}, bf16[256,128]{1,0:T(8,128)(2,1)S(1)}, u32[]{:S(2)}, u32[]{:S(2)}) %collective-permute-start.13) | collective-permute-done | bytes 65568 | tf_op jit(solution)/shard_map/ppermute | solution.py:179
  39.0 1.3 %collective-permute-start.20 = (bf16[256,128]{1,0:T(8,128)(2,1)S(1)}, bf16[256,128]{1,0:T(8,128)(2,1)S(1)}, u32[]{:S(2)}, u32[]{:S(2)}) collective-permute-start(bf16[256,128]{1,0:T(8,128)(2,1)S(1)} %get-tuple-element.82.x0), channel_id=1, source_target_pairs={{0,3},{1,2},{2,1},{3,0},{4,7},{5,6},{6,5},{7,4},{8,11},{9,10},{10,... | collective-permute-start | bytes 196616 | tf_op jit(solution)/shard_map/ppermute | solution.py:179
  40.9 1.5 %collective-permute-start.16 = (bf16[64,128]{1,0:T(8,128)(2,1)S(1)}, bf16[64,128]{1,0:T(8,128)(2,1)S(1)}, u32[]{:S(2)}, u32[]{:S(2)}) collective-permute-start(bf16[64,128]{1,0:T(8,128)(2,1)S(1)} %get-tuple-element.80), channel_id=1, source_target_pairs={{0,16},{8,24},{16,0},{24,8},{1,17},{9,25},{17,1},{25,9},{2,18},{10... | collective-permute-start | bytes 49160 | tf_op jit(solution)/shard_map/ppermute | solution.py:179
  42.5 0.7 %collective-permute-done.20.x3 = bf16[256,128]{1,0:T(8,128)(2,1)S(1)} collective-permute-done((bf16[256,128]{1,0:T(8,128)(2,1)S(1)}, bf16[256,128]{1,0:T(8,128)(2,1)S(1)}, u32[]{:S(2)}, u32[]{:S(2)}) %collective-permute-start.20) | collective-permute-done | bytes 65568 | tf_op jit(solution)/shard_map/ppermute | solution.py:179
  43.2 2.1 %collective-permute-start.17 = (bf16[64,128]{1,0:T(8,128)(2,1)S(1)}, bf16[64,128]{1,0:T(8,128)(2,1)S(1)}, u32[]{:S(2)}, u32[]{:S(2)}) collective-permute-start(bf16[64,128]{1,0:T(8,128)(2,1)S(1)} %get-tuple-element.81), channel_id=1, source_target_pairs={{0,24},{8,16},{16,8},{24,0},{1,25},{9,17},{17,9},{25,1},{2,26},{10... | collective-permute-start | bytes 49160 | tf_op jit(solution)/shard_map/ppermute | solution.py:179
  45.9 2.9 %collective-permute-done.17.t3 = bf16[64,128]{1,0:T(8,128)(2,1)S(1)} collective-permute-done((bf16[64,128]{1,0:T(8,128)(2,1)S(1)}, bf16[64,128]{1,0:T(8,128)(2,1)S(1)}, u32[]{:S(2)}, u32[]{:S(2)}) %collective-permute-start.17) | collective-permute-done | bytes 16416 | tf_op jit(solution)/shard_map/ppermute | solution.py:179
  49.1 2.5 %collective-permute-start.22 = (bf16[64,1024]{1,0:T(8,128)(2,1)S(1)}, bf16[64,1024]{1,0:T(8,128)(2,1)S(1)}, u32[]{:S(2)}, u32[]{:S(2)}) collective-permute-start(bf16[64,1024]{1,0:T(8,128)(2,1)S(1)} %get-tuple-element.87), channel_id=1, source_target_pairs={{0,16},{8,24},{16,0},{24,8},{1,17},{9,25},{17,1},{25,9},{2,18},{10... | collective-permute-start | bytes 393224 | tf_op jit(solution)/shard_map/ppermute | solution.py:179
  51.6 1.9 %collective-permute-start.23 = (bf16[64,1024]{1,0:T(8,128)(2,1)S(1)}, bf16[64,1024]{1,0:T(8,128)(2,1)S(1)}, u32[]{:S(2)}, u32[]{:S(2)}) collective-permute-start(bf16[64,1024]{1,0:T(8,128)(2,1)S(1)} %get-tuple-element.88), channel_id=1, source_target_pairs={{0,24},{8,16},{16,8},{24,0},{1,25},{9,17},{17,9},{25,1},{2,26},{10... | collective-permute-start | bytes 393224 | tf_op jit(solution)/shard_map/ppermute | solution.py:179
  53.5 1.1 %collective-permute-start.25 = (bf16[64,512]{1,0:T(8,128)(2,1)S(1)}, bf16[64,512]{1,0:T(8,128)(2,1)S(1)}, u32[]{:S(2)}, u32[]{:S(2)}) collective-permute-start(bf16[64,512]{1,0:T(8,128)(2,1)S(1)} %shard_map.161.p0), channel_id=1, source_target_pairs={{0,2},{1,3},{2,0},{3,1},{4,6},{5,7},{6,4},{7,5},{8,10},{9,11},{10,... | collective-permute-start | bytes 196616 | tf_op jit(solution)/shard_map/ppermute | solution.py:179
  54.5 3.2 %collective-permute-done.25.p2 = bf16[64,512]{1,0:T(8,128)(2,1)S(1)} collective-permute-done((bf16[64,512]{1,0:T(8,128)(2,1)S(1)}, bf16[64,512]{1,0:T(8,128)(2,1)S(1)}, u32[]{:S(2)}, u32[]{:S(2)}) %collective-permute-start.25) | collective-permute-done | bytes 65568 | tf_op jit(solution)/shard_map/ppermute | solution.py:179
  57.7 4.2 %collective-permute-done.22.y2 = bf16[64,1024]{1,0:T(8,128)(2,1)S(1)} collective-permute-done((bf16[64,1024]{1,0:T(8,128)(2,1)S(1)}, bf16[64,1024]{1,0:T(8,128)(2,1)S(1)}, u32[]{:S(2)}, u32[]{:S(2)}) %collective-permute-start.22) | collective-permute-done | bytes 131104 | tf_op jit(solution)/shard_map/ppermute | solution.py:179
  61.9 0.9 %shard_map.162 = (bf16[64,1024]{1,0:T(8,128)(2,1)}, bf16[64,2048]{1,0:T(8,128)(2,1)}) custom-call(f32[64,1024]{1,0:T(8,128)S(1)} %get-tuple-element.85.y0, bf16[64,1024]{1,0:T(8,128)(2,1)S(1)} %collective-permute-done.21.y1, bf16[64,1024]{1,0:T(8,128)(2,1)S(1)} %collective-permute-done.22.y2, bf16[64,1024]{1,0:T(8,128)(2,1)S(1)} %collective-permute-done.23.y3, ...), custom_call_target="tpu_custom_call" | custom-call | bytes 1048576 | tf_op jit(solution)/shard_map/pallas_call | solution.py:166
  (49 shorter events, 4.0 us)
Async XLA Ops:
  0.6 7.8 %copy-start.5 = (s32[1,64]{1,0:T(1,128)S(1)}, s32[1,64]{1,0:T(1,128)}, u32[]{:S(2)}) copy-start(s32[1,64]{1,0:T(1,128)} %param.23) | copy-start | bytes 772
  0.6 19.6 %copy-start = (bf16[256,1024]{1,0:T(8,128)(2,1)S(1)}, bf16[256,1024]{1,0:T(8,128)(2,1)}, u32[]{:S(2)}) copy-start(bf16[256,1024]{1,0:T(8,128)(2,1)} %own_ref.3) | copy-start | bytes 1572868
  0.7 11.4 %collective-permute-start.2 = (bf16[2,64,256]{2,1,0:T(8,128)(2,1)}, bf16[2,64,256]{2,1,0:T(8,128)(2,1)S(1)}, u32[]{:S(2)}, u32[]{:S(2)}) collective-permute-start(bf16[2,64,256]{2,1,0:T(8,128)(2,1)} %refs_0_), channel_id=1, source_target_pairs={{0,24},{8,16},{16,8},{24,0},{1,25},{9,17},{17,9},{25,1},{2,26},{10... | collective-permute-start | bytes 196616 | tf_op jit(solution)/shard_map/ppermute | solution.py:179
  5.8 6.3 %collective-permute-start.1 = (bf16[2,64,256]{2,1,0:T(8,128)(2,1)}, bf16[2,64,256]{2,1,0:T(8,128)(2,1)S(1)}, u32[]{:S(2)}, u32[]{:S(2)}) collective-permute-start(bf16[2,64,256]{2,1,0:T(8,128)(2,1)} %refs_0_), channel_id=1, source_target_pairs={{0,16},{8,24},{16,0},{24,8},{1,17},{9,25},{17,1},{25,9},{2,18},{10... | collective-permute-start | bytes 196616 | tf_op jit(solution)/shard_map/ppermute | solution.py:179
  5.8 6.3 %collective-permute-start = (bf16[2,64,256]{2,1,0:T(8,128)(2,1)}, bf16[2,64,256]{2,1,0:T(8,128)(2,1)S(1)}, u32[]{:S(2)}, u32[]{:S(2)}) collective-permute-start(bf16[2,64,256]{2,1,0:T(8,128)(2,1)} %refs_0_), channel_id=1, source_target_pairs={{0,8},{8,0},{16,24},{24,16},{1,9},{9,1},{17,25},{25,17},{2,10},{10... | collective-permute-start | bytes 196616 | tf_op jit(solution)/shard_map/ppermute | solution.py:179
  6.4 9.4 %collective-permute-start.3 = (bf16[2,64,256]{2,1,0:T(8,128)(2,1)}, bf16[2,64,256]{2,1,0:T(8,128)(2,1)S(1)}, u32[]{:S(2)}, u32[]{:S(2)}) collective-permute-start(bf16[2,64,256]{2,1,0:T(8,128)(2,1)} %refs_0_), channel_id=1, source_target_pairs={{0,4},{4,0},{1,5},{5,1},{2,6},{6,2},{3,7},{7,3},{8,12},{12,8},{9,1... | collective-permute-start | bytes 196616 | tf_op jit(solution)/shard_map/ppermute | solution.py:179
  8.1 12.2 %collective-permute-start.7 = (bf16[256,512]{1,0:T(8,128)(2,1)}, bf16[256,512]{1,0:T(8,128)(2,1)S(1)}, u32[]{:S(2)}, u32[]{:S(2)}) collective-permute-start(bf16[256,512]{1,0:T(8,128)(2,1)} %own_ref.2), channel_id=1, source_target_pairs={{0,4},{4,0},{1,5},{5,1},{2,6},{6,2},{3,7},{7,3},{8,12},{12,8},{9,1... | collective-permute-start | bytes 786440 | tf_op jit(solution)/shard_map/ppermute | solution.py:179
  10.9 10.4 %copy-start.1 = (bf16[64,2048]{1,0:T(8,128)(2,1)S(1)}, bf16[64,2048]{1,0:T(8,128)(2,1)}, u32[]{:S(2)}) copy-start(bf16[64,2048]{1,0:T(8,128)(2,1)} %res_ref.1) | copy-start | bytes 786436
  11.1 10.2 %copy-start.3 = (bf16[2,64,256]{2,1,0:T(8,128)(2,1)S(1)}, bf16[2,64,256]{2,1,0:T(8,128)(2,1)}, u32[]{:S(2)}) copy-start(bf16[2,64,256]{2,1,0:T(8,128)(2,1)} %refs_0_) | copy-start | bytes 196612
  12.0 20.8 %copy-start.2 = (bf16[256,512]{1,0:T(8,128)(2,1)S(1)}, bf16[256,512]{1,0:T(8,128)(2,1)}, u32[]{:S(2)}) copy-start(bf16[256,512]{1,0:T(8,128)(2,1)} %own_ref.2) | copy-start | bytes 786436
  12.0 6.8 %collective-permute-start.4 = (bf16[2,64,256]{2,1,0:T(8,128)(2,1)S(1)}, bf16[2,64,256]{2,1,0:T(8,128)(2,1)S(1)}, u32[]{:S(2)}, u32[]{:S(2)}) collective-permute-start(bf16[2,64,256]{2,1,0:T(8,128)(2,1)S(1)} %collective-permute-done.refs_2_), channel_id=1, source_target_pairs={{0,4},{4,0},{1,5},{5,1},{2,6},{6,2},{3,7},{7,3},{8,12},{12,8},{9,1... | collective-permute-start | bytes 196616 | tf_op jit(solution)/shard_map/ppermute | solution.py:179
  13.8 5.8 %collective-permute-start.5 = (bf16[2,64,256]{2,1,0:T(8,128)(2,1)S(1)}, bf16[2,64,256]{2,1,0:T(8,128)(2,1)S(1)}, u32[]{:S(2)}, u32[]{:S(2)}) collective-permute-start(bf16[2,64,256]{2,1,0:T(8,128)(2,1)S(1)} %collective-permute-done.1.refs_4_), channel_id=1, source_target_pairs={{0,4},{4,0},{1,5},{5,1},{2,6},{6,2},{3,7},{7,3},{8,12},{12,8},{9,1... | collective-permute-start | bytes 196616 | tf_op jit(solution)/shard_map/ppermute | solution.py:179
  14.1 6.1 %collective-permute-start.6 = (bf16[2,64,256]{2,1,0:T(8,128)(2,1)S(1)}, bf16[2,64,256]{2,1,0:T(8,128)(2,1)S(1)}, u32[]{:S(2)}, u32[]{:S(2)}) collective-permute-start(bf16[2,64,256]{2,1,0:T(8,128)(2,1)S(1)} %collective-permute-done.2.refs_6_), channel_id=1, source_target_pairs={{0,4},{4,0},{1,5},{5,1},{2,6},{6,2},{3,7},{7,3},{8,12},{12,8},{9,1... | collective-permute-start | bytes 196616 | tf_op jit(solution)/shard_map/ppermute | solution.py:179
  20.3 18.7 %collective-permute-start.14 = (bf16[256,1024]{1,0:T(8,128)(2,1)S(1)}, bf16[256,1024]{1,0:T(8,128)(2,1)S(1)}, u32[]{:S(2)}, u32[]{:S(2)}) collective-permute-start(bf16[256,1024]{1,0:T(8,128)(2,1)S(1)} %copy-done), channel_id=1, source_target_pairs={{0,4},{4,0},{1,5},{5,1},{2,6},{6,2},{3,7},{7,3},{8,12},{12,8},{9,1... | collective-permute-start | bytes 1572872 | tf_op jit(solution)/shard_map/ppermute | solution.py:179
  22.6 4.6 %collective-permute-start.8 = (bf16[64,640]{1,0:T(8,128)(2,1)S(1)}, bf16[64,640]{1,0:T(8,128)(2,1)S(1)}, u32[]{:S(2)}, u32[]{:S(2)}) collective-permute-start(bf16[64,640]{1,0:T(8,128)(2,1)S(1)} %get-tuple-element.64), channel_id=1, source_target_pairs={{0,8},{8,0},{16,24},{24,16},{1,9},{9,1},{17,25},{25,17},{2,10},{10... | collective-permute-start | bytes 245768 | tf_op jit(solution)/shard_map/ppermute | solution.py:179
  23.9 6.9 %collective-permute-start.9 = (bf16[64,640]{1,0:T(8,128)(2,1)S(1)}, bf16[64,640]{1,0:T(8,128)(2,1)S(1)}, u32[]{:S(2)}, u32[]{:S(2)}) collective-permute-start(bf16[64,640]{1,0:T(8,128)(2,1)S(1)} %get-tuple-element.65), channel_id=1, source_target_pairs={{0,16},{8,24},{16,0},{24,8},{1,17},{9,25},{17,1},{25,9},{2,18},{10... | collective-permute-start | bytes 245768 | tf_op jit(solution)/shard_map/ppermute | solution.py:179
  26.6 6.2 %collective-permute-start.10 = (bf16[64,640]{1,0:T(8,128)(2,1)S(1)}, bf16[64,640]{1,0:T(8,128)(2,1)S(1)}, u32[]{:S(2)}, u32[]{:S(2)}) collective-permute-start(bf16[64,640]{1,0:T(8,128)(2,1)S(1)} %get-tuple-element.66), channel_id=1, source_target_pairs={{0,24},{8,16},{16,8},{24,0},{1,25},{9,17},{17,9},{25,1},{2,26},{10... | collective-permute-start | bytes 245768 | tf_op jit(solution)/shard_map/ppermute | solution.py:179
  33.3 1.9 %collective-permute-start.11 = (bf16[256,128]{1,0:T(8,128)(2,1)S(1)}, bf16[256,128]{1,0:T(8,128)(2,1)S(1)}, u32[]{:S(2)}, u32[]{:S(2)}) collective-permute-start(bf16[256,128]{1,0:T(8,128)(2,1)S(1)} %get-tuple-element.69), channel_id=1, source_target_pairs={{0,1},{1,0},{2,3},{3,2},{4,5},{5,4},{6,7},{7,6},{8,9},{9,8},{10,11... | collective-permute-start | bytes 196616 | tf_op jit(solution)/shard_map/ppermute | solution.py:179
  33.3 4.5 %collective-permute-start.12 = (bf16[256,128]{1,0:T(8,128)(2,1)S(1)}, bf16[256,128]{1,0:T(8,128)(2,1)S(1)}, u32[]{:S(2)}, u32[]{:S(2)}) collective-permute-start(bf16[256,128]{1,0:T(8,128)(2,1)S(1)} %get-tuple-element.70), channel_id=1, source_target_pairs={{0,2},{1,3},{2,0},{3,1},{4,6},{5,7},{6,4},{7,5},{8,10},{9,11},{10,... | collective-permute-start | bytes 196616 | tf_op jit(solution)/shard_map/ppermute | solution.py:179
  34.9 4.0 %collective-permute-start.13 = (bf16[256,128]{1,0:T(8,128)(2,1)S(1)}, bf16[256,128]{1,0:T(8,128)(2,1)S(1)}, u32[]{:S(2)}, u32[]{:S(2)}) collective-permute-start(bf16[256,128]{1,0:T(8,128)(2,1)S(1)} %get-tuple-element.71), channel_id=1, source_target_pairs={{0,3},{1,2},{2,1},{3,0},{4,7},{5,6},{6,5},{7,4},{8,11},{9,10},{10,... | collective-permute-start | bytes 196616 | tf_op jit(solution)/shard_map/ppermute | solution.py:179
  39.0 4.2 %collective-permute-start.20 = (bf16[256,128]{1,0:T(8,128)(2,1)S(1)}, bf16[256,128]{1,0:T(8,128)(2,1)S(1)}, u32[]{:S(2)}, u32[]{:S(2)}) collective-permute-start(bf16[256,128]{1,0:T(8,128)(2,1)S(1)} %get-tuple-element.82.x0), channel_id=1, source_target_pairs={{0,3},{1,2},{2,1},{3,0},{4,7},{5,6},{6,5},{7,4},{8,11},{9,10},{10,... | collective-permute-start | bytes 196616 | tf_op jit(solution)/shard_map/ppermute | solution.py:179
  40.3 5.0 %collective-permute-start.19 = (bf16[256,128]{1,0:T(8,128)(2,1)S(1)}, bf16[256,128]{1,0:T(8,128)(2,1)S(1)}, u32[]{:S(2)}, u32[]{:S(2)}) collective-permute-start(bf16[256,128]{1,0:T(8,128)(2,1)S(1)} %get-tuple-element.82.x0), channel_id=1, source_target_pairs={{0,2},{1,3},{2,0},{3,1},{4,6},{5,7},{6,4},{7,5},{8,10},{9,11},{10,... | collective-permute-start | bytes 196616 | tf_op jit(solution)/shard_map/ppermute | solution.py:179
  40.9 4.5 %collective-permute-start.18 = (bf16[256,128]{1,0:T(8,128)(2,1)S(1)}, bf16[256,128]{1,0:T(8,128)(2,1)S(1)}, u32[]{:S(2)}, u32[]{:S(2)}) collective-permute-start(bf16[256,128]{1,0:T(8,128)(2,1)S(1)} %get-tuple-element.82.x0), channel_id=1, source_target_pairs={{0,1},{1,0},{2,3},{3,2},{4,5},{5,4},{6,7},{7,6},{8,9},{9,8},{10,11... | collective-permute-start | bytes 196616 | tf_op jit(solution)/shard_map/ppermute | solution.py:179
  40.9 4.9 %collective-permute-start.15 = (bf16[64,128]{1,0:T(8,128)(2,1)S(1)}, bf16[64,128]{1,0:T(8,128)(2,1)S(1)}, u32[]{:S(2)}, u32[]{:S(2)}) collective-permute-start(bf16[64,128]{1,0:T(8,128)(2,1)S(1)} %get-tuple-element.79), channel_id=1, source_target_pairs={{0,8},{8,0},{16,24},{24,16},{1,9},{9,1},{17,25},{25,17},{2,10},{10... | collective-permute-start | bytes 49160 | tf_op jit(solution)/shard_map/ppermute | solution.py:179
  40.9 4.9 %collective-permute-start.16 = (bf16[64,128]{1,0:T(8,128)(2,1)S(1)}, bf16[64,128]{1,0:T(8,128)(2,1)S(1)}, u32[]{:S(2)}, u32[]{:S(2)}) collective-permute-start(bf16[64,128]{1,0:T(8,128)(2,1)S(1)} %get-tuple-element.80), channel_id=1, source_target_pairs={{0,16},{8,24},{16,0},{24,8},{1,17},{9,25},{17,1},{25,9},{2,18},{10... | collective-permute-start | bytes 49160 | tf_op jit(solution)/shard_map/ppermute | solution.py:179
  43.2 5.5 %collective-permute-start.17 = (bf16[64,128]{1,0:T(8,128)(2,1)S(1)}, bf16[64,128]{1,0:T(8,128)(2,1)S(1)}, u32[]{:S(2)}, u32[]{:S(2)}) collective-permute-start(bf16[64,128]{1,0:T(8,128)(2,1)S(1)} %get-tuple-element.81), channel_id=1, source_target_pairs={{0,24},{8,16},{16,8},{24,0},{1,25},{9,17},{17,9},{25,1},{2,26},{10... | collective-permute-start | bytes 49160 | tf_op jit(solution)/shard_map/ppermute | solution.py:179
  48.8 5.8 %collective-permute-start.26 = (bf16[64,512]{1,0:T(8,128)(2,1)S(1)}, bf16[64,512]{1,0:T(8,128)(2,1)S(1)}, u32[]{:S(2)}, u32[]{:S(2)}) collective-permute-start(bf16[64,512]{1,0:T(8,128)(2,1)S(1)} %shard_map.161.p0), channel_id=1, source_target_pairs={{0,3},{1,2},{2,1},{3,0},{4,7},{5,6},{6,5},{7,4},{8,11},{9,10},{10,... | collective-permute-start | bytes 196616 | tf_op jit(solution)/shard_map/ppermute | solution.py:179
  49.1 8.7 %collective-permute-start.21 = (bf16[64,1024]{1,0:T(8,128)(2,1)S(1)}, bf16[64,1024]{1,0:T(8,128)(2,1)S(1)}, u32[]{:S(2)}, u32[]{:S(2)}) collective-permute-start(bf16[64,1024]{1,0:T(8,128)(2,1)S(1)} %get-tuple-element.86), channel_id=1, source_target_pairs={{0,8},{8,0},{16,24},{24,16},{1,9},{9,1},{17,25},{25,17},{2,10},{10... | collective-permute-start | bytes 393224 | tf_op jit(solution)/shard_map/ppermute | solution.py:179
  49.1 12.8 %collective-permute-start.22 = (bf16[64,1024]{1,0:T(8,128)(2,1)S(1)}, bf16[64,1024]{1,0:T(8,128)(2,1)S(1)}, u32[]{:S(2)}, u32[]{:S(2)}) collective-permute-start(bf16[64,1024]{1,0:T(8,128)(2,1)S(1)} %get-tuple-element.87), channel_id=1, source_target_pairs={{0,16},{8,24},{16,0},{24,8},{1,17},{9,25},{17,1},{25,9},{2,18},{10... | collective-permute-start | bytes 393224 | tf_op jit(solution)/shard_map/ppermute | solution.py:179
  51.6 10.3 %collective-permute-start.23 = (bf16[64,1024]{1,0:T(8,128)(2,1)S(1)}, bf16[64,1024]{1,0:T(8,128)(2,1)S(1)}, u32[]{:S(2)}, u32[]{:S(2)}) collective-permute-start(bf16[64,1024]{1,0:T(8,128)(2,1)S(1)} %get-tuple-element.88), channel_id=1, source_target_pairs={{0,24},{8,16},{16,8},{24,0},{1,25},{9,17},{17,9},{25,1},{2,26},{10... | collective-permute-start | bytes 393224 | tf_op jit(solution)/shard_map/ppermute | solution.py:179
  53.5 4.3 %collective-permute-start.25 = (bf16[64,512]{1,0:T(8,128)(2,1)S(1)}, bf16[64,512]{1,0:T(8,128)(2,1)S(1)}, u32[]{:S(2)}, u32[]{:S(2)}) collective-permute-start(bf16[64,512]{1,0:T(8,128)(2,1)S(1)} %shard_map.161.p0), channel_id=1, source_target_pairs={{0,2},{1,3},{2,0},{3,1},{4,6},{5,7},{6,4},{7,5},{8,10},{9,11},{10,... | collective-permute-start | bytes 196616 | tf_op jit(solution)/shard_map/ppermute | solution.py:179
  54.5 3.2 %collective-permute-start.24 = (bf16[64,512]{1,0:T(8,128)(2,1)S(1)}, bf16[64,512]{1,0:T(8,128)(2,1)S(1)}, u32[]{:S(2)}, u32[]{:S(2)}) collective-permute-start(bf16[64,512]{1,0:T(8,128)(2,1)S(1)} %shard_map.161.p0), channel_id=1, source_target_pairs={{0,1},{1,0},{2,3},{3,2},{4,5},{5,4},{6,7},{7,6},{8,9},{9,8},{10,11... | collective-permute-start | bytes 196616 | tf_op jit(solution)/shard_map/ppermute | solution.py:179
  (1 other events, 6.4 us)

commit v8 on v7

--- a/solution.py
+++ b/solution.py
@@ -98,7 +98,7 @@
         ref[:, wide:] = res_ref[:, pl.ds(chunk_offset(e ^ (2 * s), m, width), width)]
 
 
-def project_kernel(a0, a1, a2, a3, own_ref, par_ref, o0, o1, o2, o3, hold):
+def project_kernel(a2, a3, a1, a0, own_ref, par_ref, o0, o1, o2, o3, hold):
     m = mp_index()
     half, wide = own_ref.shape
     blocks = (a0, a1, a2, a3)
@@ -112,7 +112,7 @@
         out[...] = chunk + rest.astype(F32) if j == 0 else chunk.astype(BF16)
 
 
-def combine_kernel(r0, r1, r2, r3, out, t0, t1, t2, t3):
+def combine_kernel(r2, r3, r1, r0, out, t0, t1, t2, t3):
     tok = t0.shape[0]
     stream = (
         r0[...] + r1[...].astype(F32) + r2[...].astype(F32) + r3[...].astype(F32)
@@ -146,7 +146,7 @@
         out_ref[:, s * width : (s + 1) * width] = part[...]
 
 
-def finish_kernel(y0, y1, y2, y3, p0, p1, p2, p3, qkv_ref, stream_ref):
+def finish_kernel(p0, p1, p2, p3, y2, y3, y1, y0, qkv_ref, stream_ref):
     e, m = seq_index(), mp_index()
     width = p0.shape[1] // 4
     squares = jnp.zeros((p0.shape[0], width), F32)
@@ -244,7 +244,7 @@
     sums = call(
         project_kernel,
         [sds((4 * tok, width), F32)] + [sds((4 * tok, width), BF16)] * 3,
-        (sends[0], a1, a2, a3, wo_t, wo_pair),
+        (a2, a3, a1, sends[0], wo_t, wo_pair),
         scratch=[pltpu.VMEM((4 * tok, 4 * width), F32)],
         flops=1 << 27,
     )
@@ -252,7 +252,7 @@
     made = call(
         combine_kernel,
         [sds((4 * tok, width), BF16)] + [sds((tok, width), BF16)] * 4,
-        tuple(sums),
+        (sums[2], sums[3], sums[1], sums[0]),
     )
     made, wq_pair = lax.optimization_barrier((made, wq_pair))
     slices = [made[0]] + [swap(made[0], mp, j) for j in range(1, 4)]
@@ -271,7 +271,7 @@
     qkv_next, stream = call(
         finish_kernel,
         [sds((tok, columns), BF16), sds(residual.shape, BF16)],
-        (own_partial, y1, y2, y3, *pieces),
+        (*pieces, y2, y3, y1, own_partial),
     )
     return attn, stream, qkv_next
 

time: 63.6 us -> 62.9 us (0.989); the launches traced: 62.8 us -> 62.7 us
  no operation moved by 1% of the time
where the time goes in v8:
time: 62.9 us; the launch traced here: 62.7 us
  starting transfers between devices  30.3 us (48%)
  waiting for transfers between devices  24.9 us (40%)
  other arithmetic  3.5 us (6%)
  Pallas kernels  3.16 us (5%)
  between operations  0.83 us (1%)
    ppermute x27, starting transfers between devices, swap(): return lax.ppermute(value, axes, [(i, i ^ bits) for i in range(count)])  30.3 us
    ppermute x27, waiting for transfers between devices, swap(): return lax.ppermute(value, axes, [(i, i ^ bits) for i in range(count)])  24.9 us
    pallas_call x6, Pallas kernels, call(): pl.pallas_call(kernel, out_shape=out_shape, in_specs=[vmem] * len(args),...  3.16 us
  transfers between devices with their start and end apart: 27, of which 12 were waited for; matrix products, arithmetic and copies ran while one was open for 6% of the time, Pallas kernels for 4%

profile of v8, /device:TPU:0, one launch (start us, length us, event | category | flops | bytes accessed | tf_op | source)
XLA Modules:
  0.0 62.7 jit_solution(1596706771006732596)
XLA Ops:
  0.7 5.1 %collective-permute-start.2 = (bf16[2,64,256]{2,1,0:T(8,128)(2,1)}, bf16[2,64,256]{2,1,0:T(8,128)(2,1)S(1)}, u32[]{:S(2)}, u32[]{:S(2)}) collective-permute-start(bf16[2,64,256]{2,1,0:T(8,128)(2,1)} %refs_0_), channel_id=1, source_target_pairs={{0,24},{8,16},{16,8},{24,0},{1,25},{9,17},{17,9},{25,1},{2,26},{10... | collective-permute-start | bytes 196616 | tf_op jit(solution)/shard_map/ppermute | solution.py:179
  6.4 1.7 %collective-permute-start.3 = (bf16[2,64,256]{2,1,0:T(8,128)(2,1)}, bf16[2,64,256]{2,1,0:T(8,128)(2,1)S(1)}, u32[]{:S(2)}, u32[]{:S(2)}) collective-permute-start(bf16[2,64,256]{2,1,0:T(8,128)(2,1)} %refs_0_), channel_id=1, source_target_pairs={{0,4},{4,0},{1,5},{5,1},{2,6},{6,2},{3,7},{7,3},{8,12},{12,8},{9,1... | collective-permute-start | bytes 196616 | tf_op jit(solution)/shard_map/ppermute | solution.py:179
  8.5 0.7 %select_reduce_fusion.3 = s32[64]{0:T(128)S(1)} fusion(s32[4]{0:T(128)} %bitcast.8, s32[64]{0:T(128)S(1)} %bitcast.7), kind=kLoop, calls=%fused_computation.13 | loop fusion | flops 704 | bytes 528 | tf_op jit(solution)/shard_map/reduce_sum | solution.py:39
  9.3 0.8 %select_reduce_fusion.2 = (s32[64]{0:T(128)S(1)}, s32[64]{0:T(128)S(1)}, s32[64]{0:T(128)S(1)}) fusion(s32[8]{0:T(128)} %param.21, s32[64]{0:T(128)S(1)} %select_reduce_fusion.3, s32[8]{0:T(128)} %param.20, s32[8]{0:T(128)} %param.19), kind=kLoop, calls=%fused_computation.11 | loop fusion | flops 3392 | bytes 1120 | tf_op jit(solution)/shard_map/reduce_sum | solution.py:212
  10.1 0.8 %broadcast_compare_fusion = (pred[8,32,64]{2,1,0:T(8,128)(4,1)S(1)}, pred[8,32,64]{2,1,0:T(8,128)(4,1)S(1)}) fusion(s32[64]{0:T(128)S(1)} %get-tuple-element.95, s32[8,32]{1,0:T(8,128)} %param.18, pred[32,64]{1,0:T(8,128)(4,1)S(1)} %iota_compare_fusion.1, pred[8,64]{1,0:T(8,128)(4,1)S(1)} %iota_compare_fusion.2), kind=kLoop, calls=%fused_computation.3 | loop fusion | flops 32768 | bytes 36608 | tf_op jit(solution)/shard_map/eq | solution.py:222
  11.1 0.9 %pad_maximum_fusion.local_ref = bf16[64,1024]{1,0:T(8,128)(2,1)S(1)} fusion(bf16[64,256]{1,0:T(8,128)(2,1)} %param.16, bf16[64,256]{1,0:T(8,128)(2,1)} %param.15, bf16[64,512]{1,0:T(8,128)(2,1)} %param.14), kind=kLoop, calls=%fused_computation.2 | loop fusion | flops 393216 | bytes 262144 | tf_op jit(solution)/shard_map/concatenate | solution.py:230
  12.0 1.7 %collective-permute-start.4 = (bf16[2,64,256]{2,1,0:T(8,128)(2,1)S(1)}, bf16[2,64,256]{2,1,0:T(8,128)(2,1)S(1)}, u32[]{:S(2)}, u32[]{:S(2)}) collective-permute-start(bf16[2,64,256]{2,1,0:T(8,128)(2,1)S(1)} %collective-permute-done.refs_2_), channel_id=1, source_target_pairs={{0,4},{4,0},{1,5},{5,1},{2,6},{6,2},{3,7},{7,3},{8,12},{12,8},{9,1... | collective-permute-start | bytes 196616 | tf_op jit(solution)/shard_map/ppermute | solution.py:179
  14.1 1.7 %collective-permute-start.6 = (bf16[2,64,256]{2,1,0:T(8,128)(2,1)S(1)}, bf16[2,64,256]{2,1,0:T(8,128)(2,1)S(1)}, u32[]{:S(2)}, u32[]{:S(2)}) collective-permute-start(bf16[2,64,256]{2,1,0:T(8,128)(2,1)S(1)} %collective-permute-done.2.refs_6_), channel_id=1, source_target_pairs={{0,4},{4,0},{1,5},{5,1},{2,6},{6,2},{3,7},{7,3},{8,12},{12,8},{9,1... | collective-permute-start | bytes 196616 | tf_op jit(solution)/shard_map/ppermute | solution.py:179
  15.8 3.1 %collective-permute-done.4.refs_3_ = bf16[2,64,256]{2,1,0:T(8,128)(2,1)S(1)} collective-permute-done((bf16[2,64,256]{2,1,0:T(8,128)(2,1)S(1)}, bf16[2,64,256]{2,1,0:T(8,128)(2,1)S(1)}, u32[]{:S(2)}, u32[]{:S(2)}) %collective-permute-start.4) | collective-permute-done | bytes 65568 | tf_op jit(solution)/shard_map/ppermute | solution.py:179
  18.9 0.7 %collective-permute-done.5.refs_5_ = bf16[2,64,256]{2,1,0:T(8,128)(2,1)S(1)} collective-permute-done((bf16[2,64,256]{2,1,0:T(8,128)(2,1)S(1)}, bf16[2,64,256]{2,1,0:T(8,128)(2,1)S(1)}, u32[]{:S(2)}, u32[]{:S(2)}) %collective-permute-start.5) | collective-permute-done | bytes 65568 | tf_op jit(solution)/shard_map/ppermute | solution.py:179
  19.6 0.7 %collective-permute-done.6.refs_7_ = bf16[2,64,256]{2,1,0:T(8,128)(2,1)S(1)} collective-permute-done((bf16[2,64,256]{2,1,0:T(8,128)(2,1)S(1)}, bf16[2,64,256]{2,1,0:T(8,128)(2,1)S(1)}, u32[]{:S(2)}, u32[]{:S(2)}) %collective-permute-start.6) | collective-permute-done | bytes 65568 | tf_op jit(solution)/shard_map/ppermute | solution.py:179
  20.3 1.0 %collective-permute-start.14 = (bf16[256,1024]{1,0:T(8,128)(2,1)S(1)}, bf16[256,1024]{1,0:T(8,128)(2,1)S(1)}, u32[]{:S(2)}, u32[]{:S(2)}) collective-permute-start(bf16[256,1024]{1,0:T(8,128)(2,1)S(1)} %copy-done), channel_id=1, source_target_pairs={{0,4},{4,0},{1,5},{5,1},{2,6},{6,2},{3,7},{7,3},{8,12},{12,8},{9,1... | collective-permute-start | bytes 1572872 | tf_op jit(solution)/shard_map/ppermute | solution.py:179
  21.3 1.3 %shard_map.157 = (bf16[64,512]{1,0:T(8,128)(2,1)}, bf16[64,640]{1,0:T(8,128)(2,1)S(1)}, bf16[64,640]{1,0:T(8,128)(2,1)S(1)}, bf16[64,640]{1,0:T(8,128)(2,1)S(1)}, bf16[64,640]{1,0:T(8,128)(2,1)S(1)}) custom-call(bf16[64,1024]{1,0:T(8,128)(2,1)S(1)} %pad_maximum_fusion.local_ref, bf16[64,2048]{1,0:T(8,128)(2,1)S(1)} %copy-done.1, ...), custom_call_target="tpu_custom_call" | custom-call | flops 67108864 | bytes 1048576 | tf_op jit(solution)/shard_map/pallas_call | solution.py:166
  22.6 2.3 %collective-permute-start.8 = (bf16[64,640]{1,0:T(8,128)(2,1)S(1)}, bf16[64,640]{1,0:T(8,128)(2,1)S(1)}, u32[]{:S(2)}, u32[]{:S(2)}) collective-permute-start(bf16[64,640]{1,0:T(8,128)(2,1)S(1)} %get-tuple-element.63), channel_id=1, source_target_pairs={{0,16},{8,24},{16,0},{24,8},{1,17},{9,25},{17,1},{25,9},{2,18},{10... | collective-permute-start | bytes 245768 | tf_op jit(solution)/shard_map/ppermute | solution.py:179
  24.8 1.5 %collective-permute-start.9 = (bf16[64,640]{1,0:T(8,128)(2,1)S(1)}, bf16[64,640]{1,0:T(8,128)(2,1)S(1)}, u32[]{:S(2)}, u32[]{:S(2)}) collective-permute-start(bf16[64,640]{1,0:T(8,128)(2,1)S(1)} %get-tuple-element.64), channel_id=1, source_target_pairs={{0,24},{8,16},{16,8},{24,0},{1,25},{9,17},{17,9},{25,1},{2,26},{10... | collective-permute-start | bytes 245768 | tf_op jit(solution)/shard_map/ppermute | solution.py:179
  26.6 3.1 %collective-permute-done.8.a2 = bf16[64,640]{1,0:T(8,128)(2,1)S(1)} collective-permute-done((bf16[64,640]{1,0:T(8,128)(2,1)S(1)}, bf16[64,640]{1,0:T(8,128)(2,1)S(1)}, u32[]{:S(2)}, u32[]{:S(2)}) %collective-permute-start.8) | collective-permute-done | bytes 81952 | tf_op jit(solution)/shard_map/ppermute | solution.py:179
  29.7 1.5 %collective-permute-done.9.a3 = bf16[64,640]{1,0:T(8,128)(2,1)S(1)} collective-permute-done((bf16[64,640]{1,0:T(8,128)(2,1)S(1)}, bf16[64,640]{1,0:T(8,128)(2,1)S(1)}, u32[]{:S(2)}, u32[]{:S(2)}) %collective-permute-start.9) | collective-permute-done | bytes 81952 | tf_op jit(solution)/shard_map/ppermute | solution.py:179
  32.1 1.6 %collective-permute-start.11 = (bf16[256,128]{1,0:T(8,128)(2,1)S(1)}, bf16[256,128]{1,0:T(8,128)(2,1)S(1)}, u32[]{:S(2)}, u32[]{:S(2)}) collective-permute-start(bf16[256,128]{1,0:T(8,128)(2,1)S(1)} %get-tuple-element.68), channel_id=1, source_target_pairs={{0,2},{1,3},{2,0},{3,1},{4,6},{5,7},{6,4},{7,5},{8,10},{9,11},{10,... | collective-permute-start | bytes 196616 | tf_op jit(solution)/shard_map/ppermute | solution.py:179
  34.3 2.1 %collective-permute-done.11.r2 = bf16[256,128]{1,0:T(8,128)(2,1)S(1)} collective-permute-done((bf16[256,128]{1,0:T(8,128)(2,1)S(1)}, bf16[256,128]{1,0:T(8,128)(2,1)S(1)}, u32[]{:S(2)}, u32[]{:S(2)}) %collective-permute-start.11) | collective-permute-done | bytes 65568 | tf_op jit(solution)/shard_map/ppermute | solution.py:179
  36.4 1.4 %collective-permute-done.12.r3 = bf16[256,128]{1,0:T(8,128)(2,1)S(1)} collective-permute-done((bf16[256,128]{1,0:T(8,128)(2,1)S(1)}, bf16[256,128]{1,0:T(8,128)(2,1)S(1)}, u32[]{:S(2)}, u32[]{:S(2)}) %collective-permute-start.12) | collective-permute-done | bytes 65568 | tf_op jit(solution)/shard_map/ppermute | solution.py:179
  37.9 0.9 %collective-permute-start.20 = (bf16[256,128]{1,0:T(8,128)(2,1)S(1)}, bf16[256,128]{1,0:T(8,128)(2,1)S(1)}, u32[]{:S(2)}, u32[]{:S(2)}) collective-permute-start(bf16[256,128]{1,0:T(8,128)(2,1)S(1)} %get-tuple-element.82.x0), channel_id=1, source_target_pairs={{0,3},{1,2},{2,1},{3,0},{4,7},{5,6},{6,5},{7,4},{8,11},{9,10},{10,... | collective-permute-start | bytes 196616 | tf_op jit(solution)/shard_map/ppermute | solution.py:179
  38.8 0.7 %collective-permute-start.19 = (bf16[256,128]{1,0:T(8,128)(2,1)S(1)}, bf16[256,128]{1,0:T(8,128)(2,1)S(1)}, u32[]{:S(2)}, u32[]{:S(2)}) collective-permute-start(bf16[256,128]{1,0:T(8,128)(2,1)S(1)} %get-tuple-element.82.x0), channel_id=1, source_target_pairs={{0,2},{1,3},{2,0},{3,1},{4,6},{5,7},{6,4},{7,5},{8,10},{9,11},{10,... | collective-permute-start | bytes 196616 | tf_op jit(solution)/shard_map/ppermute | solution.py:179
  40.2 2.7 %collective-permute-start.16 = (bf16[64,128]{1,0:T(8,128)(2,1)S(1)}, bf16[64,128]{1,0:T(8,128)(2,1)S(1)}, u32[]{:S(2)}, u32[]{:S(2)}) collective-permute-start(bf16[64,128]{1,0:T(8,128)(2,1)S(1)} %get-tuple-element.80), channel_id=1, source_target_pairs={{0,16},{8,24},{16,0},{24,8},{1,17},{9,25},{17,1},{25,9},{2,18},{10... | collective-permute-start | bytes 49160 | tf_op jit(solution)/shard_map/ppermute | solution.py:179
  42.9 1.9 %collective-permute-start.17 = (bf16[64,128]{1,0:T(8,128)(2,1)S(1)}, bf16[64,128]{1,0:T(8,128)(2,1)S(1)}, u32[]{:S(2)}, u32[]{:S(2)}) collective-permute-start(bf16[64,128]{1,0:T(8,128)(2,1)S(1)} %get-tuple-element.81), channel_id=1, source_target_pairs={{0,24},{8,16},{16,8},{24,0},{1,25},{9,17},{17,9},{25,1},{2,26},{10... | collective-permute-start | bytes 49160 | tf_op jit(solution)/shard_map/ppermute | solution.py:179
  45.3 3.1 %collective-permute-done.17.t3 = bf16[64,128]{1,0:T(8,128)(2,1)S(1)} collective-permute-done((bf16[64,128]{1,0:T(8,128)(2,1)S(1)}, bf16[64,128]{1,0:T(8,128)(2,1)S(1)}, u32[]{:S(2)}, u32[]{:S(2)}) %collective-permute-start.17) | collective-permute-done | bytes 16416 | tf_op jit(solution)/shard_map/ppermute | solution.py:179
  48.6 1.9 %collective-permute-start.25 = (bf16[64,1024]{1,0:T(8,128)(2,1)S(1)}, bf16[64,1024]{1,0:T(8,128)(2,1)S(1)}, u32[]{:S(2)}, u32[]{:S(2)}) collective-permute-start(bf16[64,1024]{1,0:T(8,128)(2,1)S(1)} %get-tuple-element.90), channel_id=1, source_target_pairs={{0,24},{8,16},{16,8},{24,0},{1,25},{9,17},{17,9},{25,1},{2,26},{10... | collective-permute-start | bytes 393224 | tf_op jit(solution)/shard_map/ppermute | solution.py:179
  50.5 1.5 %collective-permute-start.26 = (bf16[64,1024]{1,0:T(8,128)(2,1)S(1)}, bf16[64,1024]{1,0:T(8,128)(2,1)S(1)}, u32[]{:S(2)}, u32[]{:S(2)}) collective-permute-start(bf16[64,1024]{1,0:T(8,128)(2,1)S(1)} %get-tuple-element.91), channel_id=1, source_target_pairs={{0,8},{8,0},{16,24},{24,16},{1,9},{9,1},{17,25},{25,17},{2,10},{10... | collective-permute-start | bytes 393224 | tf_op jit(solution)/shard_map/ppermute | solution.py:179
  52.1 1.0 %collective-permute-start.22 = (bf16[64,512]{1,0:T(8,128)(2,1)S(1)}, bf16[64,512]{1,0:T(8,128)(2,1)S(1)}, u32[]{:S(2)}, u32[]{:S(2)}) collective-permute-start(bf16[64,512]{1,0:T(8,128)(2,1)S(1)} %shard_map.161.p0), channel_id=1, source_target_pairs={{0,2},{1,3},{2,0},{3,1},{4,6},{5,7},{6,4},{7,5},{8,10},{9,11},{10,... | collective-permute-start | bytes 196616 | tf_op jit(solution)/shard_map/ppermute | solution.py:179
  53.1 3.2 %collective-permute-done.22.p2 = bf16[64,512]{1,0:T(8,128)(2,1)S(1)} collective-permute-done((bf16[64,512]{1,0:T(8,128)(2,1)S(1)}, bf16[64,512]{1,0:T(8,128)(2,1)S(1)}, u32[]{:S(2)}, u32[]{:S(2)}) %collective-permute-start.22) | collective-permute-done | bytes 65568 | tf_op jit(solution)/shard_map/ppermute | solution.py:179
  56.3 4.0 %collective-permute-done.24.y2 = bf16[64,1024]{1,0:T(8,128)(2,1)S(1)} collective-permute-done((bf16[64,1024]{1,0:T(8,128)(2,1)S(1)}, bf16[64,1024]{1,0:T(8,128)(2,1)S(1)}, u32[]{:S(2)}, u32[]{:S(2)}) %collective-permute-start.24) | collective-permute-done | bytes 131104 | tf_op jit(solution)/shard_map/ppermute | solution.py:179
  60.3 1.5 %collective-permute-done.26.y1 = bf16[64,1024]{1,0:T(8,128)(2,1)S(1)} collective-permute-done((bf16[64,1024]{1,0:T(8,128)(2,1)S(1)}, bf16[64,1024]{1,0:T(8,128)(2,1)S(1)}, u32[]{:S(2)}, u32[]{:S(2)}) %collective-permute-start.26) | collective-permute-done | bytes 131104 | tf_op jit(solution)/shard_map/ppermute | solution.py:179
  61.8 0.9 %shard_map.162 = (bf16[64,1024]{1,0:T(8,128)(2,1)}, bf16[64,2048]{1,0:T(8,128)(2,1)}) custom-call(bf16[64,512]{1,0:T(8,128)(2,1)S(1)} %shard_map.161.p0, bf16[64,512]{1,0:T(8,128)(2,1)S(1)} %collective-permute-done.21.p1, bf16[64,512]{1,0:T(8,128)(2,1)S(1)} %collective-permute-done.22.p2, bf16[64,512]{1,0:T(8,128)(2,1)S(1)} %collective-permute-done.23.p3, ...), custom_call_target="tpu_custom_call" | custom-call | bytes 1048576 | tf_op jit(solution)/shard_map/pallas_call | solution.py:166
  (49 shorter events, 4.9 us)
Async XLA Ops:
  0.6 7.8 %copy-start.5 = (s32[1,64]{1,0:T(1,128)S(1)}, s32[1,64]{1,0:T(1,128)}, u32[]{:S(2)}) copy-start(s32[1,64]{1,0:T(1,128)} %param.23) | copy-start | bytes 772
  0.6 19.6 %copy-start = (bf16[256,1024]{1,0:T(8,128)(2,1)S(1)}, bf16[256,1024]{1,0:T(8,128)(2,1)}, u32[]{:S(2)}) copy-start(bf16[256,1024]{1,0:T(8,128)(2,1)} %own_ref.3) | copy-start | bytes 1572868
  0.7 11.4 %collective-permute-start.2 = (bf16[2,64,256]{2,1,0:T(8,128)(2,1)}, bf16[2,64,256]{2,1,0:T(8,128)(2,1)S(1)}, u32[]{:S(2)}, u32[]{:S(2)}) collective-permute-start(bf16[2,64,256]{2,1,0:T(8,128)(2,1)} %refs_0_), channel_id=1, source_target_pairs={{0,24},{8,16},{16,8},{24,0},{1,25},{9,17},{17,9},{25,1},{2,26},{10... | collective-permute-start | bytes 196616 | tf_op jit(solution)/shard_map/ppermute | solution.py:179
  5.8 6.3 %collective-permute-start.1 = (bf16[2,64,256]{2,1,0:T(8,128)(2,1)}, bf16[2,64,256]{2,1,0:T(8,128)(2,1)S(1)}, u32[]{:S(2)}, u32[]{:S(2)}) collective-permute-start(bf16[2,64,256]{2,1,0:T(8,128)(2,1)} %refs_0_), channel_id=1, source_target_pairs={{0,16},{8,24},{16,0},{24,8},{1,17},{9,25},{17,1},{25,9},{2,18},{10... | collective-permute-start | bytes 196616 | tf_op jit(solution)/shard_map/ppermute | solution.py:179
  5.8 6.3 %collective-permute-start = (bf16[2,64,256]{2,1,0:T(8,128)(2,1)}, bf16[2,64,256]{2,1,0:T(8,128)(2,1)S(1)}, u32[]{:S(2)}, u32[]{:S(2)}) collective-permute-start(bf16[2,64,256]{2,1,0:T(8,128)(2,1)} %refs_0_), channel_id=1, source_target_pairs={{0,8},{8,0},{16,24},{24,16},{1,9},{9,1},{17,25},{25,17},{2,10},{10... | collective-permute-start | bytes 196616 | tf_op jit(solution)/shard_map/ppermute | solution.py:179
  6.4 9.4 %collective-permute-start.3 = (bf16[2,64,256]{2,1,0:T(8,128)(2,1)}, bf16[2,64,256]{2,1,0:T(8,128)(2,1)S(1)}, u32[]{:S(2)}, u32[]{:S(2)}) collective-permute-start(bf16[2,64,256]{2,1,0:T(8,128)(2,1)} %refs_0_), channel_id=1, source_target_pairs={{0,4},{4,0},{1,5},{5,1},{2,6},{6,2},{3,7},{7,3},{8,12},{12,8},{9,1... | collective-permute-start | bytes 196616 | tf_op jit(solution)/shard_map/ppermute | solution.py:179
  8.1 12.2 %collective-permute-start.7 = (bf16[256,512]{1,0:T(8,128)(2,1)}, bf16[256,512]{1,0:T(8,128)(2,1)S(1)}, u32[]{:S(2)}, u32[]{:S(2)}) collective-permute-start(bf16[256,512]{1,0:T(8,128)(2,1)} %own_ref.2), channel_id=1, source_target_pairs={{0,4},{4,0},{1,5},{5,1},{2,6},{6,2},{3,7},{7,3},{8,12},{12,8},{9,1... | collective-permute-start | bytes 786440 | tf_op jit(solution)/shard_map/ppermute | solution.py:179
  10.9 10.4 %copy-start.1 = (bf16[64,2048]{1,0:T(8,128)(2,1)S(1)}, bf16[64,2048]{1,0:T(8,128)(2,1)}, u32[]{:S(2)}) copy-start(bf16[64,2048]{1,0:T(8,128)(2,1)} %res_ref.1) | copy-start | bytes 786436
  11.1 10.2 %copy-start.3 = (bf16[2,64,256]{2,1,0:T(8,128)(2,1)S(1)}, bf16[2,64,256]{2,1,0:T(8,128)(2,1)}, u32[]{:S(2)}) copy-start(bf16[2,64,256]{2,1,0:T(8,128)(2,1)} %refs_0_) | copy-start | bytes 196612
  12.0 19.6 %copy-start.2 = (bf16[256,512]{1,0:T(8,128)(2,1)S(1)}, bf16[256,512]{1,0:T(8,128)(2,1)}, u32[]{:S(2)}) copy-start(bf16[256,512]{1,0:T(8,128)(2,1)} %own_ref.2) | copy-start | bytes 786436
  12.0 6.8 %collective-permute-start.4 = (bf16[2,64,256]{2,1,0:T(8,128)(2,1)S(1)}, bf16[2,64,256]{2,1,0:T(8,128)(2,1)S(1)}, u32[]{:S(2)}, u32[]{:S(2)}) collective-permute-start(bf16[2,64,256]{2,1,0:T(8,128)(2,1)S(1)} %collective-permute-done.refs_2_), channel_id=1, source_target_pairs={{0,4},{4,0},{1,5},{5,1},{2,6},{6,2},{3,7},{7,3},{8,12},{12,8},{9,1... | collective-permute-start | bytes 196616 | tf_op jit(solution)/shard_map/ppermute | solution.py:179
  13.8 5.8 %collective-permute-start.5 = (bf16[2,64,256]{2,1,0:T(8,128)(2,1)S(1)}, bf16[2,64,256]{2,1,0:T(8,128)(2,1)S(1)}, u32[]{:S(2)}, u32[]{:S(2)}) collective-permute-start(bf16[2,64,256]{2,1,0:T(8,128)(2,1)S(1)} %collective-permute-done.1.refs_4_), channel_id=1, source_target_pairs={{0,4},{4,0},{1,5},{5,1},{2,6},{6,2},{3,7},{7,3},{8,12},{12,8},{9,1... | collective-permute-start | bytes 196616 | tf_op jit(solution)/shard_map/ppermute | solution.py:179
  14.1 6.1 %collective-permute-start.6 = (bf16[2,64,256]{2,1,0:T(8,128)(2,1)S(1)}, bf16[2,64,256]{2,1,0:T(8,128)(2,1)S(1)}, u32[]{:S(2)}, u32[]{:S(2)}) collective-permute-start(bf16[2,64,256]{2,1,0:T(8,128)(2,1)S(1)} %collective-permute-done.2.refs_6_), channel_id=1, source_target_pairs={{0,4},{4,0},{1,5},{5,1},{2,6},{6,2},{3,7},{7,3},{8,12},{12,8},{9,1... | collective-permute-start | bytes 196616 | tf_op jit(solution)/shard_map/ppermute | solution.py:179
  20.3 17.6 %collective-permute-start.14 = (bf16[256,1024]{1,0:T(8,128)(2,1)S(1)}, bf16[256,1024]{1,0:T(8,128)(2,1)S(1)}, u32[]{:S(2)}, u32[]{:S(2)}) collective-permute-start(bf16[256,1024]{1,0:T(8,128)(2,1)S(1)} %copy-done), channel_id=1, source_target_pairs={{0,4},{4,0},{1,5},{5,1},{2,6},{6,2},{3,7},{7,3},{8,12},{12,8},{9,1... | collective-permute-start | bytes 1572872 | tf_op jit(solution)/shard_map/ppermute | solution.py:179
  22.6 7.2 %collective-permute-start.8 = (bf16[64,640]{1,0:T(8,128)(2,1)S(1)}, bf16[64,640]{1,0:T(8,128)(2,1)S(1)}, u32[]{:S(2)}, u32[]{:S(2)}) collective-permute-start(bf16[64,640]{1,0:T(8,128)(2,1)S(1)} %get-tuple-element.63), channel_id=1, source_target_pairs={{0,16},{8,24},{16,0},{24,8},{1,17},{9,25},{17,1},{25,9},{2,18},{10... | collective-permute-start | bytes 245768 | tf_op jit(solution)/shard_map/ppermute | solution.py:179
  24.8 6.4 %collective-permute-start.9 = (bf16[64,640]{1,0:T(8,128)(2,1)S(1)}, bf16[64,640]{1,0:T(8,128)(2,1)S(1)}, u32[]{:S(2)}, u32[]{:S(2)}) collective-permute-start(bf16[64,640]{1,0:T(8,128)(2,1)S(1)} %get-tuple-element.64), channel_id=1, source_target_pairs={{0,24},{8,16},{16,8},{24,0},{1,25},{9,17},{17,9},{25,1},{2,26},{10... | collective-permute-start | bytes 245768 | tf_op jit(solution)/shard_map/ppermute | solution.py:179
  26.3 5.3 %collective-permute-start.10 = (bf16[64,640]{1,0:T(8,128)(2,1)S(1)}, bf16[64,640]{1,0:T(8,128)(2,1)S(1)}, u32[]{:S(2)}, u32[]{:S(2)}) collective-permute-start(bf16[64,640]{1,0:T(8,128)(2,1)S(1)} %get-tuple-element.65), channel_id=1, source_target_pairs={{0,8},{8,0},{16,24},{24,16},{1,9},{9,1},{17,25},{25,17},{2,10},{10... | collective-permute-start | bytes 245768 | tf_op jit(solution)/shard_map/ppermute | solution.py:179
  32.1 4.3 %collective-permute-start.11 = (bf16[256,128]{1,0:T(8,128)(2,1)S(1)}, bf16[256,128]{1,0:T(8,128)(2,1)S(1)}, u32[]{:S(2)}, u32[]{:S(2)}) collective-permute-start(bf16[256,128]{1,0:T(8,128)(2,1)S(1)} %get-tuple-element.68), channel_id=1, source_target_pairs={{0,2},{1,3},{2,0},{3,1},{4,6},{5,7},{6,4},{7,5},{8,10},{9,11},{10,... | collective-permute-start | bytes 196616 | tf_op jit(solution)/shard_map/ppermute | solution.py:179
  33.6 4.2 %collective-permute-start.12 = (bf16[256,128]{1,0:T(8,128)(2,1)S(1)}, bf16[256,128]{1,0:T(8,128)(2,1)S(1)}, u32[]{:S(2)}, u32[]{:S(2)}) collective-permute-start(bf16[256,128]{1,0:T(8,128)(2,1)S(1)} %get-tuple-element.69), channel_id=1, source_target_pairs={{0,3},{1,2},{2,1},{3,0},{4,7},{5,6},{6,5},{7,4},{8,11},{9,10},{10,... | collective-permute-start | bytes 196616 | tf_op jit(solution)/shard_map/ppermute | solution.py:179
  33.6 4.2 %collective-permute-start.13 = (bf16[256,128]{1,0:T(8,128)(2,1)S(1)}, bf16[256,128]{1,0:T(8,128)(2,1)S(1)}, u32[]{:S(2)}, u32[]{:S(2)}) collective-permute-start(bf16[256,128]{1,0:T(8,128)(2,1)S(1)} %get-tuple-element.70), channel_id=1, source_target_pairs={{0,1},{1,0},{2,3},{3,2},{4,5},{5,4},{6,7},{7,6},{8,9},{9,8},{10,11... | collective-permute-start | bytes 196616 | tf_op jit(solution)/shard_map/ppermute | solution.py:179
  37.9 5.0 %collective-permute-start.20 = (bf16[256,128]{1,0:T(8,128)(2,1)S(1)}, bf16[256,128]{1,0:T(8,128)(2,1)S(1)}, u32[]{:S(2)}, u32[]{:S(2)}) collective-permute-start(bf16[256,128]{1,0:T(8,128)(2,1)S(1)} %get-tuple-element.82.x0), channel_id=1, source_target_pairs={{0,3},{1,2},{2,1},{3,0},{4,7},{5,6},{6,5},{7,4},{8,11},{9,10},{10,... | collective-permute-start | bytes 196616 | tf_op jit(solution)/shard_map/ppermute | solution.py:179
  38.8 6.0 %collective-permute-start.19 = (bf16[256,128]{1,0:T(8,128)(2,1)S(1)}, bf16[256,128]{1,0:T(8,128)(2,1)S(1)}, u32[]{:S(2)}, u32[]{:S(2)}) collective-permute-start(bf16[256,128]{1,0:T(8,128)(2,1)S(1)} %get-tuple-element.82.x0), channel_id=1, source_target_pairs={{0,2},{1,3},{2,0},{3,1},{4,6},{5,7},{6,4},{7,5},{8,10},{9,11},{10,... | collective-permute-start | bytes 196616 | tf_op jit(solution)/shard_map/ppermute | solution.py:179
  39.5 5.3 %collective-permute-start.18 = (bf16[256,128]{1,0:T(8,128)(2,1)S(1)}, bf16[256,128]{1,0:T(8,128)(2,1)S(1)}, u32[]{:S(2)}, u32[]{:S(2)}) collective-permute-start(bf16[256,128]{1,0:T(8,128)(2,1)S(1)} %get-tuple-element.82.x0), channel_id=1, source_target_pairs={{0,1},{1,0},{2,3},{3,2},{4,5},{5,4},{6,7},{7,6},{8,9},{9,8},{10,11... | collective-permute-start | bytes 196616 | tf_op jit(solution)/shard_map/ppermute | solution.py:179
  39.8 5.5 %collective-permute-start.15 = (bf16[64,128]{1,0:T(8,128)(2,1)S(1)}, bf16[64,128]{1,0:T(8,128)(2,1)S(1)}, u32[]{:S(2)}, u32[]{:S(2)}) collective-permute-start(bf16[64,128]{1,0:T(8,128)(2,1)S(1)} %get-tuple-element.79), channel_id=1, source_target_pairs={{0,8},{8,0},{16,24},{24,16},{1,9},{9,1},{17,25},{25,17},{2,10},{10... | collective-permute-start | bytes 49160 | tf_op jit(solution)/shard_map/ppermute | solution.py:179
  40.2 5.1 %collective-permute-start.16 = (bf16[64,128]{1,0:T(8,128)(2,1)S(1)}, bf16[64,128]{1,0:T(8,128)(2,1)S(1)}, u32[]{:S(2)}, u32[]{:S(2)}) collective-permute-start(bf16[64,128]{1,0:T(8,128)(2,1)S(1)} %get-tuple-element.80), channel_id=1, source_target_pairs={{0,16},{8,24},{16,0},{24,8},{1,17},{9,25},{17,1},{25,9},{2,18},{10... | collective-permute-start | bytes 49160 | tf_op jit(solution)/shard_map/ppermute | solution.py:179
  42.9 5.5 %collective-permute-start.17 = (bf16[64,128]{1,0:T(8,128)(2,1)S(1)}, bf16[64,128]{1,0:T(8,128)(2,1)S(1)}, u32[]{:S(2)}, u32[]{:S(2)}) collective-permute-start(bf16[64,128]{1,0:T(8,128)(2,1)S(1)} %get-tuple-element.81), channel_id=1, source_target_pairs={{0,24},{8,16},{16,8},{24,0},{1,25},{9,17},{17,9},{25,1},{2,26},{10... | collective-permute-start | bytes 49160 | tf_op jit(solution)/shard_map/ppermute | solution.py:179
  48.4 4.7 %collective-permute-start.23 = (bf16[64,512]{1,0:T(8,128)(2,1)S(1)}, bf16[64,512]{1,0:T(8,128)(2,1)S(1)}, u32[]{:S(2)}, u32[]{:S(2)}) collective-permute-start(bf16[64,512]{1,0:T(8,128)(2,1)S(1)} %shard_map.161.p0), channel_id=1, source_target_pairs={{0,3},{1,2},{2,1},{3,0},{4,7},{5,6},{6,5},{7,4},{8,11},{9,10},{10,... | collective-permute-start | bytes 196616 | tf_op jit(solution)/shard_map/ppermute | solution.py:179
  48.5 11.8 %collective-permute-start.24 = (bf16[64,1024]{1,0:T(8,128)(2,1)S(1)}, bf16[64,1024]{1,0:T(8,128)(2,1)S(1)}, u32[]{:S(2)}, u32[]{:S(2)}) collective-permute-start(bf16[64,1024]{1,0:T(8,128)(2,1)S(1)} %get-tuple-element.89), channel_id=1, source_target_pairs={{0,16},{8,24},{16,0},{24,8},{1,17},{9,25},{17,1},{25,9},{2,18},{10... | collective-permute-start | bytes 393224 | tf_op jit(solution)/shard_map/ppermute | solution.py:179
  48.6 11.7 %collective-permute-start.25 = (bf16[64,1024]{1,0:T(8,128)(2,1)S(1)}, bf16[64,1024]{1,0:T(8,128)(2,1)S(1)}, u32[]{:S(2)}, u32[]{:S(2)}) collective-permute-start(bf16[64,1024]{1,0:T(8,128)(2,1)S(1)} %get-tuple-element.90), channel_id=1, source_target_pairs={{0,24},{8,16},{16,8},{24,0},{1,25},{9,17},{17,9},{25,1},{2,26},{10... | collective-permute-start | bytes 393224 | tf_op jit(solution)/shard_map/ppermute | solution.py:179
  50.5 11.3 %collective-permute-start.26 = (bf16[64,1024]{1,0:T(8,128)(2,1)S(1)}, bf16[64,1024]{1,0:T(8,128)(2,1)S(1)}, u32[]{:S(2)}, u32[]{:S(2)}) collective-permute-start(bf16[64,1024]{1,0:T(8,128)(2,1)S(1)} %get-tuple-element.91), channel_id=1, source_target_pairs={{0,8},{8,0},{16,24},{24,16},{1,9},{9,1},{17,25},{25,17},{2,10},{10... | collective-permute-start | bytes 393224 | tf_op jit(solution)/shard_map/ppermute | solution.py:179
  52.1 4.3 %collective-permute-start.22 = (bf16[64,512]{1,0:T(8,128)(2,1)S(1)}, bf16[64,512]{1,0:T(8,128)(2,1)S(1)}, u32[]{:S(2)}, u32[]{:S(2)}) collective-permute-start(bf16[64,512]{1,0:T(8,128)(2,1)S(1)} %shard_map.161.p0), channel_id=1, source_target_pairs={{0,2},{1,3},{2,0},{3,1},{4,6},{5,7},{6,4},{7,5},{8,10},{9,11},{10,... | collective-permute-start | bytes 196616 | tf_op jit(solution)/shard_map/ppermute | solution.py:179
  53.1 3.2 %collective-permute-start.21 = (bf16[64,512]{1,0:T(8,128)(2,1)S(1)}, bf16[64,512]{1,0:T(8,128)(2,1)S(1)}, u32[]{:S(2)}, u32[]{:S(2)}) collective-permute-start(bf16[64,512]{1,0:T(8,128)(2,1)S(1)} %shard_map.161.p0), channel_id=1, source_target_pairs={{0,1},{1,0},{2,3},{3,2},{4,5},{5,4},{6,7},{7,6},{8,9},{9,8},{10,11... | collective-permute-start | bytes 196616 | tf_op jit(solution)/shard_map/ppermute | solution.py:179
  (1 other events, 6.9 us)

commit v9 on v6

--- a/solution.py
+++ b/solution.py
@@ -98,7 +98,7 @@
         ref[:, wide:] = res_ref[:, pl.ds(chunk_offset(e ^ (2 * s), m, width), width)]
 
 
-def project_kernel(a0, a1, a2, a3, own_ref, par_ref, o0, o1, o2, o3, hold):
+def project_kernel(a2, a3, a1, a0, own_ref, par_ref, o0, o1, o2, o3, hold):
     m = mp_index()
     half, wide = own_ref.shape
     blocks = (a0, a1, a2, a3)
@@ -112,52 +112,48 @@
         out[...] = chunk + rest.astype(F32) if j == 0 else chunk.astype(BF16)
 
 
-def combine_kernel(r0, r1, r2, r3, out, t0, t1, t2, t3):
-    tok = t0.shape[0]
-    stream = (
+def combine_kernel(r2, r3, r1, r0, out):
+    out[...] = (
         r0[...] + r1[...].astype(F32) + r2[...].astype(F32) + r3[...].astype(F32)
     ).astype(BF16)
-    out[...] = stream
-    for s, part in enumerate((t0, t1, t2, t3)):
-        part[...] = stream[s * tok : (s + 1) * tok]
-
-
-def qkv_kernel(x0, x1, x2, x3, gain_ref, own_ref, par_ref, o0, o1, o2, o3, hold):
+
+
+def qkv_kernel(x0, x1, x2, x3, gain_ref, own_ref, par_ref, o0, o1, o2, o3, hold, whole):
     e, m = seq_index(), mp_index()
     width = x0.shape[1]
-    half = 2 * width
+    half, columns = own_ref.shape
     tok = o0.shape[0]
     for j, part in enumerate((x0, x1, x2, x3)):
         k = m ^ j
         gain = gain_ref[:, pl.ds(chunk_offset(e, k, width), width)]
-        hold[:, pl.ds(pl.multiple_of(k * width, width), width)] = (
-            part[...].astype(F32) * gain
-        ).astype(BF16)
+        at = pl.ds(pl.multiple_of(k * width, width), width)
+        whole[:, at] = part[...]
+        hold[:, at] = (part[...].astype(F32) * gain).astype(BF16)
     product = jnp.dot(hold[:, :half], own_ref[...], preferred_element_type=F32) + jnp.dot(
         hold[:, half:], par_ref[...], preferred_element_type=F32
     )
     for s, out in enumerate((o0, o1, o2, o3)):
-        out[...] = product[s * tok : (s + 1) * tok].astype(out.dtype)
-
-
-def pack_kernel(t0, t1, t2, t3, out_ref):
-    width = t0.shape[1]
-    for s, part in enumerate((t0, t1, t2, t3)):
-        out_ref[:, s * width : (s + 1) * width] = part[...]
-
-
-def finish_kernel(y0, y1, y2, y3, p0, p1, p2, p3, qkv_ref, stream_ref):
-    e, m = seq_index(), mp_index()
-    width = p0.shape[1] // 4
-    squares = jnp.zeros((p0.shape[0], width), F32)
-    for j, part in enumerate((p0, p1, p2, p3)):
-        for s in range(4):
-            block = part[:, s * width : (s + 1) * width]
+        rows = slice(s * tok, (s + 1) * tok)
+        out[:, :columns] = product[rows].astype(BF16)
+        out[:, columns:] = whole[rows]
+
+
+def finish_kernel(y2, y3, y1, y0, qkv_ref, stream_ref):
+    e = seq_index()
+    tok, columns = qkv_ref.shape
+    half = (y0.shape[1] - columns) // 2
+    squares = jnp.zeros((tok, half), F32)
+    for s, ref in enumerate((y0, y1, y2, y3)):
+        for side in range(2):
+            block = ref[:, columns + side * half : columns + (side + 1) * half]
             wide = block.astype(F32)
             squares = squares + wide * wide
-            stream_ref[:, pl.ds(chunk_offset(e ^ (2 * s), m ^ j, width), width)] = block
+            at = pl.multiple_of((e ^ (2 * s) ^ side) * half, half)
+            stream_ref[:, pl.ds(at, half)] = block
     mean_square = jnp.sum(squares, axis=1, keepdims=True) / stream_ref.shape[1]
-    total = y0[...] + y1[...].astype(F32) + y2[...].astype(F32) + y3[...].astype(F32)
+    total = (y0[:, :columns].astype(F32) + y1[:, :columns].astype(F32)) + (
+        y2[:, :columns].astype(F32) + y3[:, :columns].astype(F32)
+    )
     qkv_ref[...] = (total * lax.rsqrt(mean_square + 1e-06)).astype(BF16)
 
 
@@ -203,7 +199,6 @@
 
     along = [cache] + [swap(cache, "z", s) for s in range(1, 4)]
     beside = swap(cache, "y", 1)
-
     holders = pool_root.shape[0]
     requests, token_branch = token_branches(request_branch, token_request)
     branch_ids = jnp.arange(branch_root.shape[0], dtype=jnp.int32)
@@ -212,6 +207,13 @@
         jnp.sum(jnp.where(chosen, per_branch[None, :], 0), axis=1)
         for per_branch in (branch_root, branch_owner, branch_len)
     )
+    small = (requests, token_root, token_owner, token_length, pool_root)
+    along[1:], small, mine = lax.optimization_barrier(
+        (along[1:], small, (fresh_queries, fresh_keys, fresh_values))
+    )
+    requests, token_root, token_owner, token_length, pool_root = small
+    across = [beside] + [swap(rows, "y", 1) for rows in along[1:]]
+    blocks = [block for pair in zip(along, across) for block in pair]
     positions = jnp.arange(tok, dtype=jnp.int32)
     own_seen = (requests[None, :] == requests[:, None]) & (
         positions[:, None] <= positions[None, :]
@@ -227,10 +229,7 @@
     seen = jnp.concatenate([own_seen, pool_seen], axis=0)
     bias = jnp.where(jnp.concatenate([seen, seen], axis=1), 0.0, HIDDEN).astype(F32)
 
-    local = jnp.concatenate([fresh_queries, fresh_keys, fresh_values], axis=1)
-    along[1:], bias, local = lax.optimization_barrier((along[1:], bias, local))
-    across = [beside] + [swap(mine, "y", 1) for mine in along[1:]]
-    blocks = [block for pair in zip(along, across) for block in pair]
+    local = jnp.concatenate(mine, axis=1)
     blocks, wo_later = lax.optimization_barrier((blocks, wo_t))
     wo_pair = swap(wo_later, "y", 1)
     attn, *sends = call(
@@ -243,7 +242,7 @@
     sums = call(
         project_kernel,
         [sds((4 * tok, width), F32)] + [sds((4 * tok, width), BF16)] * 3,
-        (sends[0], a1, a2, a3, wo_t, wo_pair),
+        (a2, a3, a1, sends[0], wo_t, wo_pair),
         scratch=[pltpu.VMEM((4 * tok, 4 * width), F32)],
         flops=1 << 27,
     )
@@ -252,26 +251,25 @@
     sums = [own_sum] + [swap(sums[j], mp, j) for j in range(1, 4)]
     made = call(
         combine_kernel,
-        [sds((4 * tok, width), BF16)] + [sds((tok, width), BF16)] * 4,
-        tuple(sums),
-    )
-    slices = [made[0]] + [swap(made[0], mp, j) for j in range(1, 4)]
-    home = [made[1]] + [swap(made[1 + s], "z", s) for s in range(1, 4)]
+        sds((4 * tok, width), BF16),
+        (sums[2], sums[3], sums[1], sums[0]),
+    )
+    slices = [made] + [swap(made, mp, j) for j in range(1, 4)]
     partial = call(
         qkv_kernel,
-        [sds((tok, columns), F32)] + [sds((tok, columns), BF16)] * 3,
+        [sds((tok, columns + 4 * width), BF16)] * 4,
         (*slices, norm_gain[None, :], w_qkv, wq_pair),
-        scratch=[pltpu.VMEM((4 * tok, 4 * width), BF16)],
+        scratch=[
+            pltpu.VMEM((4 * tok, 4 * width), BF16),
+            pltpu.VMEM((4 * tok, 4 * width), BF16),
+        ],
         flops=1 << 28,
     )
-    y1, y2, y3 = (swap(partial[s], "z", s) for s in (1, 2, 3))
-    home, own_partial = lax.optimization_barrier((home, partial[0]))
-    packed = call(pack_kernel, sds((tok, 4 * width), BF16), tuple(home))
-    pieces = [packed] + [swap(packed, mp, j) for j in range(1, 4)]
+    y2, y3, y1 = (swap(partial[s], "z", s) for s in (2, 3, 1))
     qkv_next, stream = call(
         finish_kernel,
         [sds((tok, columns), BF16), sds(residual.shape, BF16)],
-        (own_partial, y1, y2, y3, *pieces),
+        (y2, y3, y1, partial[0]),
     )
     return attn, stream, qkv_next
 

time: 63.9 us -> 63.8 us (level)
  starting transfers between devices: 29.6 us -> 23.9 us
  waiting for transfers between devices: 26.5 us -> 30.3 us
  other arithmetic: 0.56 us -> 4.13 us
  local copies, waits for them, and re-layouts: 2.55 us -> 0.7 us
    ppermute x27 -> x21, starting transfers between devices: 29.6 us -> 23.9 us  [swap(): return lax.ppermute(value, axes, [(i, i ^ bits) for i in range(count)])]
    ppermute x27 -> x21, waiting for transfers between devices: 26.5 us -> 30.3 us  [swap(): return lax.ppermute(value, axes, [(i, i ^ bits) for i in range(count)])]
    unnamed x28 -> x12, local copies, waits for them, and re-layouts: 2.55 us -> 0.7 us
    concatenate x1, other arithmetic: 0.01 us -> 0.79 us  [on_block(): local = jnp.concatenate(mine, axis=1)]
    and x1, other arithmetic: 0.08 us -> 0.81 us  [on_block(): (requests[None, :] == requests[:, None]) & (positions[:, None] <= positio...]
    eq x1, other arithmetic: 0.1 us -> 0.79 us  [on_block(): root_seen = pool_root[:, :, None] == token_root[None, None, :]]
    reduce_sum x1, other arithmetic: 0.09 us -> 0.77 us  [on_block(): jnp.sum(jnp.where(chosen, per_branch[None, :], 0), axis=1)]
    reduce_sum x1, other arithmetic: 0.08 us -> 0.75 us  [token_branches(): jnp.sum(jnp.where(requests[:, None] == request_ids[None, :], local_branch...]
  transfers between devices with their start and end apart: 27 -> 21, of which waited for: 15 -> 12; matrix products, arithmetic and copies ran while one was open for 1% -> 7% of each run, Pallas kernels for 3% -> 2%
where the time goes in v9:
time: 63.8 us; the launch traced here: 63 us
  waiting for transfers between devices  30.3 us (47%)
  starting transfers between devices  23.9 us (37%)
  other arithmetic  4.13 us (6%)
  Pallas kernels  3.09 us (5%)
  between operations  0.79 us (1%)
  local copies, waits for them, and re-layouts  0.7 us (1%)
    ppermute x21, waiting for transfers between devices, swap(): return lax.ppermute(value, axes, [(i, i ^ bits) for i in range(count)])  30.3 us
    ppermute x21, starting transfers between devices, swap(): return lax.ppermute(value, axes, [(i, i ^ bits) for i in range(count)])  23.9 us
    pallas_call x5, Pallas kernels, call(): pl.pallas_call(kernel, out_shape=out_shape, in_specs=[vmem] * len(args),...  3.09 us
  transfers between devices with their start and end apart: 21, of which 12 were waited for; matrix products, arithmetic and copies ran while one was open for 7% of the time, Pallas kernels for 2%

profile of v9, /device:TPU:0, one launch (start us, length us, event | category | flops | bytes accessed | tf_op | source)
XLA Modules:
  0.0 63.0 jit_solution(9911379933944350914)
XLA Ops:
  0.7 5.1 %collective-permute-start.2 = (bf16[2,64,256]{2,1,0:T(8,128)(2,1)}, bf16[2,64,256]{2,1,0:T(8,128)(2,1)S(1)}, u32[]{:S(2)}, u32[]{:S(2)}) collective-permute-start(bf16[2,64,256]{2,1,0:T(8,128)(2,1)} %refs_0_), channel_id=1, source_target_pairs={{0,24},{8,16},{16,8},{24,0},{1,25},{9,17},{17,9},{25,1},{2,26},{10... | collective-permute-start | bytes 196616 | tf_op jit(solution)/shard_map/ppermute | solution.py:175
  6.4 1.7 %collective-permute-start.3 = (bf16[2,64,256]{2,1,0:T(8,128)(2,1)}, bf16[2,64,256]{2,1,0:T(8,128)(2,1)S(1)}, u32[]{:S(2)}, u32[]{:S(2)}) collective-permute-start(bf16[2,64,256]{2,1,0:T(8,128)(2,1)} %refs_0_), channel_id=1, source_target_pairs={{0,4},{4,0},{1,5},{5,1},{2,6},{6,2},{3,7},{7,3},{8,12},{12,8},{9,1... | collective-permute-start | bytes 196616 | tf_op jit(solution)/shard_map/ppermute | solution.py:175
  8.1 0.8 %select_reduce_fusion.3 = s32[64]{0:T(128)S(1)} fusion(s32[4]{0:T(128)} %bitcast.8, s32[64]{0:T(128)} %bitcast.6), kind=kLoop, calls=%fused_computation.13 | loop fusion | flops 704 | bytes 528 | tf_op jit(solution)/shard_map/reduce_sum | solution.py:39
  8.8 0.8 %select_reduce_fusion = (s32[64]{0:T(128)S(1)}, s32[64]{0:T(128)S(1)}, s32[64]{0:T(128)S(1)}) fusion(s32[8]{0:T(128)} %param.20, s32[64]{0:T(128)S(1)} %select_reduce_fusion.3, s32[8]{0:T(128)} %param.19, s32[8]{0:T(128)} %param.21), kind=kLoop, calls=%fused_computation.9 | loop fusion | flops 3392 | bytes 1120 | tf_op jit(solution)/shard_map/reduce_sum | solution.py:207
  9.6 2.0 %collective-permute-done.1.refs_4_ = bf16[2,64,256]{2,1,0:T(8,128)(2,1)S(1)} collective-permute-done((bf16[2,64,256]{2,1,0:T(8,128)(2,1)}, bf16[2,64,256]{2,1,0:T(8,128)(2,1)S(1)}, u32[]{:S(2)}, u32[]{:S(2)}) %collective-permute-start.1) | collective-permute-done | bytes 65568 | tf_op jit(solution)/shard_map/ppermute | solution.py:175
  11.6 0.8 %fusion = pred[64,64]{1,0:T(8,128)(4,1)S(1)} fusion(s32[64]{0:T(128)} %bitcast.7), kind=kLoop, calls=%fused_computation.6 | loop fusion | flops 12288 | bytes 4352 | tf_op jit(solution)/shard_map/and | solution.py:218
  12.4 1.6 %collective-permute-start.4 = (bf16[2,64,256]{2,1,0:T(8,128)(2,1)S(1)}, bf16[2,64,256]{2,1,0:T(8,128)(2,1)S(1)}, u32[]{:S(2)}, u32[]{:S(2)}) collective-permute-start(bf16[2,64,256]{2,1,0:T(8,128)(2,1)S(1)} %collective-permute-done.refs_2_), channel_id=1, source_target_pairs={{0,4},{4,0},{1,5},{5,1},{2,6},{6,2},{3,7},{7,3},{8,12},{12,8},{9,1... | collective-permute-start | bytes 196616 | tf_op jit(solution)/shard_map/ppermute | solution.py:175
  14.5 1.5 %collective-permute-start.6 = (bf16[2,64,256]{2,1,0:T(8,128)(2,1)S(1)}, bf16[2,64,256]{2,1,0:T(8,128)(2,1)S(1)}, u32[]{:S(2)}, u32[]{:S(2)}) collective-permute-start(bf16[2,64,256]{2,1,0:T(8,128)(2,1)S(1)} %collective-permute-done.2.refs_6_), channel_id=1, source_target_pairs={{0,4},{4,0},{1,5},{5,1},{2,6},{6,2},{3,7},{7,3},{8,12},{12,8},{9,1... | collective-permute-start | bytes 196616 | tf_op jit(solution)/shard_map/ppermute | solution.py:175
  16.1 0.8 %broadcast_compare_fusion = pred[8,32,64]{2,1,0:T(8,128)(4,1)S(1)} fusion(s32[64]{0:T(128)S(1)} %get-tuple-element.45, s32[8,32]{1,0:T(8,128)} %param.18), kind=kLoop, calls=%fused_computation.3 | loop fusion | flops 16384 | bytes 17664 | tf_op jit(solution)/shard_map/eq | solution.py:224
  16.9 0.8 %pad_maximum_fusion.local_ref = bf16[64,1024]{1,0:T(8,128)(2,1)S(1)} fusion(bf16[64,256]{1,0:T(8,128)(2,1)} %param.16, bf16[64,256]{1,0:T(8,128)(2,1)} %param.15, bf16[64,512]{1,0:T(8,128)(2,1)S(1)} %copy-done.5), kind=kLoop, calls=%fused_computation.2 | loop fusion | flops 393216 | bytes 262144 | tf_op jit(solution)/shard_map/concatenate | solution.py:232
  17.7 1.2 %collective-permute-done.5.refs_5_ = bf16[2,64,256]{2,1,0:T(8,128)(2,1)S(1)} collective-permute-done((bf16[2,64,256]{2,1,0:T(8,128)(2,1)S(1)}, bf16[2,64,256]{2,1,0:T(8,128)(2,1)S(1)}, u32[]{:S(2)}, u32[]{:S(2)}) %collective-permute-start.5) | collective-permute-done | bytes 65568 | tf_op jit(solution)/shard_map/ppermute | solution.py:175
  18.9 0.7 %collective-permute-done.6.refs_7_ = bf16[2,64,256]{2,1,0:T(8,128)(2,1)S(1)} collective-permute-done((bf16[2,64,256]{2,1,0:T(8,128)(2,1)S(1)}, bf16[2,64,256]{2,1,0:T(8,128)(2,1)S(1)}, u32[]{:S(2)}, u32[]{:S(2)}) %collective-permute-start.6) | collective-permute-done | bytes 65568 | tf_op jit(solution)/shard_map/ppermute | solution.py:175
  19.6 1.1 %collective-permute-start.10 = (bf16[256,512]{1,0:T(8,128)(2,1)S(1)}, bf16[256,512]{1,0:T(8,128)(2,1)S(1)}, u32[]{:S(2)}, u32[]{:S(2)}) collective-permute-start(bf16[256,512]{1,0:T(8,128)(2,1)S(1)} %copy-done.2), channel_id=1, source_target_pairs={{0,4},{4,0},{1,5},{5,1},{2,6},{6,2},{3,7},{7,3},{8,12},{12,8},{9,1... | collective-permute-start | bytes 786440 | tf_op jit(solution)/shard_map/ppermute | solution.py:175
  20.9 0.7 %copy-done.3 = bf16[2,64,256]{2,1,0:T(8,128)(2,1)S(1)} copy-done((bf16[2,64,256]{2,1,0:T(8,128)(2,1)S(1)}, bf16[2,64,256]{2,1,0:T(8,128)(2,1)}, u32[]{:S(2)}) %copy-start.3) | copy-done | bytes 65560
  21.6 1.3 %shard_map.157 = (bf16[64,512]{1,0:T(8,128)(2,1)}, bf16[64,640]{1,0:T(8,128)(2,1)S(1)}, bf16[64,640]{1,0:T(8,128)(2,1)S(1)}, bf16[64,640]{1,0:T(8,128)(2,1)S(1)}, bf16[64,640]{1,0:T(8,128)(2,1)S(1)}) custom-call(bf16[64,1024]{1,0:T(8,128)(2,1)S(1)} %pad_maximum_fusion.local_ref, bf16[64,2048]{1,0:T(8,128)(2,1)S(1)} %copy-done.1, ...), custom_call_target="tpu_custom_call" | custom-call | flops 67108864 | bytes 1048576 | tf_op jit(solution)/shard_map/pallas_call | solution.py:162
  22.9 1.9 %collective-permute-start.7 = (bf16[64,640]{1,0:T(8,128)(2,1)S(1)}, bf16[64,640]{1,0:T(8,128)(2,1)S(1)}, u32[]{:S(2)}, u32[]{:S(2)}) collective-permute-start(bf16[64,640]{1,0:T(8,128)(2,1)S(1)} %get-tuple-element.60), channel_id=1, source_target_pairs={{0,16},{8,24},{16,0},{24,8},{1,17},{9,25},{17,1},{25,9},{2,18},{10... | collective-permute-start | bytes 245768 | tf_op jit(solution)/shard_map/ppermute | solution.py:175
  24.8 1.6 %collective-permute-start.8 = (bf16[64,640]{1,0:T(8,128)(2,1)S(1)}, bf16[64,640]{1,0:T(8,128)(2,1)S(1)}, u32[]{:S(2)}, u32[]{:S(2)}) collective-permute-start(bf16[64,640]{1,0:T(8,128)(2,1)S(1)} %get-tuple-element.61), channel_id=1, source_target_pairs={{0,24},{8,16},{16,8},{24,0},{1,25},{9,17},{17,9},{25,1},{2,26},{10... | collective-permute-start | bytes 245768 | tf_op jit(solution)/shard_map/ppermute | solution.py:175
  26.3 3.1 %collective-permute-done.7.a2 = bf16[64,640]{1,0:T(8,128)(2,1)S(1)} collective-permute-done((bf16[64,640]{1,0:T(8,128)(2,1)S(1)}, bf16[64,640]{1,0:T(8,128)(2,1)S(1)}, u32[]{:S(2)}, u32[]{:S(2)}) %collective-permute-start.7) | collective-permute-done | bytes 81952 | tf_op jit(solution)/shard_map/ppermute | solution.py:175
  29.4 1.7 %collective-permute-done.8.a3 = bf16[64,640]{1,0:T(8,128)(2,1)S(1)} collective-permute-done((bf16[64,640]{1,0:T(8,128)(2,1)S(1)}, bf16[64,640]{1,0:T(8,128)(2,1)S(1)}, u32[]{:S(2)}, u32[]{:S(2)}) %collective-permute-start.8) | collective-permute-done | bytes 81952 | tf_op jit(solution)/shard_map/ppermute | solution.py:175
  32.1 0.7 %collective-permute-start.17 = (bf16[256,1024]{1,0:T(8,128)(2,1)S(1)}, bf16[256,1024]{1,0:T(8,128)(2,1)S(1)}, u32[]{:S(2)}, u32[]{:S(2)}) collective-permute-start(bf16[256,1024]{1,0:T(8,128)(2,1)S(1)} %copy-done), channel_id=1, source_target_pairs={{0,4},{4,0},{1,5},{5,1},{2,6},{6,2},{3,7},{7,3},{8,12},{12,8},{9,1... | collective-permute-start | bytes 1572872 | tf_op jit(solution)/shard_map/ppermute | solution.py:175
  32.8 1.5 %collective-permute-start.11 = (bf16[256,128]{1,0:T(8,128)(2,1)S(1)}, bf16[256,128]{1,0:T(8,128)(2,1)S(1)}, u32[]{:S(2)}, u32[]{:S(2)}) collective-permute-start(bf16[256,128]{1,0:T(8,128)(2,1)S(1)} %get-tuple-element.65), channel_id=1, source_target_pairs={{0,2},{1,3},{2,0},{3,1},{4,6},{5,7},{6,4},{7,5},{8,10},{9,11},{10,... | collective-permute-start | bytes 196616 | tf_op jit(solution)/shard_map/ppermute | solution.py:175
  34.3 0.6 %collective-permute-start.13 = (bf16[256,128]{1,0:T(8,128)(2,1)S(1)}, bf16[256,128]{1,0:T(8,128)(2,1)S(1)}, u32[]{:S(2)}, u32[]{:S(2)}) collective-permute-start(bf16[256,128]{1,0:T(8,128)(2,1)S(1)} %get-tuple-element.67), channel_id=1, source_target_pairs={{0,1},{1,0},{2,3},{3,2},{4,5},{5,4},{6,7},{7,6},{8,9},{9,8},{10,11... | collective-permute-start | bytes 196616 | tf_op jit(solution)/shard_map/ppermute | solution.py:175
  34.9 2.1 %collective-permute-done.11.r2 = bf16[256,128]{1,0:T(8,128)(2,1)S(1)} collective-permute-done((bf16[256,128]{1,0:T(8,128)(2,1)S(1)}, bf16[256,128]{1,0:T(8,128)(2,1)S(1)}, u32[]{:S(2)}, u32[]{:S(2)}) %collective-permute-start.11) | collective-permute-done | bytes 65568 | tf_op jit(solution)/shard_map/ppermute | solution.py:175
  37.1 1.4 %collective-permute-done.12.r3 = bf16[256,128]{1,0:T(8,128)(2,1)S(1)} collective-permute-done((bf16[256,128]{1,0:T(8,128)(2,1)S(1)}, bf16[256,128]{1,0:T(8,128)(2,1)S(1)}, u32[]{:S(2)}, u32[]{:S(2)}) %collective-permute-start.12) | collective-permute-done | bytes 65568 | tf_op jit(solution)/shard_map/ppermute | solution.py:175
  38.5 1.2 %collective-permute-start.16 = (bf16[256,128]{1,0:T(8,128)(2,1)S(1)}, bf16[256,128]{1,0:T(8,128)(2,1)S(1)}, u32[]{:S(2)}, u32[]{:S(2)}) collective-permute-start(bf16[256,128]{1,0:T(8,128)(2,1)S(1)} %shard_map.159.x0), channel_id=1, source_target_pairs={{0,3},{1,2},{2,1},{3,0},{4,7},{5,6},{6,5},{7,4},{8,11},{9,10},{10,... | collective-permute-start | bytes 196616 | tf_op jit(solution)/shard_map/ppermute | solution.py:175
  40.4 2.4 %collective-permute-done.16.x3 = bf16[256,128]{1,0:T(8,128)(2,1)S(1)} collective-permute-done((bf16[256,128]{1,0:T(8,128)(2,1)S(1)}, bf16[256,128]{1,0:T(8,128)(2,1)S(1)}, u32[]{:S(2)}, u32[]{:S(2)}) %collective-permute-start.16) | collective-permute-done | bytes 65568 | tf_op jit(solution)/shard_map/ppermute | solution.py:175
  42.9 1.5 %collective-permute-done.15.x2 = bf16[256,128]{1,0:T(8,128)(2,1)S(1)} collective-permute-done((bf16[256,128]{1,0:T(8,128)(2,1)S(1)}, bf16[256,128]{1,0:T(8,128)(2,1)S(1)}, u32[]{:S(2)}, u32[]{:S(2)}) %collective-permute-start.15) | collective-permute-done | bytes 65568 | tf_op jit(solution)/shard_map/ppermute | solution.py:175
  44.9 0.7 %collective-permute-start.18 = (bf16[64,1536]{1,0:T(8,128)(2,1)S(1)}, bf16[64,1536]{1,0:T(8,128)(2,1)S(1)}, u32[]{:S(2)}, u32[]{:S(2)}) collective-permute-start(bf16[64,1536]{1,0:T(8,128)(2,1)S(1)} %get-tuple-element.71), channel_id=1, source_target_pairs={{0,16},{8,24},{16,0},{24,8},{1,17},{9,25},{17,1},{25,9},{2,18},{10... | collective-permute-start | bytes 589832 | tf_op jit(solution)/shard_map/ppermute | solution.py:175
  45.6 2.4 %collective-permute-start.19 = (bf16[64,1536]{1,0:T(8,128)(2,1)S(1)}, bf16[64,1536]{1,0:T(8,128)(2,1)S(1)}, u32[]{:S(2)}, u32[]{:S(2)}) collective-permute-start(bf16[64,1536]{1,0:T(8,128)(2,1)S(1)} %get-tuple-element.72), channel_id=1, source_target_pairs={{0,24},{8,16},{16,8},{24,0},{1,25},{9,17},{17,9},{25,1},{2,26},{10... | collective-permute-start | bytes 589832 | tf_op jit(solution)/shard_map/ppermute | solution.py:175
  48.5 12.6 %collective-permute-done.18.y2 = bf16[64,1536]{1,0:T(8,128)(2,1)S(1)} collective-permute-done((bf16[64,1536]{1,0:T(8,128)(2,1)S(1)}, bf16[64,1536]{1,0:T(8,128)(2,1)S(1)}, u32[]{:S(2)}, u32[]{:S(2)}) %collective-permute-start.18) | collective-permute-done | bytes 196640 | tf_op jit(solution)/shard_map/ppermute | solution.py:175
  61.1 1.1 %collective-permute-done.20.y1 = bf16[64,1536]{1,0:T(8,128)(2,1)S(1)} collective-permute-done((bf16[64,1536]{1,0:T(8,128)(2,1)S(1)}, bf16[64,1536]{1,0:T(8,128)(2,1)S(1)}, u32[]{:S(2)}, u32[]{:S(2)}) %collective-permute-start.20) | collective-permute-done | bytes 196640 | tf_op jit(solution)/shard_map/ppermute | solution.py:175
  62.2 0.8 %shard_map.161 = (bf16[64,1024]{1,0:T(8,128)(2,1)}, bf16[64,2048]{1,0:T(8,128)(2,1)}) custom-call(bf16[64,1536]{1,0:T(8,128)(2,1)S(1)} %collective-permute-done.18.y2, bf16[64,1536]{1,0:T(8,128)(2,1)S(1)} %collective-permute-done.19.y3, bf16[64,1536]{1,0:T(8,128)(2,1)S(1)} %collective-permute-done.20.y1, bf16[64,1536]{1,0:T(8,128)(2,1)S(1)} %get-tuple-element.74.y0), custom_call_target="tpu_custom_call" | custom-call | bytes 1048576 | tf_op jit(solution)/shard_map/pallas_call | solution.py:162
  (37 shorter events, 4.1 us)
Async XLA Ops:
  0.6 16.2 %copy-start.5 = (bf16[64,512]{1,0:T(8,128)(2,1)S(1)}, bf16[64,512]{1,0:T(8,128)(2,1)}, u32[]{:S(2)}) copy-start(bf16[64,512]{1,0:T(8,128)(2,1)} %param.14) | copy-start | bytes 196612
  0.6 18.9 %copy-start.2 = (bf16[256,512]{1,0:T(8,128)(2,1)S(1)}, bf16[256,512]{1,0:T(8,128)(2,1)}, u32[]{:S(2)}) copy-start(bf16[256,512]{1,0:T(8,128)(2,1)} %own_ref.2) | copy-start | bytes 786436
  0.7 9.0 %collective-permute-start.2 = (bf16[2,64,256]{2,1,0:T(8,128)(2,1)}, bf16[2,64,256]{2,1,0:T(8,128)(2,1)S(1)}, u32[]{:S(2)}, u32[]{:S(2)}) collective-permute-start(bf16[2,64,256]{2,1,0:T(8,128)(2,1)} %refs_0_), channel_id=1, source_target_pairs={{0,24},{8,16},{16,8},{24,0},{1,25},{9,17},{17,9},{25,1},{2,26},{10... | collective-permute-start | bytes 196616 | tf_op jit(solution)/shard_map/ppermute | solution.py:175
  5.8 5.8 %collective-permute-start.1 = (bf16[2,64,256]{2,1,0:T(8,128)(2,1)}, bf16[2,64,256]{2,1,0:T(8,128)(2,1)S(1)}, u32[]{:S(2)}, u32[]{:S(2)}) collective-permute-start(bf16[2,64,256]{2,1,0:T(8,128)(2,1)} %refs_0_), channel_id=1, source_target_pairs={{0,16},{8,24},{16,0},{24,8},{1,17},{9,25},{17,1},{25,9},{2,18},{10... | collective-permute-start | bytes 196616 | tf_op jit(solution)/shard_map/ppermute | solution.py:175
  5.8 5.8 %collective-permute-start = (bf16[2,64,256]{2,1,0:T(8,128)(2,1)}, bf16[2,64,256]{2,1,0:T(8,128)(2,1)S(1)}, u32[]{:S(2)}, u32[]{:S(2)}) collective-permute-start(bf16[2,64,256]{2,1,0:T(8,128)(2,1)} %refs_0_), channel_id=1, source_target_pairs={{0,8},{8,0},{16,24},{24,16},{1,9},{9,1},{17,25},{25,17},{2,10},{10... | collective-permute-start | bytes 196616 | tf_op jit(solution)/shard_map/ppermute | solution.py:175
  6.4 11.3 %collective-permute-start.3 = (bf16[2,64,256]{2,1,0:T(8,128)(2,1)}, bf16[2,64,256]{2,1,0:T(8,128)(2,1)S(1)}, u32[]{:S(2)}, u32[]{:S(2)}) collective-permute-start(bf16[2,64,256]{2,1,0:T(8,128)(2,1)} %refs_0_), channel_id=1, source_target_pairs={{0,4},{4,0},{1,5},{5,1},{2,6},{6,2},{3,7},{7,3},{8,12},{12,8},{9,1... | collective-permute-start | bytes 196616 | tf_op jit(solution)/shard_map/ppermute | solution.py:175
  12.4 5.3 %collective-permute-start.4 = (bf16[2,64,256]{2,1,0:T(8,128)(2,1)S(1)}, bf16[2,64,256]{2,1,0:T(8,128)(2,1)S(1)}, u32[]{:S(2)}, u32[]{:S(2)}) collective-permute-start(bf16[2,64,256]{2,1,0:T(8,128)(2,1)S(1)} %collective-permute-done.refs_2_), channel_id=1, source_target_pairs={{0,4},{4,0},{1,5},{5,1},{2,6},{6,2},{3,7},{7,3},{8,12},{12,8},{9,1... | collective-permute-start | bytes 196616 | tf_op jit(solution)/shard_map/ppermute | solution.py:175
  14.0 4.9 %collective-permute-start.5 = (bf16[2,64,256]{2,1,0:T(8,128)(2,1)S(1)}, bf16[2,64,256]{2,1,0:T(8,128)(2,1)S(1)}, u32[]{:S(2)}, u32[]{:S(2)}) collective-permute-start(bf16[2,64,256]{2,1,0:T(8,128)(2,1)S(1)} %collective-permute-done.1.refs_4_), channel_id=1, source_target_pairs={{0,4},{4,0},{1,5},{5,1},{2,6},{6,2},{3,7},{7,3},{8,12},{12,8},{9,1... | collective-permute-start | bytes 196616 | tf_op jit(solution)/shard_map/ppermute | solution.py:175
  14.5 5.0 %collective-permute-start.6 = (bf16[2,64,256]{2,1,0:T(8,128)(2,1)S(1)}, bf16[2,64,256]{2,1,0:T(8,128)(2,1)S(1)}, u32[]{:S(2)}, u32[]{:S(2)}) collective-permute-start(bf16[2,64,256]{2,1,0:T(8,128)(2,1)S(1)} %collective-permute-done.2.refs_6_), channel_id=1, source_target_pairs={{0,4},{4,0},{1,5},{5,1},{2,6},{6,2},{3,7},{7,3},{8,12},{12,8},{9,1... | collective-permute-start | bytes 196616 | tf_op jit(solution)/shard_map/ppermute | solution.py:175
  17.7 3.2 %copy-start.1 = (bf16[64,2048]{1,0:T(8,128)(2,1)S(1)}, bf16[64,2048]{1,0:T(8,128)(2,1)}, u32[]{:S(2)}) copy-start(bf16[64,2048]{1,0:T(8,128)(2,1)} %res_ref.1) | copy-start | bytes 786436
  19.6 12.1 %collective-permute-start.10 = (bf16[256,512]{1,0:T(8,128)(2,1)S(1)}, bf16[256,512]{1,0:T(8,128)(2,1)S(1)}, u32[]{:S(2)}, u32[]{:S(2)}) collective-permute-start(bf16[256,512]{1,0:T(8,128)(2,1)S(1)} %copy-done.2), channel_id=1, source_target_pairs={{0,4},{4,0},{1,5},{5,1},{2,6},{6,2},{3,7},{7,3},{8,12},{12,8},{9,1... | collective-permute-start | bytes 786440 | tf_op jit(solution)/shard_map/ppermute | solution.py:175
  20.7 0.8 %copy-start.3 = (bf16[2,64,256]{2,1,0:T(8,128)(2,1)S(1)}, bf16[2,64,256]{2,1,0:T(8,128)(2,1)}, u32[]{:S(2)}) copy-start(bf16[2,64,256]{2,1,0:T(8,128)(2,1)} %refs_0_) | copy-start | bytes 196612
  22.9 9.2 %copy-start = (bf16[256,1024]{1,0:T(8,128)(2,1)S(1)}, bf16[256,1024]{1,0:T(8,128)(2,1)}, u32[]{:S(2)}) copy-start(bf16[256,1024]{1,0:T(8,128)(2,1)} %own_ref.3) | copy-start | bytes 1572868
  22.9 6.6 %collective-permute-start.7 = (bf16[64,640]{1,0:T(8,128)(2,1)S(1)}, bf16[64,640]{1,0:T(8,128)(2,1)S(1)}, u32[]{:S(2)}, u32[]{:S(2)}) collective-permute-start(bf16[64,640]{1,0:T(8,128)(2,1)S(1)} %get-tuple-element.60), channel_id=1, source_target_pairs={{0,16},{8,24},{16,0},{24,8},{1,17},{9,25},{17,1},{25,9},{2,18},{10... | collective-permute-start | bytes 245768 | tf_op jit(solution)/shard_map/ppermute | solution.py:175
  24.8 6.4 %collective-permute-start.8 = (bf16[64,640]{1,0:T(8,128)(2,1)S(1)}, bf16[64,640]{1,0:T(8,128)(2,1)S(1)}, u32[]{:S(2)}, u32[]{:S(2)}) collective-permute-start(bf16[64,640]{1,0:T(8,128)(2,1)S(1)} %get-tuple-element.61), channel_id=1, source_target_pairs={{0,24},{8,16},{16,8},{24,0},{1,25},{9,17},{17,9},{25,1},{2,26},{10... | collective-permute-start | bytes 245768 | tf_op jit(solution)/shard_map/ppermute | solution.py:175
  26.3 5.3 %collective-permute-start.9 = (bf16[64,640]{1,0:T(8,128)(2,1)S(1)}, bf16[64,640]{1,0:T(8,128)(2,1)S(1)}, u32[]{:S(2)}, u32[]{:S(2)}) collective-permute-start(bf16[64,640]{1,0:T(8,128)(2,1)S(1)} %get-tuple-element.62), channel_id=1, source_target_pairs={{0,8},{8,0},{16,24},{24,16},{1,9},{9,1},{17,25},{25,17},{2,10},{10... | collective-permute-start | bytes 245768 | tf_op jit(solution)/shard_map/ppermute | solution.py:175
  32.1 12.3 %collective-permute-start.17 = (bf16[256,1024]{1,0:T(8,128)(2,1)S(1)}, bf16[256,1024]{1,0:T(8,128)(2,1)S(1)}, u32[]{:S(2)}, u32[]{:S(2)}) collective-permute-start(bf16[256,1024]{1,0:T(8,128)(2,1)S(1)} %copy-done), channel_id=1, source_target_pairs={{0,4},{4,0},{1,5},{5,1},{2,6},{6,2},{3,7},{7,3},{8,12},{12,8},{9,1... | collective-permute-start | bytes 1572872 | tf_op jit(solution)/shard_map/ppermute | solution.py:175
  32.8 4.3 %collective-permute-start.11 = (bf16[256,128]{1,0:T(8,128)(2,1)S(1)}, bf16[256,128]{1,0:T(8,128)(2,1)S(1)}, u32[]{:S(2)}, u32[]{:S(2)}) collective-permute-start(bf16[256,128]{1,0:T(8,128)(2,1)S(1)} %get-tuple-element.65), channel_id=1, source_target_pairs={{0,2},{1,3},{2,0},{3,1},{4,6},{5,7},{6,4},{7,5},{8,10},{9,11},{10,... | collective-permute-start | bytes 196616 | tf_op jit(solution)/shard_map/ppermute | solution.py:175
  34.3 4.2 %collective-permute-start.12 = (bf16[256,128]{1,0:T(8,128)(2,1)S(1)}, bf16[256,128]{1,0:T(8,128)(2,1)S(1)}, u32[]{:S(2)}, u32[]{:S(2)}) collective-permute-start(bf16[256,128]{1,0:T(8,128)(2,1)S(1)} %get-tuple-element.66), channel_id=1, source_target_pairs={{0,3},{1,2},{2,1},{3,0},{4,7},{5,6},{6,5},{7,4},{8,11},{9,10},{10,... | collective-permute-start | bytes 196616 | tf_op jit(solution)/shard_map/ppermute | solution.py:175
  34.3 10.1 %copy-start.4 = (f32[2048]{0:T(1024)S(1)}, f32[2048]{0:T(1024)}, u32[]{:S(2)}) copy-start(f32[2048]{0:T(1024)} %param.26) | copy-start | bytes 24580
  34.3 4.2 %collective-permute-start.13 = (bf16[256,128]{1,0:T(8,128)(2,1)S(1)}, bf16[256,128]{1,0:T(8,128)(2,1)S(1)}, u32[]{:S(2)}, u32[]{:S(2)}) collective-permute-start(bf16[256,128]{1,0:T(8,128)(2,1)S(1)} %get-tuple-element.67), channel_id=1, source_target_pairs={{0,1},{1,0},{2,3},{3,2},{4,5},{5,4},{6,7},{7,6},{8,9},{9,8},{10,11... | collective-permute-start | bytes 196616 | tf_op jit(solution)/shard_map/ppermute | solution.py:175
  38.5 4.4 %collective-permute-start.16 = (bf16[256,128]{1,0:T(8,128)(2,1)S(1)}, bf16[256,128]{1,0:T(8,128)(2,1)S(1)}, u32[]{:S(2)}, u32[]{:S(2)}) collective-permute-start(bf16[256,128]{1,0:T(8,128)(2,1)S(1)} %shard_map.159.x0), channel_id=1, source_target_pairs={{0,3},{1,2},{2,1},{3,0},{4,7},{5,6},{6,5},{7,4},{8,11},{9,10},{10,... | collective-permute-start | bytes 196616 | tf_op jit(solution)/shard_map/ppermute | solution.py:175
  39.7 4.6 %collective-permute-start.15 = (bf16[256,128]{1,0:T(8,128)(2,1)S(1)}, bf16[256,128]{1,0:T(8,128)(2,1)S(1)}, u32[]{:S(2)}, u32[]{:S(2)}) collective-permute-start(bf16[256,128]{1,0:T(8,128)(2,1)S(1)} %shard_map.159.x0), channel_id=1, source_target_pairs={{0,2},{1,3},{2,0},{3,1},{4,6},{5,7},{6,4},{7,5},{8,10},{9,11},{10,... | collective-permute-start | bytes 196616 | tf_op jit(solution)/shard_map/ppermute | solution.py:175
  40.1 4.3 %collective-permute-start.14 = (bf16[256,128]{1,0:T(8,128)(2,1)S(1)}, bf16[256,128]{1,0:T(8,128)(2,1)S(1)}, u32[]{:S(2)}, u32[]{:S(2)}) collective-permute-start(bf16[256,128]{1,0:T(8,128)(2,1)S(1)} %shard_map.159.x0), channel_id=1, source_target_pairs={{0,1},{1,0},{2,3},{3,2},{4,5},{5,4},{6,7},{7,6},{8,9},{9,8},{10,11... | collective-permute-start | bytes 196616 | tf_op jit(solution)/shard_map/ppermute | solution.py:175
  44.9 16.1 %collective-permute-start.18 = (bf16[64,1536]{1,0:T(8,128)(2,1)S(1)}, bf16[64,1536]{1,0:T(8,128)(2,1)S(1)}, u32[]{:S(2)}, u32[]{:S(2)}) collective-permute-start(bf16[64,1536]{1,0:T(8,128)(2,1)S(1)} %get-tuple-element.71), channel_id=1, source_target_pairs={{0,16},{8,24},{16,0},{24,8},{1,17},{9,25},{17,1},{25,9},{2,18},{10... | collective-permute-start | bytes 589832 | tf_op jit(solution)/shard_map/ppermute | solution.py:175
  45.6 15.4 %collective-permute-start.19 = (bf16[64,1536]{1,0:T(8,128)(2,1)S(1)}, bf16[64,1536]{1,0:T(8,128)(2,1)S(1)}, u32[]{:S(2)}, u32[]{:S(2)}) collective-permute-start(bf16[64,1536]{1,0:T(8,128)(2,1)S(1)} %get-tuple-element.72), channel_id=1, source_target_pairs={{0,24},{8,16},{16,8},{24,0},{1,25},{9,17},{17,9},{25,1},{2,26},{10... | collective-permute-start | bytes 589832 | tf_op jit(solution)/shard_map/ppermute | solution.py:175
  48.0 14.2 %collective-permute-start.20 = (bf16[64,1536]{1,0:T(8,128)(2,1)S(1)}, bf16[64,1536]{1,0:T(8,128)(2,1)S(1)}, u32[]{:S(2)}, u32[]{:S(2)}) collective-permute-start(bf16[64,1536]{1,0:T(8,128)(2,1)S(1)} %get-tuple-element.73), channel_id=1, source_target_pairs={{0,8},{8,0},{16,24},{24,16},{1,9},{9,1},{17,25},{25,17},{2,10},{10... | collective-permute-start | bytes 589832 | tf_op jit(solution)/shard_map/ppermute | solution.py:175

commit v10 on v8

--- a/solution.py
+++ b/solution.py
@@ -201,6 +201,10 @@
     sds = jax.ShapeDtypeStruct
     mp = ("x", "c")
 
+    wo_pair = swap(wo_t, "y", 1)
+    small = (pool_root, branch_owner, branch_len, branch_root, request_branch, token_request)
+    wo_pair, small = lax.optimization_barrier((wo_pair, small))
+    pool_root, branch_owner, branch_len, branch_root, request_branch, token_request = small
     along = [cache] + [swap(cache, "z", s) for s in range(1, 4)]
     beside = swap(cache, "y", 1)
 
@@ -231,8 +235,7 @@
     along[1:], bias, local = lax.optimization_barrier((along[1:], bias, local))
     across = [beside] + [swap(mine, "y", 1) for mine in along[1:]]
     blocks = [block for pair in zip(along, across) for block in pair]
-    wo_pair = swap(wo_t, "y", 1)
-    blocks, wo_pair, wq_later = lax.optimization_barrier((blocks, wo_pair, w_qkv))
+    blocks, wq_later = lax.optimization_barrier((blocks, w_qkv))
     wq_pair = swap(wq_later, "y", 1)
     attn, *sends = call(
         attend_kernel,
@@ -256,6 +259,7 @@
     )
     made, wq_pair = lax.optimization_barrier((made, wq_pair))
     slices = [made[0]] + [swap(made[0], mp, j) for j in range(1, 4)]
+    slices, made = lax.optimization_barrier((slices, made))
     home = [made[1]] + [swap(made[1 + s], "z", s) for s in range(1, 4)]
     partial = call(
         qkv_kernel,

time: 62.9 us -> 66 us (1.049)
  waiting for transfers between devices: 24.9 us -> 28.1 us
  starting transfers between devices: 30.3 us -> 29.5 us
  other arithmetic: 3.5 us -> 4.22 us
    ppermute x27, waiting for transfers between devices: 24.9 us -> 28.1 us  [swap(): return lax.ppermute(value, axes, [(i, i ^ bits) for i in range(count)])]
    ppermute x27, starting transfers between devices: 30.3 us -> 29.5 us  [swap(): return lax.ppermute(value, axes, [(i, i ^ bits) for i in range(count)])]
    and x1, other arithmetic: 0.08 us -> 0.81 us  [on_block(): (requests[None, :] == requests[:, None]) & (positions[:, None] <= positio...]
  transfers between devices with their start and end apart: 27 -> 27, of which waited for: 12 -> 16; matrix products, arithmetic and copies ran while one was open for 6% -> 6% of each run, Pallas kernels for 4% -> 3%
where the time goes in v10:
time: 66 us; the launch traced here: 65.7 us
  starting transfers between devices  29.5 us (45%)
  waiting for transfers between devices  28.1 us (43%)
  other arithmetic  4.22 us (6%)
  Pallas kernels  3.15 us (5%)
  between operations  0.8 us (1%)
    ppermute x27, starting transfers between devices, swap(): return lax.ppermute(value, axes, [(i, i ^ bits) for i in range(count)])  29.5 us
    ppermute x27, waiting for transfers between devices, swap(): return lax.ppermute(value, axes, [(i, i ^ bits) for i in range(count)])  28.1 us
    pallas_call x6, Pallas kernels, call(): pl.pallas_call(kernel, out_shape=out_shape, in_specs=[vmem] * len(args),...  3.15 us
  transfers between devices with their start and end apart: 27, of which 16 were waited for; matrix products, arithmetic and copies ran while one was open for 6% of the time, Pallas kernels for 3%

profile of v10, /device:TPU:0, one launch (start us, length us, event | category | flops | bytes accessed | tf_op | source)
XLA Modules:
  0.0 65.7 jit_solution(10001164076797403693)
XLA Ops:
  0.6 3.0 %collective-permute-start.3 = (bf16[256,512]{1,0:T(8,128)(2,1)}, bf16[256,512]{1,0:T(8,128)(2,1)S(1)}, u32[]{:S(2)}, u32[]{:S(2)}) collective-permute-start(bf16[256,512]{1,0:T(8,128)(2,1)} %own_ref.2), channel_id=1, source_target_pairs={{0,4},{4,0},{1,5},{5,1},{2,6},{6,2},{3,7},{7,3},{8,12},{12,8},{9,1... | collective-permute-start | bytes 786440 | tf_op jit(solution)/shard_map/ppermute | solution.py:179
  3.7 3.6 %collective-permute-start.2 = (bf16[2,64,256]{2,1,0:T(8,128)(2,1)}, bf16[2,64,256]{2,1,0:T(8,128)(2,1)S(1)}, u32[]{:S(2)}, u32[]{:S(2)}) collective-permute-start(bf16[2,64,256]{2,1,0:T(8,128)(2,1)} %refs_0_), channel_id=1, source_target_pairs={{0,24},{8,16},{16,8},{24,0},{1,25},{9,17},{17,9},{25,1},{2,26},{10... | collective-permute-start | bytes 196616 | tf_op jit(solution)/shard_map/ppermute | solution.py:179
  7.3 0.8 %collective-permute-start = (bf16[2,64,256]{2,1,0:T(8,128)(2,1)}, bf16[2,64,256]{2,1,0:T(8,128)(2,1)S(1)}, u32[]{:S(2)}, u32[]{:S(2)}) collective-permute-start(bf16[2,64,256]{2,1,0:T(8,128)(2,1)} %refs_0_), channel_id=1, source_target_pairs={{0,8},{8,0},{16,24},{24,16},{1,9},{9,1},{17,25},{25,17},{2,10},{10... | collective-permute-start | bytes 196616 | tf_op jit(solution)/shard_map/ppermute | solution.py:179
  8.3 0.9 %pad_maximum_fusion.local_ref = bf16[64,1024]{1,0:T(8,128)(2,1)S(1)} fusion(bf16[64,256]{1,0:T(8,128)(2,1)} %param.16, bf16[64,256]{1,0:T(8,128)(2,1)} %param.15, bf16[64,512]{1,0:T(8,128)(2,1)} %param.14), kind=kLoop, calls=%fused_computation.2 | loop fusion | flops 393216 | bytes 262144 | tf_op jit(solution)/shard_map/concatenate | solution.py:234
  9.2 1.4 %collective-permute-done.3.par_ref = bf16[256,512]{1,0:T(8,128)(2,1)S(1)} collective-permute-done((bf16[256,512]{1,0:T(8,128)(2,1)}, bf16[256,512]{1,0:T(8,128)(2,1)S(1)}, u32[]{:S(2)}, u32[]{:S(2)}) %collective-permute-start.3) | collective-permute-done | bytes 262176 | tf_op jit(solution)/shard_map/ppermute | solution.py:179
  10.7 0.8 %fusion = pred[64,64]{1,0:T(8,128)(4,1)S(1)} fusion(s32[64]{0:T(128)} %bitcast.6), kind=kLoop, calls=%fused_computation.6 | loop fusion | flops 12288 | bytes 4352 | tf_op jit(solution)/shard_map/and | solution.py:220
  13.0 0.8 %broadcast_compare_fusion = (pred[8,32,64]{2,1,0:T(8,128)(4,1)S(1)}, pred[8,32,64]{2,1,0:T(8,128)(4,1)S(1)}) fusion(s32[64]{0:T(128)S(1)} %get-tuple-element.123, s32[8,32]{1,0:T(8,128)} %param.18, pred[32,64]{1,0:T(8,128)(4,1)S(1)} %iota_compare_fusion.1, pred[8,64]{1,0:T(8,128)(4,1)S(1)} %iota_compare_fusion.2), kind=kLoop, calls=%fused_computation.3 | loop fusion | flops 32768 | bytes 36608 | tf_op jit(solution)/shard_map/eq | solution.py:226
  14.1 2.0 %collective-permute-start.5 = (bf16[2,64,256]{2,1,0:T(8,128)(2,1)S(1)}, bf16[2,64,256]{2,1,0:T(8,128)(2,1)S(1)}, u32[]{:S(2)}, u32[]{:S(2)}) collective-permute-start(bf16[2,64,256]{2,1,0:T(8,128)(2,1)S(1)} %collective-permute-done.refs_2_), channel_id=1, source_target_pairs={{0,4},{4,0},{1,5},{5,1},{2,6},{6,2},{3,7},{7,3},{8,12},{12,8},{9,1... | collective-permute-start | bytes 196616 | tf_op jit(solution)/shard_map/ppermute | solution.py:179
  16.2 1.9 %collective-permute-start.7 = (bf16[2,64,256]{2,1,0:T(8,128)(2,1)S(1)}, bf16[2,64,256]{2,1,0:T(8,128)(2,1)S(1)}, u32[]{:S(2)}, u32[]{:S(2)}) collective-permute-start(bf16[2,64,256]{2,1,0:T(8,128)(2,1)S(1)} %collective-permute-done.2.refs_6_), channel_id=1, source_target_pairs={{0,4},{4,0},{1,5},{5,1},{2,6},{6,2},{3,7},{7,3},{8,12},{12,8},{9,1... | collective-permute-start | bytes 196616 | tf_op jit(solution)/shard_map/ppermute | solution.py:179
  18.8 1.6 %collective-permute-done.6.refs_5_ = bf16[2,64,256]{2,1,0:T(8,128)(2,1)S(1)} collective-permute-done((bf16[2,64,256]{2,1,0:T(8,128)(2,1)S(1)}, bf16[2,64,256]{2,1,0:T(8,128)(2,1)S(1)}, u32[]{:S(2)}, u32[]{:S(2)}) %collective-permute-start.6) | collective-permute-done | bytes 65568 | tf_op jit(solution)/shard_map/ppermute | solution.py:179
  21.1 2.0 %collective-permute-start.14 = (bf16[256,1024]{1,0:T(8,128)(2,1)S(1)}, bf16[256,1024]{1,0:T(8,128)(2,1)S(1)}, u32[]{:S(2)}, u32[]{:S(2)}) collective-permute-start(bf16[256,1024]{1,0:T(8,128)(2,1)S(1)} %copy-done), channel_id=1, source_target_pairs={{0,4},{4,0},{1,5},{5,1},{2,6},{6,2},{3,7},{7,3},{8,12},{12,8},{9,1... | collective-permute-start | bytes 1572872 | tf_op jit(solution)/shard_map/ppermute | solution.py:179
  23.1 1.3 %shard_map.157 = (bf16[64,512]{1,0:T(8,128)(2,1)}, bf16[64,640]{1,0:T(8,128)(2,1)S(1)}, bf16[64,640]{1,0:T(8,128)(2,1)S(1)}, bf16[64,640]{1,0:T(8,128)(2,1)S(1)}, bf16[64,640]{1,0:T(8,128)(2,1)S(1)}) custom-call(bf16[64,1024]{1,0:T(8,128)(2,1)S(1)} %pad_maximum_fusion.local_ref, bf16[64,2048]{1,0:T(8,128)(2,1)S(1)} %copy-done.1, ...), custom_call_target="tpu_custom_call" | custom-call | flops 67108864 | bytes 1048576 | tf_op jit(solution)/shard_map/pallas_call | solution.py:166
  24.4 2.6 %collective-permute-start.8 = (bf16[64,640]{1,0:T(8,128)(2,1)S(1)}, bf16[64,640]{1,0:T(8,128)(2,1)S(1)}, u32[]{:S(2)}, u32[]{:S(2)}) collective-permute-start(bf16[64,640]{1,0:T(8,128)(2,1)S(1)} %get-tuple-element.83), channel_id=1, source_target_pairs={{0,16},{8,24},{16,0},{24,8},{1,17},{9,25},{17,1},{25,9},{2,18},{10... | collective-permute-start | bytes 245768 | tf_op jit(solution)/shard_map/ppermute | solution.py:179
  27.0 1.3 %collective-permute-start.9 = (bf16[64,640]{1,0:T(8,128)(2,1)S(1)}, bf16[64,640]{1,0:T(8,128)(2,1)S(1)}, u32[]{:S(2)}, u32[]{:S(2)}) collective-permute-start(bf16[64,640]{1,0:T(8,128)(2,1)S(1)} %get-tuple-element.84), channel_id=1, source_target_pairs={{0,24},{8,16},{16,8},{24,0},{1,25},{9,17},{17,9},{25,1},{2,26},{10... | collective-permute-start | bytes 245768 | tf_op jit(solution)/shard_map/ppermute | solution.py:179
  28.6 1.2 %collective-permute-done.8.a2 = bf16[64,640]{1,0:T(8,128)(2,1)S(1)} collective-permute-done((bf16[64,640]{1,0:T(8,128)(2,1)S(1)}, bf16[64,640]{1,0:T(8,128)(2,1)S(1)}, u32[]{:S(2)}, u32[]{:S(2)}) %collective-permute-start.8) | collective-permute-done | bytes 81952 | tf_op jit(solution)/shard_map/ppermute | solution.py:179
  29.8 3.6 %collective-permute-done.9.a3 = bf16[64,640]{1,0:T(8,128)(2,1)S(1)} collective-permute-done((bf16[64,640]{1,0:T(8,128)(2,1)S(1)}, bf16[64,640]{1,0:T(8,128)(2,1)S(1)}, u32[]{:S(2)}, u32[]{:S(2)}) %collective-permute-start.9) | collective-permute-done | bytes 81952 | tf_op jit(solution)/shard_map/ppermute | solution.py:179
  34.1 1.6 %collective-permute-start.11 = (bf16[256,128]{1,0:T(8,128)(2,1)S(1)}, bf16[256,128]{1,0:T(8,128)(2,1)S(1)}, u32[]{:S(2)}, u32[]{:S(2)}) collective-permute-start(bf16[256,128]{1,0:T(8,128)(2,1)S(1)} %get-tuple-element.88), channel_id=1, source_target_pairs={{0,2},{1,3},{2,0},{3,1},{4,6},{5,7},{6,4},{7,5},{8,10},{9,11},{10,... | collective-permute-start | bytes 196616 | tf_op jit(solution)/shard_map/ppermute | solution.py:179
  36.3 2.1 %collective-permute-done.11.r2 = bf16[256,128]{1,0:T(8,128)(2,1)S(1)} collective-permute-done((bf16[256,128]{1,0:T(8,128)(2,1)S(1)}, bf16[256,128]{1,0:T(8,128)(2,1)S(1)}, u32[]{:S(2)}, u32[]{:S(2)}) %collective-permute-start.11) | collective-permute-done | bytes 65568 | tf_op jit(solution)/shard_map/ppermute | solution.py:179
  38.5 1.4 %collective-permute-done.12.r3 = bf16[256,128]{1,0:T(8,128)(2,1)S(1)} collective-permute-done((bf16[256,128]{1,0:T(8,128)(2,1)S(1)}, bf16[256,128]{1,0:T(8,128)(2,1)S(1)}, u32[]{:S(2)}, u32[]{:S(2)}) %collective-permute-start.12) | collective-permute-done | bytes 65568 | tf_op jit(solution)/shard_map/ppermute | solution.py:179
  39.9 0.9 %collective-permute-start.17 = (bf16[256,128]{1,0:T(8,128)(2,1)S(1)}, bf16[256,128]{1,0:T(8,128)(2,1)S(1)}, u32[]{:S(2)}, u32[]{:S(2)}) collective-permute-start(bf16[256,128]{1,0:T(8,128)(2,1)S(1)} %get-tuple-element.107.x0), channel_id=1, source_target_pairs={{0,3},{1,2},{2,1},{3,0},{4,7},{5,6},{6,5},{7,4},{8,11},{9,10},{10,... | collective-permute-start | bytes 196616 | tf_op jit(solution)/shard_map/ppermute | solution.py:179
  41.8 2.4 %collective-permute-done.17.x3 = bf16[256,128]{1,0:T(8,128)(2,1)S(1)} collective-permute-done((bf16[256,128]{1,0:T(8,128)(2,1)S(1)}, bf16[256,128]{1,0:T(8,128)(2,1)S(1)}, u32[]{:S(2)}, u32[]{:S(2)}) %collective-permute-start.17) | collective-permute-done | bytes 65568 | tf_op jit(solution)/shard_map/ppermute | solution.py:179
  44.3 1.5 %collective-permute-done.16.x2 = bf16[256,128]{1,0:T(8,128)(2,1)S(1)} collective-permute-done((bf16[256,128]{1,0:T(8,128)(2,1)S(1)}, bf16[256,128]{1,0:T(8,128)(2,1)S(1)}, u32[]{:S(2)}, u32[]{:S(2)}) %collective-permute-start.16) | collective-permute-done | bytes 65568 | tf_op jit(solution)/shard_map/ppermute | solution.py:179
  45.8 2.8 %collective-permute-start.19 = (bf16[64,128]{1,0:T(8,128)(2,1)S(1)}, bf16[64,128]{1,0:T(8,128)(2,1)S(1)}, u32[]{:S(2)}, u32[]{:S(2)}) collective-permute-start(bf16[64,128]{1,0:T(8,128)(2,1)S(1)} %get-tuple-element.105), channel_id=1, source_target_pairs={{0,16},{8,24},{16,0},{24,8},{1,17},{9,25},{17,1},{25,9},{2,18},{10... | collective-permute-start | bytes 49160 | tf_op jit(solution)/shard_map/ppermute | solution.py:179
  48.6 1.6 %collective-permute-start.20 = (bf16[64,128]{1,0:T(8,128)(2,1)S(1)}, bf16[64,128]{1,0:T(8,128)(2,1)S(1)}, u32[]{:S(2)}, u32[]{:S(2)}) collective-permute-start(bf16[64,128]{1,0:T(8,128)(2,1)S(1)} %get-tuple-element.106), channel_id=1, source_target_pairs={{0,24},{8,16},{16,8},{24,0},{1,25},{9,17},{17,9},{25,1},{2,26},{10... | collective-permute-start | bytes 49160 | tf_op jit(solution)/shard_map/ppermute | solution.py:179
  51.2 3.2 %collective-permute-done.20.t3 = bf16[64,128]{1,0:T(8,128)(2,1)S(1)} collective-permute-done((bf16[64,128]{1,0:T(8,128)(2,1)S(1)}, bf16[64,128]{1,0:T(8,128)(2,1)S(1)}, u32[]{:S(2)}, u32[]{:S(2)}) %collective-permute-start.20) | collective-permute-done | bytes 16416 | tf_op jit(solution)/shard_map/ppermute | solution.py:179
  54.4 1.6 %collective-permute-start.25 = (bf16[64,1024]{1,0:T(8,128)(2,1)S(1)}, bf16[64,1024]{1,0:T(8,128)(2,1)S(1)}, u32[]{:S(2)}, u32[]{:S(2)}) collective-permute-start(bf16[64,1024]{1,0:T(8,128)(2,1)S(1)} %get-tuple-element.118), channel_id=1, source_target_pairs={{0,24},{8,16},{16,8},{24,0},{1,25},{9,17},{17,9},{25,1},{2,26},{10... | collective-permute-start | bytes 393224 | tf_op jit(solution)/shard_map/ppermute | solution.py:179
  56.0 0.8 %collective-permute-start.22 = (bf16[64,512]{1,0:T(8,128)(2,1)S(1)}, bf16[64,512]{1,0:T(8,128)(2,1)S(1)}, u32[]{:S(2)}, u32[]{:S(2)}) collective-permute-start(bf16[64,512]{1,0:T(8,128)(2,1)S(1)} %shard_map.161.p0), channel_id=1, source_target_pairs={{0,2},{1,3},{2,0},{3,1},{4,6},{5,7},{6,4},{7,5},{8,10},{9,11},{10,... | collective-permute-start | bytes 196616 | tf_op jit(solution)/shard_map/ppermute | solution.py:179
  56.9 1.2 %collective-permute-done.23.p3 = bf16[64,512]{1,0:T(8,128)(2,1)S(1)} collective-permute-done((bf16[64,512]{1,0:T(8,128)(2,1)S(1)}, bf16[64,512]{1,0:T(8,128)(2,1)S(1)}, u32[]{:S(2)}, u32[]{:S(2)}) %collective-permute-start.23) | collective-permute-done | bytes 65568 | tf_op jit(solution)/shard_map/ppermute | solution.py:179
  58.1 2.5 %collective-permute-done.22.p2 = bf16[64,512]{1,0:T(8,128)(2,1)S(1)} collective-permute-done((bf16[64,512]{1,0:T(8,128)(2,1)S(1)}, bf16[64,512]{1,0:T(8,128)(2,1)S(1)}, u32[]{:S(2)}, u32[]{:S(2)}) %collective-permute-start.22) | collective-permute-done | bytes 65568 | tf_op jit(solution)/shard_map/ppermute | solution.py:179
  60.6 2.1 %collective-permute-done.25.y3 = bf16[64,1024]{1,0:T(8,128)(2,1)S(1)} collective-permute-done((bf16[64,1024]{1,0:T(8,128)(2,1)S(1)}, bf16[64,1024]{1,0:T(8,128)(2,1)S(1)}, u32[]{:S(2)}, u32[]{:S(2)}) %collective-permute-start.25) | collective-permute-done | bytes 131104 | tf_op jit(solution)/shard_map/ppermute | solution.py:179
  62.7 2.1 %collective-permute-done.26.y1 = bf16[64,1024]{1,0:T(8,128)(2,1)S(1)} collective-permute-done((bf16[64,1024]{1,0:T(8,128)(2,1)S(1)}, bf16[64,1024]{1,0:T(8,128)(2,1)S(1)}, u32[]{:S(2)}, u32[]{:S(2)}) %collective-permute-start.26) | collective-permute-done | bytes 131104 | tf_op jit(solution)/shard_map/ppermute | solution.py:179
  64.8 0.9 %shard_map.162 = (bf16[64,1024]{1,0:T(8,128)(2,1)}, bf16[64,2048]{1,0:T(8,128)(2,1)}) custom-call(bf16[64,512]{1,0:T(8,128)(2,1)S(1)} %shard_map.161.p0, bf16[64,512]{1,0:T(8,128)(2,1)S(1)} %collective-permute-done.21.p1, bf16[64,512]{1,0:T(8,128)(2,1)S(1)} %collective-permute-done.22.p2, bf16[64,512]{1,0:T(8,128)(2,1)S(1)} %collective-permute-done.23.p3, ...), custom_call_target="tpu_custom_call" | custom-call | bytes 1048576 | tf_op jit(solution)/shard_map/pallas_call | solution.py:166
  (47 shorter events, 7.2 us)
Async XLA Ops:
  0.6 20.5 %copy-start = (bf16[256,1024]{1,0:T(8,128)(2,1)S(1)}, bf16[256,1024]{1,0:T(8,128)(2,1)}, u32[]{:S(2)}) copy-start(bf16[256,1024]{1,0:T(8,128)(2,1)} %own_ref.3) | copy-start | bytes 1572868
  0.6 10.0 %collective-permute-start.3 = (bf16[256,512]{1,0:T(8,128)(2,1)}, bf16[256,512]{1,0:T(8,128)(2,1)S(1)}, u32[]{:S(2)}, u32[]{:S(2)}) collective-permute-start(bf16[256,512]{1,0:T(8,128)(2,1)} %own_ref.2), channel_id=1, source_target_pairs={{0,4},{4,0},{1,5},{5,1},{2,6},{6,2},{3,7},{7,3},{8,12},{12,8},{9,1... | collective-permute-start | bytes 786440 | tf_op jit(solution)/shard_map/ppermute | solution.py:179
  3.7 10.4 %collective-permute-start.2 = (bf16[2,64,256]{2,1,0:T(8,128)(2,1)}, bf16[2,64,256]{2,1,0:T(8,128)(2,1)S(1)}, u32[]{:S(2)}, u32[]{:S(2)}) collective-permute-start(bf16[2,64,256]{2,1,0:T(8,128)(2,1)} %refs_0_), channel_id=1, source_target_pairs={{0,24},{8,16},{16,8},{24,0},{1,25},{9,17},{17,9},{25,1},{2,26},{10... | collective-permute-start | bytes 196616 | tf_op jit(solution)/shard_map/ppermute | solution.py:179
  7.3 6.8 %collective-permute-start.1 = (bf16[2,64,256]{2,1,0:T(8,128)(2,1)}, bf16[2,64,256]{2,1,0:T(8,128)(2,1)S(1)}, u32[]{:S(2)}, u32[]{:S(2)}) collective-permute-start(bf16[2,64,256]{2,1,0:T(8,128)(2,1)} %refs_0_), channel_id=1, source_target_pairs={{0,16},{8,24},{16,0},{24,8},{1,17},{9,25},{17,1},{25,9},{2,18},{10... | collective-permute-start | bytes 196616 | tf_op jit(solution)/shard_map/ppermute | solution.py:179
  7.3 6.8 %collective-permute-start = (bf16[2,64,256]{2,1,0:T(8,128)(2,1)}, bf16[2,64,256]{2,1,0:T(8,128)(2,1)S(1)}, u32[]{:S(2)}, u32[]{:S(2)}) collective-permute-start(bf16[2,64,256]{2,1,0:T(8,128)(2,1)} %refs_0_), channel_id=1, source_target_pairs={{0,8},{8,0},{16,24},{24,16},{1,9},{9,1},{17,25},{25,17},{2,10},{10... | collective-permute-start | bytes 196616 | tf_op jit(solution)/shard_map/ppermute | solution.py:179
  8.1 10.1 %collective-permute-start.4 = (bf16[2,64,256]{2,1,0:T(8,128)(2,1)}, bf16[2,64,256]{2,1,0:T(8,128)(2,1)S(1)}, u32[]{:S(2)}, u32[]{:S(2)}) collective-permute-start(bf16[2,64,256]{2,1,0:T(8,128)(2,1)} %refs_0_), channel_id=1, source_target_pairs={{0,4},{4,0},{1,5},{5,1},{2,6},{6,2},{3,7},{7,3},{8,12},{12,8},{9,1... | collective-permute-start | bytes 196616 | tf_op jit(solution)/shard_map/ppermute | solution.py:179
  13.8 9.3 %copy-start.1 = (bf16[64,2048]{1,0:T(8,128)(2,1)S(1)}, bf16[64,2048]{1,0:T(8,128)(2,1)}, u32[]{:S(2)}) copy-start(bf16[64,2048]{1,0:T(8,128)(2,1)} %res_ref.1) | copy-start | bytes 786436
  13.9 9.2 %copy-start.3 = (bf16[2,64,256]{2,1,0:T(8,128)(2,1)S(1)}, bf16[2,64,256]{2,1,0:T(8,128)(2,1)}, u32[]{:S(2)}) copy-start(bf16[2,64,256]{2,1,0:T(8,128)(2,1)} %refs_0_) | copy-start | bytes 196612
  14.1 19.6 %copy-start.2 = (bf16[256,512]{1,0:T(8,128)(2,1)S(1)}, bf16[256,512]{1,0:T(8,128)(2,1)}, u32[]{:S(2)}) copy-start(bf16[256,512]{1,0:T(8,128)(2,1)} %own_ref.2) | copy-start | bytes 786436
  14.1 4.7 %collective-permute-start.5 = (bf16[2,64,256]{2,1,0:T(8,128)(2,1)S(1)}, bf16[2,64,256]{2,1,0:T(8,128)(2,1)S(1)}, u32[]{:S(2)}, u32[]{:S(2)}) collective-permute-start(bf16[2,64,256]{2,1,0:T(8,128)(2,1)S(1)} %collective-permute-done.refs_2_), channel_id=1, source_target_pairs={{0,4},{4,0},{1,5},{5,1},{2,6},{6,2},{3,7},{7,3},{8,12},{12,8},{9,1... | collective-permute-start | bytes 196616 | tf_op jit(solution)/shard_map/ppermute | solution.py:179
  16.1 4.3 %collective-permute-start.6 = (bf16[2,64,256]{2,1,0:T(8,128)(2,1)S(1)}, bf16[2,64,256]{2,1,0:T(8,128)(2,1)S(1)}, u32[]{:S(2)}, u32[]{:S(2)}) collective-permute-start(bf16[2,64,256]{2,1,0:T(8,128)(2,1)S(1)} %collective-permute-done.1.refs_4_), channel_id=1, source_target_pairs={{0,4},{4,0},{1,5},{5,1},{2,6},{6,2},{3,7},{7,3},{8,12},{12,8},{9,1... | collective-permute-start | bytes 196616 | tf_op jit(solution)/shard_map/ppermute | solution.py:179
  16.2 4.9 %collective-permute-start.7 = (bf16[2,64,256]{2,1,0:T(8,128)(2,1)S(1)}, bf16[2,64,256]{2,1,0:T(8,128)(2,1)S(1)}, u32[]{:S(2)}, u32[]{:S(2)}) collective-permute-start(bf16[2,64,256]{2,1,0:T(8,128)(2,1)S(1)} %collective-permute-done.2.refs_6_), channel_id=1, source_target_pairs={{0,4},{4,0},{1,5},{5,1},{2,6},{6,2},{3,7},{7,3},{8,12},{12,8},{9,1... | collective-permute-start | bytes 196616 | tf_op jit(solution)/shard_map/ppermute | solution.py:179
  21.1 18.8 %collective-permute-start.14 = (bf16[256,1024]{1,0:T(8,128)(2,1)S(1)}, bf16[256,1024]{1,0:T(8,128)(2,1)S(1)}, u32[]{:S(2)}, u32[]{:S(2)}) collective-permute-start(bf16[256,1024]{1,0:T(8,128)(2,1)S(1)} %copy-done), channel_id=1, source_target_pairs={{0,4},{4,0},{1,5},{5,1},{2,6},{6,2},{3,7},{7,3},{8,12},{12,8},{9,1... | collective-permute-start | bytes 1572872 | tf_op jit(solution)/shard_map/ppermute | solution.py:179
  24.4 5.3 %collective-permute-start.8 = (bf16[64,640]{1,0:T(8,128)(2,1)S(1)}, bf16[64,640]{1,0:T(8,128)(2,1)S(1)}, u32[]{:S(2)}, u32[]{:S(2)}) collective-permute-start(bf16[64,640]{1,0:T(8,128)(2,1)S(1)} %get-tuple-element.83), channel_id=1, source_target_pairs={{0,16},{8,24},{16,0},{24,8},{1,17},{9,25},{17,1},{25,9},{2,18},{10... | collective-permute-start | bytes 245768 | tf_op jit(solution)/shard_map/ppermute | solution.py:179
  27.0 6.4 %collective-permute-start.9 = (bf16[64,640]{1,0:T(8,128)(2,1)S(1)}, bf16[64,640]{1,0:T(8,128)(2,1)S(1)}, u32[]{:S(2)}, u32[]{:S(2)}) collective-permute-start(bf16[64,640]{1,0:T(8,128)(2,1)S(1)} %get-tuple-element.84), channel_id=1, source_target_pairs={{0,24},{8,16},{16,8},{24,0},{1,25},{9,17},{17,9},{25,1},{2,26},{10... | collective-permute-start | bytes 245768 | tf_op jit(solution)/shard_map/ppermute | solution.py:179
  28.4 5.3 %collective-permute-start.10 = (bf16[64,640]{1,0:T(8,128)(2,1)S(1)}, bf16[64,640]{1,0:T(8,128)(2,1)S(1)}, u32[]{:S(2)}, u32[]{:S(2)}) collective-permute-start(bf16[64,640]{1,0:T(8,128)(2,1)S(1)} %get-tuple-element.85), channel_id=1, source_target_pairs={{0,8},{8,0},{16,24},{24,16},{1,9},{9,1},{17,25},{25,17},{2,10},{10... | collective-permute-start | bytes 245768 | tf_op jit(solution)/shard_map/ppermute | solution.py:179
  34.1 4.3 %collective-permute-start.11 = (bf16[256,128]{1,0:T(8,128)(2,1)S(1)}, bf16[256,128]{1,0:T(8,128)(2,1)S(1)}, u32[]{:S(2)}, u32[]{:S(2)}) collective-permute-start(bf16[256,128]{1,0:T(8,128)(2,1)S(1)} %get-tuple-element.88), channel_id=1, source_target_pairs={{0,2},{1,3},{2,0},{3,1},{4,6},{5,7},{6,4},{7,5},{8,10},{9,11},{10,... | collective-permute-start | bytes 196616 | tf_op jit(solution)/shard_map/ppermute | solution.py:179
  35.7 4.2 %collective-permute-start.12 = (bf16[256,128]{1,0:T(8,128)(2,1)S(1)}, bf16[256,128]{1,0:T(8,128)(2,1)S(1)}, u32[]{:S(2)}, u32[]{:S(2)}) collective-permute-start(bf16[256,128]{1,0:T(8,128)(2,1)S(1)} %get-tuple-element.89), channel_id=1, source_target_pairs={{0,3},{1,2},{2,1},{3,0},{4,7},{5,6},{6,5},{7,4},{8,11},{9,10},{10,... | collective-permute-start | bytes 196616 | tf_op jit(solution)/shard_map/ppermute | solution.py:179
  35.7 4.2 %collective-permute-start.13 = (bf16[256,128]{1,0:T(8,128)(2,1)S(1)}, bf16[256,128]{1,0:T(8,128)(2,1)S(1)}, u32[]{:S(2)}, u32[]{:S(2)}) collective-permute-start(bf16[256,128]{1,0:T(8,128)(2,1)S(1)} %get-tuple-element.90), channel_id=1, source_target_pairs={{0,1},{1,0},{2,3},{3,2},{4,5},{5,4},{6,7},{7,6},{8,9},{9,8},{10,11... | collective-permute-start | bytes 196616 | tf_op jit(solution)/shard_map/ppermute | solution.py:179
  39.9 10.3 %copy-start.4 = (f32[2048]{0:T(1024)S(1)}, f32[2048]{0:T(1024)}, u32[]{:S(2)}) copy-start(f32[2048]{0:T(1024)} %param.26) | copy-start | bytes 24580
  39.9 4.4 %collective-permute-start.17 = (bf16[256,128]{1,0:T(8,128)(2,1)S(1)}, bf16[256,128]{1,0:T(8,128)(2,1)S(1)}, u32[]{:S(2)}, u32[]{:S(2)}) collective-permute-start(bf16[256,128]{1,0:T(8,128)(2,1)S(1)} %get-tuple-element.107.x0), channel_id=1, source_target_pairs={{0,3},{1,2},{2,1},{3,0},{4,7},{5,6},{6,5},{7,4},{8,11},{9,10},{10,... | collective-permute-start | bytes 196616 | tf_op jit(solution)/shard_map/ppermute | solution.py:179
  40.9 4.9 %collective-permute-start.16 = (bf16[256,128]{1,0:T(8,128)(2,1)S(1)}, bf16[256,128]{1,0:T(8,128)(2,1)S(1)}, u32[]{:S(2)}, u32[]{:S(2)}) collective-permute-start(bf16[256,128]{1,0:T(8,128)(2,1)S(1)} %get-tuple-element.107.x0), channel_id=1, source_target_pairs={{0,2},{1,3},{2,0},{3,1},{4,6},{5,7},{6,4},{7,5},{8,10},{9,11},{10,... | collective-permute-start | bytes 196616 | tf_op jit(solution)/shard_map/ppermute | solution.py:179
  41.5 4.3 %collective-permute-start.15 = (bf16[256,128]{1,0:T(8,128)(2,1)S(1)}, bf16[256,128]{1,0:T(8,128)(2,1)S(1)}, u32[]{:S(2)}, u32[]{:S(2)}) collective-permute-start(bf16[256,128]{1,0:T(8,128)(2,1)S(1)} %get-tuple-element.107.x0), channel_id=1, source_target_pairs={{0,1},{1,0},{2,3},{3,2},{4,5},{5,4},{6,7},{7,6},{8,9},{9,8},{10,11... | collective-permute-start | bytes 196616 | tf_op jit(solution)/shard_map/ppermute | solution.py:179
  45.8 5.4 %collective-permute-start.18 = (bf16[64,128]{1,0:T(8,128)(2,1)S(1)}, bf16[64,128]{1,0:T(8,128)(2,1)S(1)}, u32[]{:S(2)}, u32[]{:S(2)}) collective-permute-start(bf16[64,128]{1,0:T(8,128)(2,1)S(1)} %get-tuple-element.104), channel_id=1, source_target_pairs={{0,8},{8,0},{16,24},{24,16},{1,9},{9,1},{17,25},{25,17},{2,10},{10... | collective-permute-start | bytes 49160 | tf_op jit(solution)/shard_map/ppermute | solution.py:179
  45.8 5.4 %collective-permute-start.19 = (bf16[64,128]{1,0:T(8,128)(2,1)S(1)}, bf16[64,128]{1,0:T(8,128)(2,1)S(1)}, u32[]{:S(2)}, u32[]{:S(2)}) collective-permute-start(bf16[64,128]{1,0:T(8,128)(2,1)S(1)} %get-tuple-element.105), channel_id=1, source_target_pairs={{0,16},{8,24},{16,0},{24,8},{1,17},{9,25},{17,1},{25,9},{2,18},{10... | collective-permute-start | bytes 49160 | tf_op jit(solution)/shard_map/ppermute | solution.py:179
  48.6 5.8 %collective-permute-start.20 = (bf16[64,128]{1,0:T(8,128)(2,1)S(1)}, bf16[64,128]{1,0:T(8,128)(2,1)S(1)}, u32[]{:S(2)}, u32[]{:S(2)}) collective-permute-start(bf16[64,128]{1,0:T(8,128)(2,1)S(1)} %get-tuple-element.106), channel_id=1, source_target_pairs={{0,24},{8,16},{16,8},{24,0},{1,25},{9,17},{17,9},{25,1},{2,26},{10... | collective-permute-start | bytes 49160 | tf_op jit(solution)/shard_map/ppermute | solution.py:179
  50.7 10.0 %collective-permute-start.24 = (bf16[64,1024]{1,0:T(8,128)(2,1)S(1)}, bf16[64,1024]{1,0:T(8,128)(2,1)S(1)}, u32[]{:S(2)}, u32[]{:S(2)}) collective-permute-start(bf16[64,1024]{1,0:T(8,128)(2,1)S(1)} %get-tuple-element.117), channel_id=1, source_target_pairs={{0,16},{8,24},{16,0},{24,8},{1,17},{9,25},{17,1},{25,9},{2,18},{10... | collective-permute-start | bytes 393224 | tf_op jit(solution)/shard_map/ppermute | solution.py:179
  54.4 3.8 %collective-permute-start.23 = (bf16[64,512]{1,0:T(8,128)(2,1)S(1)}, bf16[64,512]{1,0:T(8,128)(2,1)S(1)}, u32[]{:S(2)}, u32[]{:S(2)}) collective-permute-start(bf16[64,512]{1,0:T(8,128)(2,1)S(1)} %shard_map.161.p0), channel_id=1, source_target_pairs={{0,3},{1,2},{2,1},{3,0},{4,7},{5,6},{6,5},{7,4},{8,11},{9,10},{10,... | collective-permute-start | bytes 196616 | tf_op jit(solution)/shard_map/ppermute | solution.py:179
  54.4 8.3 %collective-permute-start.25 = (bf16[64,1024]{1,0:T(8,128)(2,1)S(1)}, bf16[64,1024]{1,0:T(8,128)(2,1)S(1)}, u32[]{:S(2)}, u32[]{:S(2)}) collective-permute-start(bf16[64,1024]{1,0:T(8,128)(2,1)S(1)} %get-tuple-element.118), channel_id=1, source_target_pairs={{0,24},{8,16},{16,8},{24,0},{1,25},{9,17},{17,9},{25,1},{2,26},{10... | collective-permute-start | bytes 393224 | tf_op jit(solution)/shard_map/ppermute | solution.py:179
  56.0 8.8 %collective-permute-start.26 = (bf16[64,1024]{1,0:T(8,128)(2,1)S(1)}, bf16[64,1024]{1,0:T(8,128)(2,1)S(1)}, u32[]{:S(2)}, u32[]{:S(2)}) collective-permute-start(bf16[64,1024]{1,0:T(8,128)(2,1)S(1)} %get-tuple-element.119), channel_id=1, source_target_pairs={{0,8},{8,0},{16,24},{24,16},{1,9},{9,1},{17,25},{25,17},{2,10},{10... | collective-permute-start | bytes 393224 | tf_op jit(solution)/shard_map/ppermute | solution.py:179
  56.0 4.6 %collective-permute-start.22 = (bf16[64,512]{1,0:T(8,128)(2,1)S(1)}, bf16[64,512]{1,0:T(8,128)(2,1)S(1)}, u32[]{:S(2)}, u32[]{:S(2)}) collective-permute-start(bf16[64,512]{1,0:T(8,128)(2,1)S(1)} %shard_map.161.p0), channel_id=1, source_target_pairs={{0,2},{1,3},{2,0},{3,1},{4,6},{5,7},{6,4},{7,5},{8,10},{9,11},{10,... | collective-permute-start | bytes 196616 | tf_op jit(solution)/shard_map/ppermute | solution.py:179
  58.1 2.5 %collective-permute-start.21 = (bf16[64,512]{1,0:T(8,128)(2,1)S(1)}, bf16[64,512]{1,0:T(8,128)(2,1)S(1)}, u32[]{:S(2)}, u32[]{:S(2)}) collective-permute-start(bf16[64,512]{1,0:T(8,128)(2,1)S(1)} %shard_map.161.p0), channel_id=1, source_target_pairs={{0,1},{1,0},{2,3},{3,2},{4,5},{5,4},{6,7},{7,6},{8,9},{9,8},{10,11... | collective-permute-start | bytes 196616 | tf_op jit(solution)/shard_map/ppermute | solution.py:179

commit v11 on v8

--- a/solution.py
+++ b/solution.py
@@ -112,52 +112,60 @@
         out[...] = chunk + rest.astype(F32) if j == 0 else chunk.astype(BF16)
 
 
-def combine_kernel(r2, r3, r1, r0, out, t0, t1, t2, t3):
-    tok = t0.shape[0]
+def combine_kernel(r2, r3, r1, r0, out, t2, t3):
+    tok = t2.shape[0]
     stream = (
         r0[...] + r1[...].astype(F32) + r2[...].astype(F32) + r3[...].astype(F32)
     ).astype(BF16)
     out[...] = stream
-    for s, part in enumerate((t0, t1, t2, t3)):
-        part[...] = stream[s * tok : (s + 1) * tok]
-
-
-def qkv_kernel(x0, x1, x2, x3, gain_ref, own_ref, par_ref, o0, o1, o2, o3, hold):
+    t2[...] = stream[2 * tok : 3 * tok]
+    t3[...] = stream[3 * tok :]
+
+
+def qkv_kernel(x0, x1, x2, x3, gain_ref, own_ref, par_ref, t3, t2, o0, o1, o2, o3, near, packed, hold):
     e, m = seq_index(), mp_index()
     width = x0.shape[1]
-    half = 2 * width
+    half, columns = own_ref.shape
     tok = o0.shape[0]
     for j, part in enumerate((x0, x1, x2, x3)):
         k = m ^ j
         gain = gain_ref[:, pl.ds(chunk_offset(e, k, width), width)]
-        hold[:, pl.ds(pl.multiple_of(k * width, width), width)] = (
-            part[...].astype(F32) * gain
-        ).astype(BF16)
+        at = pl.multiple_of(k * width, width)
+        hold[:, pl.ds(at, width)] = (part[...].astype(F32) * gain).astype(BF16)
+        near[:, pl.ds(at, width)] = part[:tok]
+        o1[:, pl.ds(pl.multiple_of(columns + at, width), width)] = part[tok : 2 * tok]
+    packed[:, :width] = t2[...]
+    packed[:, width:] = t3[...]
     product = jnp.dot(hold[:, :half], own_ref[...], preferred_element_type=F32) + jnp.dot(
         hold[:, half:], par_ref[...], preferred_element_type=F32
     )
     for s, out in enumerate((o0, o1, o2, o3)):
-        out[...] = product[s * tok : (s + 1) * tok].astype(out.dtype)
-
-
-def pack_kernel(t0, t1, t2, t3, out_ref):
-    width = t0.shape[1]
-    for s, part in enumerate((t0, t1, t2, t3)):
-        out_ref[:, s * width : (s + 1) * width] = part[...]
-
-
-def finish_kernel(p0, p1, p2, p3, y2, y3, y1, y0, qkv_ref, stream_ref):
+        out[:, :columns] = product[s * tok : (s + 1) * tok].astype(out.dtype)
+
+
+def finish_kernel(p0, p1, p2, p3, y2, y3, y1, y0, near, qkv_ref, stream_ref):
     e, m = seq_index(), mp_index()
-    width = p0.shape[1] // 4
-    squares = jnp.zeros((p0.shape[0], width), F32)
+    tok, columns = qkv_ref.shape
+    width = p0.shape[1] // 2
+    squares = jnp.zeros((tok, width), F32)
+    blocks = []
+    for k in range(4):
+        lanes = slice(k * width, (k + 1) * width)
+        blocks.append((chunk_offset(e, k, width), near[:, lanes]))
+        lanes = slice(columns + k * width, columns + (k + 1) * width)
+        blocks.append((chunk_offset(e ^ 2, k, width), y1[:, lanes]))
     for j, part in enumerate((p0, p1, p2, p3)):
-        for s in range(4):
-            block = part[:, s * width : (s + 1) * width]
-            wide = block.astype(F32)
-            squares = squares + wide * wide
-            stream_ref[:, pl.ds(chunk_offset(e ^ (2 * s), m ^ j, width), width)] = block
+        for i, s in enumerate((2, 3)):
+            lanes = slice(i * width, (i + 1) * width)
+            blocks.append((chunk_offset(e ^ (2 * s), m ^ j, width), part[:, lanes]))
+    for at, block in blocks:
+        wide = block.astype(F32)
+        squares = squares + wide * wide
+        stream_ref[:, pl.ds(at, width)] = block
     mean_square = jnp.sum(squares, axis=1, keepdims=True) / stream_ref.shape[1]
-    total = y0[...] + y1[...].astype(F32) + y2[...].astype(F32) + y3[...].astype(F32)
+    total = (
+        y0[...] + y1[:, :columns].astype(F32) + y2[...].astype(F32) + y3[...].astype(F32)
+    )
     qkv_ref[...] = (total * lax.rsqrt(mean_square + 1e-06)).astype(BF16)
 
 
@@ -227,12 +235,13 @@
     seen = jnp.concatenate([own_seen, pool_seen], axis=0)
     bias = jnp.where(jnp.concatenate([seen, seen], axis=1), 0.0, HIDDEN).astype(F32)
 
-    local = jnp.concatenate([fresh_queries, fresh_keys, fresh_values], axis=1)
+    mine = (fresh_queries, fresh_keys, fresh_values)
+    wo_pair, mine = lax.optimization_barrier((swap(wo_t, "y", 1), mine))
+    local = jnp.concatenate(mine, axis=1)
     along[1:], bias, local = lax.optimization_barrier((along[1:], bias, local))
     across = [beside] + [swap(mine, "y", 1) for mine in along[1:]]
     blocks = [block for pair in zip(along, across) for block in pair]
-    wo_pair = swap(wo_t, "y", 1)
-    blocks, wo_pair, wq_later = lax.optimization_barrier((blocks, wo_pair, w_qkv))
+    blocks, wq_later = lax.optimization_barrier((blocks, w_qkv))
     wq_pair = swap(wq_later, "y", 1)
     attn, *sends = call(
         attend_kernel,
@@ -251,27 +260,33 @@
     sums = [sums[0]] + [swap(sums[j], mp, j) for j in range(1, 4)]
     made = call(
         combine_kernel,
-        [sds((4 * tok, width), BF16)] + [sds((tok, width), BF16)] * 4,
+        [sds((4 * tok, width), BF16)] + [sds((tok, width), BF16)] * 2,
         (sums[2], sums[3], sums[1], sums[0]),
     )
     made, wq_pair = lax.optimization_barrier((made, wq_pair))
     slices = [made[0]] + [swap(made[0], mp, j) for j in range(1, 4)]
-    home = [made[1]] + [swap(made[1 + s], "z", s) for s in range(1, 4)]
+    home = [swap(made[2], "z", 3), swap(made[1], "z", 2)]
     partial = call(
         qkv_kernel,
-        [sds((tok, columns), F32)] + [sds((tok, columns), BF16)] * 3,
-        (*slices, norm_gain[None, :], w_qkv, wq_pair),
+        [
+            sds((tok, columns), F32),
+            sds((tok, columns + 4 * width), BF16),
+            sds((tok, columns), BF16),
+            sds((tok, columns), BF16),
+            sds((tok, 4 * width), BF16),
+            sds((tok, 2 * width), BF16),
+        ],
+        (*slices, norm_gain[None, :], w_qkv, wq_pair, *home),
         scratch=[pltpu.VMEM((4 * tok, 4 * width), BF16)],
         flops=1 << 28,
     )
     y1, y2, y3 = (swap(partial[s], "z", s) for s in (1, 2, 3))
-    home, own_partial = lax.optimization_barrier((home, partial[0]))
-    packed = call(pack_kernel, sds((tok, 4 * width), BF16), tuple(home))
+    packed = partial[5]
     pieces = [packed] + [swap(packed, mp, j) for j in range(1, 4)]
     qkv_next, stream = call(
         finish_kernel,
         [sds((tok, columns), BF16), sds(residual.shape, BF16)],
-        (*pieces, y2, y3, y1, own_partial),
+        (*pieces, y2, y3, y1, partial[0], partial[4]),
     )
     return attn, stream, qkv_next
 

time: 62.9 us -> 64.2 us (1.021)
  waiting for transfers between devices: 24.9 us -> 28 us
  starting transfers between devices: 30.3 us -> 27.8 us
  other arithmetic: 3.5 us -> 4.22 us
    ppermute x27 -> x26, waiting for transfers between devices: 24.9 us -> 28 us  [swap(): return lax.ppermute(value, axes, [(i, i ^ bits) for i in range(count)])]
    ppermute x27 -> x26, starting transfers between devices: 30.3 us -> 27.8 us  [swap(): return lax.ppermute(value, axes, [(i, i ^ bits) for i in range(count)])]
    and x1, other arithmetic: 0.08 us -> 0.81 us  [on_block(): (requests[None, :] == requests[:, None]) & (positions[:, None] <= positio...]
    pallas_call x6 -> x5, Pallas kernels: 3.16 us -> 3.17 us  [call(): pl.pallas_call(kernel, out_shape=out_shape, in_specs=[vmem] * len(args),...]
  transfers between devices with their start and end apart: 27 -> 26, of which waited for: 12 -> 15; matrix products, arithmetic and copies ran while one was open for 6% -> 7% of each run, Pallas kernels for 4% -> 3%
where the time goes in v11:
time: 64.2 us; the launch traced here: 64 us
  waiting for transfers between devices  28 us (44%)
  starting transfers between devices  27.8 us (43%)
  other arithmetic  4.22 us (7%)
  Pallas kernels  3.17 us (5%)
  between operations  0.8 us (1%)
    ppermute x26, waiting for transfers between devices, swap(): return lax.ppermute(value, axes, [(i, i ^ bits) for i in range(count)])  28 us
    ppermute x26, starting transfers between devices, swap(): return lax.ppermute(value, axes, [(i, i ^ bits) for i in range(count)])  27.8 us
    pallas_call x5, Pallas kernels, call(): pl.pallas_call(kernel, out_shape=out_shape, in_specs=[vmem] * len(args),...  3.17 us
  transfers between devices with their start and end apart: 26, of which 15 were waited for; matrix products, arithmetic and copies ran while one was open for 7% of the time, Pallas kernels for 3%

profile of v11, /device:TPU:0, one launch (start us, length us, event | category | flops | bytes accessed | tf_op | source)
XLA Modules:
  0.0 64.0 jit_solution(8851188116799624358)
XLA Ops:
  0.6 5.1 %collective-permute-start.2 = (bf16[2,64,256]{2,1,0:T(8,128)(2,1)}, bf16[2,64,256]{2,1,0:T(8,128)(2,1)S(1)}, u32[]{:S(2)}, u32[]{:S(2)}) collective-permute-start(bf16[2,64,256]{2,1,0:T(8,128)(2,1)} %refs_0_), channel_id=1, source_target_pairs={{0,24},{8,16},{16,8},{24,0},{1,25},{9,17},{17,9},{25,1},{2,26},{10... | collective-permute-start | bytes 196616 | tf_op jit(solution)/shard_map/ppermute | solution.py:187
  6.4 1.7 %collective-permute-start.4 = (bf16[2,64,256]{2,1,0:T(8,128)(2,1)}, bf16[2,64,256]{2,1,0:T(8,128)(2,1)S(1)}, u32[]{:S(2)}, u32[]{:S(2)}) collective-permute-start(bf16[2,64,256]{2,1,0:T(8,128)(2,1)} %refs_0_), channel_id=1, source_target_pairs={{0,4},{4,0},{1,5},{5,1},{2,6},{6,2},{3,7},{7,3},{8,12},{12,8},{9,1... | collective-permute-start | bytes 196616 | tf_op jit(solution)/shard_map/ppermute | solution.py:187
  10.0 0.8 %broadcast_compare_fusion = (pred[8,32,64]{2,1,0:T(8,128)(4,1)S(1)}, pred[8,32,64]{2,1,0:T(8,128)(4,1)S(1)}) fusion(s32[64]{0:T(128)S(1)} %get-tuple-element.87, s32[8,32]{1,0:T(8,128)} %param.18, pred[32,64]{1,0:T(8,128)(4,1)S(1)} %iota_compare_fusion.1, pred[8,64]{1,0:T(8,128)(4,1)S(1)} %iota_compare_fusion.2), kind=kLoop, calls=%fused_computation.3 | loop fusion | flops 32768 | bytes 36608 | tf_op jit(solution)/shard_map/eq | solution.py:230
  10.8 0.8 %fusion = pred[64,64]{1,0:T(8,128)(4,1)S(1)} fusion(s32[64]{0:T(128)} %bitcast.7), kind=kLoop, calls=%fused_computation.6 | loop fusion | flops 12288 | bytes 4352 | tf_op jit(solution)/shard_map/and | solution.py:224
  11.8 4.2 %collective-permute-done.3.par_ref = bf16[256,512]{1,0:T(8,128)(2,1)S(1)} collective-permute-done((bf16[256,512]{1,0:T(8,128)(2,1)}, bf16[256,512]{1,0:T(8,128)(2,1)S(1)}, u32[]{:S(2)}, u32[]{:S(2)}) %collective-permute-start.3) | collective-permute-done | bytes 262176 | tf_op jit(solution)/shard_map/ppermute | solution.py:187
  16.0 0.9 %pad_maximum_fusion.local_ref = bf16[64,1024]{1,0:T(8,128)(2,1)S(1)} fusion(bf16[64,256]{1,0:T(8,128)(2,1)} %param.16, bf16[64,256]{1,0:T(8,128)(2,1)} %param.15, bf16[64,512]{1,0:T(8,128)(2,1)} %param.14), kind=kLoop, calls=%fused_computation.2 | loop fusion | flops 393216 | bytes 262144 | tf_op jit(solution)/shard_map/concatenate | solution.py:240
  17.0 1.0 %collective-permute-start.5 = (bf16[2,64,256]{2,1,0:T(8,128)(2,1)S(1)}, bf16[2,64,256]{2,1,0:T(8,128)(2,1)S(1)}, u32[]{:S(2)}, u32[]{:S(2)}) collective-permute-start(bf16[2,64,256]{2,1,0:T(8,128)(2,1)S(1)} %collective-permute-done.refs_2_), channel_id=1, source_target_pairs={{0,4},{4,0},{1,5},{5,1},{2,6},{6,2},{3,7},{7,3},{8,12},{12,8},{9,1... | collective-permute-start | bytes 196616 | tf_op jit(solution)/shard_map/ppermute | solution.py:187
  18.0 1.0 %collective-permute-start.6 = (bf16[2,64,256]{2,1,0:T(8,128)(2,1)S(1)}, bf16[2,64,256]{2,1,0:T(8,128)(2,1)S(1)}, u32[]{:S(2)}, u32[]{:S(2)}) collective-permute-start(bf16[2,64,256]{2,1,0:T(8,128)(2,1)S(1)} %collective-permute-done.1.refs_4_), channel_id=1, source_target_pairs={{0,4},{4,0},{1,5},{5,1},{2,6},{6,2},{3,7},{7,3},{8,12},{12,8},{9,1... | collective-permute-start | bytes 196616 | tf_op jit(solution)/shard_map/ppermute | solution.py:187
  19.1 1.0 %collective-permute-start.7 = (bf16[2,64,256]{2,1,0:T(8,128)(2,1)S(1)}, bf16[2,64,256]{2,1,0:T(8,128)(2,1)S(1)}, u32[]{:S(2)}, u32[]{:S(2)}) collective-permute-start(bf16[2,64,256]{2,1,0:T(8,128)(2,1)S(1)} %collective-permute-done.2.refs_6_), channel_id=1, source_target_pairs={{0,4},{4,0},{1,5},{5,1},{2,6},{6,2},{3,7},{7,3},{8,12},{12,8},{9,1... | collective-permute-start | bytes 196616 | tf_op jit(solution)/shard_map/ppermute | solution.py:187
  20.1 1.3 %collective-permute-done.5.refs_3_ = bf16[2,64,256]{2,1,0:T(8,128)(2,1)S(1)} collective-permute-done((bf16[2,64,256]{2,1,0:T(8,128)(2,1)S(1)}, bf16[2,64,256]{2,1,0:T(8,128)(2,1)S(1)}, u32[]{:S(2)}, u32[]{:S(2)}) %collective-permute-start.5) | collective-permute-done | bytes 65568 | tf_op jit(solution)/shard_map/ppermute | solution.py:187
  21.3 1.0 %collective-permute-done.6.refs_5_ = bf16[2,64,256]{2,1,0:T(8,128)(2,1)S(1)} collective-permute-done((bf16[2,64,256]{2,1,0:T(8,128)(2,1)S(1)}, bf16[2,64,256]{2,1,0:T(8,128)(2,1)S(1)}, u32[]{:S(2)}, u32[]{:S(2)}) %collective-permute-start.6) | collective-permute-done | bytes 65568 | tf_op jit(solution)/shard_map/ppermute | solution.py:187
  22.3 1.5 %collective-permute-done.7.refs_7_ = bf16[2,64,256]{2,1,0:T(8,128)(2,1)S(1)} collective-permute-done((bf16[2,64,256]{2,1,0:T(8,128)(2,1)S(1)}, bf16[2,64,256]{2,1,0:T(8,128)(2,1)S(1)}, u32[]{:S(2)}, u32[]{:S(2)}) %collective-permute-start.7) | collective-permute-done | bytes 65568 | tf_op jit(solution)/shard_map/ppermute | solution.py:187
  23.8 1.0 %collective-permute-start.14 = (bf16[256,1024]{1,0:T(8,128)(2,1)S(1)}, bf16[256,1024]{1,0:T(8,128)(2,1)S(1)}, u32[]{:S(2)}, u32[]{:S(2)}) collective-permute-start(bf16[256,1024]{1,0:T(8,128)(2,1)S(1)} %copy-done), channel_id=1, source_target_pairs={{0,4},{4,0},{1,5},{5,1},{2,6},{6,2},{3,7},{7,3},{8,12},{12,8},{9,1... | collective-permute-start | bytes 1572872 | tf_op jit(solution)/shard_map/ppermute | solution.py:187
  24.8 1.3 %shard_map.157 = (bf16[64,512]{1,0:T(8,128)(2,1)}, bf16[64,640]{1,0:T(8,128)(2,1)S(1)}, bf16[64,640]{1,0:T(8,128)(2,1)S(1)}, bf16[64,640]{1,0:T(8,128)(2,1)S(1)}, bf16[64,640]{1,0:T(8,128)(2,1)S(1)}) custom-call(bf16[64,1024]{1,0:T(8,128)(2,1)S(1)} %pad_maximum_fusion.local_ref, bf16[64,2048]{1,0:T(8,128)(2,1)S(1)} %copy-done.1, ...), custom_call_target="tpu_custom_call" | custom-call | flops 67108864 | bytes 1048576 | tf_op jit(solution)/shard_map/pallas_call | solution.py:174
  26.1 2.2 %collective-permute-start.8 = (bf16[64,640]{1,0:T(8,128)(2,1)S(1)}, bf16[64,640]{1,0:T(8,128)(2,1)S(1)}, u32[]{:S(2)}, u32[]{:S(2)}) collective-permute-start(bf16[64,640]{1,0:T(8,128)(2,1)S(1)} %get-tuple-element.62), channel_id=1, source_target_pairs={{0,16},{8,24},{16,0},{24,8},{1,17},{9,25},{17,1},{25,9},{2,18},{10... | collective-permute-start | bytes 245768 | tf_op jit(solution)/shard_map/ppermute | solution.py:187
  28.4 1.5 %collective-permute-start.9 = (bf16[64,640]{1,0:T(8,128)(2,1)S(1)}, bf16[64,640]{1,0:T(8,128)(2,1)S(1)}, u32[]{:S(2)}, u32[]{:S(2)}) collective-permute-start(bf16[64,640]{1,0:T(8,128)(2,1)S(1)} %get-tuple-element.63), channel_id=1, source_target_pairs={{0,24},{8,16},{16,8},{24,0},{1,25},{9,17},{17,9},{25,1},{2,26},{10... | collective-permute-start | bytes 245768 | tf_op jit(solution)/shard_map/ppermute | solution.py:187
  30.3 1.2 %collective-permute-done.8.a2 = bf16[64,640]{1,0:T(8,128)(2,1)S(1)} collective-permute-done((bf16[64,640]{1,0:T(8,128)(2,1)S(1)}, bf16[64,640]{1,0:T(8,128)(2,1)S(1)}, u32[]{:S(2)}, u32[]{:S(2)}) %collective-permute-start.8) | collective-permute-done | bytes 81952 | tf_op jit(solution)/shard_map/ppermute | solution.py:187
  31.5 3.3 %collective-permute-done.9.a3 = bf16[64,640]{1,0:T(8,128)(2,1)S(1)} collective-permute-done((bf16[64,640]{1,0:T(8,128)(2,1)S(1)}, bf16[64,640]{1,0:T(8,128)(2,1)S(1)}, u32[]{:S(2)}, u32[]{:S(2)}) %collective-permute-start.9) | collective-permute-done | bytes 81952 | tf_op jit(solution)/shard_map/ppermute | solution.py:187
  35.6 1.6 %collective-permute-start.11 = (bf16[256,128]{1,0:T(8,128)(2,1)S(1)}, bf16[256,128]{1,0:T(8,128)(2,1)S(1)}, u32[]{:S(2)}, u32[]{:S(2)}) collective-permute-start(bf16[256,128]{1,0:T(8,128)(2,1)S(1)} %get-tuple-element.67), channel_id=1, source_target_pairs={{0,2},{1,3},{2,0},{3,1},{4,6},{5,7},{6,4},{7,5},{8,10},{9,11},{10,... | collective-permute-start | bytes 196616 | tf_op jit(solution)/shard_map/ppermute | solution.py:187
  37.8 2.1 %collective-permute-done.11.r2 = bf16[256,128]{1,0:T(8,128)(2,1)S(1)} collective-permute-done((bf16[256,128]{1,0:T(8,128)(2,1)S(1)}, bf16[256,128]{1,0:T(8,128)(2,1)S(1)}, u32[]{:S(2)}, u32[]{:S(2)}) %collective-permute-start.11) | collective-permute-done | bytes 65568 | tf_op jit(solution)/shard_map/ppermute | solution.py:187
  39.9 1.4 %collective-permute-done.12.r3 = bf16[256,128]{1,0:T(8,128)(2,1)S(1)} collective-permute-done((bf16[256,128]{1,0:T(8,128)(2,1)S(1)}, bf16[256,128]{1,0:T(8,128)(2,1)S(1)}, u32[]{:S(2)}, u32[]{:S(2)}) %collective-permute-start.12) | collective-permute-done | bytes 65568 | tf_op jit(solution)/shard_map/ppermute | solution.py:187
  41.4 0.9 %collective-permute-start.17 = (bf16[256,128]{1,0:T(8,128)(2,1)S(1)}, bf16[256,128]{1,0:T(8,128)(2,1)S(1)}, u32[]{:S(2)}, u32[]{:S(2)}) collective-permute-start(bf16[256,128]{1,0:T(8,128)(2,1)S(1)} %get-tuple-element.75.x0), channel_id=1, source_target_pairs={{0,3},{1,2},{2,1},{3,0},{4,7},{5,6},{6,5},{7,4},{8,11},{9,10},{10,... | collective-permute-start | bytes 196616 | tf_op jit(solution)/shard_map/ppermute | solution.py:187
  43.3 2.1 %collective-permute-start.18 = (bf16[64,128]{1,0:T(8,128)(2,1)S(1)}, bf16[64,128]{1,0:T(8,128)(2,1)S(1)}, u32[]{:S(2)}, u32[]{:S(2)}) collective-permute-start(bf16[64,128]{1,0:T(8,128)(2,1)S(1)} %get-tuple-element.77), channel_id=1, source_target_pairs={{0,24},{8,16},{16,8},{24,0},{1,25},{9,17},{17,9},{25,1},{2,26},{10... | collective-permute-start | bytes 49160 | tf_op jit(solution)/shard_map/ppermute | solution.py:187
  45.4 3.4 %collective-permute-done.18.t3 = bf16[64,128]{1,0:T(8,128)(2,1)S(1)} collective-permute-done((bf16[64,128]{1,0:T(8,128)(2,1)S(1)}, bf16[64,128]{1,0:T(8,128)(2,1)S(1)}, u32[]{:S(2)}, u32[]{:S(2)}) %collective-permute-start.18) | collective-permute-done | bytes 16416 | tf_op jit(solution)/shard_map/ppermute | solution.py:187
  48.8 1.2 %collective-permute-done.19.t2 = bf16[64,128]{1,0:T(8,128)(2,1)S(1)} collective-permute-done((bf16[64,128]{1,0:T(8,128)(2,1)S(1)}, bf16[64,128]{1,0:T(8,128)(2,1)S(1)}, u32[]{:S(2)}, u32[]{:S(2)}) %collective-permute-start.19) | collective-permute-done | bytes 16416 | tf_op jit(solution)/shard_map/ppermute | solution.py:187
  50.6 2.3 %collective-permute-start.23 = (bf16[64,1024]{1,0:T(8,128)(2,1)S(1)}, bf16[64,1024]{1,0:T(8,128)(2,1)S(1)}, u32[]{:S(2)}, u32[]{:S(2)}) collective-permute-start(bf16[64,1024]{1,0:T(8,128)(2,1)S(1)} %get-tuple-element.80), channel_id=1, source_target_pairs={{0,16},{8,24},{16,0},{24,8},{1,17},{9,25},{17,1},{25,9},{2,18},{10... | collective-permute-start | bytes 393224 | tf_op jit(solution)/shard_map/ppermute | solution.py:187
  52.9 2.1 %collective-permute-start.24 = (bf16[64,1024]{1,0:T(8,128)(2,1)S(1)}, bf16[64,1024]{1,0:T(8,128)(2,1)S(1)}, u32[]{:S(2)}, u32[]{:S(2)}) collective-permute-start(bf16[64,1024]{1,0:T(8,128)(2,1)S(1)} %get-tuple-element.81), channel_id=1, source_target_pairs={{0,24},{8,16},{16,8},{24,0},{1,25},{9,17},{17,9},{25,1},{2,26},{10... | collective-permute-start | bytes 393224 | tf_op jit(solution)/shard_map/ppermute | solution.py:187
  55.0 1.1 %collective-permute-start.21 = (bf16[64,256]{1,0:T(8,128)(2,1)S(1)}, bf16[64,256]{1,0:T(8,128)(2,1)S(1)}, u32[]{:S(2)}, u32[]{:S(2)}) collective-permute-start(bf16[64,256]{1,0:T(8,128)(2,1)S(1)} %get-tuple-element.79.p0), channel_id=1, source_target_pairs={{0,2},{1,3},{2,0},{3,1},{4,6},{5,7},{6,4},{7,5},{8,10},{9,11},{10,... | collective-permute-start | bytes 98312 | tf_op jit(solution)/shard_map/ppermute | solution.py:187
  56.1 2.3 %collective-permute-done.22.p3 = bf16[64,256]{1,0:T(8,128)(2,1)S(1)} collective-permute-done((bf16[64,256]{1,0:T(8,128)(2,1)S(1)}, bf16[64,256]{1,0:T(8,128)(2,1)S(1)}, u32[]{:S(2)}, u32[]{:S(2)}) %collective-permute-start.22) | collective-permute-done | bytes 32800 | tf_op jit(solution)/shard_map/ppermute | solution.py:187
  58.3 0.8 %collective-permute-done.21.p2 = bf16[64,256]{1,0:T(8,128)(2,1)S(1)} collective-permute-done((bf16[64,256]{1,0:T(8,128)(2,1)S(1)}, bf16[64,256]{1,0:T(8,128)(2,1)S(1)}, u32[]{:S(2)}, u32[]{:S(2)}) %collective-permute-start.21) | collective-permute-done | bytes 32800 | tf_op jit(solution)/shard_map/ppermute | solution.py:187
  59.6 3.5 %collective-permute-done.23.y2 = bf16[64,1024]{1,0:T(8,128)(2,1)S(1)} collective-permute-done((bf16[64,1024]{1,0:T(8,128)(2,1)S(1)}, bf16[64,1024]{1,0:T(8,128)(2,1)S(1)}, u32[]{:S(2)}, u32[]{:S(2)}) %collective-permute-start.23) | collective-permute-done | bytes 131104 | tf_op jit(solution)/shard_map/ppermute | solution.py:187
  63.1 0.9 %shard_map.161 = (bf16[64,1024]{1,0:T(8,128)(2,1)}, bf16[64,2048]{1,0:T(8,128)(2,1)}) custom-call(bf16[64,256]{1,0:T(8,128)(2,1)S(1)} %get-tuple-element.79.p0, bf16[64,256]{1,0:T(8,128)(2,1)S(1)} %collective-permute-done.20.p1, bf16[64,256]{1,0:T(8,128)(2,1)S(1)} %collective-permute-done.21.p2, bf16[64,256]{1,0:T(8,128)(2,1)S(1)} %collective-permute-done.22.p3, ...), custom_call_target="tpu_custom_call" | custom-call | bytes 1048576 | tf_op jit(solution)/shard_map/pallas_call | solution.py:174
  (44 shorter events, 6.7 us)
Async XLA Ops:
  0.6 23.2 %copy-start = (bf16[256,1024]{1,0:T(8,128)(2,1)S(1)}, bf16[256,1024]{1,0:T(8,128)(2,1)}, u32[]{:S(2)}) copy-start(bf16[256,1024]{1,0:T(8,128)(2,1)} %own_ref.3) | copy-start | bytes 1572868
  0.6 16.3 %collective-permute-start.2 = (bf16[2,64,256]{2,1,0:T(8,128)(2,1)}, bf16[2,64,256]{2,1,0:T(8,128)(2,1)S(1)}, u32[]{:S(2)}, u32[]{:S(2)}) collective-permute-start(bf16[2,64,256]{2,1,0:T(8,128)(2,1)} %refs_0_), channel_id=1, source_target_pairs={{0,24},{8,16},{16,8},{24,0},{1,25},{9,17},{17,9},{25,1},{2,26},{10... | collective-permute-start | bytes 196616 | tf_op jit(solution)/shard_map/ppermute | solution.py:187
  5.8 11.2 %collective-permute-start.1 = (bf16[2,64,256]{2,1,0:T(8,128)(2,1)}, bf16[2,64,256]{2,1,0:T(8,128)(2,1)S(1)}, u32[]{:S(2)}, u32[]{:S(2)}) collective-permute-start(bf16[2,64,256]{2,1,0:T(8,128)(2,1)} %refs_0_), channel_id=1, source_target_pairs={{0,16},{8,24},{16,0},{24,8},{1,17},{9,25},{17,1},{25,9},{2,18},{10... | collective-permute-start | bytes 196616 | tf_op jit(solution)/shard_map/ppermute | solution.py:187
  5.8 11.2 %collective-permute-start = (bf16[2,64,256]{2,1,0:T(8,128)(2,1)}, bf16[2,64,256]{2,1,0:T(8,128)(2,1)S(1)}, u32[]{:S(2)}, u32[]{:S(2)}) collective-permute-start(bf16[2,64,256]{2,1,0:T(8,128)(2,1)} %refs_0_), channel_id=1, source_target_pairs={{0,8},{8,0},{16,24},{24,16},{1,9},{9,1},{17,25},{25,17},{2,10},{10... | collective-permute-start | bytes 196616 | tf_op jit(solution)/shard_map/ppermute | solution.py:187
  6.4 13.7 %collective-permute-start.4 = (bf16[2,64,256]{2,1,0:T(8,128)(2,1)}, bf16[2,64,256]{2,1,0:T(8,128)(2,1)S(1)}, u32[]{:S(2)}, u32[]{:S(2)}) collective-permute-start(bf16[2,64,256]{2,1,0:T(8,128)(2,1)} %refs_0_), channel_id=1, source_target_pairs={{0,4},{4,0},{1,5},{5,1},{2,6},{6,2},{3,7},{7,3},{8,12},{12,8},{9,1... | collective-permute-start | bytes 196616 | tf_op jit(solution)/shard_map/ppermute | solution.py:187
  8.1 8.0 %collective-permute-start.3 = (bf16[256,512]{1,0:T(8,128)(2,1)}, bf16[256,512]{1,0:T(8,128)(2,1)S(1)}, u32[]{:S(2)}, u32[]{:S(2)}) collective-permute-start(bf16[256,512]{1,0:T(8,128)(2,1)} %own_ref.2), channel_id=1, source_target_pairs={{0,4},{4,0},{1,5},{5,1},{2,6},{6,2},{3,7},{7,3},{8,12},{12,8},{9,1... | collective-permute-start | bytes 786440 | tf_op jit(solution)/shard_map/ppermute | solution.py:187
  11.6 13.2 %copy-start.1 = (bf16[64,2048]{1,0:T(8,128)(2,1)S(1)}, bf16[64,2048]{1,0:T(8,128)(2,1)}, u32[]{:S(2)}) copy-start(bf16[64,2048]{1,0:T(8,128)(2,1)} %res_ref.1) | copy-start | bytes 786436
  11.8 13.0 %copy-start.3 = (bf16[2,64,256]{2,1,0:T(8,128)(2,1)S(1)}, bf16[2,64,256]{2,1,0:T(8,128)(2,1)}, u32[]{:S(2)}) copy-start(bf16[2,64,256]{2,1,0:T(8,128)(2,1)} %refs_0_) | copy-start | bytes 196612
  16.9 18.2 %copy-start.2 = (bf16[256,512]{1,0:T(8,128)(2,1)S(1)}, bf16[256,512]{1,0:T(8,128)(2,1)}, u32[]{:S(2)}) copy-start(bf16[256,512]{1,0:T(8,128)(2,1)} %own_ref.2) | copy-start | bytes 786436
  17.0 4.3 %collective-permute-start.5 = (bf16[2,64,256]{2,1,0:T(8,128)(2,1)S(1)}, bf16[2,64,256]{2,1,0:T(8,128)(2,1)S(1)}, u32[]{:S(2)}, u32[]{:S(2)}) collective-permute-start(bf16[2,64,256]{2,1,0:T(8,128)(2,1)S(1)} %collective-permute-done.refs_2_), channel_id=1, source_target_pairs={{0,4},{4,0},{1,5},{5,1},{2,6},{6,2},{3,7},{7,3},{8,12},{12,8},{9,1... | collective-permute-start | bytes 196616 | tf_op jit(solution)/shard_map/ppermute | solution.py:187
  18.0 4.3 %collective-permute-start.6 = (bf16[2,64,256]{2,1,0:T(8,128)(2,1)S(1)}, bf16[2,64,256]{2,1,0:T(8,128)(2,1)S(1)}, u32[]{:S(2)}, u32[]{:S(2)}) collective-permute-start(bf16[2,64,256]{2,1,0:T(8,128)(2,1)S(1)} %collective-permute-done.1.refs_4_), channel_id=1, source_target_pairs={{0,4},{4,0},{1,5},{5,1},{2,6},{6,2},{3,7},{7,3},{8,12},{12,8},{9,1... | collective-permute-start | bytes 196616 | tf_op jit(solution)/shard_map/ppermute | solution.py:187
  19.1 4.7 %collective-permute-start.7 = (bf16[2,64,256]{2,1,0:T(8,128)(2,1)S(1)}, bf16[2,64,256]{2,1,0:T(8,128)(2,1)S(1)}, u32[]{:S(2)}, u32[]{:S(2)}) collective-permute-start(bf16[2,64,256]{2,1,0:T(8,128)(2,1)S(1)} %collective-permute-done.2.refs_6_), channel_id=1, source_target_pairs={{0,4},{4,0},{1,5},{5,1},{2,6},{6,2},{3,7},{7,3},{8,12},{12,8},{9,1... | collective-permute-start | bytes 196616 | tf_op jit(solution)/shard_map/ppermute | solution.py:187
  23.8 17.5 %collective-permute-start.14 = (bf16[256,1024]{1,0:T(8,128)(2,1)S(1)}, bf16[256,1024]{1,0:T(8,128)(2,1)S(1)}, u32[]{:S(2)}, u32[]{:S(2)}) collective-permute-start(bf16[256,1024]{1,0:T(8,128)(2,1)S(1)} %copy-done), channel_id=1, source_target_pairs={{0,4},{4,0},{1,5},{5,1},{2,6},{6,2},{3,7},{7,3},{8,12},{12,8},{9,1... | collective-permute-start | bytes 1572872 | tf_op jit(solution)/shard_map/ppermute | solution.py:187
  26.1 5.4 %collective-permute-start.8 = (bf16[64,640]{1,0:T(8,128)(2,1)S(1)}, bf16[64,640]{1,0:T(8,128)(2,1)S(1)}, u32[]{:S(2)}, u32[]{:S(2)}) collective-permute-start(bf16[64,640]{1,0:T(8,128)(2,1)S(1)} %get-tuple-element.62), channel_id=1, source_target_pairs={{0,16},{8,24},{16,0},{24,8},{1,17},{9,25},{17,1},{25,9},{2,18},{10... | collective-permute-start | bytes 245768 | tf_op jit(solution)/shard_map/ppermute | solution.py:187
  28.4 6.4 %collective-permute-start.9 = (bf16[64,640]{1,0:T(8,128)(2,1)S(1)}, bf16[64,640]{1,0:T(8,128)(2,1)S(1)}, u32[]{:S(2)}, u32[]{:S(2)}) collective-permute-start(bf16[64,640]{1,0:T(8,128)(2,1)S(1)} %get-tuple-element.63), channel_id=1, source_target_pairs={{0,24},{8,16},{16,8},{24,0},{1,25},{9,17},{17,9},{25,1},{2,26},{10... | collective-permute-start | bytes 245768 | tf_op jit(solution)/shard_map/ppermute | solution.py:187
  29.8 5.3 %collective-permute-start.10 = (bf16[64,640]{1,0:T(8,128)(2,1)S(1)}, bf16[64,640]{1,0:T(8,128)(2,1)S(1)}, u32[]{:S(2)}, u32[]{:S(2)}) collective-permute-start(bf16[64,640]{1,0:T(8,128)(2,1)S(1)} %get-tuple-element.64), channel_id=1, source_target_pairs={{0,8},{8,0},{16,24},{24,16},{1,9},{9,1},{17,25},{25,17},{2,10},{10... | collective-permute-start | bytes 245768 | tf_op jit(solution)/shard_map/ppermute | solution.py:187
  35.6 4.3 %collective-permute-start.11 = (bf16[256,128]{1,0:T(8,128)(2,1)S(1)}, bf16[256,128]{1,0:T(8,128)(2,1)S(1)}, u32[]{:S(2)}, u32[]{:S(2)}) collective-permute-start(bf16[256,128]{1,0:T(8,128)(2,1)S(1)} %get-tuple-element.67), channel_id=1, source_target_pairs={{0,2},{1,3},{2,0},{3,1},{4,6},{5,7},{6,4},{7,5},{8,10},{9,11},{10,... | collective-permute-start | bytes 196616 | tf_op jit(solution)/shard_map/ppermute | solution.py:187
  37.1 4.2 %collective-permute-start.12 = (bf16[256,128]{1,0:T(8,128)(2,1)S(1)}, bf16[256,128]{1,0:T(8,128)(2,1)S(1)}, u32[]{:S(2)}, u32[]{:S(2)}) collective-permute-start(bf16[256,128]{1,0:T(8,128)(2,1)S(1)} %get-tuple-element.68), channel_id=1, source_target_pairs={{0,3},{1,2},{2,1},{3,0},{4,7},{5,6},{6,5},{7,4},{8,11},{9,10},{10,... | collective-permute-start | bytes 196616 | tf_op jit(solution)/shard_map/ppermute | solution.py:187
  37.1 4.2 %collective-permute-start.13 = (bf16[256,128]{1,0:T(8,128)(2,1)S(1)}, bf16[256,128]{1,0:T(8,128)(2,1)S(1)}, u32[]{:S(2)}, u32[]{:S(2)}) collective-permute-start(bf16[256,128]{1,0:T(8,128)(2,1)S(1)} %get-tuple-element.69), channel_id=1, source_target_pairs={{0,1},{1,0},{2,3},{3,2},{4,5},{5,4},{6,7},{7,6},{8,9},{9,8},{10,11... | collective-permute-start | bytes 196616 | tf_op jit(solution)/shard_map/ppermute | solution.py:187
  41.3 8.7 %copy-start.4 = (f32[2048]{0:T(1024)S(1)}, f32[2048]{0:T(1024)}, u32[]{:S(2)}) copy-start(f32[2048]{0:T(1024)} %param.26) | copy-start | bytes 24580
  41.4 8.7 %collective-permute-start.17 = (bf16[256,128]{1,0:T(8,128)(2,1)S(1)}, bf16[256,128]{1,0:T(8,128)(2,1)S(1)}, u32[]{:S(2)}, u32[]{:S(2)}) collective-permute-start(bf16[256,128]{1,0:T(8,128)(2,1)S(1)} %get-tuple-element.75.x0), channel_id=1, source_target_pairs={{0,3},{1,2},{2,1},{3,0},{4,7},{5,6},{6,5},{7,4},{8,11},{9,10},{10,... | collective-permute-start | bytes 196616 | tf_op jit(solution)/shard_map/ppermute | solution.py:187
  42.3 7.7 %collective-permute-start.16 = (bf16[256,128]{1,0:T(8,128)(2,1)S(1)}, bf16[256,128]{1,0:T(8,128)(2,1)S(1)}, u32[]{:S(2)}, u32[]{:S(2)}) collective-permute-start(bf16[256,128]{1,0:T(8,128)(2,1)S(1)} %get-tuple-element.75.x0), channel_id=1, source_target_pairs={{0,2},{1,3},{2,0},{3,1},{4,6},{5,7},{6,4},{7,5},{8,10},{9,11},{10,... | collective-permute-start | bytes 196616 | tf_op jit(solution)/shard_map/ppermute | solution.py:187
  43.0 7.1 %collective-permute-start.15 = (bf16[256,128]{1,0:T(8,128)(2,1)S(1)}, bf16[256,128]{1,0:T(8,128)(2,1)S(1)}, u32[]{:S(2)}, u32[]{:S(2)}) collective-permute-start(bf16[256,128]{1,0:T(8,128)(2,1)S(1)} %get-tuple-element.75.x0), channel_id=1, source_target_pairs={{0,1},{1,0},{2,3},{3,2},{4,5},{5,4},{6,7},{7,6},{8,9},{9,8},{10,11... | collective-permute-start | bytes 196616 | tf_op jit(solution)/shard_map/ppermute | solution.py:187
  43.3 5.5 %collective-permute-start.18 = (bf16[64,128]{1,0:T(8,128)(2,1)S(1)}, bf16[64,128]{1,0:T(8,128)(2,1)S(1)}, u32[]{:S(2)}, u32[]{:S(2)}) collective-permute-start(bf16[64,128]{1,0:T(8,128)(2,1)S(1)} %get-tuple-element.77), channel_id=1, source_target_pairs={{0,24},{8,16},{16,8},{24,0},{1,25},{9,17},{17,9},{25,1},{2,26},{10... | collective-permute-start | bytes 49160 | tf_op jit(solution)/shard_map/ppermute | solution.py:187
  45.4 4.6 %collective-permute-start.19 = (bf16[64,128]{1,0:T(8,128)(2,1)S(1)}, bf16[64,128]{1,0:T(8,128)(2,1)S(1)}, u32[]{:S(2)}, u32[]{:S(2)}) collective-permute-start(bf16[64,128]{1,0:T(8,128)(2,1)S(1)} %get-tuple-element.78), channel_id=1, source_target_pairs={{0,16},{8,24},{16,0},{24,8},{1,17},{9,25},{17,1},{25,9},{2,18},{10... | collective-permute-start | bytes 49160 | tf_op jit(solution)/shard_map/ppermute | solution.py:187
  50.6 12.5 %collective-permute-start.25 = (bf16[64,1536]{1,0:T(8,128)(2,1)S(1)}, bf16[64,1536]{1,0:T(8,128)(2,1)S(1)}, u32[]{:S(2)}, u32[]{:S(2)}) collective-permute-start(bf16[64,1536]{1,0:T(8,128)(2,1)S(1)} %get-tuple-element.82), channel_id=1, source_target_pairs={{0,8},{8,0},{16,24},{24,16},{1,9},{9,1},{17,25},{25,17},{2,10},{10... | collective-permute-start | bytes 589832 | tf_op jit(solution)/shard_map/ppermute | solution.py:187
  50.6 12.4 %collective-permute-start.23 = (bf16[64,1024]{1,0:T(8,128)(2,1)S(1)}, bf16[64,1024]{1,0:T(8,128)(2,1)S(1)}, u32[]{:S(2)}, u32[]{:S(2)}) collective-permute-start(bf16[64,1024]{1,0:T(8,128)(2,1)S(1)} %get-tuple-element.80), channel_id=1, source_target_pairs={{0,16},{8,24},{16,0},{24,8},{1,17},{9,25},{17,1},{25,9},{2,18},{10... | collective-permute-start | bytes 393224 | tf_op jit(solution)/shard_map/ppermute | solution.py:187
  52.9 10.1 %collective-permute-start.24 = (bf16[64,1024]{1,0:T(8,128)(2,1)S(1)}, bf16[64,1024]{1,0:T(8,128)(2,1)S(1)}, u32[]{:S(2)}, u32[]{:S(2)}) collective-permute-start(bf16[64,1024]{1,0:T(8,128)(2,1)S(1)} %get-tuple-element.81), channel_id=1, source_target_pairs={{0,24},{8,16},{16,8},{24,0},{1,25},{9,17},{17,9},{25,1},{2,26},{10... | collective-permute-start | bytes 393224 | tf_op jit(solution)/shard_map/ppermute | solution.py:187
  55.0 3.3 %collective-permute-start.22 = (bf16[64,256]{1,0:T(8,128)(2,1)S(1)}, bf16[64,256]{1,0:T(8,128)(2,1)S(1)}, u32[]{:S(2)}, u32[]{:S(2)}) collective-permute-start(bf16[64,256]{1,0:T(8,128)(2,1)S(1)} %get-tuple-element.79.p0), channel_id=1, source_target_pairs={{0,3},{1,2},{2,1},{3,0},{4,7},{5,6},{6,5},{7,4},{8,11},{9,10},{10,... | collective-permute-start | bytes 98312 | tf_op jit(solution)/shard_map/ppermute | solution.py:187
  55.0 4.1 %collective-permute-start.21 = (bf16[64,256]{1,0:T(8,128)(2,1)S(1)}, bf16[64,256]{1,0:T(8,128)(2,1)S(1)}, u32[]{:S(2)}, u32[]{:S(2)}) collective-permute-start(bf16[64,256]{1,0:T(8,128)(2,1)S(1)} %get-tuple-element.79.p0), channel_id=1, source_target_pairs={{0,2},{1,3},{2,0},{3,1},{4,6},{5,7},{6,4},{7,5},{8,10},{9,11},{10,... | collective-permute-start | bytes 98312 | tf_op jit(solution)/shard_map/ppermute | solution.py:187
  58.3 1.2 %collective-permute-start.20 = (bf16[64,256]{1,0:T(8,128)(2,1)S(1)}, bf16[64,256]{1,0:T(8,128)(2,1)S(1)}, u32[]{:S(2)}, u32[]{:S(2)}) collective-permute-start(bf16[64,256]{1,0:T(8,128)(2,1)S(1)} %get-tuple-element.79.p0), channel_id=1, source_target_pairs={{0,1},{1,0},{2,3},{3,2},{4,5},{5,4},{6,7},{7,6},{8,9},{9,8},{10,11... | collective-permute-start | bytes 98312 | tf_op jit(solution)/shard_map/ppermute | solution.py:187

commit v12 on v11

--- a/solution.py
+++ b/solution.py
@@ -235,13 +235,12 @@
     seen = jnp.concatenate([own_seen, pool_seen], axis=0)
     bias = jnp.where(jnp.concatenate([seen, seen], axis=1), 0.0, HIDDEN).astype(F32)
 
-    mine = (fresh_queries, fresh_keys, fresh_values)
-    wo_pair, mine = lax.optimization_barrier((swap(wo_t, "y", 1), mine))
-    local = jnp.concatenate(mine, axis=1)
+    local = jnp.concatenate([fresh_queries, fresh_keys, fresh_values], axis=1)
     along[1:], bias, local = lax.optimization_barrier((along[1:], bias, local))
     across = [beside] + [swap(mine, "y", 1) for mine in along[1:]]
     blocks = [block for pair in zip(along, across) for block in pair]
-    blocks, wq_later = lax.optimization_barrier((blocks, w_qkv))
+    wo_pair = swap(wo_t, "y", 1)
+    blocks, wo_pair, wq_later = lax.optimization_barrier((blocks, wo_pair, w_qkv))
     wq_pair = swap(wq_later, "y", 1)
     attn, *sends = call(
         attend_kernel,

time: 64.2 us -> 60.9 us (0.949)
  waiting for transfers between devices: 28 us -> 24.4 us
  starting transfers between devices: 27.8 us -> 28.7 us
  other arithmetic: 4.22 us -> 3.5 us
    ppermute x26, waiting for transfers between devices: 28 us -> 24.4 us  [swap(): return lax.ppermute(value, axes, [(i, i ^ bits) for i in range(count)])]
    ppermute x26, starting transfers between devices: 27.8 us -> 28.7 us  [swap(): return lax.ppermute(value, axes, [(i, i ^ bits) for i in range(count)])]
    and x1, other arithmetic: 0.81 us -> 0.08 us  [on_block(): (requests[None, :] == requests[:, None]) & (positions[:, None] <= positio...]
  transfers between devices with their start and end apart: 26 -> 26, of which waited for: 15 -> 14; matrix products, arithmetic and copies ran while one was open for 7% -> 6% of each run, Pallas kernels for 3% -> 3%
where the time goes in v12:
time: 60.9 us; the launch traced here: 60.7 us
  starting transfers between devices  28.7 us (47%)
  waiting for transfers between devices  24.4 us (40%)
  other arithmetic  3.5 us (6%)
  Pallas kernels  3.17 us (5%)
  between operations  0.8 us (1%)
    ppermute x26, starting transfers between devices, swap(): return lax.ppermute(value, axes, [(i, i ^ bits) for i in range(count)])  28.7 us
    ppermute x26, waiting for transfers between devices, swap(): return lax.ppermute(value, axes, [(i, i ^ bits) for i in range(count)])  24.4 us
    pallas_call x5, Pallas kernels, call(): pl.pallas_call(kernel, out_shape=out_shape, in_specs=[vmem] * len(args),...  3.17 us
  transfers between devices with their start and end apart: 26, of which 14 were waited for; matrix products, arithmetic and copies ran while one was open for 6% of the time, Pallas kernels for 3%

profile of v12, /device:TPU:0, one launch (start us, length us, event | category | flops | bytes accessed | tf_op | source)
XLA Modules:
  0.0 60.7 jit_solution(11862902225493741129)
XLA Ops:
  0.7 5.1 %collective-permute-start.2 = (bf16[2,64,256]{2,1,0:T(8,128)(2,1)}, bf16[2,64,256]{2,1,0:T(8,128)(2,1)S(1)}, u32[]{:S(2)}, u32[]{:S(2)}) collective-permute-start(bf16[2,64,256]{2,1,0:T(8,128)(2,1)} %refs_0_), channel_id=1, source_target_pairs={{0,24},{8,16},{16,8},{24,0},{1,25},{9,17},{17,9},{25,1},{2,26},{10... | collective-permute-start | bytes 196616 | tf_op jit(solution)/shard_map/ppermute | solution.py:187
  6.4 1.7 %collective-permute-start.3 = (bf16[2,64,256]{2,1,0:T(8,128)(2,1)}, bf16[2,64,256]{2,1,0:T(8,128)(2,1)S(1)}, u32[]{:S(2)}, u32[]{:S(2)}) collective-permute-start(bf16[2,64,256]{2,1,0:T(8,128)(2,1)} %refs_0_), channel_id=1, source_target_pairs={{0,4},{4,0},{1,5},{5,1},{2,6},{6,2},{3,7},{7,3},{8,12},{12,8},{9,1... | collective-permute-start | bytes 196616 | tf_op jit(solution)/shard_map/ppermute | solution.py:187
  8.5 0.7 %select_reduce_fusion.3 = s32[64]{0:T(128)S(1)} fusion(s32[4]{0:T(128)} %bitcast.8, s32[64]{0:T(128)S(1)} %bitcast.7), kind=kLoop, calls=%fused_computation.13 | loop fusion | flops 704 | bytes 528 | tf_op jit(solution)/shard_map/reduce_sum | solution.py:39
  9.3 0.8 %select_reduce_fusion.2 = (s32[64]{0:T(128)S(1)}, s32[64]{0:T(128)S(1)}, s32[64]{0:T(128)S(1)}) fusion(s32[8]{0:T(128)} %param.21, s32[64]{0:T(128)S(1)} %select_reduce_fusion.3, s32[8]{0:T(128)} %param.20, s32[8]{0:T(128)} %param.19), kind=kLoop, calls=%fused_computation.11 | loop fusion | flops 3392 | bytes 1120 | tf_op jit(solution)/shard_map/reduce_sum | solution.py:220
  10.1 0.8 %broadcast_compare_fusion = (pred[8,32,64]{2,1,0:T(8,128)(4,1)S(1)}, pred[8,32,64]{2,1,0:T(8,128)(4,1)S(1)}) fusion(s32[64]{0:T(128)S(1)} %get-tuple-element.81, s32[8,32]{1,0:T(8,128)} %param.18, pred[32,64]{1,0:T(8,128)(4,1)S(1)} %iota_compare_fusion.1, pred[8,64]{1,0:T(8,128)(4,1)S(1)} %iota_compare_fusion.2), kind=kLoop, calls=%fused_computation.3 | loop fusion | flops 32768 | bytes 36608 | tf_op jit(solution)/shard_map/eq | solution.py:230
  11.1 0.9 %pad_maximum_fusion.local_ref = bf16[64,1024]{1,0:T(8,128)(2,1)S(1)} fusion(bf16[64,256]{1,0:T(8,128)(2,1)} %param.16, bf16[64,256]{1,0:T(8,128)(2,1)} %param.15, bf16[64,512]{1,0:T(8,128)(2,1)} %param.14), kind=kLoop, calls=%fused_computation.2 | loop fusion | flops 393216 | bytes 262144 | tf_op jit(solution)/shard_map/concatenate | solution.py:238
  12.0 1.7 %collective-permute-start.4 = (bf16[2,64,256]{2,1,0:T(8,128)(2,1)S(1)}, bf16[2,64,256]{2,1,0:T(8,128)(2,1)S(1)}, u32[]{:S(2)}, u32[]{:S(2)}) collective-permute-start(bf16[2,64,256]{2,1,0:T(8,128)(2,1)S(1)} %collective-permute-done.refs_2_), channel_id=1, source_target_pairs={{0,4},{4,0},{1,5},{5,1},{2,6},{6,2},{3,7},{7,3},{8,12},{12,8},{9,1... | collective-permute-start | bytes 196616 | tf_op jit(solution)/shard_map/ppermute | solution.py:187
  14.1 1.7 %collective-permute-start.6 = (bf16[2,64,256]{2,1,0:T(8,128)(2,1)S(1)}, bf16[2,64,256]{2,1,0:T(8,128)(2,1)S(1)}, u32[]{:S(2)}, u32[]{:S(2)}) collective-permute-start(bf16[2,64,256]{2,1,0:T(8,128)(2,1)S(1)} %collective-permute-done.2.refs_6_), channel_id=1, source_target_pairs={{0,4},{4,0},{1,5},{5,1},{2,6},{6,2},{3,7},{7,3},{8,12},{12,8},{9,1... | collective-permute-start | bytes 196616 | tf_op jit(solution)/shard_map/ppermute | solution.py:187
  15.8 3.1 %collective-permute-done.4.refs_3_ = bf16[2,64,256]{2,1,0:T(8,128)(2,1)S(1)} collective-permute-done((bf16[2,64,256]{2,1,0:T(8,128)(2,1)S(1)}, bf16[2,64,256]{2,1,0:T(8,128)(2,1)S(1)}, u32[]{:S(2)}, u32[]{:S(2)}) %collective-permute-start.4) | collective-permute-done | bytes 65568 | tf_op jit(solution)/shard_map/ppermute | solution.py:187
  18.9 0.7 %collective-permute-done.5.refs_5_ = bf16[2,64,256]{2,1,0:T(8,128)(2,1)S(1)} collective-permute-done((bf16[2,64,256]{2,1,0:T(8,128)(2,1)S(1)}, bf16[2,64,256]{2,1,0:T(8,128)(2,1)S(1)}, u32[]{:S(2)}, u32[]{:S(2)}) %collective-permute-start.5) | collective-permute-done | bytes 65568 | tf_op jit(solution)/shard_map/ppermute | solution.py:187
  19.6 0.7 %collective-permute-done.6.refs_7_ = bf16[2,64,256]{2,1,0:T(8,128)(2,1)S(1)} collective-permute-done((bf16[2,64,256]{2,1,0:T(8,128)(2,1)S(1)}, bf16[2,64,256]{2,1,0:T(8,128)(2,1)S(1)}, u32[]{:S(2)}, u32[]{:S(2)}) %collective-permute-start.6) | collective-permute-done | bytes 65568 | tf_op jit(solution)/shard_map/ppermute | solution.py:187
  20.3 1.0 %collective-permute-start.14 = (bf16[256,1024]{1,0:T(8,128)(2,1)S(1)}, bf16[256,1024]{1,0:T(8,128)(2,1)S(1)}, u32[]{:S(2)}, u32[]{:S(2)}) collective-permute-start(bf16[256,1024]{1,0:T(8,128)(2,1)S(1)} %copy-done), channel_id=1, source_target_pairs={{0,4},{4,0},{1,5},{5,1},{2,6},{6,2},{3,7},{7,3},{8,12},{12,8},{9,1... | collective-permute-start | bytes 1572872 | tf_op jit(solution)/shard_map/ppermute | solution.py:187
  21.3 1.3 %shard_map.157 = (bf16[64,512]{1,0:T(8,128)(2,1)}, bf16[64,640]{1,0:T(8,128)(2,1)S(1)}, bf16[64,640]{1,0:T(8,128)(2,1)S(1)}, bf16[64,640]{1,0:T(8,128)(2,1)S(1)}, bf16[64,640]{1,0:T(8,128)(2,1)S(1)}) custom-call(bf16[64,1024]{1,0:T(8,128)(2,1)S(1)} %pad_maximum_fusion.local_ref, bf16[64,2048]{1,0:T(8,128)(2,1)S(1)} %copy-done.1, ...), custom_call_target="tpu_custom_call" | custom-call | flops 67108864 | bytes 1048576 | tf_op jit(solution)/shard_map/pallas_call | solution.py:174
  22.6 2.3 %collective-permute-start.8 = (bf16[64,640]{1,0:T(8,128)(2,1)S(1)}, bf16[64,640]{1,0:T(8,128)(2,1)S(1)}, u32[]{:S(2)}, u32[]{:S(2)}) collective-permute-start(bf16[64,640]{1,0:T(8,128)(2,1)S(1)} %get-tuple-element.56), channel_id=1, source_target_pairs={{0,16},{8,24},{16,0},{24,8},{1,17},{9,25},{17,1},{25,9},{2,18},{10... | collective-permute-start | bytes 245768 | tf_op jit(solution)/shard_map/ppermute | solution.py:187
  24.8 1.5 %collective-permute-start.9 = (bf16[64,640]{1,0:T(8,128)(2,1)S(1)}, bf16[64,640]{1,0:T(8,128)(2,1)S(1)}, u32[]{:S(2)}, u32[]{:S(2)}) collective-permute-start(bf16[64,640]{1,0:T(8,128)(2,1)S(1)} %get-tuple-element.57), channel_id=1, source_target_pairs={{0,24},{8,16},{16,8},{24,0},{1,25},{9,17},{17,9},{25,1},{2,26},{10... | collective-permute-start | bytes 245768 | tf_op jit(solution)/shard_map/ppermute | solution.py:187
  26.6 3.1 %collective-permute-done.8.a2 = bf16[64,640]{1,0:T(8,128)(2,1)S(1)} collective-permute-done((bf16[64,640]{1,0:T(8,128)(2,1)S(1)}, bf16[64,640]{1,0:T(8,128)(2,1)S(1)}, u32[]{:S(2)}, u32[]{:S(2)}) %collective-permute-start.8) | collective-permute-done | bytes 81952 | tf_op jit(solution)/shard_map/ppermute | solution.py:187
  29.7 1.5 %collective-permute-done.9.a3 = bf16[64,640]{1,0:T(8,128)(2,1)S(1)} collective-permute-done((bf16[64,640]{1,0:T(8,128)(2,1)S(1)}, bf16[64,640]{1,0:T(8,128)(2,1)S(1)}, u32[]{:S(2)}, u32[]{:S(2)}) %collective-permute-start.9) | collective-permute-done | bytes 81952 | tf_op jit(solution)/shard_map/ppermute | solution.py:187
  32.1 1.6 %collective-permute-start.11 = (bf16[256,128]{1,0:T(8,128)(2,1)S(1)}, bf16[256,128]{1,0:T(8,128)(2,1)S(1)}, u32[]{:S(2)}, u32[]{:S(2)}) collective-permute-start(bf16[256,128]{1,0:T(8,128)(2,1)S(1)} %get-tuple-element.61), channel_id=1, source_target_pairs={{0,2},{1,3},{2,0},{3,1},{4,6},{5,7},{6,4},{7,5},{8,10},{9,11},{10,... | collective-permute-start | bytes 196616 | tf_op jit(solution)/shard_map/ppermute | solution.py:187
  34.3 2.1 %collective-permute-done.11.r2 = bf16[256,128]{1,0:T(8,128)(2,1)S(1)} collective-permute-done((bf16[256,128]{1,0:T(8,128)(2,1)S(1)}, bf16[256,128]{1,0:T(8,128)(2,1)S(1)}, u32[]{:S(2)}, u32[]{:S(2)}) %collective-permute-start.11) | collective-permute-done | bytes 65568 | tf_op jit(solution)/shard_map/ppermute | solution.py:187
  36.4 1.4 %collective-permute-done.12.r3 = bf16[256,128]{1,0:T(8,128)(2,1)S(1)} collective-permute-done((bf16[256,128]{1,0:T(8,128)(2,1)S(1)}, bf16[256,128]{1,0:T(8,128)(2,1)S(1)}, u32[]{:S(2)}, u32[]{:S(2)}) %collective-permute-start.12) | collective-permute-done | bytes 65568 | tf_op jit(solution)/shard_map/ppermute | solution.py:187
  37.9 0.9 %collective-permute-start.17 = (bf16[256,128]{1,0:T(8,128)(2,1)S(1)}, bf16[256,128]{1,0:T(8,128)(2,1)S(1)}, u32[]{:S(2)}, u32[]{:S(2)}) collective-permute-start(bf16[256,128]{1,0:T(8,128)(2,1)S(1)} %get-tuple-element.69.x0), channel_id=1, source_target_pairs={{0,3},{1,2},{2,1},{3,0},{4,7},{5,6},{6,5},{7,4},{8,11},{9,10},{10,... | collective-permute-start | bytes 196616 | tf_op jit(solution)/shard_map/ppermute | solution.py:187
  38.8 0.7 %collective-permute-start.16 = (bf16[256,128]{1,0:T(8,128)(2,1)S(1)}, bf16[256,128]{1,0:T(8,128)(2,1)S(1)}, u32[]{:S(2)}, u32[]{:S(2)}) collective-permute-start(bf16[256,128]{1,0:T(8,128)(2,1)S(1)} %get-tuple-element.69.x0), channel_id=1, source_target_pairs={{0,2},{1,3},{2,0},{3,1},{4,6},{5,7},{6,4},{7,5},{8,10},{9,11},{10,... | collective-permute-start | bytes 196616 | tf_op jit(solution)/shard_map/ppermute | solution.py:187
  39.8 2.5 %collective-permute-start.18 = (bf16[64,128]{1,0:T(8,128)(2,1)S(1)}, bf16[64,128]{1,0:T(8,128)(2,1)S(1)}, u32[]{:S(2)}, u32[]{:S(2)}) collective-permute-start(bf16[64,128]{1,0:T(8,128)(2,1)S(1)} %get-tuple-element.71), channel_id=1, source_target_pairs={{0,24},{8,16},{16,8},{24,0},{1,25},{9,17},{17,9},{25,1},{2,26},{10... | collective-permute-start | bytes 49160 | tf_op jit(solution)/shard_map/ppermute | solution.py:187
  42.3 3.0 %collective-permute-done.18.t3 = bf16[64,128]{1,0:T(8,128)(2,1)S(1)} collective-permute-done((bf16[64,128]{1,0:T(8,128)(2,1)S(1)}, bf16[64,128]{1,0:T(8,128)(2,1)S(1)}, u32[]{:S(2)}, u32[]{:S(2)}) %collective-permute-start.18) | collective-permute-done | bytes 16416 | tf_op jit(solution)/shard_map/ppermute | solution.py:187
  45.3 1.6 %collective-permute-done.19.t2 = bf16[64,128]{1,0:T(8,128)(2,1)S(1)} collective-permute-done((bf16[64,128]{1,0:T(8,128)(2,1)S(1)}, bf16[64,128]{1,0:T(8,128)(2,1)S(1)}, u32[]{:S(2)}, u32[]{:S(2)}) %collective-permute-start.19) | collective-permute-done | bytes 16416 | tf_op jit(solution)/shard_map/ppermute | solution.py:187
  47.6 1.8 %collective-permute-start.23 = (bf16[64,1024]{1,0:T(8,128)(2,1)S(1)}, bf16[64,1024]{1,0:T(8,128)(2,1)S(1)}, u32[]{:S(2)}, u32[]{:S(2)}) collective-permute-start(bf16[64,1024]{1,0:T(8,128)(2,1)S(1)} %get-tuple-element.74), channel_id=1, source_target_pairs={{0,16},{8,24},{16,0},{24,8},{1,17},{9,25},{17,1},{25,9},{2,18},{10... | collective-permute-start | bytes 393224 | tf_op jit(solution)/shard_map/ppermute | solution.py:187
  49.4 2.5 %collective-permute-start.24 = (bf16[64,1024]{1,0:T(8,128)(2,1)S(1)}, bf16[64,1024]{1,0:T(8,128)(2,1)S(1)}, u32[]{:S(2)}, u32[]{:S(2)}) collective-permute-start(bf16[64,1024]{1,0:T(8,128)(2,1)S(1)} %get-tuple-element.75), channel_id=1, source_target_pairs={{0,24},{8,16},{16,8},{24,0},{1,25},{9,17},{17,9},{25,1},{2,26},{10... | collective-permute-start | bytes 393224 | tf_op jit(solution)/shard_map/ppermute | solution.py:187
  52.0 1.1 %collective-permute-start.21 = (bf16[64,256]{1,0:T(8,128)(2,1)S(1)}, bf16[64,256]{1,0:T(8,128)(2,1)S(1)}, u32[]{:S(2)}, u32[]{:S(2)}) collective-permute-start(bf16[64,256]{1,0:T(8,128)(2,1)S(1)} %get-tuple-element.73.p0), channel_id=1, source_target_pairs={{0,2},{1,3},{2,0},{3,1},{4,6},{5,7},{6,4},{7,5},{8,10},{9,11},{10,... | collective-permute-start | bytes 98312 | tf_op jit(solution)/shard_map/ppermute | solution.py:187
  53.0 2.3 %collective-permute-done.22.p3 = bf16[64,256]{1,0:T(8,128)(2,1)S(1)} collective-permute-done((bf16[64,256]{1,0:T(8,128)(2,1)S(1)}, bf16[64,256]{1,0:T(8,128)(2,1)S(1)}, u32[]{:S(2)}, u32[]{:S(2)}) %collective-permute-start.22) | collective-permute-done | bytes 32800 | tf_op jit(solution)/shard_map/ppermute | solution.py:187
  55.3 0.8 %collective-permute-done.21.p2 = bf16[64,256]{1,0:T(8,128)(2,1)S(1)} collective-permute-done((bf16[64,256]{1,0:T(8,128)(2,1)S(1)}, bf16[64,256]{1,0:T(8,128)(2,1)S(1)}, u32[]{:S(2)}, u32[]{:S(2)}) %collective-permute-start.21) | collective-permute-done | bytes 32800 | tf_op jit(solution)/shard_map/ppermute | solution.py:187
  56.5 3.3 %collective-permute-done.23.y2 = bf16[64,1024]{1,0:T(8,128)(2,1)S(1)} collective-permute-done((bf16[64,1024]{1,0:T(8,128)(2,1)S(1)}, bf16[64,1024]{1,0:T(8,128)(2,1)S(1)}, u32[]{:S(2)}, u32[]{:S(2)}) %collective-permute-start.23) | collective-permute-done | bytes 131104 | tf_op jit(solution)/shard_map/ppermute | solution.py:187
  59.8 0.9 %shard_map.161 = (bf16[64,1024]{1,0:T(8,128)(2,1)}, bf16[64,2048]{1,0:T(8,128)(2,1)}) custom-call(bf16[64,256]{1,0:T(8,128)(2,1)S(1)} %get-tuple-element.73.p0, bf16[64,256]{1,0:T(8,128)(2,1)S(1)} %collective-permute-done.20.p1, bf16[64,256]{1,0:T(8,128)(2,1)S(1)} %collective-permute-done.21.p2, bf16[64,256]{1,0:T(8,128)(2,1)S(1)} %collective-permute-done.22.p3, ...), custom_call_target="tpu_custom_call" | custom-call | bytes 1048576 | tf_op jit(solution)/shard_map/pallas_call | solution.py:174
  (46 shorter events, 4.8 us)
Async XLA Ops:
  0.6 7.8 %copy-start.5 = (s32[1,64]{1,0:T(1,128)S(1)}, s32[1,64]{1,0:T(1,128)}, u32[]{:S(2)}) copy-start(s32[1,64]{1,0:T(1,128)} %param.23) | copy-start | bytes 772
  0.6 19.6 %copy-start = (bf16[256,1024]{1,0:T(8,128)(2,1)S(1)}, bf16[256,1024]{1,0:T(8,128)(2,1)}, u32[]{:S(2)}) copy-start(bf16[256,1024]{1,0:T(8,128)(2,1)} %own_ref.3) | copy-start | bytes 1572868
  0.7 11.4 %collective-permute-start.2 = (bf16[2,64,256]{2,1,0:T(8,128)(2,1)}, bf16[2,64,256]{2,1,0:T(8,128)(2,1)S(1)}, u32[]{:S(2)}, u32[]{:S(2)}) collective-permute-start(bf16[2,64,256]{2,1,0:T(8,128)(2,1)} %refs_0_), channel_id=1, source_target_pairs={{0,24},{8,16},{16,8},{24,0},{1,25},{9,17},{17,9},{25,1},{2,26},{10... | collective-permute-start | bytes 196616 | tf_op jit(solution)/shard_map/ppermute | solution.py:187
  5.8 6.3 %collective-permute-start.1 = (bf16[2,64,256]{2,1,0:T(8,128)(2,1)}, bf16[2,64,256]{2,1,0:T(8,128)(2,1)S(1)}, u32[]{:S(2)}, u32[]{:S(2)}) collective-permute-start(bf16[2,64,256]{2,1,0:T(8,128)(2,1)} %refs_0_), channel_id=1, source_target_pairs={{0,16},{8,24},{16,0},{24,8},{1,17},{9,25},{17,1},{25,9},{2,18},{10... | collective-permute-start | bytes 196616 | tf_op jit(solution)/shard_map/ppermute | solution.py:187
  5.8 6.3 %collective-permute-start = (bf16[2,64,256]{2,1,0:T(8,128)(2,1)}, bf16[2,64,256]{2,1,0:T(8,128)(2,1)S(1)}, u32[]{:S(2)}, u32[]{:S(2)}) collective-permute-start(bf16[2,64,256]{2,1,0:T(8,128)(2,1)} %refs_0_), channel_id=1, source_target_pairs={{0,8},{8,0},{16,24},{24,16},{1,9},{9,1},{17,25},{25,17},{2,10},{10... | collective-permute-start | bytes 196616 | tf_op jit(solution)/shard_map/ppermute | solution.py:187
  6.4 9.4 %collective-permute-start.3 = (bf16[2,64,256]{2,1,0:T(8,128)(2,1)}, bf16[2,64,256]{2,1,0:T(8,128)(2,1)S(1)}, u32[]{:S(2)}, u32[]{:S(2)}) collective-permute-start(bf16[2,64,256]{2,1,0:T(8,128)(2,1)} %refs_0_), channel_id=1, source_target_pairs={{0,4},{4,0},{1,5},{5,1},{2,6},{6,2},{3,7},{7,3},{8,12},{12,8},{9,1... | collective-permute-start | bytes 196616 | tf_op jit(solution)/shard_map/ppermute | solution.py:187
  8.1 12.2 %collective-permute-start.7 = (bf16[256,512]{1,0:T(8,128)(2,1)}, bf16[256,512]{1,0:T(8,128)(2,1)S(1)}, u32[]{:S(2)}, u32[]{:S(2)}) collective-permute-start(bf16[256,512]{1,0:T(8,128)(2,1)} %own_ref.2), channel_id=1, source_target_pairs={{0,4},{4,0},{1,5},{5,1},{2,6},{6,2},{3,7},{7,3},{8,12},{12,8},{9,1... | collective-permute-start | bytes 786440 | tf_op jit(solution)/shard_map/ppermute | solution.py:187
  10.9 10.4 %copy-start.1 = (bf16[64,2048]{1,0:T(8,128)(2,1)S(1)}, bf16[64,2048]{1,0:T(8,128)(2,1)}, u32[]{:S(2)}) copy-start(bf16[64,2048]{1,0:T(8,128)(2,1)} %res_ref.1) | copy-start | bytes 786436
  11.1 10.2 %copy-start.3 = (bf16[2,64,256]{2,1,0:T(8,128)(2,1)S(1)}, bf16[2,64,256]{2,1,0:T(8,128)(2,1)}, u32[]{:S(2)}) copy-start(bf16[2,64,256]{2,1,0:T(8,128)(2,1)} %refs_0_) | copy-start | bytes 196612
  12.0 19.6 %copy-start.2 = (bf16[256,512]{1,0:T(8,128)(2,1)S(1)}, bf16[256,512]{1,0:T(8,128)(2,1)}, u32[]{:S(2)}) copy-start(bf16[256,512]{1,0:T(8,128)(2,1)} %own_ref.2) | copy-start | bytes 786436
  12.0 6.8 %collective-permute-start.4 = (bf16[2,64,256]{2,1,0:T(8,128)(2,1)S(1)}, bf16[2,64,256]{2,1,0:T(8,128)(2,1)S(1)}, u32[]{:S(2)}, u32[]{:S(2)}) collective-permute-start(bf16[2,64,256]{2,1,0:T(8,128)(2,1)S(1)} %collective-permute-done.refs_2_), channel_id=1, source_target_pairs={{0,4},{4,0},{1,5},{5,1},{2,6},{6,2},{3,7},{7,3},{8,12},{12,8},{9,1... | collective-permute-start | bytes 196616 | tf_op jit(solution)/shard_map/ppermute | solution.py:187
  13.8 5.8 %collective-permute-start.5 = (bf16[2,64,256]{2,1,0:T(8,128)(2,1)S(1)}, bf16[2,64,256]{2,1,0:T(8,128)(2,1)S(1)}, u32[]{:S(2)}, u32[]{:S(2)}) collective-permute-start(bf16[2,64,256]{2,1,0:T(8,128)(2,1)S(1)} %collective-permute-done.1.refs_4_), channel_id=1, source_target_pairs={{0,4},{4,0},{1,5},{5,1},{2,6},{6,2},{3,7},{7,3},{8,12},{12,8},{9,1... | collective-permute-start | bytes 196616 | tf_op jit(solution)/shard_map/ppermute | solution.py:187
  14.1 6.1 %collective-permute-start.6 = (bf16[2,64,256]{2,1,0:T(8,128)(2,1)S(1)}, bf16[2,64,256]{2,1,0:T(8,128)(2,1)S(1)}, u32[]{:S(2)}, u32[]{:S(2)}) collective-permute-start(bf16[2,64,256]{2,1,0:T(8,128)(2,1)S(1)} %collective-permute-done.2.refs_6_), channel_id=1, source_target_pairs={{0,4},{4,0},{1,5},{5,1},{2,6},{6,2},{3,7},{7,3},{8,12},{12,8},{9,1... | collective-permute-start | bytes 196616 | tf_op jit(solution)/shard_map/ppermute | solution.py:187
  20.3 17.6 %collective-permute-start.14 = (bf16[256,1024]{1,0:T(8,128)(2,1)S(1)}, bf16[256,1024]{1,0:T(8,128)(2,1)S(1)}, u32[]{:S(2)}, u32[]{:S(2)}) collective-permute-start(bf16[256,1024]{1,0:T(8,128)(2,1)S(1)} %copy-done), channel_id=1, source_target_pairs={{0,4},{4,0},{1,5},{5,1},{2,6},{6,2},{3,7},{7,3},{8,12},{12,8},{9,1... | collective-permute-start | bytes 1572872 | tf_op jit(solution)/shard_map/ppermute | solution.py:187
  22.6 7.2 %collective-permute-start.8 = (bf16[64,640]{1,0:T(8,128)(2,1)S(1)}, bf16[64,640]{1,0:T(8,128)(2,1)S(1)}, u32[]{:S(2)}, u32[]{:S(2)}) collective-permute-start(bf16[64,640]{1,0:T(8,128)(2,1)S(1)} %get-tuple-element.56), channel_id=1, source_target_pairs={{0,16},{8,24},{16,0},{24,8},{1,17},{9,25},{17,1},{25,9},{2,18},{10... | collective-permute-start | bytes 245768 | tf_op jit(solution)/shard_map/ppermute | solution.py:187
  24.8 6.4 %collective-permute-start.9 = (bf16[64,640]{1,0:T(8,128)(2,1)S(1)}, bf16[64,640]{1,0:T(8,128)(2,1)S(1)}, u32[]{:S(2)}, u32[]{:S(2)}) collective-permute-start(bf16[64,640]{1,0:T(8,128)(2,1)S(1)} %get-tuple-element.57), channel_id=1, source_target_pairs={{0,24},{8,16},{16,8},{24,0},{1,25},{9,17},{17,9},{25,1},{2,26},{10... | collective-permute-start | bytes 245768 | tf_op jit(solution)/shard_map/ppermute | solution.py:187
  26.3 5.3 %collective-permute-start.10 = (bf16[64,640]{1,0:T(8,128)(2,1)S(1)}, bf16[64,640]{1,0:T(8,128)(2,1)S(1)}, u32[]{:S(2)}, u32[]{:S(2)}) collective-permute-start(bf16[64,640]{1,0:T(8,128)(2,1)S(1)} %get-tuple-element.58), channel_id=1, source_target_pairs={{0,8},{8,0},{16,24},{24,16},{1,9},{9,1},{17,25},{25,17},{2,10},{10... | collective-permute-start | bytes 245768 | tf_op jit(solution)/shard_map/ppermute | solution.py:187
  32.1 4.3 %collective-permute-start.11 = (bf16[256,128]{1,0:T(8,128)(2,1)S(1)}, bf16[256,128]{1,0:T(8,128)(2,1)S(1)}, u32[]{:S(2)}, u32[]{:S(2)}) collective-permute-start(bf16[256,128]{1,0:T(8,128)(2,1)S(1)} %get-tuple-element.61), channel_id=1, source_target_pairs={{0,2},{1,3},{2,0},{3,1},{4,6},{5,7},{6,4},{7,5},{8,10},{9,11},{10,... | collective-permute-start | bytes 196616 | tf_op jit(solution)/shard_map/ppermute | solution.py:187
  33.6 4.2 %collective-permute-start.12 = (bf16[256,128]{1,0:T(8,128)(2,1)S(1)}, bf16[256,128]{1,0:T(8,128)(2,1)S(1)}, u32[]{:S(2)}, u32[]{:S(2)}) collective-permute-start(bf16[256,128]{1,0:T(8,128)(2,1)S(1)} %get-tuple-element.62), channel_id=1, source_target_pairs={{0,3},{1,2},{2,1},{3,0},{4,7},{5,6},{6,5},{7,4},{8,11},{9,10},{10,... | collective-permute-start | bytes 196616 | tf_op jit(solution)/shard_map/ppermute | solution.py:187
  33.6 4.2 %collective-permute-start.13 = (bf16[256,128]{1,0:T(8,128)(2,1)S(1)}, bf16[256,128]{1,0:T(8,128)(2,1)S(1)}, u32[]{:S(2)}, u32[]{:S(2)}) collective-permute-start(bf16[256,128]{1,0:T(8,128)(2,1)S(1)} %get-tuple-element.63), channel_id=1, source_target_pairs={{0,1},{1,0},{2,3},{3,2},{4,5},{5,4},{6,7},{7,6},{8,9},{9,8},{10,11... | collective-permute-start | bytes 196616 | tf_op jit(solution)/shard_map/ppermute | solution.py:187
  37.8 9.2 %copy-start.4 = (f32[2048]{0:T(1024)S(1)}, f32[2048]{0:T(1024)}, u32[]{:S(2)}) copy-start(f32[2048]{0:T(1024)} %param.26) | copy-start | bytes 24580
  37.9 9.1 %collective-permute-start.17 = (bf16[256,128]{1,0:T(8,128)(2,1)S(1)}, bf16[256,128]{1,0:T(8,128)(2,1)S(1)}, u32[]{:S(2)}, u32[]{:S(2)}) collective-permute-start(bf16[256,128]{1,0:T(8,128)(2,1)S(1)} %get-tuple-element.69.x0), channel_id=1, source_target_pairs={{0,3},{1,2},{2,1},{3,0},{4,7},{5,6},{6,5},{7,4},{8,11},{9,10},{10,... | collective-permute-start | bytes 196616 | tf_op jit(solution)/shard_map/ppermute | solution.py:187
  38.8 8.2 %collective-permute-start.16 = (bf16[256,128]{1,0:T(8,128)(2,1)S(1)}, bf16[256,128]{1,0:T(8,128)(2,1)S(1)}, u32[]{:S(2)}, u32[]{:S(2)}) collective-permute-start(bf16[256,128]{1,0:T(8,128)(2,1)S(1)} %get-tuple-element.69.x0), channel_id=1, source_target_pairs={{0,2},{1,3},{2,0},{3,1},{4,6},{5,7},{6,4},{7,5},{8,10},{9,11},{10,... | collective-permute-start | bytes 196616 | tf_op jit(solution)/shard_map/ppermute | solution.py:187
  39.5 7.5 %collective-permute-start.15 = (bf16[256,128]{1,0:T(8,128)(2,1)S(1)}, bf16[256,128]{1,0:T(8,128)(2,1)S(1)}, u32[]{:S(2)}, u32[]{:S(2)}) collective-permute-start(bf16[256,128]{1,0:T(8,128)(2,1)S(1)} %get-tuple-element.69.x0), channel_id=1, source_target_pairs={{0,1},{1,0},{2,3},{3,2},{4,5},{5,4},{6,7},{7,6},{8,9},{9,8},{10,11... | collective-permute-start | bytes 196616 | tf_op jit(solution)/shard_map/ppermute | solution.py:187
  39.8 5.6 %collective-permute-start.18 = (bf16[64,128]{1,0:T(8,128)(2,1)S(1)}, bf16[64,128]{1,0:T(8,128)(2,1)S(1)}, u32[]{:S(2)}, u32[]{:S(2)}) collective-permute-start(bf16[64,128]{1,0:T(8,128)(2,1)S(1)} %get-tuple-element.71), channel_id=1, source_target_pairs={{0,24},{8,16},{16,8},{24,0},{1,25},{9,17},{17,9},{25,1},{2,26},{10... | collective-permute-start | bytes 49160 | tf_op jit(solution)/shard_map/ppermute | solution.py:187
  42.3 4.6 %collective-permute-start.19 = (bf16[64,128]{1,0:T(8,128)(2,1)S(1)}, bf16[64,128]{1,0:T(8,128)(2,1)S(1)}, u32[]{:S(2)}, u32[]{:S(2)}) collective-permute-start(bf16[64,128]{1,0:T(8,128)(2,1)S(1)} %get-tuple-element.72), channel_id=1, source_target_pairs={{0,16},{8,24},{16,0},{24,8},{1,17},{9,25},{17,1},{25,9},{2,18},{10... | collective-permute-start | bytes 49160 | tf_op jit(solution)/shard_map/ppermute | solution.py:187
  47.5 12.3 %collective-permute-start.25 = (bf16[64,1536]{1,0:T(8,128)(2,1)S(1)}, bf16[64,1536]{1,0:T(8,128)(2,1)S(1)}, u32[]{:S(2)}, u32[]{:S(2)}) collective-permute-start(bf16[64,1536]{1,0:T(8,128)(2,1)S(1)} %get-tuple-element.76), channel_id=1, source_target_pairs={{0,8},{8,0},{16,24},{24,16},{1,9},{9,1},{17,25},{25,17},{2,10},{10... | collective-permute-start | bytes 589832 | tf_op jit(solution)/shard_map/ppermute | solution.py:187
  47.6 12.2 %collective-permute-start.23 = (bf16[64,1024]{1,0:T(8,128)(2,1)S(1)}, bf16[64,1024]{1,0:T(8,128)(2,1)S(1)}, u32[]{:S(2)}, u32[]{:S(2)}) collective-permute-start(bf16[64,1024]{1,0:T(8,128)(2,1)S(1)} %get-tuple-element.74), channel_id=1, source_target_pairs={{0,16},{8,24},{16,0},{24,8},{1,17},{9,25},{17,1},{25,9},{2,18},{10... | collective-permute-start | bytes 393224 | tf_op jit(solution)/shard_map/ppermute | solution.py:187
  49.4 10.4 %collective-permute-start.24 = (bf16[64,1024]{1,0:T(8,128)(2,1)S(1)}, bf16[64,1024]{1,0:T(8,128)(2,1)S(1)}, u32[]{:S(2)}, u32[]{:S(2)}) collective-permute-start(bf16[64,1024]{1,0:T(8,128)(2,1)S(1)} %get-tuple-element.75), channel_id=1, source_target_pairs={{0,24},{8,16},{16,8},{24,0},{1,25},{9,17},{17,9},{25,1},{2,26},{10... | collective-permute-start | bytes 393224 | tf_op jit(solution)/shard_map/ppermute | solution.py:187
  51.9 3.3 %collective-permute-start.22 = (bf16[64,256]{1,0:T(8,128)(2,1)S(1)}, bf16[64,256]{1,0:T(8,128)(2,1)S(1)}, u32[]{:S(2)}, u32[]{:S(2)}) collective-permute-start(bf16[64,256]{1,0:T(8,128)(2,1)S(1)} %get-tuple-element.73.p0), channel_id=1, source_target_pairs={{0,3},{1,2},{2,1},{3,0},{4,7},{5,6},{6,5},{7,4},{8,11},{9,10},{10,... | collective-permute-start | bytes 98312 | tf_op jit(solution)/shard_map/ppermute | solution.py:187
  52.0 4.1 %collective-permute-start.21 = (bf16[64,256]{1,0:T(8,128)(2,1)S(1)}, bf16[64,256]{1,0:T(8,128)(2,1)S(1)}, u32[]{:S(2)}, u32[]{:S(2)}) collective-permute-start(bf16[64,256]{1,0:T(8,128)(2,1)S(1)} %get-tuple-element.73.p0), channel_id=1, source_target_pairs={{0,2},{1,3},{2,0},{3,1},{4,6},{5,7},{6,4},{7,5},{8,10},{9,11},{10,... | collective-permute-start | bytes 98312 | tf_op jit(solution)/shard_map/ppermute | solution.py:187
  55.3 1.2 %collective-permute-start.20 = (bf16[64,256]{1,0:T(8,128)(2,1)S(1)}, bf16[64,256]{1,0:T(8,128)(2,1)S(1)}, u32[]{:S(2)}, u32[]{:S(2)}) collective-permute-start(bf16[64,256]{1,0:T(8,128)(2,1)S(1)} %get-tuple-element.73.p0), channel_id=1, source_target_pairs={{0,1},{1,0},{2,3},{3,2},{4,5},{5,4},{6,7},{7,6},{8,9},{9,8},{10,11... | collective-permute-start | bytes 98312 | tf_op jit(solution)/shard_map/ppermute | solution.py:187

commit v13 on v12

--- a/solution.py
+++ b/solution.py
@@ -58,8 +58,14 @@
     return 2 * lax.axis_index("x") + lax.axis_index("c")
 
 
+def join_kernel(z1, z2, z3, out_ref):
+    for i, part in enumerate((z1, z2, z3)):
+        out_ref[2 * i : 2 * i + 2] = part[...]
+
+
 def attend_kernel(local_ref, res_ref, bias_ref, *refs):
-    caches, out_ref, sends = refs[:-5], refs[-5], refs[-4:]
+    own, beside, z1, z2, z3, moved, out_ref, *sends = refs
+    caches = (own, beside, z1, moved.at[:2], z2, moved.at[2:4], z3, moved.at[4:])
     e, m = seq_index(), mp_index()
     tok, wide = out_ref.shape
     kv = caches[0].shape[2]
@@ -237,8 +243,10 @@
 
     local = jnp.concatenate([fresh_queries, fresh_keys, fresh_values], axis=1)
     along[1:], bias, local = lax.optimization_barrier((along[1:], bias, local))
-    across = [beside] + [swap(mine, "y", 1) for mine in along[1:]]
-    blocks = [block for pair in zip(along, across) for block in pair]
+    joined = call(
+        join_kernel, sds((3 * cache.shape[0],) + cache.shape[1:], BF16), tuple(along[1:])
+    )
+    blocks = [cache, beside, *along[1:], swap(joined, "y", 1)]
     wo_pair = swap(wo_t, "y", 1)
     blocks, wo_pair, wq_later = lax.optimization_barrier((blocks, wo_pair, w_qkv))
     wq_pair = swap(wq_later, "y", 1)

time: 60.9 us -> 60.9 us (level)
  other arithmetic: 3.5 us -> 0.56 us
  local copies, waits for them, and re-layouts: 0.03 us -> 2.56 us
  waiting for transfers between devices: 24.4 us -> 26.4 us
  starting transfers between devices: 28.7 us -> 27.1 us
    unnamed x12 -> x28, local copies, waits for them, and re-layouts: 0.03 us -> 2.56 us
    ppermute x26 -> x24, waiting for transfers between devices: 24.4 us -> 26.4 us  [swap(): return lax.ppermute(value, axes, [(i, i ^ bits) for i in range(count)])]
    ppermute x26 -> x24, starting transfers between devices: 28.7 us -> 27.1 us  [swap(): return lax.ppermute(value, axes, [(i, i ^ bits) for i in range(count)])]
    concatenate x1, other arithmetic: 0.92 us -> 0.01 us  [on_block(): local = jnp.concatenate([fresh_queries, fresh_keys, fresh_values], axis=1)]
    eq x1, other arithmetic: 0.79 us -> 0.1 us  [on_block(): root_seen = pool_root[:, :, None] == token_root[None, None, :]]
    reduce_sum x1, other arithmetic: 0.77 us -> 0.09 us  [on_block(): jnp.sum(jnp.where(chosen, per_branch[None, :], 0), axis=1)]
    reduce_sum x1, other arithmetic: 0.74 us -> 0.08 us  [token_branches(): jnp.sum(jnp.where(requests[:, None] == request_ids[None, :], local_branch...]
    pallas_call x5 -> x6, Pallas kernels: 3.17 us -> 3.19 us  [call(): pl.pallas_call(kernel, out_shape=out_shape, in_specs=[vmem] * len(args),...]
  transfers between devices with their start and end apart: 26 -> 24, of which waited for: 14 -> 13; matrix products, arithmetic and copies ran while one was open for 6% -> 1% of each run, Pallas kernels for 3% -> 3%
where the time goes in v13:
time: 60.9 us; the launch traced here: 60.7 us
  starting transfers between devices  27.1 us (44%)
  waiting for transfers between devices  26.4 us (43%)
  Pallas kernels  3.19 us (5%)
  local copies, waits for them, and re-layouts  2.56 us (4%)
  between operations  0.84 us (1%)
    ppermute x24, starting transfers between devices, swap(): return lax.ppermute(value, axes, [(i, i ^ bits) for i in range(count)])  27.1 us
    ppermute x24, waiting for transfers between devices, swap(): return lax.ppermute(value, axes, [(i, i ^ bits) for i in range(count)])  26.4 us
    pallas_call x6, Pallas kernels, call(): pl.pallas_call(kernel, out_shape=out_shape, in_specs=[vmem] * len(args),...  3.19 us
    unnamed x28, local copies, waits for them, and re-layouts  2.56 us
  transfers between devices with their start and end apart: 24, of which 13 were waited for; matrix products, arithmetic and copies ran while one was open for 1% of the time, Pallas kernels for 3%

profile of v13, /device:TPU:0, one launch (start us, length us, event | category | flops | bytes accessed | tf_op | source)
XLA Modules:
  0.0 60.7 jit_solution(1103261010073127000)
XLA Ops:
  0.6 5.1 %collective-permute-start.2 = (bf16[2,64,256]{2,1,0:T(8,128)(2,1)}, bf16[2,64,256]{2,1,0:T(8,128)(2,1)S(1)}, u32[]{:S(2)}, u32[]{:S(2)}) collective-permute-start(bf16[2,64,256]{2,1,0:T(8,128)(2,1)} %refs_0_), channel_id=1, source_target_pairs={{0,24},{8,16},{16,8},{24,0},{1,25},{9,17},{17,9},{25,1},{2,26},{10... | collective-permute-start | bytes 196616 | tf_op jit(solution)/shard_map/ppermute | solution.py:193
  5.8 0.6 %collective-permute-start = (bf16[2,64,256]{2,1,0:T(8,128)(2,1)}, bf16[2,64,256]{2,1,0:T(8,128)(2,1)S(1)}, u32[]{:S(2)}, u32[]{:S(2)}) collective-permute-start(bf16[2,64,256]{2,1,0:T(8,128)(2,1)} %refs_0_), channel_id=1, source_target_pairs={{0,8},{8,0},{16,24},{24,16},{1,9},{9,1},{17,25},{25,17},{2,10},{10... | collective-permute-start | bytes 196616 | tf_op jit(solution)/shard_map/ppermute | solution.py:193
  6.4 1.7 %collective-permute-start.5 = (bf16[256,512]{1,0:T(8,128)(2,1)}, bf16[256,512]{1,0:T(8,128)(2,1)S(1)}, u32[]{:S(2)}, u32[]{:S(2)}) collective-permute-start(bf16[256,512]{1,0:T(8,128)(2,1)} %own_ref.2), channel_id=1, source_target_pairs={{0,4},{4,0},{1,5},{5,1},{2,6},{6,2},{3,7},{7,3},{8,12},{12,8},{9,1... | collective-permute-start | bytes 786440 | tf_op jit(solution)/shard_map/ppermute | solution.py:193
  8.2 0.6 %copy-done.13 = s32[1,4]{1,0:T(1,128)S(1)} copy-done((s32[1,4]{1,0:T(1,128)S(1)}, s32[1,4]{1,0:T(1,128)}, u32[]{:S(2)}) %copy-start.13) | copy-done | bytes 40
  8.9 0.6 copy-done.10
  9.6 0.7 %copy-done.8 = s32[8,32]{1,0:T(8,128)S(1)} copy-done((s32[8,32]{1,0:T(8,128)S(1)}, s32[8,32]{1,0:T(8,128)}, u32[]{:S(2)}) %copy-start.8) | copy-done | bytes 1048
  10.6 0.6 copy-done.5
  11.6 1.6 %collective-permute-start.4 = (bf16[6,64,256]{2,1,0:T(8,128)(2,1)S(1)}, bf16[6,64,256]{2,1,0:T(8,128)(2,1)S(1)}, u32[]{:S(2)}, u32[]{:S(2)}) collective-permute-start(bf16[6,64,256]{2,1,0:T(8,128)(2,1)S(1)} %shard_map.157), channel_id=1, source_target_pairs={{0,4},{4,0},{1,5},{5,1},{2,6},{6,2},{3,7},{7,3},{8,12},{12,8},{9,1... | collective-permute-start | bytes 589832 | tf_op jit(solution)/shard_map/ppermute | solution.py:193
  13.7 6.0 %collective-permute-done.3.refs_1_ = bf16[2,64,256]{2,1,0:T(8,128)(2,1)S(1)} collective-permute-done((bf16[2,64,256]{2,1,0:T(8,128)(2,1)S(1)}, bf16[2,64,256]{2,1,0:T(8,128)(2,1)S(1)}, u32[]{:S(2)}, u32[]{:S(2)}) %collective-permute-start.3) | collective-permute-done | bytes 65568 | tf_op jit(solution)/shard_map/ppermute | solution.py:193
  19.7 1.6 %collective-permute-start.12 = (bf16[256,1024]{1,0:T(8,128)(2,1)S(1)}, bf16[256,1024]{1,0:T(8,128)(2,1)S(1)}, u32[]{:S(2)}, u32[]{:S(2)}) collective-permute-start(bf16[256,1024]{1,0:T(8,128)(2,1)S(1)} %copy-done), channel_id=1, source_target_pairs={{0,4},{4,0},{1,5},{5,1},{2,6},{6,2},{3,7},{7,3},{8,12},{12,8},{9,1... | collective-permute-start | bytes 1572872 | tf_op jit(solution)/shard_map/ppermute | solution.py:193
  21.3 1.3 %shard_map.158 = (bf16[64,512]{1,0:T(8,128)(2,1)}, bf16[64,640]{1,0:T(8,128)(2,1)S(1)}, bf16[64,640]{1,0:T(8,128)(2,1)S(1)}, bf16[64,640]{1,0:T(8,128)(2,1)S(1)}, bf16[64,640]{1,0:T(8,128)(2,1)S(1)}) custom-call(bf16[64,1024]{1,0:T(8,128)(2,1)S(1)} %pad_maximum_fusion.local_ref, bf16[64,2048]{1,0:T(8,128)(2,1)S(1)} %copy-done.1, ...), custom_call_target="tpu_custom_call" | custom-call | flops 67108864 | bytes 1048576 | tf_op jit(solution)/shard_map/pallas_call | solution.py:180
  22.6 2.3 %collective-permute-start.6 = (bf16[64,640]{1,0:T(8,128)(2,1)S(1)}, bf16[64,640]{1,0:T(8,128)(2,1)S(1)}, u32[]{:S(2)}, u32[]{:S(2)}) collective-permute-start(bf16[64,640]{1,0:T(8,128)(2,1)S(1)} %get-tuple-element.52), channel_id=1, source_target_pairs={{0,16},{8,24},{16,0},{24,8},{1,17},{9,25},{17,1},{25,9},{2,18},{10... | collective-permute-start | bytes 245768 | tf_op jit(solution)/shard_map/ppermute | solution.py:193
  24.9 1.5 %collective-permute-start.7 = (bf16[64,640]{1,0:T(8,128)(2,1)S(1)}, bf16[64,640]{1,0:T(8,128)(2,1)S(1)}, u32[]{:S(2)}, u32[]{:S(2)}) collective-permute-start(bf16[64,640]{1,0:T(8,128)(2,1)S(1)} %get-tuple-element.53), channel_id=1, source_target_pairs={{0,24},{8,16},{16,8},{24,0},{1,25},{9,17},{17,9},{25,1},{2,26},{10... | collective-permute-start | bytes 245768 | tf_op jit(solution)/shard_map/ppermute | solution.py:193
  26.7 3.5 %collective-permute-done.6.a2 = bf16[64,640]{1,0:T(8,128)(2,1)S(1)} collective-permute-done((bf16[64,640]{1,0:T(8,128)(2,1)S(1)}, bf16[64,640]{1,0:T(8,128)(2,1)S(1)}, u32[]{:S(2)}, u32[]{:S(2)}) %collective-permute-start.6) | collective-permute-done | bytes 81952 | tf_op jit(solution)/shard_map/ppermute | solution.py:193
  30.1 1.2 %collective-permute-done.7.a3 = bf16[64,640]{1,0:T(8,128)(2,1)S(1)} collective-permute-done((bf16[64,640]{1,0:T(8,128)(2,1)S(1)}, bf16[64,640]{1,0:T(8,128)(2,1)S(1)}, u32[]{:S(2)}, u32[]{:S(2)}) %collective-permute-start.7) | collective-permute-done | bytes 81952 | tf_op jit(solution)/shard_map/ppermute | solution.py:193
  31.3 0.5 collective-permute-done.8.a1
  32.3 1.6 %collective-permute-start.9 = (bf16[256,128]{1,0:T(8,128)(2,1)S(1)}, bf16[256,128]{1,0:T(8,128)(2,1)S(1)}, u32[]{:S(2)}, u32[]{:S(2)}) collective-permute-start(bf16[256,128]{1,0:T(8,128)(2,1)S(1)} %get-tuple-element.57), channel_id=1, source_target_pairs={{0,2},{1,3},{2,0},{3,1},{4,6},{5,7},{6,4},{7,5},{8,10},{9,11},{10,... | collective-permute-start | bytes 196616 | tf_op jit(solution)/shard_map/ppermute | solution.py:193
  33.9 0.6 %collective-permute-start.11 = (bf16[256,128]{1,0:T(8,128)(2,1)S(1)}, bf16[256,128]{1,0:T(8,128)(2,1)S(1)}, u32[]{:S(2)}, u32[]{:S(2)}) collective-permute-start(bf16[256,128]{1,0:T(8,128)(2,1)S(1)} %get-tuple-element.59), channel_id=1, source_target_pairs={{0,1},{1,0},{2,3},{3,2},{4,5},{5,4},{6,7},{7,6},{8,9},{9,8},{10,11... | collective-permute-start | bytes 196616 | tf_op jit(solution)/shard_map/ppermute | solution.py:193
  34.5 2.1 %collective-permute-done.9.r2 = bf16[256,128]{1,0:T(8,128)(2,1)S(1)} collective-permute-done((bf16[256,128]{1,0:T(8,128)(2,1)S(1)}, bf16[256,128]{1,0:T(8,128)(2,1)S(1)}, u32[]{:S(2)}, u32[]{:S(2)}) %collective-permute-start.9) | collective-permute-done | bytes 65568 | tf_op jit(solution)/shard_map/ppermute | solution.py:193
  36.6 1.4 %collective-permute-done.10.r3 = bf16[256,128]{1,0:T(8,128)(2,1)S(1)} collective-permute-done((bf16[256,128]{1,0:T(8,128)(2,1)S(1)}, bf16[256,128]{1,0:T(8,128)(2,1)S(1)}, u32[]{:S(2)}, u32[]{:S(2)}) %collective-permute-start.10) | collective-permute-done | bytes 65568 | tf_op jit(solution)/shard_map/ppermute | solution.py:193
  38.1 0.9 %collective-permute-start.15 = (bf16[256,128]{1,0:T(8,128)(2,1)S(1)}, bf16[256,128]{1,0:T(8,128)(2,1)S(1)}, u32[]{:S(2)}, u32[]{:S(2)}) collective-permute-start(bf16[256,128]{1,0:T(8,128)(2,1)S(1)} %get-tuple-element.65.x0), channel_id=1, source_target_pairs={{0,3},{1,2},{2,1},{3,0},{4,7},{5,6},{6,5},{7,4},{8,11},{9,10},{10,... | collective-permute-start | bytes 196616 | tf_op jit(solution)/shard_map/ppermute | solution.py:193
  39.0 0.7 %collective-permute-start.14 = (bf16[256,128]{1,0:T(8,128)(2,1)S(1)}, bf16[256,128]{1,0:T(8,128)(2,1)S(1)}, u32[]{:S(2)}, u32[]{:S(2)}) collective-permute-start(bf16[256,128]{1,0:T(8,128)(2,1)S(1)} %get-tuple-element.65.x0), channel_id=1, source_target_pairs={{0,2},{1,3},{2,0},{3,1},{4,6},{5,7},{6,4},{7,5},{8,10},{9,11},{10,... | collective-permute-start | bytes 196616 | tf_op jit(solution)/shard_map/ppermute | solution.py:193
  40.0 2.3 %collective-permute-start.16 = (bf16[64,128]{1,0:T(8,128)(2,1)S(1)}, bf16[64,128]{1,0:T(8,128)(2,1)S(1)}, u32[]{:S(2)}, u32[]{:S(2)}) collective-permute-start(bf16[64,128]{1,0:T(8,128)(2,1)S(1)} %get-tuple-element.67), channel_id=1, source_target_pairs={{0,24},{8,16},{16,8},{24,0},{1,25},{9,17},{17,9},{25,1},{2,26},{10... | collective-permute-start | bytes 49160 | tf_op jit(solution)/shard_map/ppermute | solution.py:193
  42.3 3.2 %collective-permute-done.16.t3 = bf16[64,128]{1,0:T(8,128)(2,1)S(1)} collective-permute-done((bf16[64,128]{1,0:T(8,128)(2,1)S(1)}, bf16[64,128]{1,0:T(8,128)(2,1)S(1)}, u32[]{:S(2)}, u32[]{:S(2)}) %collective-permute-start.16) | collective-permute-done | bytes 16416 | tf_op jit(solution)/shard_map/ppermute | solution.py:193
  45.5 1.4 %collective-permute-done.17.t2 = bf16[64,128]{1,0:T(8,128)(2,1)S(1)} collective-permute-done((bf16[64,128]{1,0:T(8,128)(2,1)S(1)}, bf16[64,128]{1,0:T(8,128)(2,1)S(1)}, u32[]{:S(2)}, u32[]{:S(2)}) %collective-permute-start.17) | collective-permute-done | bytes 16416 | tf_op jit(solution)/shard_map/ppermute | solution.py:193
  47.6 2.0 %collective-permute-start.21 = (bf16[64,1024]{1,0:T(8,128)(2,1)S(1)}, bf16[64,1024]{1,0:T(8,128)(2,1)S(1)}, u32[]{:S(2)}, u32[]{:S(2)}) collective-permute-start(bf16[64,1024]{1,0:T(8,128)(2,1)S(1)} %get-tuple-element.70), channel_id=1, source_target_pairs={{0,16},{8,24},{16,0},{24,8},{1,17},{9,25},{17,1},{25,9},{2,18},{10... | collective-permute-start | bytes 393224 | tf_op jit(solution)/shard_map/ppermute | solution.py:193
  49.6 2.3 %collective-permute-start.22 = (bf16[64,1024]{1,0:T(8,128)(2,1)S(1)}, bf16[64,1024]{1,0:T(8,128)(2,1)S(1)}, u32[]{:S(2)}, u32[]{:S(2)}) collective-permute-start(bf16[64,1024]{1,0:T(8,128)(2,1)S(1)} %get-tuple-element.71), channel_id=1, source_target_pairs={{0,24},{8,16},{16,8},{24,0},{1,25},{9,17},{17,9},{25,1},{2,26},{10... | collective-permute-start | bytes 393224 | tf_op jit(solution)/shard_map/ppermute | solution.py:193
  52.0 1.1 %collective-permute-start.19 = (bf16[64,256]{1,0:T(8,128)(2,1)S(1)}, bf16[64,256]{1,0:T(8,128)(2,1)S(1)}, u32[]{:S(2)}, u32[]{:S(2)}) collective-permute-start(bf16[64,256]{1,0:T(8,128)(2,1)S(1)} %get-tuple-element.69.p0), channel_id=1, source_target_pairs={{0,2},{1,3},{2,0},{3,1},{4,6},{5,7},{6,4},{7,5},{8,10},{9,11},{10,... | collective-permute-start | bytes 98312 | tf_op jit(solution)/shard_map/ppermute | solution.py:193
  53.1 2.3 %collective-permute-done.20.p3 = bf16[64,256]{1,0:T(8,128)(2,1)S(1)} collective-permute-done((bf16[64,256]{1,0:T(8,128)(2,1)S(1)}, bf16[64,256]{1,0:T(8,128)(2,1)S(1)}, u32[]{:S(2)}, u32[]{:S(2)}) %collective-permute-start.20) | collective-permute-done | bytes 32800 | tf_op jit(solution)/shard_map/ppermute | solution.py:193
  55.3 0.8 %collective-permute-done.19.p2 = bf16[64,256]{1,0:T(8,128)(2,1)S(1)} collective-permute-done((bf16[64,256]{1,0:T(8,128)(2,1)S(1)}, bf16[64,256]{1,0:T(8,128)(2,1)S(1)}, u32[]{:S(2)}, u32[]{:S(2)}) %collective-permute-start.19) | collective-permute-done | bytes 32800 | tf_op jit(solution)/shard_map/ppermute | solution.py:193
  56.5 3.3 %collective-permute-done.21.y2 = bf16[64,1024]{1,0:T(8,128)(2,1)S(1)} collective-permute-done((bf16[64,1024]{1,0:T(8,128)(2,1)S(1)}, bf16[64,1024]{1,0:T(8,128)(2,1)S(1)}, u32[]{:S(2)}, u32[]{:S(2)}) %collective-permute-start.21) | collective-permute-done | bytes 131104 | tf_op jit(solution)/shard_map/ppermute | solution.py:193
  59.8 0.9 %shard_map.162 = (bf16[64,1024]{1,0:T(8,128)(2,1)}, bf16[64,2048]{1,0:T(8,128)(2,1)}) custom-call(bf16[64,256]{1,0:T(8,128)(2,1)S(1)} %get-tuple-element.69.p0, bf16[64,256]{1,0:T(8,128)(2,1)S(1)} %collective-permute-done.18.p1, bf16[64,256]{1,0:T(8,128)(2,1)S(1)} %collective-permute-done.19.p2, bf16[64,256]{1,0:T(8,128)(2,1)S(1)} %collective-permute-done.20.p3, ...), custom_call_target="tpu_custom_call" | custom-call | bytes 1048576 | tf_op jit(solution)/shard_map/pallas_call | solution.py:180
  (59 shorter events, 3.6 us)
Async XLA Ops:
  0.6 7.4 %copy-start.9 = (s32[1,64]{1,0:T(1,128)S(1)}, s32[1,64]{1,0:T(1,128)}, u32[]{:S(2)}) copy-start(s32[1,64]{1,0:T(1,128)} %param.23) | copy-start | bytes 772
  0.6 10.6 %collective-permute-start.2 = (bf16[2,64,256]{2,1,0:T(8,128)(2,1)}, bf16[2,64,256]{2,1,0:T(8,128)(2,1)S(1)}, u32[]{:S(2)}, u32[]{:S(2)}) collective-permute-start(bf16[2,64,256]{2,1,0:T(8,128)(2,1)} %refs_0_), channel_id=1, source_target_pairs={{0,24},{8,16},{16,8},{24,0},{1,25},{9,17},{17,9},{25,1},{2,26},{10... | collective-permute-start | bytes 196616 | tf_op jit(solution)/shard_map/ppermute | solution.py:193
  5.8 5.8 %collective-permute-start.1 = (bf16[2,64,256]{2,1,0:T(8,128)(2,1)}, bf16[2,64,256]{2,1,0:T(8,128)(2,1)S(1)}, u32[]{:S(2)}, u32[]{:S(2)}) collective-permute-start(bf16[2,64,256]{2,1,0:T(8,128)(2,1)} %refs_0_), channel_id=1, source_target_pairs={{0,16},{8,24},{16,0},{24,8},{1,17},{9,25},{17,1},{25,9},{2,18},{10... | collective-permute-start | bytes 196616 | tf_op jit(solution)/shard_map/ppermute | solution.py:193
  5.8 5.8 %collective-permute-start = (bf16[2,64,256]{2,1,0:T(8,128)(2,1)}, bf16[2,64,256]{2,1,0:T(8,128)(2,1)S(1)}, u32[]{:S(2)}, u32[]{:S(2)}) collective-permute-start(bf16[2,64,256]{2,1,0:T(8,128)(2,1)} %refs_0_), channel_id=1, source_target_pairs={{0,8},{8,0},{16,24},{24,16},{1,9},{9,1},{17,25},{25,17},{2,10},{10... | collective-permute-start | bytes 196616 | tf_op jit(solution)/shard_map/ppermute | solution.py:193
  6.4 13.3 %collective-permute-start.5 = (bf16[256,512]{1,0:T(8,128)(2,1)}, bf16[256,512]{1,0:T(8,128)(2,1)S(1)}, u32[]{:S(2)}, u32[]{:S(2)}) collective-permute-start(bf16[256,512]{1,0:T(8,128)(2,1)} %own_ref.2), channel_id=1, source_target_pairs={{0,4},{4,0},{1,5},{5,1},{2,6},{6,2},{3,7},{7,3},{8,12},{12,8},{9,1... | collective-permute-start | bytes 786440 | tf_op jit(solution)/shard_map/ppermute | solution.py:193
  10.4 0.8 %copy-start.5 = (bf16[64,512]{1,0:T(8,128)(2,1)S(1)}, bf16[64,512]{1,0:T(8,128)(2,1)}, u32[]{:S(2)}) copy-start(bf16[64,512]{1,0:T(8,128)(2,1)} %param.14) | copy-start | bytes 196612
  10.4 0.8 %copy-start.6 = (bf16[64,256]{1,0:T(8,128)(2,1)S(1)}, bf16[64,256]{1,0:T(8,128)(2,1)}, u32[]{:S(2)}) copy-start(bf16[64,256]{1,0:T(8,128)(2,1)} %param.16) | copy-start | bytes 98308
  10.5 9.3 %copy-start = (bf16[256,1024]{1,0:T(8,128)(2,1)S(1)}, bf16[256,1024]{1,0:T(8,128)(2,1)}, u32[]{:S(2)}) copy-start(bf16[256,1024]{1,0:T(8,128)(2,1)} %own_ref.3) | copy-start | bytes 1572868
  11.2 1.9 %copy-start.3 = (bf16[2,64,256]{2,1,0:T(8,128)(2,1)S(1)}, bf16[2,64,256]{2,1,0:T(8,128)(2,1)}, u32[]{:S(2)}) copy-start(bf16[2,64,256]{2,1,0:T(8,128)(2,1)} %refs_0_) | copy-start | bytes 196612
  11.3 10.1 %copy-start.1 = (bf16[64,2048]{1,0:T(8,128)(2,1)S(1)}, bf16[64,2048]{1,0:T(8,128)(2,1)}, u32[]{:S(2)}) copy-start(bf16[64,2048]{1,0:T(8,128)(2,1)} %res_ref.1) | copy-start | bytes 786436
  11.6 20.3 %copy-start.2 = (bf16[256,512]{1,0:T(8,128)(2,1)S(1)}, bf16[256,512]{1,0:T(8,128)(2,1)}, u32[]{:S(2)}) copy-start(bf16[256,512]{1,0:T(8,128)(2,1)} %own_ref.2) | copy-start | bytes 786436
  11.6 8.1 %collective-permute-start.4 = (bf16[6,64,256]{2,1,0:T(8,128)(2,1)S(1)}, bf16[6,64,256]{2,1,0:T(8,128)(2,1)S(1)}, u32[]{:S(2)}, u32[]{:S(2)}) collective-permute-start(bf16[6,64,256]{2,1,0:T(8,128)(2,1)S(1)} %shard_map.157), channel_id=1, source_target_pairs={{0,4},{4,0},{1,5},{5,1},{2,6},{6,2},{3,7},{7,3},{8,12},{12,8},{9,1... | collective-permute-start | bytes 589832 | tf_op jit(solution)/shard_map/ppermute | solution.py:193
  13.2 6.5 %collective-permute-start.3 = (bf16[2,64,256]{2,1,0:T(8,128)(2,1)S(1)}, bf16[2,64,256]{2,1,0:T(8,128)(2,1)S(1)}, u32[]{:S(2)}, u32[]{:S(2)}) collective-permute-start(bf16[2,64,256]{2,1,0:T(8,128)(2,1)S(1)} %copy-done.3), channel_id=1, source_target_pairs={{0,4},{4,0},{1,5},{5,1},{2,6},{6,2},{3,7},{7,3},{8,12},{12,8},{9,1... | collective-permute-start | bytes 196616 | tf_op jit(solution)/shard_map/ppermute | solution.py:193
  19.7 18.3 %collective-permute-start.12 = (bf16[256,1024]{1,0:T(8,128)(2,1)S(1)}, bf16[256,1024]{1,0:T(8,128)(2,1)S(1)}, u32[]{:S(2)}, u32[]{:S(2)}) collective-permute-start(bf16[256,1024]{1,0:T(8,128)(2,1)S(1)} %copy-done), channel_id=1, source_target_pairs={{0,4},{4,0},{1,5},{5,1},{2,6},{6,2},{3,7},{7,3},{8,12},{12,8},{9,1... | collective-permute-start | bytes 1572872 | tf_op jit(solution)/shard_map/ppermute | solution.py:193
  22.6 7.5 %collective-permute-start.6 = (bf16[64,640]{1,0:T(8,128)(2,1)S(1)}, bf16[64,640]{1,0:T(8,128)(2,1)S(1)}, u32[]{:S(2)}, u32[]{:S(2)}) collective-permute-start(bf16[64,640]{1,0:T(8,128)(2,1)S(1)} %get-tuple-element.52), channel_id=1, source_target_pairs={{0,16},{8,24},{16,0},{24,8},{1,17},{9,25},{17,1},{25,9},{2,18},{10... | collective-permute-start | bytes 245768 | tf_op jit(solution)/shard_map/ppermute | solution.py:193
  24.9 6.4 %collective-permute-start.7 = (bf16[64,640]{1,0:T(8,128)(2,1)S(1)}, bf16[64,640]{1,0:T(8,128)(2,1)S(1)}, u32[]{:S(2)}, u32[]{:S(2)}) collective-permute-start(bf16[64,640]{1,0:T(8,128)(2,1)S(1)} %get-tuple-element.53), channel_id=1, source_target_pairs={{0,24},{8,16},{16,8},{24,0},{1,25},{9,17},{17,9},{25,1},{2,26},{10... | collective-permute-start | bytes 245768 | tf_op jit(solution)/shard_map/ppermute | solution.py:193
  26.4 5.5 %collective-permute-start.8 = (bf16[64,640]{1,0:T(8,128)(2,1)S(1)}, bf16[64,640]{1,0:T(8,128)(2,1)S(1)}, u32[]{:S(2)}, u32[]{:S(2)}) collective-permute-start(bf16[64,640]{1,0:T(8,128)(2,1)S(1)} %get-tuple-element.54), channel_id=1, source_target_pairs={{0,8},{8,0},{16,24},{24,16},{1,9},{9,1},{17,25},{25,17},{2,10},{10... | collective-permute-start | bytes 245768 | tf_op jit(solution)/shard_map/ppermute | solution.py:193
  32.3 4.3 %collective-permute-start.9 = (bf16[256,128]{1,0:T(8,128)(2,1)S(1)}, bf16[256,128]{1,0:T(8,128)(2,1)S(1)}, u32[]{:S(2)}, u32[]{:S(2)}) collective-permute-start(bf16[256,128]{1,0:T(8,128)(2,1)S(1)} %get-tuple-element.57), channel_id=1, source_target_pairs={{0,2},{1,3},{2,0},{3,1},{4,6},{5,7},{6,4},{7,5},{8,10},{9,11},{10,... | collective-permute-start | bytes 196616 | tf_op jit(solution)/shard_map/ppermute | solution.py:193
  33.9 4.2 %collective-permute-start.10 = (bf16[256,128]{1,0:T(8,128)(2,1)S(1)}, bf16[256,128]{1,0:T(8,128)(2,1)S(1)}, u32[]{:S(2)}, u32[]{:S(2)}) collective-permute-start(bf16[256,128]{1,0:T(8,128)(2,1)S(1)} %get-tuple-element.58), channel_id=1, source_target_pairs={{0,3},{1,2},{2,1},{3,0},{4,7},{5,6},{6,5},{7,4},{8,11},{9,10},{10,... | collective-permute-start | bytes 196616 | tf_op jit(solution)/shard_map/ppermute | solution.py:193
  33.9 4.2 %collective-permute-start.11 = (bf16[256,128]{1,0:T(8,128)(2,1)S(1)}, bf16[256,128]{1,0:T(8,128)(2,1)S(1)}, u32[]{:S(2)}, u32[]{:S(2)}) collective-permute-start(bf16[256,128]{1,0:T(8,128)(2,1)S(1)} %get-tuple-element.59), channel_id=1, source_target_pairs={{0,1},{1,0},{2,3},{3,2},{4,5},{5,4},{6,7},{7,6},{8,9},{9,8},{10,11... | collective-permute-start | bytes 196616 | tf_op jit(solution)/shard_map/ppermute | solution.py:193
  38.0 9.0 %copy-start.4 = (f32[2048]{0:T(1024)S(1)}, f32[2048]{0:T(1024)}, u32[]{:S(2)}) copy-start(f32[2048]{0:T(1024)} %param.26) | copy-start | bytes 24580
  38.1 8.9 %collective-permute-start.15 = (bf16[256,128]{1,0:T(8,128)(2,1)S(1)}, bf16[256,128]{1,0:T(8,128)(2,1)S(1)}, u32[]{:S(2)}, u32[]{:S(2)}) collective-permute-start(bf16[256,128]{1,0:T(8,128)(2,1)S(1)} %get-tuple-element.65.x0), channel_id=1, source_target_pairs={{0,3},{1,2},{2,1},{3,0},{4,7},{5,6},{6,5},{7,4},{8,11},{9,10},{10,... | collective-permute-start | bytes 196616 | tf_op jit(solution)/shard_map/ppermute | solution.py:193
  39.0 8.0 %collective-permute-start.14 = (bf16[256,128]{1,0:T(8,128)(2,1)S(1)}, bf16[256,128]{1,0:T(8,128)(2,1)S(1)}, u32[]{:S(2)}, u32[]{:S(2)}) collective-permute-start(bf16[256,128]{1,0:T(8,128)(2,1)S(1)} %get-tuple-element.65.x0), channel_id=1, source_target_pairs={{0,2},{1,3},{2,0},{3,1},{4,6},{5,7},{6,4},{7,5},{8,10},{9,11},{10,... | collective-permute-start | bytes 196616 | tf_op jit(solution)/shard_map/ppermute | solution.py:193
  39.7 7.3 %collective-permute-start.13 = (bf16[256,128]{1,0:T(8,128)(2,1)S(1)}, bf16[256,128]{1,0:T(8,128)(2,1)S(1)}, u32[]{:S(2)}, u32[]{:S(2)}) collective-permute-start(bf16[256,128]{1,0:T(8,128)(2,1)S(1)} %get-tuple-element.65.x0), channel_id=1, source_target_pairs={{0,1},{1,0},{2,3},{3,2},{4,5},{5,4},{6,7},{7,6},{8,9},{9,8},{10,11... | collective-permute-start | bytes 196616 | tf_op jit(solution)/shard_map/ppermute | solution.py:193
  40.0 5.5 %collective-permute-start.16 = (bf16[64,128]{1,0:T(8,128)(2,1)S(1)}, bf16[64,128]{1,0:T(8,128)(2,1)S(1)}, u32[]{:S(2)}, u32[]{:S(2)}) collective-permute-start(bf16[64,128]{1,0:T(8,128)(2,1)S(1)} %get-tuple-element.67), channel_id=1, source_target_pairs={{0,24},{8,16},{16,8},{24,0},{1,25},{9,17},{17,9},{25,1},{2,26},{10... | collective-permute-start | bytes 49160 | tf_op jit(solution)/shard_map/ppermute | solution.py:193
  42.3 4.6 %collective-permute-start.17 = (bf16[64,128]{1,0:T(8,128)(2,1)S(1)}, bf16[64,128]{1,0:T(8,128)(2,1)S(1)}, u32[]{:S(2)}, u32[]{:S(2)}) collective-permute-start(bf16[64,128]{1,0:T(8,128)(2,1)S(1)} %get-tuple-element.68), channel_id=1, source_target_pairs={{0,16},{8,24},{16,0},{24,8},{1,17},{9,25},{17,1},{25,9},{2,18},{10... | collective-permute-start | bytes 49160 | tf_op jit(solution)/shard_map/ppermute | solution.py:193
  47.5 12.3 %collective-permute-start.23 = (bf16[64,1536]{1,0:T(8,128)(2,1)S(1)}, bf16[64,1536]{1,0:T(8,128)(2,1)S(1)}, u32[]{:S(2)}, u32[]{:S(2)}) collective-permute-start(bf16[64,1536]{1,0:T(8,128)(2,1)S(1)} %get-tuple-element.72), channel_id=1, source_target_pairs={{0,8},{8,0},{16,24},{24,16},{1,9},{9,1},{17,25},{25,17},{2,10},{10... | collective-permute-start | bytes 589832 | tf_op jit(solution)/shard_map/ppermute | solution.py:193
  47.6 12.2 %collective-permute-start.21 = (bf16[64,1024]{1,0:T(8,128)(2,1)S(1)}, bf16[64,1024]{1,0:T(8,128)(2,1)S(1)}, u32[]{:S(2)}, u32[]{:S(2)}) collective-permute-start(bf16[64,1024]{1,0:T(8,128)(2,1)S(1)} %get-tuple-element.70), channel_id=1, source_target_pairs={{0,16},{8,24},{16,0},{24,8},{1,17},{9,25},{17,1},{25,9},{2,18},{10... | collective-permute-start | bytes 393224 | tf_op jit(solution)/shard_map/ppermute | solution.py:193
  49.6 10.2 %collective-permute-start.22 = (bf16[64,1024]{1,0:T(8,128)(2,1)S(1)}, bf16[64,1024]{1,0:T(8,128)(2,1)S(1)}, u32[]{:S(2)}, u32[]{:S(2)}) collective-permute-start(bf16[64,1024]{1,0:T(8,128)(2,1)S(1)} %get-tuple-element.71), channel_id=1, source_target_pairs={{0,24},{8,16},{16,8},{24,0},{1,25},{9,17},{17,9},{25,1},{2,26},{10... | collective-permute-start | bytes 393224 | tf_op jit(solution)/shard_map/ppermute | solution.py:193
  52.0 3.3 %collective-permute-start.20 = (bf16[64,256]{1,0:T(8,128)(2,1)S(1)}, bf16[64,256]{1,0:T(8,128)(2,1)S(1)}, u32[]{:S(2)}, u32[]{:S(2)}) collective-permute-start(bf16[64,256]{1,0:T(8,128)(2,1)S(1)} %get-tuple-element.69.p0), channel_id=1, source_target_pairs={{0,3},{1,2},{2,1},{3,0},{4,7},{5,6},{6,5},{7,4},{8,11},{9,10},{10,... | collective-permute-start | bytes 98312 | tf_op jit(solution)/shard_map/ppermute | solution.py:193
  52.0 4.1 %collective-permute-start.19 = (bf16[64,256]{1,0:T(8,128)(2,1)S(1)}, bf16[64,256]{1,0:T(8,128)(2,1)S(1)}, u32[]{:S(2)}, u32[]{:S(2)}) collective-permute-start(bf16[64,256]{1,0:T(8,128)(2,1)S(1)} %get-tuple-element.69.p0), channel_id=1, source_target_pairs={{0,2},{1,3},{2,0},{3,1},{4,6},{5,7},{6,4},{7,5},{8,10},{9,11},{10,... | collective-permute-start | bytes 98312 | tf_op jit(solution)/shard_map/ppermute | solution.py:193
  55.3 1.2 %collective-permute-start.18 = (bf16[64,256]{1,0:T(8,128)(2,1)S(1)}, bf16[64,256]{1,0:T(8,128)(2,1)S(1)}, u32[]{:S(2)}, u32[]{:S(2)}) collective-permute-start(bf16[64,256]{1,0:T(8,128)(2,1)S(1)} %get-tuple-element.69.p0), channel_id=1, source_target_pairs={{0,1},{1,0},{2,3},{3,2},{4,5},{5,4},{6,7},{7,6},{8,9},{9,8},{10,11... | collective-permute-start | bytes 98312 | tf_op jit(solution)/shard_map/ppermute | solution.py:193
  (6 other events, 4.2 us)
